TPU v7x, 256 devices: a whole 4x4x8 slice. The times are simulated.
256 devices in a mesh: group: 4 (over x), blk: 64 (over z, y, core).
Axes of the slice: x: 4, y: 4, z: 8, core: 2. Of those that a mesh axis runs over, the one named last changes fastest.
Arguments:
- features: bfloat16 [196608, 512], P(('group', 'blk')), may hold values from -6 to 6
- cotangent: bfloat16 [196608, 512], P(('group', 'blk')), may hold values from -6 to 6
- w_self: bfloat16 [512, 512], replicated, may hold values from -0.25 to 0.25
- w_neigh: bfloat16 [512, 512], replicated, may hold values from -0.25 to 0.25
- tile_src: int32 [256, 8, 2048], P(('group', 'blk')), may hold values from 0 to 767
- tile_dst: int32 [256, 8, 2048], P(('group', 'blk')), may hold values from 0 to 767
- tile_count: int32 [256, 8], P(('group', 'blk')), may hold values from 0 to 2048, as said below
- send_ids: int32 [256, 4, 256], P(('group', 'blk')), may hold values from 0 to 767
- recv_dst: int32 [256, 4, 256], P(('group', 'blk')), may hold values from 0 to 767
- recv_count: int32 [256, 4], P(('group', 'blk')), may hold values from 0 to 256, as said below
Outputs:
- grad_features: float32 [196608, 512], P(('group', 'blk'))
- grad_self: float32 [512, 512], replicated
- grad_neigh: float32 [512, 512], replicated
Inputs may be any that keep to these rules, and one draw needn't show every extreme that they name: `tile_count`: some partition pair has exactly 2048 live slots; pairs differ in load, and some pairs have none. `recv_count`: some partition takes exactly 256 live slots from every group.
All inputs are finite; a program needn't handle non-finite values.
Results may differ from a plain program's by a relative error of at most 0.0027.
Values may be sent and summed in bfloat16 or wider, within the bound.
No kernel may reach another device: no remote copies, remote signals or barrier semaphores. Data moves between devices by JAX's collectives and lax.ppermute only.
A program may use at most 128 MiB of HBM per device.

v0:
```python
import math

import jax
import jax.numpy as jnp
from jax import lax
from jax.sharding import PartitionSpec as P


def passed_along(value, axis, by):
    length = lax.axis_size(axis)
    return lax.ppermute(value, axis, [(i, (i + by) % length) for i in range(length)])


def build_tile(source, target, count, nodes):
    valid = (jnp.arange(source.shape[0], dtype=jnp.int32) < count).astype(jnp.float32)
    tile = jnp.zeros((nodes, nodes), jnp.float32).at[target, source].add(valid)
    return tile.astype(jnp.bfloat16)


def dot_across(tile, values):
    return lax.dot_general(
        tile, values, (((0,), (0,)), ((), ())), preferred_element_type=jnp.float32
    )


def on_device(
    features,
    cotangent,
    w_self,
    w_neigh,
    tile_src,
    tile_dst,
    tile_count,
    send_ids,
    recv_dst,
    recv_count,
):
    nodes, width = features.shape
    offs = tile_src.shape[1]
    ngroup = send_ids.shape[1]
    cap = send_ids.shape[2]
    source = tile_src[0]
    target = tile_dst[0]
    counts = tile_count[0]
    valid = (jnp.arange(source.shape[1], dtype=jnp.int32)[None, :] < counts[:, None]).astype(
        jnp.float32
    )
    tiles = [build_tile(source[s], target[s], counts[s], nodes) for s in range(offs)]
    outgoing = features[send_ids[0].reshape(-1)].reshape(ngroup, cap, width)
    incoming = lax.all_to_all(outgoing, "group", split_axis=0, concat_axis=0, tiled=True)
    bvalid = (jnp.arange(cap, dtype=jnp.int32)[None, :] < recv_count[0][:, None]).astype(
        jnp.float32
    )
    bdst = recv_dst[0].reshape(-1)
    bflat = bvalid.reshape(-1)
    summed = jax.ops.segment_sum(
        incoming.reshape(-1, width).astype(jnp.float32) * bflat[:, None], bdst, num_segments=nodes
    )
    degree = jax.ops.segment_sum(valid.reshape(-1), target.reshape(-1), num_segments=nodes)
    degree = degree + jax.ops.segment_sum(bflat, bdst, num_segments=nodes)
    inverse = 1.0 / jnp.maximum(degree, 1.0)
    summed = summed + jnp.dot(tiles[0], features, preferred_element_type=jnp.float32)
    moving = features
    for s in range(1, offs):
        moving = passed_along(moving, "blk", 1)
        summed = summed + jnp.dot(tiles[s], moving, preferred_element_type=jnp.float32)
    aggregated = (inverse[:, None] * summed).astype(jnp.bfloat16)
    neigh = jnp.dot(cotangent, w_neigh.T, preferred_element_type=jnp.float32)
    scaled = (inverse[:, None] * neigh).astype(jnp.bfloat16)
    back = (
        (scaled[bdst].astype(jnp.float32) * bflat[:, None])
        .astype(jnp.bfloat16)
        .reshape(ngroup, cap, width)
    )
    returned = lax.all_to_all(back, "group", split_axis=0, concat_axis=0, tiled=True)
    total = jnp.dot(cotangent, w_self.T, preferred_element_type=jnp.float32)
    total = total + jax.ops.segment_sum(
        returned.reshape(-1, width).astype(jnp.float32), send_ids[0].reshape(-1), num_segments=nodes
    )
    carried = dot_across(tiles[offs - 1], scaled)
    for s in range(offs - 2, -1, -1):
        carried = passed_along(carried, "blk", -1) + dot_across(tiles[s], scaled)
    total = total + carried
    self_part = dot_across(features, cotangent)
    neigh_part = dot_across(aggregated, cotangent)
    summed_self, summed_neigh = lax.psum((self_part, neigh_part), ("group", "blk"))
    factor = 1.0 / math.sqrt(nodes * lax.axis_size("group") * lax.axis_size("blk"))
    return (total, summed_self * factor, summed_neigh * factor)


def solution(mesh):
    placed = (
        P(("group", "blk"), None),
        P(("group", "blk"), None),
        P(),
        P(),
        P(("group", "blk"), None, None),
        P(("group", "blk"), None, None),
        P(("group", "blk"), None),
        P(("group", "blk"), None, None),
        P(("group", "blk"), None, None),
        P(("group", "blk"), None),
    )
    return jax.shard_map(
        on_device,
        mesh=mesh,
        in_specs=placed,
        out_specs=(P(("group", "blk"), None), P(), P()),
        check_vma=False,
    )
```

profile of v0, /device:TPU:1, one launch (start us, length us, event | category | flops | bytes accessed | tf_op | source)
XLA Modules:
  0.0 705.6 jit_solution(1166809856374998064)
XLA Ops:
  13.8 12.8 %scatter_custom_fusion.4 = f32[589824]{0:T(1024)} fusion(s32[2048]{0:T(1024)S(1)} %broadcast_select_fusion.7, f32[2048]{0:T(1024)S(1)} %fusion.23, f32[]{:T(128)} %constant.5.clone.1), kind=kCustom, calls=%fused_computation.39 | custom fusion | flops 2048 | bytes 2359300
  33.2 113.4 %scatter_custom_fusion = f32[768]{0:T(1024)S(1)} fusion(s32[16384]{0:T(1024)S(1)} %bitcast.111, f32[16384]{0:T(1024)S(1)} %bitcast.112, f32[]{:T(128)} %constant.5.clone.1), kind=kCustom, calls=%fused_computation.121 | custom fusion | flops 16384 | bytes 3076 | tf_op jit(solution)/shard_map/scatter-add | solution.py:59
  146.6 7.6 %scatter_custom_fusion.1 = f32[768]{0:T(1024)S(1)} fusion(s32[1024]{0:T(1024)S(1)} %bitcast.124, f32[1024]{0:T(1024)S(1)} %bitcast.114, f32[]{:T(128)} %constant.5.clone.1), kind=kCustom, calls=%fused_computation.119 | custom fusion | flops 1024 | bytes 3076 | tf_op jit(solution)/shard_map/scatter-add | solution.py:60
  160.8 12.8 %scatter_custom_fusion.5 = f32[589824]{0:T(1024)} fusion(s32[2048]{0:T(1024)S(1)} %broadcast_select_fusion.6, f32[2048]{0:T(1024)S(1)} %fusion.24, f32[]{:T(128)} %constant.5.clone.1), kind=kCustom, calls=%fused_computation.37 | custom fusion | flops 2048 | bytes 2359300
  182.4 6.0 collective-permute-start.1
  189.2 5.3 gather_fusion.1
  194.5 4.2 all-to-all-start.1
  202.7 12.9 %scatter_custom_fusion.6 = f32[589824]{0:T(1024)} fusion(s32[2048]{0:T(1024)} %broadcast_select_fusion.5, f32[2048]{0:T(1024)} %fusion.25, f32[]{:T(128)} %constant.5.clone.1), kind=kCustom, calls=%fused_computation.35 | custom fusion | flops 2048 | bytes 2359808
  228.2 4.6 collective-permute-start.2
  235.2 12.9 %scatter_custom_fusion.7 = f32[589824]{0:T(1024)} fusion(s32[2048]{0:T(1024)} %broadcast_select_fusion.4, f32[2048]{0:T(1024)} %fusion.26, f32[]{:T(128)} %constant.5.clone.1), kind=kCustom, calls=%fused_computation.33 | custom fusion | flops 2048 | bytes 2359808
  264.6 5.0 collective-permute-start.3
  270.9 13.1 %scatter_custom_fusion.8 = f32[589824]{0:T(1024)} fusion(s32[2048]{0:T(1024)} %broadcast_select_fusion.3, f32[2048]{0:T(1024)} %fusion.27, f32[]{:T(128)} %constant.5.clone.1), kind=kCustom, calls=%fused_computation.31 | custom fusion | flops 2048 | bytes 2359808
  290.1 12.9 %scatter_custom_fusion.9 = f32[589824]{0:T(1024)} fusion(s32[2048]{0:T(1024)} %broadcast_select_fusion.2, f32[2048]{0:T(1024)} %fusion.28, f32[]{:T(128)} %constant.5.clone.1), kind=kCustom, calls=%fused_computation.29 | custom fusion | flops 2048 | bytes 2359808
  314.8 5.2 collective-permute-done.10
  323.7 12.9 %scatter_custom_fusion.10 = f32[589824]{0:T(1024)} fusion(s32[2048]{0:T(1024)} %broadcast_select_fusion.1, f32[2048]{0:T(1024)} %fusion.29, f32[]{:T(128)} %constant.5.clone.1), kind=kCustom, calls=%fused_computation.27 | custom fusion | flops 2048 | bytes 2359808
  349.0 8.4 %collective-permute-start.4 = (f32[768,512]{1,0:T(8,128)}, f32[768,512]{1,0:T(8,128)}, u32[]{:S(2)}, u32[]{:S(2)}) collective-permute-start(f32[768,512]{1,0:T(8,128)} %add.282), channel_id=1, source_target_pairs={{0,63},{1,0},{2,1},{3,2},{4,3},{5,4},{6,5},{7,6},{8,7},{9,8},{10,9... | collective-permute-start | bytes 4718600 | tf_op jit(solution)/shard_map/ppermute | solution.py:11
  358.6 13.3 %scatter_custom_fusion.11 = f32[589824]{0:T(1024)} fusion(s32[2048]{0:T(1024)S(1)} %broadcast_select_fusion, f32[2048]{0:T(1024)} %fusion.30, f32[]{:T(128)} %constant.5.clone.1), kind=kCustom, calls=%fused_computation.25 | custom fusion | flops 2048 | bytes 2359808
  396.8 8.4 %collective-permute-start.5 = (f32[768,512]{1,0:T(8,128)}, f32[768,512]{1,0:T(8,128)}, u32[]{:S(2)}, u32[]{:S(2)}) collective-permute-start(f32[768,512]{1,0:T(8,128)} %add.285), channel_id=1, source_target_pairs={{0,63},{1,0},{2,1},{3,2},{4,3},{5,4},{6,5},{7,6},{8,7},{9,8},{10,9... | collective-permute-start | bytes 4718600 | tf_op jit(solution)/shard_map/ppermute | solution.py:11
  409.5 8.2 %scatter_custom_fusion.3 = f32[768,512]{1,0:T(8,128)S(1)} fusion(f32[768,512]{1,0:T(8,128)S(1)} %add_add_fusion, s32[1024]{0:T(1024)} %bitcast.125, bf16[1024,512]{1,0:T(8,128)(2,1)} %bitcast.34, f32[1024]{0:T(1024)S(1)} %bitcast.115), kind=kCustom, calls=%fused_computation.15 | custom fusion | flops 1572864 | bytes 2625536 | tf_op jit(solution)/shard_map/scatter-add | solution.py:56
  423.6 7.8 %collective-permute-start.6 = (f32[768,512]{1,0:T(8,128)}, f32[768,512]{1,0:T(8,128)}, u32[]{:S(2)}, u32[]{:S(2)}) collective-permute-start(f32[768,512]{1,0:T(8,128)} %add.288), channel_id=1, source_target_pairs={{0,63},{1,0},{2,1},{3,2},{4,3},{5,4},{6,5},{7,6},{8,7},{9,8},{10,9... | collective-permute-start | bytes 4718600 | tf_op jit(solution)/shard_map/ppermute | solution.py:11
  431.4 4.0 gather_fusion
  436.8 4.6 all-to-all-start
  445.1 236.5 %all-reduce.3.cloned.1.call-done = (f32[512,512]{1,0:T(8,128)}, f32[512,512]{1,0:T(8,128)}) async-done(((f32[512,512]{1,0:T(8,128)}, f32[512,512]{1,0:T(8,128)}), (f32[512,512]{1,0:T(8,128)}, f32[512,512]{1,0:T(8,128)})) %all-reduce.3.cloned.1.call-update) | async-done | bytes 2097168 | tf_op jit(solution)/shard_map/psum | solution.py:86
  688.9 9.7 %scatter_custom_fusion.2 = f32[768,512]{1,0:T(8,128)} fusion(f32[768,512]{1,0:T(8,128)} %add_add_fusion.1, s32[1024]{0:T(1024)S(1)} %bitcast.126, bf16[1024,512]{1,0:T(8,128)(2,1)} %bitcast.33), kind=kCustom, calls=%fused_computation.16 | custom fusion | flops 1048576 | bytes 2621440 | tf_op jit(solution)/shard_map/scatter-add | solution.py:77
  (196 shorter events, 148.1 us)
Async XLA Ops:
  7.2 147.1 %copy-start = (bf16[768,512]{1,0:T(8,128)(2,1)S(1)}, bf16[768,512]{1,0:T(8,128)(2,1)}, u32[]{:S(2)}) copy-start(bf16[768,512]{1,0:T(8,128)(2,1)} %param.11) | copy-start | bytes 2359300
  9.9 19.5 %copy-start.26 = (s32[2048,1]{0,1:T(1,128)}, s32[2048,1]{0,1:T(1,128)S(1)}, u32[]{:S(2)}) copy-start(s32[2048,1]{0,1:T(1,128)S(1)} %get-tuple-element.16) | copy-start | bytes 24580
  9.9 19.5 %copy-start.27 = (s32[2048,1]{0,1:T(1,128)}, s32[2048,1]{0,1:T(1,128)S(1)}, u32[]{:S(2)}) copy-start(s32[2048,1]{0,1:T(1,128)S(1)} %get-tuple-element.17) | copy-start | bytes 24580
  29.5 124.8 %copy-start.43 = (bf16[512,512]{1,0:T(8,128)(2,1)S(1)}, bf16[512,512]{1,0:T(8,128)(2,1)}, u32[]{:S(2)}) copy-start(bf16[512,512]{1,0:T(8,128)(2,1)} %param.13) | copy-start | bytes 1572868
  32.1 124.7 %copy-start.2 = (bf16[768,768]{1,0:T(8,128)(2,1)}, bf16[768,768]{1,0:T(8,128)(2,1)S(1)}, u32[]{:S(2)}) copy-start(bf16[768,768]{1,0:T(8,128)(2,1)S(1)} %reshape.638) | copy-start | bytes 3538948
  32.3 114.3 %copy-start.41 = (s32[1,2,4,128]{3,1,2,0:T(2,128)}, s32[1,2,4,128]{3,1,2,0:T(2,128)S(1)}, u32[]{:S(2)}) copy-start(s32[1,2,4,128]{3,1,2,0:T(2,128)S(1)} %copy.15) | copy-start | bytes 12292
  33.2 121.1 %copy-start.34 = (f32[1,2,4,128]{3,1,2,0:T(2,128)}, f32[1,2,4,128]{3,1,2,0:T(2,128)S(1)}, u32[]{:S(2)}) copy-start(f32[1,2,4,128]{3,1,2,0:T(2,128)S(1)} %copy.16) | copy-start | bytes 12292
  156.9 22.1 %collective-permute-start = (f32[768,512]{1,0:T(8,128)}, f32[768,512]{1,0:T(8,128)}, u32[]{:S(2)}, u32[]{:S(2)}) collective-permute-start(f32[768,512]{1,0:T(8,128)} %fusion.39), channel_id=1, source_target_pairs={{0,63},{1,0},{2,1},{3,2},{4,3},{5,4},{6,5},{7,6},{8,7},{9,8},{10,9... | collective-permute-start | bytes 4718600 | tf_op jit(solution)/shard_map/ppermute | solution.py:11
  182.4 42.9 %collective-permute-start.1 = (f32[768,512]{1,0:T(8,128)}, f32[768,512]{1,0:T(8,128)}, u32[]{:S(2)}, u32[]{:S(2)}) collective-permute-start(f32[768,512]{1,0:T(8,128)} %convolution_add_fusion), channel_id=1, source_target_pairs={{0,63},{1,0},{2,1},{3,2},{4,3},{5,4},{6,5},{7,6},{8,7},{9,8},{10,9... | collective-permute-start | bytes 4718600 | tf_op jit(solution)/shard_map/ppermute | solution.py:11
  188.4 45.6 %collective-permute-start.7 = (bf16[768,512]{1,0:T(8,128)(2,1)S(1)}, bf16[768,512]{1,0:T(8,128)(2,1)}, u32[]{:S(2)}, u32[]{:S(2)}) collective-permute-start(bf16[768,512]{1,0:T(8,128)(2,1)S(1)} %copy-done.1), channel_id=1, source_target_pairs={{0,1},{1,2},{2,3},{3,4},{4,5},{5,6},{6,7},{7,8},{8,9},{9,10},{10,1... | collective-permute-start | bytes 2359304 | tf_op jit(solution)/shard_map/ppermute | solution.py:11
  194.5 214.9 %all-to-all-start.1 = ((bf16[4,256,512]{2,1,0:T(8,128)(2,1)}), bf16[4,256,512]{2,1,0:T(8,128)(2,1)}, u32[]{:S(2)}, u32[]{:S(2)}) async-start(bf16[4,256,512]{2,1,0:T(8,128)(2,1)} %bitcast.108), calls=%async_computation.1 | async-start | bytes 2097152 | tf_op jit(solution)/shard_map/all_to_all | solution.py:50
  198.8 482.8 %all-reduce.3.cloned.1.call-start = ((), (), s32[]{:S(2)}) async-start(), calls=%async_computation.2 | async-start | bytes 4194304 | tf_op jit(solution)/shard_map/psum | solution.py:86
  228.2 33.5 %collective-permute-start.2 = (f32[768,512]{1,0:T(8,128)}, f32[768,512]{1,0:T(8,128)}, u32[]{:S(2)}, u32[]{:S(2)}) collective-permute-start(f32[768,512]{1,0:T(8,128)} %add.276), channel_id=1, source_target_pairs={{0,63},{1,0},{2,1},{3,2},{4,3},{5,4},{6,5},{7,6},{8,7},{9,8},{10,9... | collective-permute-start | bytes 4718600 | tf_op jit(solution)/shard_map/ppermute | solution.py:11
  234.0 24.4 %collective-permute-start.8 = (bf16[768,512]{1,0:T(8,128)(2,1)}, bf16[768,512]{1,0:T(8,128)(2,1)}, u32[]{:S(2)}, u32[]{:S(2)}) collective-permute-start(bf16[768,512]{1,0:T(8,128)(2,1)} %collective-permute-done.7), channel_id=1, source_target_pairs={{0,1},{1,2},{2,3},{3,4},{4,5},{5,6},{6,7},{7,8},{8,9},{9,10},{10,1... | collective-permute-start | bytes 2359304 | tf_op jit(solution)/shard_map/ppermute | solution.py:11
  258.4 52.4 %collective-permute-start.9 = (bf16[768,512]{1,0:T(8,128)(2,1)}, bf16[768,512]{1,0:T(8,128)(2,1)}, u32[]{:S(2)}, u32[]{:S(2)}) collective-permute-start(bf16[768,512]{1,0:T(8,128)(2,1)} %collective-permute-done.8), channel_id=1, source_target_pairs={{0,1},{1,2},{2,3},{3,4},{4,5},{5,6},{6,7},{7,8},{8,9},{9,10},{10,1... | collective-permute-start | bytes 2359304 | tf_op jit(solution)/shard_map/ppermute | solution.py:11
  264.6 81.4 %collective-permute-start.3 = (f32[768,512]{1,0:T(8,128)}, f32[768,512]{1,0:T(8,128)}, u32[]{:S(2)}, u32[]{:S(2)}) collective-permute-start(f32[768,512]{1,0:T(8,128)} %add.279), channel_id=1, source_target_pairs={{0,63},{1,0},{2,1},{3,2},{4,3},{5,4},{6,5},{7,6},{8,7},{9,8},{10,9... | collective-permute-start | bytes 4718600 | tf_op jit(solution)/shard_map/ppermute | solution.py:11
  310.8 9.3 %collective-permute-start.10 = (bf16[768,512]{1,0:T(8,128)(2,1)}, bf16[768,512]{1,0:T(8,128)(2,1)}, u32[]{:S(2)}, u32[]{:S(2)}) collective-permute-start(bf16[768,512]{1,0:T(8,128)(2,1)} %collective-permute-done.9), channel_id=1, source_target_pairs={{0,1},{1,2},{2,3},{3,4},{4,5},{5,6},{6,7},{7,8},{8,9},{9,10},{10,1... | collective-permute-start | bytes 2359304 | tf_op jit(solution)/shard_map/ppermute | solution.py:11
  320.0 60.2 %collective-permute-start.11 = (bf16[768,512]{1,0:T(8,128)(2,1)}, bf16[768,512]{1,0:T(8,128)(2,1)}, u32[]{:S(2)}, u32[]{:S(2)}) collective-permute-start(bf16[768,512]{1,0:T(8,128)(2,1)} %collective-permute-done.10), channel_id=1, source_target_pairs={{0,1},{1,2},{2,3},{3,4},{4,5},{5,6},{6,7},{7,8},{8,9},{9,10},{10,1... | collective-permute-start | bytes 2359304 | tf_op jit(solution)/shard_map/ppermute | solution.py:11
  349.0 44.8 %collective-permute-start.4 = (f32[768,512]{1,0:T(8,128)}, f32[768,512]{1,0:T(8,128)}, u32[]{:S(2)}, u32[]{:S(2)}) collective-permute-start(f32[768,512]{1,0:T(8,128)} %add.282), channel_id=1, source_target_pairs={{0,63},{1,0},{2,1},{3,2},{4,3},{5,4},{6,5},{7,6},{8,7},{9,8},{10,9... | collective-permute-start | bytes 4718600 | tf_op jit(solution)/shard_map/ppermute | solution.py:11
  380.2 9.3 %collective-permute-start.12 = (bf16[768,512]{1,0:T(8,128)(2,1)}, bf16[768,512]{1,0:T(8,128)(2,1)S(1)}, u32[]{:S(2)}, u32[]{:S(2)}) collective-permute-start(bf16[768,512]{1,0:T(8,128)(2,1)} %collective-permute-done.11), channel_id=1, source_target_pairs={{0,1},{1,2},{2,3},{3,4},{4,5},{5,6},{6,7},{7,8},{8,9},{9,10},{10,1... | collective-permute-start | bytes 2359304 | tf_op jit(solution)/shard_map/ppermute | solution.py:11
  389.5 18.4 %collective-permute-start.13 = (bf16[768,512]{1,0:T(8,128)(2,1)S(1)}, bf16[768,512]{1,0:T(8,128)(2,1)S(1)}, u32[]{:S(2)}, u32[]{:S(2)}) collective-permute-start(bf16[768,512]{1,0:T(8,128)(2,1)S(1)} %collective-permute-done.12), channel_id=1, source_target_pairs={{0,1},{1,2},{2,3},{3,4},{4,5},{5,6},{6,7},{7,8},{8,9},{9,10},{10,1... | collective-permute-start | bytes 2359304 | tf_op jit(solution)/shard_map/ppermute | solution.py:11
  396.8 22.6 %collective-permute-start.5 = (f32[768,512]{1,0:T(8,128)}, f32[768,512]{1,0:T(8,128)}, u32[]{:S(2)}, u32[]{:S(2)}) collective-permute-start(f32[768,512]{1,0:T(8,128)} %add.285), channel_id=1, source_target_pairs={{0,63},{1,0},{2,1},{3,2},{4,3},{5,4},{6,5},{7,6},{8,7},{9,8},{10,9... | collective-permute-start | bytes 4718600 | tf_op jit(solution)/shard_map/ppermute | solution.py:11
  423.6 261.4 %collective-permute-start.6 = (f32[768,512]{1,0:T(8,128)}, f32[768,512]{1,0:T(8,128)}, u32[]{:S(2)}, u32[]{:S(2)}) collective-permute-start(f32[768,512]{1,0:T(8,128)} %add.288), channel_id=1, source_target_pairs={{0,63},{1,0},{2,1},{3,2},{4,3},{5,4},{6,5},{7,6},{8,7},{9,8},{10,9... | collective-permute-start | bytes 4718600 | tf_op jit(solution)/shard_map/ppermute | solution.py:11
  436.8 252.1 %all-to-all-start = ((bf16[4,256,512]{2,1,0:T(8,128)(2,1)}), bf16[4,256,512]{2,1,0:T(8,128)(2,1)}, u32[]{:S(2)}, u32[]{:S(2)}) async-start(bf16[4,256,512]{2,1,0:T(8,128)(2,1)} %fusion.3), calls=%async_computation | async-start | bytes 2097152 | tf_op jit(solution)/shard_map/all_to_all | solution.py:75
  (37 other events, 265.3 us)
Sparse Core Ops, SparseCore 0:
  419.5 262.0 all-reduce.2
where the time goes:
time: 717 us; the launch traced here: 706 us
  other arithmetic  311 us (43%)
  waiting for transfers between devices  245 us (34%)
  starting transfers between devices  57.3 us (8%)
  local copies, waits for them, and re-layouts  39 us (5%)
  matrix products  38 us (5%)
  between operations  15 us (2%)
    psum x1, waiting for transfers between devices, on_device(): lax.psum((self_part, neigh_part), ('group', 'blk'))  237 us
    unnamed x22, other arithmetic  115 us
    scatter-add x1, other arithmetic, on_device(): jax.ops.segment_sum(valid.reshape(-1), target.reshape(-1), num_segments=n...  113 us
    ppermute x14, starting transfers between devices, passed_along(): lax.ppermute(value, axis, [(i, (i + by) % length) for i in range(length)])  48.5 us
    convert_element_type x8, local copies, waits for them, and re-layouts, build_tile(): return tile.astype(jnp.bfloat16)  25.3 us
    convert_element_type x8, other arithmetic, build_tile(): return tile.astype(jnp.bfloat16)  22.4 us
    dot_general x10, matrix products, dot_across(): lax.dot_general(tile, values, (((0,), (0,)), ((), ())), preferred_element...  22 us
    add x5, other arithmetic, on_device(): carried = passed_along(carried, 'blk', -1) + dot_across(tiles[s], scaled)  14.6 us
  transfers between devices with their start and end apart: 17, of which 3 were waited for; matrix products, arithmetic and copies ran while one was open for 32% of the time, Pallas kernels for 0%

commit v1 on v0

v1 whole, which is shorter than its diff:
```python
import math

import jax
import jax.numpy as jnp
from jax import lax
from jax.experimental import pallas as pl
from jax.experimental.pallas import tpu as pltpu
from jax.sharding import PartitionSpec as P

F32 = jnp.float32
BF16 = jnp.bfloat16
I32 = jnp.int32
CHUNK = 1024
ALONG = (((1,), (1,)), ((), ()))
DOWN = (((0,), (0,)), ((), ()))


def dot(a, b, dims=(((1,), (0,)), ((), ()))):
    return lax.dot_general(a, b, dims, preferred_element_type=F32)


def hot(rows, ids):
    spots = lax.broadcasted_iota(I32, (rows, ids.shape[1]), 0)
    return jnp.where(spots == ids, 1.0, 0.0).astype(BF16)


def small_hot(rows, ids):
    spots = lax.broadcasted_iota(jnp.int16, (rows, ids.shape[1]), 0)
    ones = jnp.where(spots == ids.astype(jnp.int16), jnp.ones((), BF16), jnp.zeros((), BF16))
    return ones.astype(jnp.float8_e4m3fn)


def prepare(tcount, rcount, tdst, rdst, rcol, cot, x_out, rows_out):
    nodes = cot.shape[0]
    offs, ept = tdst.shape[1], tdst.shape[2]
    ngroup, cap = rdst.shape[1], rdst.shape[2]
    counts = jnp.zeros((32, 32), F32)

    def tally(ids, live):
        ids = jnp.where(lax.broadcasted_iota(I32, ids.shape, 1) < live, ids, 1023)
        return dot(hot(32, ids >> 5), hot(32, ids & 31), ALONG)

    for s in range(offs):
        counts = counts + tally(tdst[0, s : s + 1, :], tcount[0, s])
    for g in range(ngroup):
        counts = counts + tally(rdst[0, g : g + 1, :], rcount[0, g])
    upper = jnp.floor(counts * (1.0 / 128.0))
    lower = counts - upper * 128.0
    node = lax.broadcasted_iota(I32, (nodes, 32), 0)
    lane = lax.broadcasted_iota(I32, (nodes, 32), 1)
    pick = jnp.where((node >> 5) == lane, 1.0, 0.0).astype(BF16)
    spread = dot(pick, upper.astype(BF16)) * 128.0 + dot(pick, lower.astype(BF16))
    degree = jnp.sum(jnp.where((node & 31) == lane, spread, 0.0), axis=1, keepdims=True)
    inverse = 1.0 / jnp.maximum(degree, 1.0)
    x = (inverse * cot[...].astype(F32)).astype(BF16)
    x_out[...] = x
    slot = lax.broadcasted_iota(I32, (cap, 1), 0)
    along = lax.broadcasted_iota(I32, (cap, nodes), 1)
    for g in range(ngroup):
        ids = jnp.where(slot < rcount[0, g], rcol[:, g : g + 1], -1)
        pickrow = jnp.where(along == ids, 1.0, 0.0).astype(BF16)
        rows_out[g] = dot(pickrow, x).astype(BF16)


def build(chunks, edges, tile_out, acc):
    s = pl.program_id(0)
    nodes = acc.shape[0]
    acc[...] = jnp.zeros_like(acc)

    def step(i, carry):
        packed = edges[0, :, pl.ds(pl.multiple_of(i * CHUNK, CHUNK), CHUNK)]
        acc[...] += dot(small_hot(nodes, packed >> 10), small_hot(nodes, packed & 1023), ALONG)
        return carry

    lax.fori_loop(0, chunks[s], step, 0)
    tile_out[0] = acc[...].astype(BF16)


def first_sum(tile0, tile1, x0, x1, ids, rows, out):
    i = pl.program_id(0)
    block = out.shape[0]
    total = dot(tile0[0], x0[...]) + dot(tile1[0], x1[...])
    spots = lax.broadcasted_iota(I32, (block, ids.shape[1]), 0) + i * block
    sel = jnp.where(spots == ids[...], 1.0, 0.0).astype(BF16)
    out[...] = total + dot(sel, rows[...])


def middle_sum(before, t0, t1, t2, t3, x0, x1, x2, x3, out):
    total = before[...] + dot(t0[0], x0[...]) + dot(t1[0], x1[...])
    out[...] = total + dot(t2[0], x2[...]) + dot(t3[0], x3[...])


def last_sum(before, t0, t1, x0, x1, feats, out, grad):
    i = pl.program_id(0)
    total = before[...] + dot(t0[0], x0[...]) + dot(t1[0], x1[...])
    out[...] = total
    top = total.astype(BF16)
    rest = (total - top.astype(F32)).astype(BF16)
    part = dot(feats[...], top, DOWN) + dot(feats[...], rest, DOWN)

    @pl.when(i == 0)
    def _():
        grad[...] = part

    @pl.when(i > 0)
    def _():
        grad[...] += part


def finish(summed, cot, w_self, w_neigh, out):
    total = summed[...]
    top = total.astype(BF16)
    rest = (total - top.astype(F32)).astype(BF16)
    out[...] = (
        dot(cot[...], w_self[...], ALONG)
        + dot(top, w_neigh[...], ALONG)
        + dot(rest, w_neigh[...], ALONG)
    )


BLOCK = 256
LIMIT = 40 * 1024 * 1024


def params():
    return pltpu.CompilerParams(vmem_limit_bytes=LIMIT)


def whole(shape):
    return pl.BlockSpec(shape, lambda i: (0,) * len(shape))


def tile_spec(slot, nodes):
    return pl.BlockSpec((1, BLOCK, nodes), lambda i: (slot, i, 0))


def row_spec(width):
    return pl.BlockSpec((BLOCK, width), lambda i: (i, 0))


def estimate(macs, moved):
    return pl.CostEstimate(flops=2 * macs, bytes_accessed=moved, transcendentals=0)


def run_prepare(tile_count, recv_count, tile_dst, recv_dst, recv_col, cotangent):
    nodes, width = cotangent.shape
    ngroup, cap = recv_dst.shape[1], recv_dst.shape[2]
    vm = pl.BlockSpec(memory_space=pltpu.VMEM)
    sm = pl.BlockSpec(memory_space=pltpu.SMEM)
    return pl.pallas_call(
        prepare,
        out_shape=(
            jax.ShapeDtypeStruct((nodes, width), BF16),
            jax.ShapeDtypeStruct((ngroup, cap, width), BF16),
        ),
        in_specs=[sm, sm, vm, vm, vm, vm],
        out_specs=(vm, vm),
        compiler_params=params(),
        cost_estimate=estimate(ngroup * cap * nodes * width, 4 * nodes * width),
        name="prepare",
    )(tile_count, recv_count, tile_dst, recv_dst, recv_col, cotangent)


def run_build(chunks, edges, nodes):
    slots, _, ept = edges.shape
    return pl.pallas_call(
        build,
        grid_spec=pltpu.PrefetchScalarGridSpec(
            num_scalar_prefetch=1,
            grid=(slots,),
            in_specs=[pl.BlockSpec((1, 1, ept), lambda s, c: (s, 0, 0))],
            out_specs=pl.BlockSpec((1, nodes, nodes), lambda s, c: (s, 0, 0)),
            scratch_shapes=[pltpu.VMEM((nodes, nodes), F32)],
        ),
        out_shape=jax.ShapeDtypeStruct((slots, nodes, nodes), BF16),
        compiler_params=params(),
        cost_estimate=estimate(slots * nodes * nodes * ept, 2 * slots * nodes * nodes),
        name="build",
    )(chunks, edges)


def run_first(tiles, x0, x1, ids, rows):
    nodes, width = x0.shape
    return pl.pallas_call(
        first_sum,
        grid=(nodes // BLOCK,),
        in_specs=[
            tile_spec(0, nodes),
            tile_spec(1, nodes),
            whole(x0.shape),
            whole(x1.shape),
            whole(ids.shape),
            whole(rows.shape),
        ],
        out_specs=row_spec(width),
        out_shape=jax.ShapeDtypeStruct((nodes, width), F32),
        compiler_params=params(),
        cost_estimate=estimate(3 * nodes * nodes * width, 12 * nodes * width),
        name="first_sum",
    )(tiles, tiles, x0, x1, ids, rows)


def run_middle(before, tiles, slots, xs):
    nodes, width = before.shape
    return pl.pallas_call(
        middle_sum,
        grid=(nodes // BLOCK,),
        in_specs=[row_spec(width)]
        + [tile_spec(s, nodes) for s in slots]
        + [whole(x.shape) for x in xs],
        out_specs=row_spec(width),
        out_shape=jax.ShapeDtypeStruct((nodes, width), F32),
        compiler_params=params(),
        cost_estimate=estimate(4 * nodes * nodes * width, 16 * nodes * width),
        name="middle_sum",
    )(before, *([tiles] * len(slots)), *xs)


def run_last(before, tiles, slots, xs, features):
    nodes, width = before.shape
    return pl.pallas_call(
        last_sum,
        grid=(nodes // BLOCK,),
        in_specs=[row_spec(width)]
        + [tile_spec(s, nodes) for s in slots]
        + [whole(x.shape) for x in xs]
        + [row_spec(width)],
        out_specs=(row_spec(width), whole((width, width))),
        out_shape=(
            jax.ShapeDtypeStruct((nodes, width), F32),
            jax.ShapeDtypeStruct((width, width), F32),
        ),
        compiler_params=params(),
        cost_estimate=estimate(3 * nodes * nodes * width, 16 * nodes * width),
        name="last_sum",
    )(before, *([tiles] * len(slots)), *xs, features)


def run_finish(summed, cotangent, w_self, w_neigh):
    nodes, width = summed.shape
    return pl.pallas_call(
        finish,
        grid=(nodes // BLOCK,),
        in_specs=[row_spec(width), row_spec(width), whole(w_self.shape), whole(w_neigh.shape)],
        out_specs=row_spec(width),
        out_shape=jax.ShapeDtypeStruct((nodes, width), F32),
        compiler_params=params(),
        cost_estimate=estimate(3 * nodes * width * width, 10 * nodes * width),
        name="finish",
    )(summed, cotangent, w_self, w_neigh)


def moved(value, perm):
    return lax.ppermute(value, "blk", perm)


def pick_piece(pieces, index):
    out = pieces[0]
    for k in range(1, len(pieces)):
        out = jnp.where(index == k, pieces[k], out)
    return out


def scatter_sum(value, index, count, send):
    size = value.shape[0] // count
    pieces = [value[k * size : (k + 1) * size] for k in range(count)]
    total = pick_piece(pieces, index)
    for s in range(1, count):
        total = total + send(pick_piece(pieces, (index + s) % count), s)
    return total


def gather_all(piece, index, count, send):
    held = [piece] + [send(piece, s) for s in range(1, count)]
    return jnp.concatenate(
        [pick_piece(held, (index - k) % count) for k in range(count)], axis=0
    )


def on_device(
    features,
    cotangent,
    w_self,
    w_neigh,
    tile_src,
    tile_dst,
    tile_count,
    send_ids,
    recv_dst,
    recv_count,
):
    nodes, width = features.shape
    offs, ept = tile_src.shape[1], tile_src.shape[2]
    ngroup, cap = send_ids.shape[1], send_ids.shape[2]
    nblk = lax.axis_size("blk")
    gi = lax.axis_index("group")
    bi = lax.axis_index("blk")
    core = bi % 2
    ypos = (bi // 2) % 4
    ring = range(nblk)
    swap = [(i, i ^ 1) for i in ring]

    def yshift(by):
        return [(i, (i // 8) * 8 + (i % 8 + 2 * by) % 8) for i in ring]

    def zflip(k):
        return [(i, (i // 8 ^ k) * 8 + i % 8) for i in ring]

    live = lax.broadcasted_iota(I32, (offs, ept), 1) < tile_count[0][:, None]
    lists = jnp.where(live, tile_src[0] * 1024 + tile_dst[0], -1)[:, None, :]
    mine = [lists[s] for s in range(offs)]
    slots = [None] * offs
    slots[0] = mine[0]
    slots[1] = moved(
        jnp.where(core == 1, mine[1], mine[7]),
        [(i, (i - 1 if i % 2 else i - 7) % nblk) for i in ring],
    )
    for j in (1, 2, 3):
        slots[2 * j] = moved(mine[2 * j], [(i, (i - 2 * j) % nblk) for i in ring])
        slots[2 * j + 1] = moved(
            jnp.where(core == 1, mine[2 * j + 1], mine[2 * j - 1]),
            [(i, (i - 2 * j + 1 - 2 * (i % 2)) % nblk) for i in ring],
        )
    edges = jnp.stack(slots)
    chunks = jnp.sum((edges[:, 0, ::CHUNK] >= 0).astype(I32), axis=1)

    x, rows = run_prepare(
        tile_count, recv_count, tile_dst, recv_dst, recv_dst[0].T, cotangent
    )
    returned = lax.all_to_all(rows, "group", split_axis=0, concat_axis=0, tiled=True)
    far = moved(x, [(i, (i - 8) % nblk) for i in ring])
    one = moved(jnp.where(ypos == 0, far, x), yshift(-1))
    three = moved(jnp.where(ypos == 3, x, far), yshift(1))
    side = moved(jnp.where(core == 1, x, far), swap)
    two = moved(
        jnp.where(core == 0, one, three),
        [(i, (i - 2 if i % 2 == 0 else i + 2) % nblk) for i in ring],
    )
    one_b = moved(one, swap)
    three_b = moved(three, swap)
    two_b = moved(two, swap)

    tiles = run_build(chunks, edges, nodes)
    summed = run_first(
        tiles, x, side, send_ids.reshape(1, ngroup * cap), returned.reshape(ngroup * cap, width)
    )
    summed = run_middle(summed, tiles, (2, 3, 6, 7), (one, one_b, three, three_b))
    summed, neigh_part = run_last(summed, tiles, (4, 5), (two, two_b), features)
    total = run_finish(summed, cotangent, w_self, w_neigh)
    self_part = dot(features, cotangent, DOWN)

    grads = jnp.stack([self_part, neigh_part]).reshape(2, width, width)
    grads = grads.transpose(1, 0, 2)

    def over_core(v, s):
        return moved(v, swap)

    def over_group(v, s):
        return lax.ppermute(v, "group", [(i, (i + s) % ngroup) for i in range(ngroup)])

    def over_y(v, s):
        return moved(v, yshift(s))

    grads = scatter_sum(grads, core, 2, over_core)
    grads = scatter_sum(grads, gi, ngroup, over_group)
    grads = scatter_sum(grads, ypos, 4, over_y)
    for k in (1, 2, 4):
        grads = grads + moved(grads, zflip(k))
    grads = gather_all(grads, ypos, 4, over_y)
    grads = gather_all(grads, gi, ngroup, over_group)
    grads = gather_all(grads, core, 2, over_core)
    factor = 1.0 / math.sqrt(nodes * lax.axis_size("group") * nblk)
    return (total, grads[:, 0] * factor, grads[:, 1] * factor)


def solution(mesh):
    both = ("group", "blk")
    placed = (
        P(both, None),
        P(both, None),
        P(),
        P(),
        P(both, None, None),
        P(both, None, None),
        P(both, None),
        P(both, None, None),
        P(both, None, None),
        P(both, None),
    )
    return jax.shard_map(
        on_device,
        mesh=mesh,
        in_specs=placed,
        out_specs=(P(both, None), P(), P()),
        check_vma=False,
    )
```

time: 717 us -> 210 us (0.29); the launches traced: 706 us -> 208 us
  other arithmetic: 311 us -> 19.3 us
  waiting for transfers between devices: 245 us -> 77.9 us
  matrix products: 38 us -> 1.57 us
  Pallas kernels: 0 us -> 27.2 us
  local copies, waits for them, and re-layouts: 39 us -> 18.6 us
  between operations: 15 us -> 1 us
    psum x1 -> x0, waiting for transfers between devices: 237 us -> none  [on_device(): lax.psum((self_part, neigh_part), ('group', 'blk'))]
    scatter-add x4 -> x0, other arithmetic: 139 us -> none  [the longest x1 113 us: on_device(): jax.ops.segment_sum(valid.reshape(-1), target.reshape(-1), num_segments=n...]
    unnamed x22 -> x0, other arithmetic: 115 us -> none
    ppermute x14 -> x32, waiting for transfers between devices: 8.5 us -> 77.9 us  [the longest x26 56.3 us: moved(): return lax.ppermute(value, 'blk', perm)]
    dot_general x20 -> x1, matrix products: 38 us -> 1.57 us  [dot(): return lax.dot_general(a, b, dims, preferred_element_type=F32)]
    convert_element_type x18 -> x0, other arithmetic: 33.3 us -> none  [the longest x8 22.4 us: build_tile(): return tile.astype(jnp.bfloat16)]
    pallas_call x0 -> x6, Pallas kernels: none -> 27.2 us  [the longest x1 7.3 us: run_build(): pl.pallas_call(build, grid_spec=pltpu.PrefetchScalarGridSpec(num_scalar_p...]
    convert_element_type x8 -> x0, local copies, waits for them, and re-layouts: 25.3 us -> none  [build_tile(): return tile.astype(jnp.bfloat16)]
  transfers between devices with their start and end apart: 17 -> 33, of which waited for: 3 -> 18; matrix products, arithmetic and copies ran while one was open for 32% -> 4% of each run, Pallas kernels for 0% -> 11%
where the time goes in v1:
time: 210 us; the launch traced here: 208 us
  waiting for transfers between devices  77.9 us (37%)
  starting transfers between devices  62.8 us (30%)
  Pallas kernels  27.2 us (13%)
  other arithmetic  19.3 us (9%)
  local copies, waits for them, and re-layouts  18.6 us (9%)
    ppermute x26, waiting for transfers between devices, moved(): return lax.ppermute(value, 'blk', perm)  56.3 us
    ppermute x26, starting transfers between devices, moved(): return lax.ppermute(value, 'blk', perm)  50 us
    ppermute x6, waiting for transfers between devices, over_group(): lax.ppermute(v, 'group', [(i, (i + s) % ngroup) for i in range(ngroup)])  21.6 us
    unnamed x63, local copies, waits for them, and re-layouts  18.5 us
    ppermute x6, starting transfers between devices, over_group(): lax.ppermute(v, 'group', [(i, (i + s) % ngroup) for i in range(ngroup)])  8.68 us
    select_n x9, other arithmetic, pick_piece(): out = jnp.where(index == k, pieces[k], out)  7.55 us
    pallas_call x1, Pallas kernels, run_build(): pl.pallas_call(build, grid_spec=pltpu.PrefetchScalarGridSpec(num_scalar_p...  7.3 us
    pallas_call x1, Pallas kernels, run_middle(): pl.pallas_call(middle_sum, grid=(nodes // BLOCK,), in_specs=[row_spec(wid...  5.34 us
  transfers between devices with their start and end apart: 33, of which 18 were waited for; matrix products, arithmetic and copies ran while one was open for 4% of the time, Pallas kernels for 11%

profile of v1, /device:TPU:1, one launch (start us, length us, event | category | flops | bytes accessed | tf_op | source)
XLA Modules:
  0.0 208.4 jit_solution(7382635929719104233)
XLA Ops:
  2.3 3.2 %collective-permute-start = (s32[1,2048]{1,0:T(1,128)}, s32[1,2048]{1,0:T(1,128)}, u32[]{:S(2)}, u32[]{:S(2)}) collective-permute-start(s32[1,2048]{1,0:T(1,128)} %get-tuple-element.36), channel_id=1, source_target_pairs={{0,57},{1,0},{2,59},{3,2},{4,61},{5,4},{6,63},{7,6},{8,1},{9,8},{1... | collective-permute-start | bytes 24584 | tf_op jit(solution)/shard_map/ppermute | solution.py:254
  5.5 6.3 %collective-permute-start.1 = (s32[1,2048]{1,0:T(1,128)}, s32[1,2048]{1,0:T(1,128)}, u32[]{:S(2)}, u32[]{:S(2)}) collective-permute-start(s32[1,2048]{1,0:T(1,128)} %get-tuple-element.33), channel_id=1, source_target_pairs={{0,62},{1,63},{2,0},{3,1},{4,2},{5,3},{6,4},{7,5},{8,6},{9,7},{10,... | collective-permute-start | bytes 24584 | tf_op jit(solution)/shard_map/ppermute | solution.py:254
  12.9 3.3 %collective-permute-start.4 = (s32[1,2048]{1,0:T(1,128)}, s32[1,2048]{1,0:T(1,128)}, u32[]{:S(2)}, u32[]{:S(2)}) collective-permute-start(s32[1,2048]{1,0:T(1,128)} %get-tuple-element.35), channel_id=1, source_target_pairs={{0,61},{1,60},{2,63},{3,62},{4,1},{5,0},{6,3},{7,2},{8,5},{9,4},{1... | collective-permute-start | bytes 24584 | tf_op jit(solution)/shard_map/ppermute | solution.py:254
  21.0 3.0 %prepare.1 = (bf16[768,512]{1,0:T(8,128)(2,1)S(1)}, bf16[4,256,512]{2,1,0:T(8,128)(2,1)S(1)}) custom-call(s32[1,8]{1,0:T(1,128)S(1)} %copy-done.14, s32[1,4]{1,0:T(1,128)S(1)} %copy-done.15, s32[1,8,2048]{2,1,0:T(8,128)S(1)} %copy-done.12, s32[1,4,256]{2,1,0:T(4,128)S(1)} %copy-done.13, s32[256,4]{1,0:T(8,128)S(1)} %bitcast.40, bf16[768,512]{1,0:T(8,128)(2,1)S(1)} %copy-done.3), custom_call_target="tpu_custom_call" | custom-call | flops 805306368 | bytes 1572864 | tf_op jit(solution)/shard_map/prepare/pallas_call | solution.py:150
  25.0 4.1 %all-to-all-start = ((bf16[4,256,512]{2,1,0:T(8,128)(2,1)}), bf16[4,256,512]{2,1,0:T(8,128)(2,1)S(1)}, u32[]{:S(2)}, u32[]{:S(2)}) async-start(bf16[4,256,512]{2,1,0:T(8,128)(2,1)} %copy-done.9), calls=%async_computation | async-start | bytes 2097152 | tf_op jit(solution)/shard_map/all_to_all | solution.py:330
  35.7 15.5 %collective-permute-done.7 = bf16[768,512]{1,0:T(8,128)(2,1)S(1)} collective-permute-done((bf16[768,512]{1,0:T(8,128)(2,1)S(1)}, bf16[768,512]{1,0:T(8,128)(2,1)S(1)}, u32[]{:S(2)}, u32[]{:S(2)}) %collective-permute-start.7) | collective-permute-done | bytes 786464 | tf_op jit(solution)/shard_map/ppermute | solution.py:254
  55.1 14.2 %collective-permute-done.9.x0 = bf16[768,512]{1,0:T(8,128)(2,1)S(1)} collective-permute-done((bf16[768,512]{1,0:T(8,128)(2,1)S(1)}, bf16[768,512]{1,0:T(8,128)(2,1)S(1)}, u32[]{:S(2)}, u32[]{:S(2)}) %collective-permute-start.9) | collective-permute-done | bytes 786464 | tf_op jit(solution)/shard_map/ppermute | solution.py:254
  72.9 6.0 %collective-permute-start.8 = (bf16[768,512]{1,0:T(8,128)(2,1)}, bf16[768,512]{1,0:T(8,128)(2,1)}, u32[]{:S(2)}, u32[]{:S(2)}) collective-permute-start(bf16[768,512]{1,0:T(8,128)(2,1)} %get-tuple-element.17), channel_id=1, source_target_pairs={{0,1},{1,0},{2,3},{3,2},{4,5},{5,4},{6,7},{7,6},{8,9},{9,8},{10,11... | collective-permute-start | bytes 2359304 | tf_op jit(solution)/shard_map/ppermute | solution.py:254
  79.4 7.6 %collective-permute-done.13.x0 = bf16[768,512]{1,0:T(8,128)(2,1)} collective-permute-done((bf16[768,512]{1,0:T(8,128)(2,1)}, bf16[768,512]{1,0:T(8,128)(2,1)}, u32[]{:S(2)}, u32[]{:S(2)}) %collective-permute-start.13) | collective-permute-done | bytes 786464 | tf_op jit(solution)/shard_map/ppermute | solution.py:254
  88.3 7.3 %build.1.tile0.tile1.t0.t1.t2.t3 = bf16[8,768,768]{2,1,0:T(8,128)(2,1)S(1)} custom-call(s32[8]{0:T(128)S(1)} %fusion.5.chunks, s32[8,1,2048]{2,1,0:T(1,128)S(1)} %constant_dynamic-update-slice_fusion.edges), custom_call_target="tpu_custom_call" | custom-call | flops 19327352832 | bytes 9437184 | tf_op jit(solution)/shard_map/build/pallas_call | solution.py:166
  95.6 3.7 %copy-done = bf16[8,768,768]{2,1,0:T(8,128)(2,1)} copy-done((bf16[8,768,768]{2,1,0:T(8,128)(2,1)}, bf16[8,768,768]{2,1,0:T(8,128)(2,1)S(1)}, u32[]{:S(2)}) %copy-start) | copy-done | bytes 9437208
  99.3 3.7 %copy-done.1 = bf16[8,768,768]{2,1,0:T(8,128)(2,1)S(1)} copy-done((bf16[8,768,768]{2,1,0:T(8,128)(2,1)S(1)}, bf16[8,768,768]{2,1,0:T(8,128)(2,1)}, u32[]{:S(2)}) %copy-start.1) | copy-done | bytes 9437208
  103.0 3.8 %first_sum.1.before = f32[768,512]{1,0:T(8,128)S(1)} custom-call(bf16[8,768,768]{2,1,0:T(8,128)(2,1)S(1)} %copy-done.1, bf16[8,768,768]{2,1,0:T(8,128)(2,1)S(1)} %copy-done.1, bf16[768,512]{1,0:T(8,128)(2,1)S(1)} %get-tuple-element.7.x0, bf16[768,512]{1,0:T(8,128)(2,1)} %collective-permute-done.8.x1, s32[1,1024]{1,0:T(1,128)S(1)} %bitcast.41, ...), custom_call_target="tpu_custom_call" | custom-call | flops 1811939328 | bytes 4718592 | tf_op jit(solution)/shard_map/first_sum/pallas_call | solution.py:184
  106.8 5.3 %middle_sum.1.before = f32[768,512]{1,0:T(8,128)S(1)} custom-call(f32[768,512]{1,0:T(8,128)S(1)} %first_sum.1.before, bf16[8,768,768]{2,1,0:T(8,128)(2,1)} %copy-done, bf16[8,768,768]{2,1,0:T(8,128)(2,1)} %copy-done, bf16[8,768,768]{2,1,0:T(8,128)(2,1)} %copy-done, bf16[8,768,768]{2,1,0:T(8,128)(2,1)} %copy-done, bf16[768,512]{1,0:T(8,128)(2,1)S(1)} %copy-done.6, ...), custom_call_target="tpu_custom_call" | custom-call | flops 2415919104 | bytes 6291456 | tf_op jit(solution)/shard_map/middle_sum/pallas_call | solution.py:205
  112.2 5.0 %last_sum.1 = (f32[768,512]{1,0:T(8,128)S(1)}, f32[512,512]{1,0:T(8,128)S(1)}) custom-call(f32[768,512]{1,0:T(8,128)S(1)} %middle_sum.1.before, bf16[8,768,768]{2,1,0:T(8,128)(2,1)} %copy-done, bf16[8,768,768]{2,1,0:T(8,128)(2,1)} %copy-done, bf16[768,512]{1,0:T(8,128)(2,1)} %collective-permute-done.13.x0, bf16[768,512]{1,0:T(8,128)(2,1)} %collective-permute-done.14.x1, ...), custom_call_target="tpu_custom_call" | custom-call | flops 1811939328 | bytes 6291456 | tf_op jit(solution)/shard_map/last_sum/pallas_call | solution.py:221
  127.1 5.5 %collective-permute-start.18 = (f32[64,2,512]{2,0,1:T(8,128)S(1)}, f32[64,2,512]{2,0,1:T(8,128)S(1)}, u32[]{:S(2)}, u32[]{:S(2)}) collective-permute-start(f32[64,2,512]{2,0,1:T(8,128)S(1)} %select_select_fusion.4), channel_id=1, source_target_pairs={{0,192},{64,0},{128,64},{192,128},{1,193},{65,1},{129,65},{193,129... | collective-permute-start | bytes 786440 | tf_op jit(solution)/shard_map/ppermute | solution.py:359
  134.9 8.7 %collective-permute-done.18 = f32[64,2,512]{2,0,1:T(8,128)S(1)} collective-permute-done((f32[64,2,512]{2,0,1:T(8,128)S(1)}, f32[64,2,512]{2,0,1:T(8,128)S(1)}, u32[]{:S(2)}, u32[]{:S(2)}) %collective-permute-start.18) | collective-permute-done | bytes 262176 | tf_op jit(solution)/shard_map/ppermute | solution.py:359
  143.6 4.9 %collective-permute-done.16 = f32[64,2,512]{2,0,1:T(8,128)S(1)} collective-permute-done((f32[64,2,512]{2,0,1:T(8,128)}, f32[64,2,512]{2,0,1:T(8,128)S(1)}, u32[]{:S(2)}, u32[]{:S(2)}) %collective-permute-start.16) | collective-permute-done | bytes 262176 | tf_op jit(solution)/shard_map/ppermute | solution.py:359
  153.2 3.5 %collective-permute-done.20 = f32[16,2,512]{2,0,1:T(8,128)S(1)} collective-permute-done((f32[16,2,512]{2,0,1:T(8,128)S(1)}, f32[16,2,512]{2,0,1:T(8,128)S(1)}, u32[]{:S(2)}, u32[]{:S(2)}) %collective-permute-start.20) | collective-permute-done | bytes 65568 | tf_op jit(solution)/shard_map/ppermute | solution.py:254
  164.4 5.4 %collective-permute-start.24 = (f32[16,2,512]{2,0,1:T(8,128)S(1)}, f32[16,2,512]{2,0,1:T(8,128)S(1)}, u32[]{:S(2)}, u32[]{:S(2)}) collective-permute-start(f32[16,2,512]{2,0,1:T(8,128)S(1)} %add.152), channel_id=1, source_target_pairs={{0,32},{1,33},{2,34},{3,35},{4,36},{5,37},{6,38},{7,39},{8,40},{9,... | collective-permute-start | bytes 196616 | tf_op jit(solution)/shard_map/ppermute | solution.py:254
  180.6 3.8 %collective-permute-done.28 = f32[64,2,512]{2,0,1:T(8,128)S(1)} collective-permute-done((f32[64,2,512]{2,0,1:T(8,128)S(1)}, f32[64,2,512]{2,0,1:T(8,128)S(1)}, u32[]{:S(2)}, u32[]{:S(2)}) %collective-permute-start.28) | collective-permute-done | bytes 262176 | tf_op jit(solution)/shard_map/ppermute | solution.py:359
  185.8 2.8 %collective-permute-done.30 = f32[64,2,512]{2,0,1:T(8,128)} collective-permute-done((f32[64,2,512]{2,0,1:T(8,128)S(1)}, f32[64,2,512]{2,0,1:T(8,128)}, u32[]{:S(2)}, u32[]{:S(2)}) %collective-permute-start.30) | collective-permute-done | bytes 262176 | tf_op jit(solution)/shard_map/ppermute | solution.py:359
  192.7 8.8 %collective-permute-start.31 = (f32[256,2,512]{2,0,1:T(8,128)}, f32[256,2,512]{2,0,1:T(8,128)}, u32[]{:S(2)}, u32[]{:S(2)}) collective-permute-start(f32[256,2,512]{2,0,1:T(8,128)} %pad_maximum_fusion.1), channel_id=1, source_target_pairs={{0,1},{1,0},{2,3},{3,2},{4,5},{5,4},{6,7},{7,6},{8,9},{9,8},{10,11... | collective-permute-start | bytes 3145736 | tf_op jit(solution)/shard_map/ppermute | solution.py:254
  202.6 2.8 %finish.1 = f32[768,512]{1,0:T(8,128)} custom-call(f32[768,512]{1,0:T(8,128)S(1)} %get-tuple-element.9.summed, bf16[768,512]{1,0:T(8,128)(2,1)S(1)} %copy-done.4, bf16[512,512]{1,0:T(8,128)(2,1)S(1)} %copy-done.10, bf16[512,512]{1,0:T(8,128)(2,1)S(1)} %copy-done.11), custom_call_target="tpu_custom_call" | custom-call | flops 1207959552 | bytes 3932160 | tf_op jit(solution)/shard_map/finish/pallas_call | solution.py:241
  (138 shorter events, 69.3 us)
Async XLA Ops:
  2.3 28.5 %collective-permute-start = (s32[1,2048]{1,0:T(1,128)}, s32[1,2048]{1,0:T(1,128)}, u32[]{:S(2)}, u32[]{:S(2)}) collective-permute-start(s32[1,2048]{1,0:T(1,128)} %get-tuple-element.36), channel_id=1, source_target_pairs={{0,57},{1,0},{2,59},{3,2},{4,61},{5,4},{6,63},{7,6},{8,1},{9,8},{1... | collective-permute-start | bytes 24584 | tf_op jit(solution)/shard_map/ppermute | solution.py:254
  5.5 27.5 %collective-permute-start.1 = (s32[1,2048]{1,0:T(1,128)}, s32[1,2048]{1,0:T(1,128)}, u32[]{:S(2)}, u32[]{:S(2)}) collective-permute-start(s32[1,2048]{1,0:T(1,128)} %get-tuple-element.33), channel_id=1, source_target_pairs={{0,62},{1,63},{2,0},{3,1},{4,2},{5,3},{6,4},{7,5},{8,6},{9,7},{10,... | collective-permute-start | bytes 24584 | tf_op jit(solution)/shard_map/ppermute | solution.py:254
  11.8 22.7 %collective-permute-start.2 = (s32[1,2048]{1,0:T(1,128)}, s32[1,2048]{1,0:T(1,128)}, u32[]{:S(2)}, u32[]{:S(2)}) collective-permute-start(s32[1,2048]{1,0:T(1,128)} %get-tuple-element.34), channel_id=1, source_target_pairs={{0,63},{1,62},{2,1},{3,0},{4,3},{5,2},{6,5},{7,4},{8,7},{9,6},{10,... | collective-permute-start | bytes 24584 | tf_op jit(solution)/shard_map/ppermute | solution.py:254
  12.9 40.4 %collective-permute-start.3 = (s32[1,2048]{1,0:T(1,128)}, s32[1,2048]{1,0:T(1,128)}, u32[]{:S(2)}, u32[]{:S(2)}) collective-permute-start(s32[1,2048]{1,0:T(1,128)} %get-tuple-element.32), channel_id=1, source_target_pairs={{0,60},{1,61},{2,62},{3,63},{4,0},{5,1},{6,2},{7,3},{8,4},{9,5},{1... | collective-permute-start | bytes 24584 | tf_op jit(solution)/shard_map/ppermute | solution.py:254
  12.9 41.5 %collective-permute-start.4 = (s32[1,2048]{1,0:T(1,128)}, s32[1,2048]{1,0:T(1,128)}, u32[]{:S(2)}, u32[]{:S(2)}) collective-permute-start(s32[1,2048]{1,0:T(1,128)} %get-tuple-element.35), channel_id=1, source_target_pairs={{0,61},{1,60},{2,63},{3,62},{4,1},{5,0},{6,3},{7,2},{8,5},{9,4},{1... | collective-permute-start | bytes 24584 | tf_op jit(solution)/shard_map/ppermute | solution.py:254
  25.0 74.2 %all-to-all-start = ((bf16[4,256,512]{2,1,0:T(8,128)(2,1)}), bf16[4,256,512]{2,1,0:T(8,128)(2,1)S(1)}, u32[]{:S(2)}, u32[]{:S(2)}) async-start(bf16[4,256,512]{2,1,0:T(8,128)(2,1)} %copy-done.9), calls=%async_computation | async-start | bytes 2097152 | tf_op jit(solution)/shard_map/all_to_all | solution.py:330
  30.8 41.7 %collective-permute-start.5 = (s32[1,2048]{1,0:T(1,128)}, s32[1,2048]{1,0:T(1,128)S(1)}, u32[]{:S(2)}, u32[]{:S(2)}) collective-permute-start(s32[1,2048]{1,0:T(1,128)} %get-tuple-element.31), channel_id=1, source_target_pairs={{0,58},{1,59},{2,60},{3,61},{4,62},{5,63},{6,0},{7,1},{8,2},{9,3},... | collective-permute-start | bytes 24584 | tf_op jit(solution)/shard_map/ppermute | solution.py:254
  33.0 18.1 %collective-permute-start.7 = (bf16[768,512]{1,0:T(8,128)(2,1)S(1)}, bf16[768,512]{1,0:T(8,128)(2,1)S(1)}, u32[]{:S(2)}, u32[]{:S(2)}) collective-permute-start(bf16[768,512]{1,0:T(8,128)(2,1)S(1)} %get-tuple-element.7.x0), channel_id=1, source_target_pairs={{0,56},{1,57},{2,58},{3,59},{4,60},{5,61},{6,62},{7,63},{8,0},{9,1... | collective-permute-start | bytes 2359304 | tf_op jit(solution)/shard_map/ppermute | solution.py:254
  34.5 38.1 %collective-permute-start.6 = (s32[1,2048]{1,0:T(1,128)S(1)}, s32[1,2048]{1,0:T(1,128)S(1)}, u32[]{:S(2)}, u32[]{:S(2)}) collective-permute-start(s32[1,2048]{1,0:T(1,128)S(1)} %get-tuple-element.30), channel_id=1, source_target_pairs={{0,59},{1,58},{2,61},{3,60},{4,63},{5,62},{6,1},{7,0},{8,3},{9,2},... | collective-permute-start | bytes 24584 | tf_op jit(solution)/shard_map/ppermute | solution.py:254
  52.2 17.1 %collective-permute-start.9 = (bf16[768,512]{1,0:T(8,128)(2,1)S(1)}, bf16[768,512]{1,0:T(8,128)(2,1)S(1)}, u32[]{:S(2)}, u32[]{:S(2)}) collective-permute-start(bf16[768,512]{1,0:T(8,128)(2,1)S(1)} %get-tuple-element.16), channel_id=1, source_target_pairs={{0,6},{1,7},{2,0},{3,1},{4,2},{5,3},{6,4},{7,5},{8,14},{9,15},{10,... | collective-permute-start | bytes 2359304 | tf_op jit(solution)/shard_map/ppermute | solution.py:254
  53.3 18.0 %collective-permute-start.11 = (bf16[768,512]{1,0:T(8,128)(2,1)S(1)}, bf16[768,512]{1,0:T(8,128)(2,1)S(1)}, u32[]{:S(2)}, u32[]{:S(2)}) collective-permute-start(bf16[768,512]{1,0:T(8,128)(2,1)S(1)} %get-tuple-element.15), channel_id=1, source_target_pairs={{0,2},{1,3},{2,4},{3,5},{4,6},{5,7},{6,0},{7,1},{8,10},{9,11},{10,... | collective-permute-start | bytes 2359304 | tf_op jit(solution)/shard_map/ppermute | solution.py:254
  72.5 14.5 %collective-permute-start.13 = (bf16[768,512]{1,0:T(8,128)(2,1)}, bf16[768,512]{1,0:T(8,128)(2,1)}, u32[]{:S(2)}, u32[]{:S(2)}) collective-permute-start(bf16[768,512]{1,0:T(8,128)(2,1)} %broadcast_select_fusion), channel_id=1, source_target_pairs={{0,62},{1,3},{2,0},{3,5},{4,2},{5,7},{6,4},{7,9},{8,6},{9,11},{10,... | collective-permute-start | bytes 2359304 | tf_op jit(solution)/shard_map/ppermute | solution.py:254
  72.9 26.4 %collective-permute-start.8 = (bf16[768,512]{1,0:T(8,128)(2,1)}, bf16[768,512]{1,0:T(8,128)(2,1)}, u32[]{:S(2)}, u32[]{:S(2)}) collective-permute-start(bf16[768,512]{1,0:T(8,128)(2,1)} %get-tuple-element.17), channel_id=1, source_target_pairs={{0,1},{1,0},{2,3},{3,2},{4,5},{5,4},{6,7},{7,6},{8,9},{9,8},{10,11... | collective-permute-start | bytes 2359304 | tf_op jit(solution)/shard_map/ppermute | solution.py:254
  78.9 27.8 %collective-permute-start.10 = (bf16[768,512]{1,0:T(8,128)(2,1)}, bf16[768,512]{1,0:T(8,128)(2,1)}, u32[]{:S(2)}, u32[]{:S(2)}) collective-permute-start(bf16[768,512]{1,0:T(8,128)(2,1)} %copy-done.5), channel_id=1, source_target_pairs={{0,1},{1,0},{2,3},{3,2},{4,5},{5,4},{6,7},{7,6},{8,9},{9,8},{10,11... | collective-permute-start | bytes 2359304 | tf_op jit(solution)/shard_map/ppermute | solution.py:254
  79.0 27.7 %collective-permute-start.12 = (bf16[768,512]{1,0:T(8,128)(2,1)}, bf16[768,512]{1,0:T(8,128)(2,1)}, u32[]{:S(2)}, u32[]{:S(2)}) collective-permute-start(bf16[768,512]{1,0:T(8,128)(2,1)} %copy-done.7), channel_id=1, source_target_pairs={{0,1},{1,0},{2,3},{3,2},{4,5},{5,4},{6,7},{7,6},{8,9},{9,8},{10,11... | collective-permute-start | bytes 2359304 | tf_op jit(solution)/shard_map/ppermute | solution.py:254
  87.0 25.2 %collective-permute-start.14 = (bf16[768,512]{1,0:T(8,128)(2,1)}, bf16[768,512]{1,0:T(8,128)(2,1)}, u32[]{:S(2)}, u32[]{:S(2)}) collective-permute-start(bf16[768,512]{1,0:T(8,128)(2,1)} %collective-permute-done.13.x0), channel_id=1, source_target_pairs={{0,1},{1,0},{2,3},{3,2},{4,5},{5,4},{6,7},{7,6},{8,9},{9,8},{10,11... | collective-permute-start | bytes 2359304 | tf_op jit(solution)/shard_map/ppermute | solution.py:254
  127.1 16.4 %collective-permute-start.18 = (f32[64,2,512]{2,0,1:T(8,128)S(1)}, f32[64,2,512]{2,0,1:T(8,128)S(1)}, u32[]{:S(2)}, u32[]{:S(2)}) collective-permute-start(f32[64,2,512]{2,0,1:T(8,128)S(1)} %select_select_fusion.4), channel_id=1, source_target_pairs={{0,192},{64,0},{128,64},{192,128},{1,193},{65,1},{129,65},{193,129... | collective-permute-start | bytes 786440 | tf_op jit(solution)/shard_map/ppermute | solution.py:359
  133.5 10.0 %collective-permute-start.17 = (f32[64,2,512]{2,0,1:T(8,128)}, f32[64,2,512]{2,0,1:T(8,128)S(1)}, u32[]{:S(2)}, u32[]{:S(2)}) collective-permute-start(f32[64,2,512]{2,0,1:T(8,128)} %get-tuple-element.23), channel_id=1, source_target_pairs={{0,128},{64,192},{128,0},{192,64},{1,129},{65,193},{129,1},{193,65... | collective-permute-start | bytes 786440 | tf_op jit(solution)/shard_map/ppermute | solution.py:359
  133.5 15.0 %collective-permute-start.16 = (f32[64,2,512]{2,0,1:T(8,128)}, f32[64,2,512]{2,0,1:T(8,128)S(1)}, u32[]{:S(2)}, u32[]{:S(2)}) collective-permute-start(f32[64,2,512]{2,0,1:T(8,128)} %get-tuple-element.22), channel_id=1, source_target_pairs={{0,64},{64,128},{128,192},{192,0},{1,65},{65,129},{129,193},{193,1... | collective-permute-start | bytes 786440 | tf_op jit(solution)/shard_map/ppermute | solution.py:359
  164.4 7.2 %collective-permute-start.24 = (f32[16,2,512]{2,0,1:T(8,128)S(1)}, f32[16,2,512]{2,0,1:T(8,128)S(1)}, u32[]{:S(2)}, u32[]{:S(2)}) collective-permute-start(f32[16,2,512]{2,0,1:T(8,128)S(1)} %add.152), channel_id=1, source_target_pairs={{0,32},{1,33},{2,34},{3,35},{4,36},{5,37},{6,38},{7,39},{8,40},{9,... | collective-permute-start | bytes 196616 | tf_op jit(solution)/shard_map/ppermute | solution.py:254
  178.8 5.6 %collective-permute-start.28 = (f32[64,2,512]{2,0,1:T(8,128)S(1)}, f32[64,2,512]{2,0,1:T(8,128)S(1)}, u32[]{:S(2)}, u32[]{:S(2)}) collective-permute-start(f32[64,2,512]{2,0,1:T(8,128)S(1)} %pad_maximum_fusion.2), channel_id=1, source_target_pairs={{0,192},{64,0},{128,64},{192,128},{1,193},{65,1},{129,65},{193,129... | collective-permute-start | bytes 786440 | tf_op jit(solution)/shard_map/ppermute | solution.py:359
  179.0 6.9 %collective-permute-start.29 = (f32[64,2,512]{2,0,1:T(8,128)S(1)}, f32[64,2,512]{2,0,1:T(8,128)S(1)}, u32[]{:S(2)}, u32[]{:S(2)}) collective-permute-start(f32[64,2,512]{2,0,1:T(8,128)S(1)} %pad_maximum_fusion.2), channel_id=1, source_target_pairs={{0,128},{64,192},{128,0},{192,64},{1,129},{65,193},{129,1},{193,65... | collective-permute-start | bytes 786440 | tf_op jit(solution)/shard_map/ppermute | solution.py:359
  179.9 8.8 %collective-permute-start.30 = (f32[64,2,512]{2,0,1:T(8,128)S(1)}, f32[64,2,512]{2,0,1:T(8,128)}, u32[]{:S(2)}, u32[]{:S(2)}) collective-permute-start(f32[64,2,512]{2,0,1:T(8,128)S(1)} %pad_maximum_fusion.2), channel_id=1, source_target_pairs={{0,64},{64,128},{128,192},{192,0},{1,65},{65,129},{129,193},{193,1... | collective-permute-start | bytes 786440 | tf_op jit(solution)/shard_map/ppermute | solution.py:359
  192.7 12.7 %collective-permute-start.31 = (f32[256,2,512]{2,0,1:T(8,128)}, f32[256,2,512]{2,0,1:T(8,128)}, u32[]{:S(2)}, u32[]{:S(2)}) collective-permute-start(f32[256,2,512]{2,0,1:T(8,128)} %pad_maximum_fusion.1), channel_id=1, source_target_pairs={{0,1},{1,0},{2,3},{3,2},{4,5},{5,4},{6,7},{7,6},{8,9},{9,8},{10,11... | collective-permute-start | bytes 3145736 | tf_op jit(solution)/shard_map/ppermute | solution.py:254
  (36 other events, 134.5 us)

commit v2 on v1

v2 whole, which is shorter than its diff:
```python
import math

import jax
import jax.numpy as jnp
from jax import lax
from jax.experimental import pallas as pl
from jax.experimental.pallas import tpu as pltpu
from jax.sharding import PartitionSpec as P

F32 = jnp.float32
BF16 = jnp.bfloat16
I32 = jnp.int32
CHUNK = 1024
ALONG = (((1,), (1,)), ((), ()))
DOWN = (((0,), (0,)), ((), ()))


def dot(a, b, dims=(((1,), (0,)), ((), ()))):
    return lax.dot_general(a, b, dims, preferred_element_type=F32)


def hot(rows, ids):
    spots = lax.broadcasted_iota(I32, (rows, ids.shape[1]), 0)
    return jnp.where(spots == ids, 1.0, 0.0).astype(BF16)


def small_hot(rows, ids):
    spots = lax.broadcasted_iota(jnp.int16, (rows, ids.shape[1]), 0)
    ones = jnp.where(spots == ids.astype(jnp.int16), jnp.ones((), BF16), jnp.zeros((), BF16))
    return ones.astype(jnp.float8_e4m3fn)


def prepare(tcount, rcount, tsrc, tdst, rdst, cot, x_out, rows_out, own, first, pair1, pair2, pair3):
    nodes = cot.shape[0]
    offs, ept = tdst.shape[1], tdst.shape[2]
    ngroup, cap = rdst.shape[1], rdst.shape[2]
    odd = lax.rem(lax.axis_index("blk"), 2) == 1
    slot = lax.broadcasted_iota(I32, (1, ept), 1)
    counts = jnp.zeros((32, 32), F32)
    lists = []
    for s in range(offs):
        live = slot < tcount[0:1, s : s + 1]
        ids = jnp.where(live, tdst[0, s : s + 1, :], 1023)
        counts = counts + dot(hot(32, ids >> 5), hot(32, ids & 31), ALONG)
        lists.append(jnp.where(live, tsrc[0, s : s + 1, :] * 1024 + ids, -1))
    own[...] = lists[0]
    first[...] = jnp.where(odd, lists[1], lists[7])
    for j, pair in ((1, pair1), (2, pair2), (3, pair3)):
        pair[0:1, :] = lists[2 * j]
        pair[1:2, :] = jnp.where(odd, lists[2 * j + 1], lists[2 * j - 1])
    slot = lax.broadcasted_iota(I32, (1, cap), 1)
    marked = []
    for g in range(ngroup):
        ids = jnp.where(slot < rcount[0:1, g : g + 1], rdst[0, g : g + 1, :], 1023)
        counts = counts + dot(hot(32, ids >> 5), hot(32, ids & 31), ALONG)
        marked.append(hot(nodes, ids))
    upper = jnp.floor(counts * (1.0 / 128.0))
    lower = counts - upper * 128.0
    node = lax.broadcasted_iota(I32, (nodes, 32), 0)
    lane = lax.broadcasted_iota(I32, (nodes, 32), 1)
    pick = jnp.where((node >> 5) == lane, 1.0, 0.0).astype(BF16)
    spread = dot(pick, upper.astype(BF16)) * 128.0 + dot(pick, lower.astype(BF16))
    degree = jnp.sum(jnp.where((node & 31) == lane, spread, 0.0), axis=1, keepdims=True)
    inverse = 1.0 / jnp.maximum(degree, 1.0)
    x = (inverse * cot[...].astype(F32)).astype(BF16)
    x_out[...] = x
    for g in range(ngroup):
        rows_out[g] = dot(marked[g], x, DOWN).astype(BF16)


def build(edges, tile_out, acc):
    nodes = acc.shape[0]
    acc[...] = jnp.zeros_like(acc)
    live = jnp.sum((edges[0] >= 0).astype(I32))

    def step(i, carry):
        packed = edges[0, :, pl.ds(pl.multiple_of(i * CHUNK, CHUNK), CHUNK)]
        acc[...] += dot(small_hot(nodes, packed >> 10), small_hot(nodes, packed & 1023), ALONG)
        return carry

    lax.fori_loop(0, (live + CHUNK - 1) // CHUNK, step, 0)
    tile_out[0] = acc[...].astype(BF16)


def first_sum(tile0, tile1, x0, x1, ids, rows, out):
    i = pl.program_id(0)
    block = out.shape[0]
    total = dot(tile0[0], x0[...]) + dot(tile1[0], x1[...])
    spots = lax.broadcasted_iota(I32, (block, ids.shape[1]), 0) + i * block
    sel = jnp.where(spots == ids[...], 1.0, 0.0).astype(BF16)
    out[...] = total + dot(sel, rows[...])


def middle_sum(before, t0, t1, t2, t3, x0, x1, x2, x3, out):
    total = before[...] + dot(t0[0], x0[...]) + dot(t1[0], x1[...])
    out[...] = total + dot(t2[0], x2[...]) + dot(t3[0], x3[...])


def last_sum(before, t0, t1, x0, x1, feats, out, send, keep, grad):
    nodes = before.shape[0]
    for i in range(nodes // BLOCK):
        rows = slice(i * BLOCK, (i + 1) * BLOCK)
        total = before[rows, :] + dot(t0[0, rows, :], x0[...]) + dot(t1[0, rows, :], x1[...])
        out[rows, :] = total
        top = total.astype(BF16)
        rest = (total - top.astype(F32)).astype(BF16)
        part = dot(feats[rows, :], top, DOWN) + dot(feats[rows, :], rest, DOWN)
        if i == 0:
            grad[...] = part
        else:
            grad[...] += part
    half = send.shape[0]
    core = lax.rem(lax.axis_index("blk"), 2)
    keep[...] = grad[pl.ds(pl.multiple_of(core * half, half), half), :]
    send[...] = grad[pl.ds(pl.multiple_of((1 - core) * half, half), half), :]


def place(factor, *refs):
    out_self, out_neigh = refs[-2], refs[-1]
    ngroup = (len(refs) - 2) // 2
    size = refs[0].shape[1]
    group, core = lax.axis_index("group"), lax.rem(lax.axis_index("blk"), 2)
    for n in range(2 * ngroup):
        k = core if n < ngroup else 1 - core
        g = lax.rem(group - n % ngroup + ngroup, ngroup)
        at = pl.multiple_of((k * ngroup + g) * size, size)
        out_self[pl.ds(at, size), :] = refs[n][0] * factor
        out_neigh[pl.ds(at, size), :] = refs[n][1] * factor


def finish(summed, cot, w_self, w_neigh, out):
    total = summed[...]
    top = total.astype(BF16)
    rest = (total - top.astype(F32)).astype(BF16)
    out[...] = (
        dot(cot[...], w_self[...], ALONG)
        + dot(top, w_neigh[...], ALONG)
        + dot(rest, w_neigh[...], ALONG)
    )


BLOCK = 256
MIB = 1024 * 1024


def params(mib):
    return pltpu.CompilerParams(vmem_limit_bytes=mib * MIB)


def whole(shape):
    return pl.BlockSpec(shape, lambda i: (0,) * len(shape))


def tile_spec(slot, nodes):
    return pl.BlockSpec((1, BLOCK, nodes), lambda i: (slot, i, 0))


def row_spec(width):
    return pl.BlockSpec((BLOCK, width), lambda i: (i, 0))


def estimate(macs, moved):
    return pl.CostEstimate(flops=2 * macs, bytes_accessed=moved, transcendentals=0)


def run_prepare(tile_count, recv_count, tile_src, tile_dst, recv_dst, cotangent):
    nodes, width = cotangent.shape
    ngroup, cap = recv_dst.shape[1], recv_dst.shape[2]
    ept = tile_src.shape[2]
    given = (tile_count, recv_count, tile_src, tile_dst, recv_dst, cotangent)
    made = [((nodes, width), BF16), ((ngroup, cap, width), BF16)]
    made += [((1, ept), I32)] * 2 + [((2, ept), I32)] * 3
    return pl.pallas_call(
        prepare,
        grid=(1,),
        out_shape=[jax.ShapeDtypeStruct(*m) for m in made],
        in_specs=[whole(v.shape) for v in given],
        out_specs=[whole(m[0]) for m in made],
        compiler_params=params(60),
        cost_estimate=estimate(ngroup * cap * nodes * width, 4 * nodes * width),
        name="prepare",
    )(*given)


def run_build(edges, nodes):
    slots, _, ept = edges.shape
    return pl.pallas_call(
        build,
        grid=(slots,),
        in_specs=[pl.BlockSpec((1, 1, ept), lambda s: (s, 0, 0))],
        out_specs=pl.BlockSpec((1, nodes, nodes), lambda s: (s, 0, 0)),
        scratch_shapes=[pltpu.VMEM((nodes, nodes), F32)],
        out_shape=jax.ShapeDtypeStruct((slots, nodes, nodes), BF16),
        compiler_params=params(24),
        cost_estimate=estimate(slots * nodes * nodes * ept // 2, 2 * slots * nodes * nodes),
        name="build",
    )(edges)


def run_first(tiles, x0, x1, ids, rows):
    nodes, width = x0.shape
    return pl.pallas_call(
        first_sum,
        grid=(nodes // BLOCK,),
        in_specs=[
            tile_spec(0, nodes),
            tile_spec(1, nodes),
            whole(x0.shape),
            whole(x1.shape),
            whole(ids.shape),
            whole(rows.shape),
        ],
        out_specs=row_spec(width),
        out_shape=jax.ShapeDtypeStruct((nodes, width), F32),
        compiler_params=params(24),
        cost_estimate=estimate(3 * nodes * nodes * width, 12 * nodes * width),
        name="first_sum",
    )(tiles, tiles, x0, x1, ids, rows)


def run_middle(before, own, other, xs):
    nodes, width = before.shape
    return pl.pallas_call(
        middle_sum,
        grid=(nodes // BLOCK,),
        in_specs=[row_spec(width)]
        + [tile_spec(s, nodes) for s in (0, 1, 0, 1)]
        + [whole(x.shape) for x in xs],
        out_specs=row_spec(width),
        out_shape=jax.ShapeDtypeStruct((nodes, width), F32),
        compiler_params=params(24),
        cost_estimate=estimate(4 * nodes * nodes * width, 16 * nodes * width),
        name="middle_sum",
    )(before, own, own, other, other, *xs)


def run_last(before, own, other, xs, features):
    nodes, width = before.shape
    vm = pl.BlockSpec(memory_space=pltpu.VMEM)
    return pl.pallas_call(
        last_sum,
        in_specs=[vm] * 6,
        out_specs=[vm] * 3,
        out_shape=(
            jax.ShapeDtypeStruct((nodes, width), F32),
            jax.ShapeDtypeStruct((width // 2, width), F32),
            jax.ShapeDtypeStruct((width // 2, width), F32),
        ),
        scratch_shapes=[pltpu.VMEM((width, width), F32)],
        compiler_params=params(24),
        cost_estimate=estimate(3 * nodes * nodes * width, 16 * nodes * width),
        name="last_sum",
    )(before, own, other, *xs, features)


def run_place(pieces, factor, width):
    return pl.pallas_call(
        lambda *refs: place(factor, *refs),
        grid=(1,),
        in_specs=[whole(v.shape) for v in pieces],
        out_specs=[whole((width, width))] * 2,
        out_shape=[jax.ShapeDtypeStruct((width, width), F32)] * 2,
        compiler_params=params(24),
        cost_estimate=estimate(width * width, 16 * width * width),
        name="place",
    )(*pieces)


def run_finish(summed, cotangent, w_self, w_neigh):
    nodes, width = summed.shape
    return pl.pallas_call(
        finish,
        grid=(nodes // BLOCK,),
        in_specs=[row_spec(width), row_spec(width), whole(w_self.shape), whole(w_neigh.shape)],
        out_specs=row_spec(width),
        out_shape=jax.ShapeDtypeStruct((nodes, width), F32),
        compiler_params=params(24),
        cost_estimate=estimate(3 * nodes * width * width, 10 * nodes * width),
        name="finish",
    )(summed, cotangent, w_self, w_neigh)


def moved(value, perm):
    return lax.ppermute(value, "blk", perm)


def over_group(value):
    return lax.all_to_all(value, "group", split_axis=0, concat_axis=0, tiled=True)


def fence(values):
    return lax.optimization_barrier(values)


def on_device(
    features,
    cotangent,
    w_self,
    w_neigh,
    tile_src,
    tile_dst,
    tile_count,
    send_ids,
    recv_dst,
    recv_count,
):
    nodes, width = features.shape
    ngroup, cap = send_ids.shape[1], send_ids.shape[2]
    ny = 4
    nblk = lax.axis_size("blk")
    bi = lax.axis_index("blk")
    core = bi % 2
    ypos = (bi // 2) % ny
    ring = range(nblk)
    swap = [(i, i ^ 1) for i in ring]

    def yshift(by):
        return [(i, (i // 8) * 8 + (i % 8 + 2 * by) % 8) for i in ring]

    x, rows, own, first, pair1, pair2, pair3 = run_prepare(
        tile_count, recv_count, tile_src, tile_dst, recv_dst, cotangent
    )
    far = moved(x, [(i, (i - 8) % nblk) for i in ring])
    first = moved(first, [(i, (i - 1 if i % 2 else i - 7) % nblk) for i in ring])
    pairs = [
        moved(p, [(i, (i - 2 * j) % nblk) for i in ring])
        for j, p in ((1, pair1), (2, pair2), (3, pair3))
    ]
    self_part = dot(features, cotangent, DOWN)
    near = run_build(jnp.stack([own, first]), nodes)
    mine = run_build(jnp.stack([pairs[0][0:1], pairs[2][0:1]]), nodes)
    x, far, rows = fence((x, far, rows, near, mine, self_part))[:3]

    one = moved(jnp.where(ypos == 0, far, x), yshift(-1))
    three = moved(jnp.where(ypos == 3, x, far), yshift(1))
    other = moved(jnp.concatenate([p[1:2] for p in pairs], axis=0), swap)
    side = moved(jnp.where(core == 1, x, far), swap)
    returned = lax.all_to_all(rows, "group", split_axis=0, concat_axis=0, tiled=True)
    theirs = run_build(jnp.stack([other[0:1], other[2:3]]), nodes)
    mid_own = run_build(pairs[1][None, 0:1], nodes)
    mid_other = run_build(other[None, 1:2], nodes)
    summed = run_first(
        near, x, side, send_ids.reshape(1, ngroup * cap), returned.reshape(ngroup * cap, width)
    )
    one, three = fence((one, three, theirs, mid_own, mid_other, summed))[:2]

    two = moved(
        jnp.where(core == 0, one, three),
        [(i, (i - 2 if i % 2 == 0 else i + 2) % nblk) for i in ring],
    )
    one_b = moved(one, swap)
    three_b = moved(three, swap)
    half = width // 2
    self_part = jnp.where(core == 0, self_part[:half], self_part[half:]) + moved(
        jnp.where(core == 0, self_part[half:], self_part[:half]), swap
    )
    self_part = over_group(self_part.reshape(ngroup, half // ngroup, width)).sum(0)
    summed = run_middle(summed, mine, theirs, (one, three, one_b, three_b))
    two = fence((two, summed, self_part))[0]

    two_b = moved(two, swap)
    summed, send, keep = run_last(summed, mid_own, mid_other, (two, two_b), features)

    part = keep + moved(send, swap)
    part = over_group(part.reshape(ngroup, half // ngroup, width)).sum(0)
    rest = nblk // 2
    size = half // ngroup // rest
    planes = [[2 * i + c for i in range(rest)] for c in range(2)]

    def over_plane(v):
        return lax.all_to_all(
            v, "blk", split_axis=0, concat_axis=0, tiled=True, axis_index_groups=planes
        )

    part = jnp.stack([self_part, part]).reshape(2, rest, size, width).transpose(1, 0, 2, 3)
    part = over_plane(part).sum(0)
    part = over_plane(jnp.broadcast_to(part[None], (rest, 2, size, width)))
    part = part.transpose(1, 0, 2, 3).reshape(2, rest * size, width)
    held = [part] + [
        lax.ppermute(part, "group", [(i, (i + s) % ngroup) for i in range(ngroup)])
        for s in range(1, ngroup)
    ]
    held = held + [moved(v, swap) for v in held]
    total = run_finish(summed, cotangent, w_self, w_neigh)
    factor = 1.0 / math.sqrt(nodes * lax.axis_size("group") * nblk)
    grad_self, grad_neigh = run_place(held, factor, width)
    return (total, grad_self, grad_neigh)


def solution(mesh):
    both = ("group", "blk")
    placed = (
        P(both, None),
        P(both, None),
        P(),
        P(),
        P(both, None, None),
        P(both, None, None),
        P(both, None),
        P(both, None, None),
        P(both, None, None),
        P(both, None),
    )
    return jax.shard_map(
        on_device,
        mesh=mesh,
        in_specs=placed,
        out_specs=(P(both, None), P(), P()),
        check_vma=False,
    )
```

time: 210 us -> 171 us (0.81)
  waiting for transfers between devices: 77.9 us -> 26.8 us
  blocking collectives: 0 us -> 40.3 us
  starting transfers between devices: 62.8 us -> 49.7 us
  other arithmetic: 19.3 us -> 8.16 us
  local copies, waits for them, and re-layouts: 18.6 us -> 12.3 us
  Pallas kernels: 27.2 us -> 31.4 us
    ppermute x26 -> x19, waiting for transfers between devices: 56.3 us -> 9.56 us  [moved(): return lax.ppermute(value, 'blk', perm)]
    all_to_all x0 -> x3, blocking collectives: none -> 40.3 us  [the longest x2 30.3 us: over_plane(): lax.all_to_all(v, 'blk', split_axis=0, concat_axis=0, tiled=True, axis_in...]
    ppermute x6 -> x3, waiting for transfers between devices: 21.6 us -> 2.03 us  [on_device(): lax.ppermute(part, 'group', [(i, (i + s) % ngroup) for i in range(ngroup)])]
    ppermute x26 -> x19, starting transfers between devices: 50 us -> 39.4 us  [moved(): return lax.ppermute(value, 'blk', perm)]
    all_to_all x0 -> x1, waiting for transfers between devices: none -> 9.11 us  [over_group(): lax.all_to_all(value, 'group', split_axis=0, concat_axis=0, tiled=True)]
    select_n x11 -> x1, other arithmetic: 9.16 us -> 0.98 us  [on_device(): jnp.where(core == 0, self_part[half:], self_part[:half])]
    unnamed x63 -> x45, local copies, waits for them, and re-layouts: 18.5 us -> 11.9 us
    all_to_all x1, waiting for transfers between devices: 0.01 us -> 6.15 us  [on_device(): lax.all_to_all(rows, 'group', split_axis=0, concat_axis=0, tiled=True)]
  transfers between devices with their start and end apart: 33 -> 24, of which waited for: 18 -> 9; matrix products, arithmetic and copies ran while one was open for 4% -> 5% of each run, Pallas kernels for 11% -> 13%
where the time goes in v2:
time: 171 us; the launch traced here: 170 us
  starting transfers between devices  49.7 us (29%)
  blocking collectives  40.3 us (24%)
  Pallas kernels  31.4 us (18%)
  waiting for transfers between devices  26.8 us (16%)
  local copies, waits for them, and re-layouts  12.3 us (7%)
  other arithmetic  8.16 us (5%)
    ppermute x19, starting transfers between devices, moved(): return lax.ppermute(value, 'blk', perm)  39.4 us
    all_to_all x2, blocking collectives, over_plane(): lax.all_to_all(v, 'blk', split_axis=0, concat_axis=0, tiled=True, axis_in...  30.3 us
    unnamed x45, local copies, waits for them, and re-layouts  11.9 us
    pallas_call x5, Pallas kernels, run_build(): pl.pallas_call(build, grid=(slots,), in_specs=[pl.BlockSpec((1, 1, ept),...  10.2 us
    all_to_all x1, blocking collectives, over_group(): lax.all_to_all(value, 'group', split_axis=0, concat_axis=0, tiled=True)  10 us
    ppermute x19, waiting for transfers between devices, moved(): return lax.ppermute(value, 'blk', perm)  9.56 us
    all_to_all x1, waiting for transfers between devices, over_group(): lax.all_to_all(value, 'group', split_axis=0, concat_axis=0, tiled=True)  9.11 us
    all_to_all x1, waiting for transfers between devices, on_device(): lax.all_to_all(rows, 'group', split_axis=0, concat_axis=0, tiled=True)  6.15 us
  transfers between devices with their start and end apart: 24, of which 9 were waited for; matrix products, arithmetic and copies ran while one was open for 5% of the time, Pallas kernels for 13%

profile of v2, /device:TPU:1, one launch (start us, length us, event | category | flops | bytes accessed | tf_op | source)
XLA Modules:
  0.0 170.4 jit_solution(3108991987184734913)
XLA Ops:
  0.7 4.8 %prepare.1 = (bf16[768,512]{1,0:T(8,128)(2,1)}, bf16[4,256,512]{2,1,0:T(8,128)(2,1)}, s32[1,2048]{1,0:T(1,128)}, s32[1,2048]{1,0:T(1,128)}, s32[2,2048]{1,0:T(2,...) custom-call(s32[1,8]{1,0:T(1,128)} %tcount.1, s32[1,4]{1,0:T(1,128)} %rcount.1, s32[1,8,2048]{2,1,0:T(8,128)} %tsrc.1, ...), custom_call_target="tpu_custom_call" | custom-call | flops 805306368 | bytes 1572864 | tf_op jit(solution)/shard_map/prepare/pallas_call | solution.py:173
  5.4 3.2 %collective-permute-start = (s32[1,2048]{1,0:T(1,128)}, s32[1,2048]{1,0:T(1,128)S(1)}, u32[]{:S(2)}, u32[]{:S(2)}) collective-permute-start(s32[1,2048]{1,0:T(1,128)} %get-tuple-element.22), channel_id=1, source_target_pairs={{0,57},{1,0},{2,59},{3,2},{4,61},{5,4},{6,63},{7,6},{8,1},{9,8},{1... | collective-permute-start | bytes 24584 | tf_op jit(solution)/shard_map/ppermute | solution.py:284
  8.6 3.8 %collective-permute-start.1 = (bf16[768,512]{1,0:T(8,128)(2,1)}, bf16[768,512]{1,0:T(8,128)(2,1)S(1)}, u32[]{:S(2)}, u32[]{:S(2)}) collective-permute-start(bf16[768,512]{1,0:T(8,128)(2,1)} %get-tuple-element.27.x0), channel_id=1, source_target_pairs={{0,56},{1,57},{2,58},{3,59},{4,60},{5,61},{6,62},{7,63},{8,0},{9,1... | collective-permute-start | bytes 2359304 | tf_op jit(solution)/shard_map/ppermute | solution.py:284
  15.7 2.1 %collective-permute-start.5 = (s32[2,2048]{1,0:T(2,128)}, s32[2,2048]{1,0:T(2,128)S(1)}, u32[]{:S(2)}, u32[]{:S(2)}) collective-permute-start(s32[2,2048]{1,0:T(2,128)} %get-tuple-element.30), channel_id=1, source_target_pairs={{0,60},{1,61},{2,62},{3,63},{4,0},{5,1},{6,2},{7,3},{8,4},{9,5},{1... | collective-permute-start | bytes 49160 | tf_op jit(solution)/shard_map/ppermute | solution.py:284
  21.1 2.2 %build.5.tile0.tile1 = bf16[2,768,768]{2,1,0:T(8,128)(2,1)S(1)} custom-call(s32[2,1,2048]{2,1,0:T(1,128)S(1)} %pad_add_fusion.1.edges), custom_call_target="tpu_custom_call" | custom-call | flops 2415919104 | bytes 2359296 | tf_op jit(solution)/shard_map/build/pallas_call | solution.py:187
  24.7 4.9 %collective-permute-done.3 = s32[2,2048]{1,0:T(2,128)S(1)} collective-permute-done((s32[2,2048]{1,0:T(2,128)}, s32[2,2048]{1,0:T(2,128)S(1)}, u32[]{:S(2)}, u32[]{:S(2)}) %collective-permute-start.3) | collective-permute-done | bytes 16416 | tf_op jit(solution)/shard_map/ppermute | solution.py:284
  33.8 2.9 %build.6.t0.t1 = bf16[2,768,768]{2,1,0:T(8,128)(2,1)S(1)} custom-call(s32[2,1,2048]{2,1,0:T(1,128)S(1)} %pad_add_fusion.2.edges), custom_call_target="tpu_custom_call" | custom-call | flops 2415919104 | bytes 2359296 | tf_op jit(solution)/shard_map/build/pallas_call | solution.py:187
  38.4 4.0 %all-to-all-start = ((bf16[4,256,512]{2,1,0:T(8,128)(2,1)}), bf16[4,256,512]{2,1,0:T(8,128)(2,1)S(1)}, u32[]{:S(2)}, u32[]{:S(2)}) async-start(bf16[4,256,512]{2,1,0:T(8,128)(2,1)} %get-tuple-element.29), calls=%async_computation | async-start | bytes 2097152 | tf_op jit(solution)/shard_map/all_to_all | solution.py:338
  44.1 2.9 %build.7.t2.t3 = bf16[2,768,768]{2,1,0:T(8,128)(2,1)S(1)} custom-call(s32[2,1,2048]{2,1,0:T(1,128)S(1)} %pad_add_fusion.3.edges), custom_call_target="tpu_custom_call" | custom-call | flops 2415919104 | bytes 2359296 | tf_op jit(solution)/shard_map/build/pallas_call | solution.py:187
  50.6 6.2 %all-to-all-done = bf16[4,256,512]{2,1,0:T(8,128)(2,1)S(1)} async-done(((bf16[4,256,512]{2,1,0:T(8,128)(2,1)}), bf16[4,256,512]{2,1,0:T(8,128)(2,1)S(1)}, u32[]{:S(2)}, u32[]{:S(2)}) %all-to-all-start) | async-done | bytes 1048608 | tf_op jit(solution)/shard_map/all_to_all | solution.py:338
  59.6 3.7 %first_sum.1.before = f32[768,512]{1,0:T(8,128)S(1)} custom-call(bf16[2,768,768]{2,1,0:T(8,128)(2,1)S(1)} %copy-done.1, bf16[2,768,768]{2,1,0:T(8,128)(2,1)S(1)} %copy-done.1, bf16[768,512]{1,0:T(8,128)(2,1)S(1)} %copy-done.9, bf16[768,512]{1,0:T(8,128)(2,1)} %collective-permute-done.4.x1, s32[1,1024]{1,0:T(1,128)S(1)} %bitcast.25, ...), custom_call_target="tpu_custom_call" | custom-call | flops 1811939328 | bytes 4718592 | tf_op jit(solution)/shard_map/first_sum/pallas_call | solution.py:202
  65.3 2.1 %broadcast_select_fusion = bf16[768,512]{1,0:T(8,128)(2,1)} fusion(bf16[768,512]{1,0:T(8,128)(2,1)} %collective-permute-done.7.x0, bf16[768,512]{1,0:T(8,128)(2,1)} %collective-permute-done.8.x1, pred[]{:T(512)S(6)} %eq.20), kind=kLoop, calls=%fused_computation | loop fusion | flops 393216 | bytes 2359297 | tf_op jit(solution)/shard_map/jit(_where)/select_n | solution.py:348
  70.2 10.0 %all_to_all.25 = f32[4,64,512]{2,1,0:T(8,128)} all-to-all(f32[4,64,512]{2,1,0:T(8,128)S(1)} %bitcast.26), channel_id=1, replica_groups=mesh['group'=4,'blk'=64] {'group'}, dimensions={0} | all-to-all | bytes 1048576 | tf_op jit(solution)/shard_map/all_to_all | solution.py:288
  84.4 4.7 %middle_sum.1.before = f32[768,512]{1,0:T(8,128)S(1)} custom-call(f32[768,512]{1,0:T(8,128)S(1)} %copy-done.5, bf16[2,768,768]{2,1,0:T(8,128)(2,1)S(1)} %build.6.t0.t1, bf16[2,768,768]{2,1,0:T(8,128)(2,1)S(1)} %build.6.t0.t1, bf16[2,768,768]{2,1,0:T(8,128)(2,1)S(1)} %copy-done.3, bf16[2,768,768]{2,1,0:T(8,128)(2,1)S(1)} %copy-done.3, ...), custom_call_target="tpu_custom_call" | custom-call | flops 2415919104 | bytes 6291456 | tf_op jit(solution)/shard_map/middle_sum/pallas_call | solution.py:223
  89.1 7.2 %collective-permute-start.13 = (bf16[768,512]{1,0:T(8,128)(2,1)}, bf16[768,512]{1,0:T(8,128)(2,1)S(1)}, u32[]{:S(2)}, u32[]{:S(2)}) collective-permute-start(bf16[768,512]{1,0:T(8,128)(2,1)} %collective-permute-done.11.x0), channel_id=1, source_target_pairs={{0,1},{1,0},{2,3},{3,2},{4,5},{5,4},{6,7},{7,6},{8,9},{9,8},{10,11... | collective-permute-start | bytes 2359304 | tf_op jit(solution)/shard_map/ppermute | solution.py:284
  96.3 2.1 %collective-permute-done.13.x1 = bf16[768,512]{1,0:T(8,128)(2,1)S(1)} collective-permute-done((bf16[768,512]{1,0:T(8,128)(2,1)}, bf16[768,512]{1,0:T(8,128)(2,1)S(1)}, u32[]{:S(2)}, u32[]{:S(2)}) %collective-permute-start.13) | collective-permute-done | bytes 786464 | tf_op jit(solution)/shard_map/ppermute | solution.py:284
  98.4 3.9 %last_sum.1 = (f32[768,512]{1,0:T(8,128)S(1)}, f32[256,512]{1,0:T(8,128)S(1)}, f32[256,512]{1,0:T(8,128)S(1)}) custom-call(f32[768,512]{1,0:T(8,128)S(1)} %middle_sum.1.before, bf16[1,768,768]{2,1,0:T(8,128)(2,1)S(1)} %copy-done.15, bf16[1,768,768]{2,1,0:T(8,128)(2,1)S(1)} %copy-done.17, bf16[768,512]{1,0:T(8,128)(2,1)} %collective-permute-done.11.x0, ...), custom_call_target="tpu_custom_call" | custom-call | flops 1811939328 | bytes 6291456 | tf_op jit(solution)/shard_map/last_sum/pallas_call | solution.py:240
  105.1 3.5 %all-to-all-start.2 = ((f32[4,64,512]{2,1,0:T(8,128)}), f32[4,64,512]{2,1,0:T(8,128)S(1)}, u32[]{:S(2)}, u32[]{:S(2)}) async-start(f32[4,64,512]{2,1,0:T(8,128)} %bitcast.10), calls=%async_computation.2 | async-start | bytes 1048576 | tf_op jit(solution)/shard_map/all_to_all | solution.py:288
  108.7 9.1 %all-to-all-done.2 = f32[4,64,512]{2,1,0:T(8,128)S(1)} async-done(((f32[4,64,512]{2,1,0:T(8,128)}), f32[4,64,512]{2,1,0:T(8,128)S(1)}, u32[]{:S(2)}, u32[]{:S(2)}) %all-to-all-start.2) | async-done | bytes 524320 | tf_op jit(solution)/shard_map/all_to_all | solution.py:288
  118.1 14.9 %all_to_all.26 = f32[32,2,2,512]{3,2,1,0:T(2,128)S(1)} all-to-all(f32[32,2,2,512]{3,2,1,0:T(2,128)S(1)} %maximum_bitcast_fusion), channel_id=1, replica_groups={{0,2,4,6,8,10,12,14,16,18,20,22,24,26,28,30,32,34,36,38,40,42,44,46,48,..., dimensions={0} | all-to-all | bytes 524288 | tf_op jit(solution)/shard_map/all_to_all | solution.py:371
  133.1 15.4 %all_to_all.27 = f32[32,2,2,512]{3,2,1,0:T(2,128)S(1)} all-to-all(f32[32,2,2,512]{3,2,1,0:T(2,128)S(1)} %broadcast_in_dim.14), channel_id=1, replica_groups={{0,2,4,6,8,10,12,14,16,18,20,22,24,26,28,30,32,34,36,38,40,42,44,46,48,..., dimensions={0} | all-to-all | bytes 524288 | tf_op jit(solution)/shard_map/all_to_all | solution.py:371
  151.6 4.3 %collective-permute-start.18 = (f32[2,64,512]{2,1,0:T(8,128)S(1)}, f32[2,64,512]{2,1,0:T(8,128)S(1)}, u32[]{:S(2)}, u32[]{:S(2)}) collective-permute-start(f32[2,64,512]{2,1,0:T(8,128)S(1)} %reshape.31.refs_0_), channel_id=1, source_target_pairs={{0,1},{1,0},{2,3},{3,2},{4,5},{5,4},{6,7},{7,6},{8,9},{9,8},{10,11... | collective-permute-start | bytes 786440 | tf_op jit(solution)/shard_map/ppermute | solution.py:284
  157.9 6.4 %collective-permute-start.19 = (f32[2,64,512]{2,1,0:T(8,128)S(1)}, f32[2,64,512]{2,1,0:T(8,128)S(1)}, u32[]{:S(2)}, u32[]{:S(2)}) collective-permute-start(f32[2,64,512]{2,1,0:T(8,128)S(1)} %collective-permute-done.15.refs_1_), channel_id=1, source_target_pairs={{0,1},{1,0},{2,3},{3,2},{4,5},{5,4},{6,7},{7,6},{8,9},{9,8},{10,11... | collective-permute-start | bytes 786440 | tf_op jit(solution)/shard_map/ppermute | solution.py:284
  166.1 2.8 %finish.1 = f32[768,512]{1,0:T(8,128)} custom-call(f32[768,512]{1,0:T(8,128)S(1)} %get-tuple-element.34.summed, bf16[768,512]{1,0:T(8,128)(2,1)S(1)} %copy-done.7, bf16[512,512]{1,0:T(8,128)(2,1)S(1)} %copy-done.12, bf16[512,512]{1,0:T(8,128)(2,1)S(1)} %copy-done.13), custom_call_target="tpu_custom_call" | custom-call | flops 1207959552 | bytes 3932160 | tf_op jit(solution)/shard_map/finish/pallas_call | solution.py:271
  (106 shorter events, 42.4 us)
Async XLA Ops:
  5.4 14.0 %collective-permute-start = (s32[1,2048]{1,0:T(1,128)}, s32[1,2048]{1,0:T(1,128)S(1)}, u32[]{:S(2)}, u32[]{:S(2)}) collective-permute-start(s32[1,2048]{1,0:T(1,128)} %get-tuple-element.22), channel_id=1, source_target_pairs={{0,57},{1,0},{2,59},{3,2},{4,61},{5,4},{6,63},{7,6},{8,1},{9,8},{1... | collective-permute-start | bytes 24584 | tf_op jit(solution)/shard_map/ppermute | solution.py:284
  8.6 28.1 %collective-permute-start.1 = (bf16[768,512]{1,0:T(8,128)(2,1)}, bf16[768,512]{1,0:T(8,128)(2,1)S(1)}, u32[]{:S(2)}, u32[]{:S(2)}) collective-permute-start(bf16[768,512]{1,0:T(8,128)(2,1)} %get-tuple-element.27.x0), channel_id=1, source_target_pairs={{0,56},{1,57},{2,58},{3,59},{4,60},{5,61},{6,62},{7,63},{8,0},{9,1... | collective-permute-start | bytes 2359304 | tf_op jit(solution)/shard_map/ppermute | solution.py:284
  12.5 17.0 %collective-permute-start.3 = (s32[2,2048]{1,0:T(2,128)}, s32[2,2048]{1,0:T(2,128)S(1)}, u32[]{:S(2)}, u32[]{:S(2)}) collective-permute-start(s32[2,2048]{1,0:T(2,128)} %get-tuple-element.26), channel_id=1, source_target_pairs={{0,58},{1,59},{2,60},{3,61},{4,62},{5,63},{6,0},{7,1},{8,2},{9,3},... | collective-permute-start | bytes 49160 | tf_op jit(solution)/shard_map/ppermute | solution.py:284
  14.2 15.6 %collective-permute-start.2 = (s32[2,2048]{1,0:T(2,128)}, s32[2,2048]{1,0:T(2,128)S(1)}, u32[]{:S(2)}, u32[]{:S(2)}) collective-permute-start(s32[2,2048]{1,0:T(2,128)} %get-tuple-element.25), channel_id=1, source_target_pairs={{0,62},{1,63},{2,0},{3,1},{4,2},{5,3},{6,4},{7,5},{8,6},{9,7},{10,... | collective-permute-start | bytes 49160 | tf_op jit(solution)/shard_map/ppermute | solution.py:284
  15.7 14.6 %collective-permute-start.5 = (s32[2,2048]{1,0:T(2,128)}, s32[2,2048]{1,0:T(2,128)S(1)}, u32[]{:S(2)}, u32[]{:S(2)}) collective-permute-start(s32[2,2048]{1,0:T(2,128)} %get-tuple-element.30), channel_id=1, source_target_pairs={{0,60},{1,61},{2,62},{3,63},{4,0},{5,1},{6,2},{7,3},{8,4},{9,5},{1... | collective-permute-start | bytes 49160 | tf_op jit(solution)/shard_map/ppermute | solution.py:284
  19.4 49.6 %collective-permute-start.12 = (f32[256,512]{1,0:T(8,128)}, f32[256,512]{1,0:T(8,128)}, u32[]{:S(2)}, u32[]{:S(2)}) collective-permute-start(f32[256,512]{1,0:T(8,128)} %slice_select_fusion), channel_id=1, source_target_pairs={{0,1},{1,0},{2,3},{3,2},{4,5},{5,4},{6,7},{7,6},{8,9},{9,8},{10,11... | collective-permute-start | bytes 1572872 | tf_op jit(solution)/shard_map/ppermute | solution.py:284
  30.3 13.8 %collective-permute-start.6 = (s32[3,2048]{1,0:T(4,128)S(1)}, s32[3,2048]{1,0:T(4,128)S(1)}, u32[]{:S(2)}, u32[]{:S(2)}) collective-permute-start(s32[3,2048]{1,0:T(4,128)S(1)} %pad_add_fusion), channel_id=1, source_target_pairs={{0,1},{1,0},{2,3},{3,2},{4,5},{5,4},{6,7},{7,6},{8,9},{9,8},{10,11... | collective-permute-start | bytes 73736 | tf_op jit(solution)/shard_map/ppermute | solution.py:284
  38.4 12.2 %collective-permute-start.4 = (bf16[768,512]{1,0:T(8,128)(2,1)}, bf16[768,512]{1,0:T(8,128)(2,1)}, u32[]{:S(2)}, u32[]{:S(2)}) collective-permute-start(bf16[768,512]{1,0:T(8,128)(2,1)} %get-tuple-element.41), channel_id=1, source_target_pairs={{0,1},{1,0},{2,3},{3,2},{4,5},{5,4},{6,7},{7,6},{8,9},{9,8},{10,11... | collective-permute-start | bytes 2359304 | tf_op jit(solution)/shard_map/ppermute | solution.py:284
  38.4 18.4 %all-to-all-start = ((bf16[4,256,512]{2,1,0:T(8,128)(2,1)}), bf16[4,256,512]{2,1,0:T(8,128)(2,1)S(1)}, u32[]{:S(2)}, u32[]{:S(2)}) async-start(bf16[4,256,512]{2,1,0:T(8,128)(2,1)} %get-tuple-element.29), calls=%async_computation | async-start | bytes 2097152 | tf_op jit(solution)/shard_map/all_to_all | solution.py:338
  42.4 20.9 %collective-permute-start.7 = (bf16[768,512]{1,0:T(8,128)(2,1)}, bf16[768,512]{1,0:T(8,128)(2,1)}, u32[]{:S(2)}, u32[]{:S(2)}) collective-permute-start(bf16[768,512]{1,0:T(8,128)(2,1)} %get-tuple-element.40), channel_id=1, source_target_pairs={{0,6},{1,7},{2,0},{3,1},{4,2},{5,3},{6,4},{7,5},{8,14},{9,15},{10,... | collective-permute-start | bytes 2359304 | tf_op jit(solution)/shard_map/ppermute | solution.py:284
  43.1 20.5 %collective-permute-start.8 = (bf16[768,512]{1,0:T(8,128)(2,1)}, bf16[768,512]{1,0:T(8,128)(2,1)}, u32[]{:S(2)}, u32[]{:S(2)}) collective-permute-start(bf16[768,512]{1,0:T(8,128)(2,1)} %get-tuple-element.39), channel_id=1, source_target_pairs={{0,2},{1,3},{2,4},{3,5},{4,6},{5,7},{6,0},{7,1},{8,10},{9,11},{10,... | collective-permute-start | bytes 2359304 | tf_op jit(solution)/shard_map/ppermute | solution.py:284
  63.6 17.7 %collective-permute-start.9 = (bf16[768,512]{1,0:T(8,128)(2,1)}, bf16[768,512]{1,0:T(8,128)(2,1)S(1)}, u32[]{:S(2)}, u32[]{:S(2)}) collective-permute-start(bf16[768,512]{1,0:T(8,128)(2,1)} %collective-permute-done.7.x0), channel_id=1, source_target_pairs={{0,1},{1,0},{2,3},{3,2},{4,5},{5,4},{6,7},{7,6},{8,9},{9,8},{10,11... | collective-permute-start | bytes 2359304 | tf_op jit(solution)/shard_map/ppermute | solution.py:284
  65.3 16.0 %collective-permute-start.10 = (bf16[768,512]{1,0:T(8,128)(2,1)}, bf16[768,512]{1,0:T(8,128)(2,1)}, u32[]{:S(2)}, u32[]{:S(2)}) collective-permute-start(bf16[768,512]{1,0:T(8,128)(2,1)} %collective-permute-done.8.x1), channel_id=1, source_target_pairs={{0,1},{1,0},{2,3},{3,2},{4,5},{5,4},{6,7},{7,6},{8,9},{9,8},{10,11... | collective-permute-start | bytes 2359304 | tf_op jit(solution)/shard_map/ppermute | solution.py:284
  67.4 21.7 %collective-permute-start.11 = (bf16[768,512]{1,0:T(8,128)(2,1)}, bf16[768,512]{1,0:T(8,128)(2,1)}, u32[]{:S(2)}, u32[]{:S(2)}) collective-permute-start(bf16[768,512]{1,0:T(8,128)(2,1)} %broadcast_select_fusion), channel_id=1, source_target_pairs={{0,62},{1,3},{2,0},{3,5},{4,2},{5,7},{6,4},{7,9},{8,6},{9,11},{10,... | collective-permute-start | bytes 2359304 | tf_op jit(solution)/shard_map/ppermute | solution.py:284
  89.1 9.3 %collective-permute-start.13 = (bf16[768,512]{1,0:T(8,128)(2,1)}, bf16[768,512]{1,0:T(8,128)(2,1)S(1)}, u32[]{:S(2)}, u32[]{:S(2)}) collective-permute-start(bf16[768,512]{1,0:T(8,128)(2,1)} %collective-permute-done.11.x0), channel_id=1, source_target_pairs={{0,1},{1,0},{2,3},{3,2},{4,5},{5,4},{6,7},{7,6},{8,9},{9,8},{10,11... | collective-permute-start | bytes 2359304 | tf_op jit(solution)/shard_map/ppermute | solution.py:284
  102.3 2.0 %collective-permute-start.14 = (f32[256,512]{1,0:T(8,128)S(1)}, f32[256,512]{1,0:T(8,128)S(1)}, u32[]{:S(2)}, u32[]{:S(2)}) collective-permute-start(f32[256,512]{1,0:T(8,128)S(1)} %get-tuple-element.36), channel_id=1, source_target_pairs={{0,1},{1,0},{2,3},{3,2},{4,5},{5,4},{6,7},{7,6},{8,9},{9,8},{10,11... | collective-permute-start | bytes 1572872 | tf_op jit(solution)/shard_map/ppermute | solution.py:284
  105.1 12.7 %all-to-all-start.2 = ((f32[4,64,512]{2,1,0:T(8,128)}), f32[4,64,512]{2,1,0:T(8,128)S(1)}, u32[]{:S(2)}, u32[]{:S(2)}) async-start(f32[4,64,512]{2,1,0:T(8,128)} %bitcast.10), calls=%async_computation.2 | async-start | bytes 1048576 | tf_op jit(solution)/shard_map/all_to_all | solution.py:288
  148.7 9.2 %collective-permute-start.15 = (f32[2,64,512]{2,1,0:T(8,128)S(1)}, f32[2,64,512]{2,1,0:T(8,128)S(1)}, u32[]{:S(2)}, u32[]{:S(2)}) collective-permute-start(f32[2,64,512]{2,1,0:T(8,128)S(1)} %reshape.31.refs_0_), channel_id=1, source_target_pairs={{0,64},{64,128},{128,192},{192,0},{1,65},{65,129},{129,193},{193,1... | collective-permute-start | bytes 786440 | tf_op jit(solution)/shard_map/ppermute | solution.py:380
  149.1 15.3 %collective-permute-start.16 = (f32[2,64,512]{2,1,0:T(8,128)S(1)}, f32[2,64,512]{2,1,0:T(8,128)S(1)}, u32[]{:S(2)}, u32[]{:S(2)}) collective-permute-start(f32[2,64,512]{2,1,0:T(8,128)S(1)} %reshape.31.refs_0_), channel_id=1, source_target_pairs={{0,128},{64,192},{128,0},{192,64},{1,129},{65,193},{129,1},{193,65... | collective-permute-start | bytes 786440 | tf_op jit(solution)/shard_map/ppermute | solution.py:380
  150.9 13.5 %collective-permute-start.17 = (f32[2,64,512]{2,1,0:T(8,128)S(1)}, f32[2,64,512]{2,1,0:T(8,128)S(1)}, u32[]{:S(2)}, u32[]{:S(2)}) collective-permute-start(f32[2,64,512]{2,1,0:T(8,128)S(1)} %reshape.31.refs_0_), channel_id=1, source_target_pairs={{0,192},{64,0},{128,64},{192,128},{1,193},{65,1},{129,65},{193,129... | collective-permute-start | bytes 786440 | tf_op jit(solution)/shard_map/ppermute | solution.py:380
  151.6 17.3 %collective-permute-start.18 = (f32[2,64,512]{2,1,0:T(8,128)S(1)}, f32[2,64,512]{2,1,0:T(8,128)S(1)}, u32[]{:S(2)}, u32[]{:S(2)}) collective-permute-start(f32[2,64,512]{2,1,0:T(8,128)S(1)} %reshape.31.refs_0_), channel_id=1, source_target_pairs={{0,1},{1,0},{2,3},{3,2},{4,5},{5,4},{6,7},{7,6},{8,9},{9,8},{10,11... | collective-permute-start | bytes 786440 | tf_op jit(solution)/shard_map/ppermute | solution.py:284
  157.9 10.9 %collective-permute-start.19 = (f32[2,64,512]{2,1,0:T(8,128)S(1)}, f32[2,64,512]{2,1,0:T(8,128)S(1)}, u32[]{:S(2)}, u32[]{:S(2)}) collective-permute-start(f32[2,64,512]{2,1,0:T(8,128)S(1)} %collective-permute-done.15.refs_1_), channel_id=1, source_target_pairs={{0,1},{1,0},{2,3},{3,2},{4,5},{5,4},{6,7},{7,6},{8,9},{9,8},{10,11... | collective-permute-start | bytes 786440 | tf_op jit(solution)/shard_map/ppermute | solution.py:284
  164.3 4.5 %collective-permute-start.20 = (f32[2,64,512]{2,1,0:T(8,128)S(1)}, f32[2,64,512]{2,1,0:T(8,128)S(1)}, u32[]{:S(2)}, u32[]{:S(2)}) collective-permute-start(f32[2,64,512]{2,1,0:T(8,128)S(1)} %collective-permute-done.16.refs_2_), channel_id=1, source_target_pairs={{0,1},{1,0},{2,3},{3,2},{4,5},{5,4},{6,7},{7,6},{8,9},{9,8},{10,11... | collective-permute-start | bytes 786440 | tf_op jit(solution)/shard_map/ppermute | solution.py:284
  164.3 4.5 %collective-permute-start.21 = (f32[2,64,512]{2,1,0:T(8,128)S(1)}, f32[2,64,512]{2,1,0:T(8,128)S(1)}, u32[]{:S(2)}, u32[]{:S(2)}) collective-permute-start(f32[2,64,512]{2,1,0:T(8,128)S(1)} %collective-permute-done.17.refs_3_), channel_id=1, source_target_pairs={{0,1},{1,0},{2,3},{3,2},{4,5},{5,4},{6,7},{7,6},{8,9},{9,8},{10,11... | collective-permute-start | bytes 786440 | tf_op jit(solution)/shard_map/ppermute | solution.py:284
  (22 other events, 207.6 us)

commit v3 on v2

--- a/solution.py
+++ b/solution.py
@@ -5,6 +5,7 @@
 from jax import lax
 from jax.experimental import pallas as pl
 from jax.experimental.pallas import tpu as pltpu
+from jax.sharding import Mesh
 from jax.sharding import PartitionSpec as P
 
 F32 = jnp.float32
@@ -30,24 +31,32 @@
     return ones.astype(jnp.float8_e4m3fn)
 
 
-def prepare(tcount, rcount, tsrc, tdst, rdst, cot, x_out, rows_out, own, first, pair1, pair2, pair3):
-    nodes = cot.shape[0]
+def pack(tcount, tsrc, tdst, own, first, pair1, pair2, pair3):
     offs, ept = tdst.shape[1], tdst.shape[2]
-    ngroup, cap = rdst.shape[1], rdst.shape[2]
-    odd = lax.rem(lax.axis_index("blk"), 2) == 1
+    odd = lax.axis_index("core") == 1
     slot = lax.broadcasted_iota(I32, (1, ept), 1)
-    counts = jnp.zeros((32, 32), F32)
-    lists = []
-    for s in range(offs):
+
+    def packed(s):
         live = slot < tcount[0:1, s : s + 1]
-        ids = jnp.where(live, tdst[0, s : s + 1, :], 1023)
-        counts = counts + dot(hot(32, ids >> 5), hot(32, ids & 31), ALONG)
-        lists.append(jnp.where(live, tsrc[0, s : s + 1, :] * 1024 + ids, -1))
+        return jnp.where(live, tsrc[0, s : s + 1, :] * 1024 + tdst[0, s : s + 1, :], -1)
+
+    lists = [packed(s) for s in range(offs)]
     own[...] = lists[0]
     first[...] = jnp.where(odd, lists[1], lists[7])
     for j, pair in ((1, pair1), (2, pair2), (3, pair3)):
         pair[0:1, :] = lists[2 * j]
         pair[1:2, :] = jnp.where(odd, lists[2 * j + 1], lists[2 * j - 1])
+
+
+def prepare(tcount, rcount, tdst, rdst, cot, x_out, rows_out):
+    nodes = cot.shape[0]
+    offs, ept = tdst.shape[1], tdst.shape[2]
+    ngroup, cap = rdst.shape[1], rdst.shape[2]
+    slot = lax.broadcasted_iota(I32, (1, ept), 1)
+    counts = jnp.zeros((32, 32), F32)
+    for s in range(offs):
+        ids = jnp.where(slot < tcount[0:1, s : s + 1], tdst[0, s : s + 1, :], 1023)
+        counts = counts + dot(hot(32, ids >> 5), hot(32, ids & 31), ALONG)
     slot = lax.broadcasted_iota(I32, (1, cap), 1)
     marked = []
     for g in range(ngroup):
@@ -110,7 +119,7 @@
         else:
             grad[...] += part
     half = send.shape[0]
-    core = lax.rem(lax.axis_index("blk"), 2)
+    core = lax.axis_index("core")
     keep[...] = grad[pl.ds(pl.multiple_of(core * half, half), half), :]
     send[...] = grad[pl.ds(pl.multiple_of((1 - core) * half, half), half), :]
 
@@ -118,14 +127,16 @@
 def place(factor, *refs):
     out_self, out_neigh = refs[-2], refs[-1]
     ngroup = (len(refs) - 2) // 2
-    size = refs[0].shape[1]
-    group, core = lax.axis_index("group"), lax.rem(lax.axis_index("blk"), 2)
+    ny, _, size, _ = refs[0].shape
+    group, core, ypos = (lax.axis_index(a) for a in ("group", "core", "y"))
     for n in range(2 * ngroup):
         k = core if n < ngroup else 1 - core
         g = lax.rem(group - n % ngroup + ngroup, ngroup)
-        at = pl.multiple_of((k * ngroup + g) * size, size)
-        out_self[pl.ds(at, size), :] = refs[n][0] * factor
-        out_neigh[pl.ds(at, size), :] = refs[n][1] * factor
+        for t in range(ny):
+            y = lax.rem(ypos - t + ny, ny)
+            at = pl.multiple_of(((k * ngroup + g) * ny + y) * size, size)
+            out_self[pl.ds(at, size), :] = refs[n][t, 0] * factor
+            out_neigh[pl.ds(at, size), :] = refs[n][t, 1] * factor
 
 
 def finish(summed, cot, w_self, w_neigh, out):
@@ -163,22 +174,16 @@
     return pl.CostEstimate(flops=2 * macs, bytes_accessed=moved, transcendentals=0)
 
 
-def run_prepare(tile_count, recv_count, tile_src, tile_dst, recv_dst, cotangent):
-    nodes, width = cotangent.shape
-    ngroup, cap = recv_dst.shape[1], recv_dst.shape[2]
-    ept = tile_src.shape[2]
-    given = (tile_count, recv_count, tile_src, tile_dst, recv_dst, cotangent)
-    made = [((nodes, width), BF16), ((ngroup, cap, width), BF16)]
-    made += [((1, ept), I32)] * 2 + [((2, ept), I32)] * 3
-    return pl.pallas_call(
-        prepare,
+def run_whole(kernel, given, made, macs, name):
+    return pl.pallas_call(
+        kernel,
         grid=(1,),
         out_shape=[jax.ShapeDtypeStruct(*m) for m in made],
         in_specs=[whole(v.shape) for v in given],
         out_specs=[whole(m[0]) for m in made],
-        compiler_params=params(60),
-        cost_estimate=estimate(ngroup * cap * nodes * width, 4 * nodes * width),
-        name="prepare",
+        compiler_params=params(63),
+        cost_estimate=estimate(macs, sum(2 * v.size for v in given)),
+        name=name,
     )(*given)
 
 
@@ -191,8 +196,8 @@
         out_specs=pl.BlockSpec((1, nodes, nodes), lambda s: (s, 0, 0)),
         scratch_shapes=[pltpu.VMEM((nodes, nodes), F32)],
         out_shape=jax.ShapeDtypeStruct((slots, nodes, nodes), BF16),
-        compiler_params=params(24),
-        cost_estimate=estimate(slots * nodes * nodes * ept // 2, 2 * slots * nodes * nodes),
+        compiler_params=params(60),
+        cost_estimate=estimate(slots * nodes * nodes * ept // 16, 2 * slots * nodes * nodes),
         name="build",
     )(edges)
 
@@ -212,7 +217,7 @@
         ],
         out_specs=row_spec(width),
         out_shape=jax.ShapeDtypeStruct((nodes, width), F32),
-        compiler_params=params(24),
+        compiler_params=params(36),
         cost_estimate=estimate(3 * nodes * nodes * width, 12 * nodes * width),
         name="first_sum",
     )(tiles, tiles, x0, x1, ids, rows)
@@ -228,7 +233,7 @@
         + [whole(x.shape) for x in xs],
         out_specs=row_spec(width),
         out_shape=jax.ShapeDtypeStruct((nodes, width), F32),
-        compiler_params=params(24),
+        compiler_params=params(36),
         cost_estimate=estimate(4 * nodes * nodes * width, 16 * nodes * width),
         name="middle_sum",
     )(before, own, own, other, other, *xs)
@@ -280,12 +285,16 @@
     )(summed, cotangent, w_self, w_neigh)
 
 
+BLK = ("z", "y", "core")
+
+
 def moved(value, perm):
-    return lax.ppermute(value, "blk", perm)
-
-
-def over_group(value):
-    return lax.all_to_all(value, "group", split_axis=0, concat_axis=0, tiled=True)
+    return lax.ppermute(value, BLK, perm)
+
+
+def turned(value, axis, by):
+    length = lax.axis_size(axis)
+    return lax.ppermute(value, axis, [(i, (i + by) % length) for i in range(length)])
 
 
 def fence(values):
@@ -306,38 +315,54 @@
 ):
     nodes, width = features.shape
     ngroup, cap = send_ids.shape[1], send_ids.shape[2]
-    ny = 4
-    nblk = lax.axis_size("blk")
-    bi = lax.axis_index("blk")
-    core = bi % 2
-    ypos = (bi // 2) % ny
+    ept = tile_src.shape[2]
+    nz, ny = lax.axis_size("z"), lax.axis_size("y")
+    nblk = nz * ny * 2
+    core, ypos = lax.axis_index("core"), lax.axis_index("y")
     ring = range(nblk)
-    swap = [(i, i ^ 1) for i in ring]
-
-    def yshift(by):
-        return [(i, (i // 8) * 8 + (i % 8 + 2 * by) % 8) for i in ring]
-
-    x, rows, own, first, pair1, pair2, pair3 = run_prepare(
-        tile_count, recv_count, tile_src, tile_dst, recv_dst, cotangent
-    )
-    far = moved(x, [(i, (i - 8) % nblk) for i in ring])
+    swap = [(0, 1), (1, 0)]
+
+    def swapped(v):
+        return lax.ppermute(v, "core", swap)
+
+    own, first, pair1, pair2, pair3 = run_whole(
+        pack,
+        (tile_count, tile_src, tile_dst),
+        [((1, ept), I32)] * 2 + [((2, ept), I32)] * 3,
+        8 * ept,
+        "pack",
+    )
     first = moved(first, [(i, (i - 1 if i % 2 else i - 7) % nblk) for i in ring])
     pairs = [
         moved(p, [(i, (i - 2 * j) % nblk) for i in ring])
         for j, p in ((1, pair1), (2, pair2), (3, pair3))
     ]
+    x, rows = run_whole(
+        prepare,
+        (tile_count, recv_count, tile_dst, recv_dst, cotangent),
+        [((nodes, width), BF16), ((ngroup, cap, width), BF16)],
+        ngroup * cap * nodes * width,
+        "prepare",
+    )
+    x, own, first, pairs = fence((x, own, first, pairs))
+    far = turned(x, "z", -1)
+    other = swapped(jnp.concatenate([p[1:2] for p in pairs], axis=0))
     self_part = dot(features, cotangent, DOWN)
+    half = width // 2
+    self_part = jnp.where(core == 0, self_part[:half], self_part[half:]) + swapped(
+        jnp.where(core == 0, self_part[half:], self_part[:half])
+    )
     near = run_build(jnp.stack([own, first]), nodes)
+    rows = fence((rows, near))[0]
+    returned = lax.all_to_all(rows, "group", split_axis=0, concat_axis=0, tiled=True)
     mine = run_build(jnp.stack([pairs[0][0:1], pairs[2][0:1]]), nodes)
-    x, far, rows = fence((x, far, rows, near, mine, self_part))[:3]
-
-    one = moved(jnp.where(ypos == 0, far, x), yshift(-1))
-    three = moved(jnp.where(ypos == 3, x, far), yshift(1))
-    other = moved(jnp.concatenate([p[1:2] for p in pairs], axis=0), swap)
-    side = moved(jnp.where(core == 1, x, far), swap)
-    returned = lax.all_to_all(rows, "group", split_axis=0, concat_axis=0, tiled=True)
+    mid_own = run_build(pairs[1][None, 0:1], nodes)
+    x, far = fence((x, far, near, mine, mid_own, self_part, other))[:2]
+
+    one = turned(jnp.where(ypos == 0, far, x), "y", -1)
+    three = turned(jnp.where(ypos == ny - 1, x, far), "y", 1)
+    side = swapped(jnp.where(core == 1, x, far))
     theirs = run_build(jnp.stack([other[0:1], other[2:3]]), nodes)
-    mid_own = run_build(pairs[1][None, 0:1], nodes)
     mid_other = run_build(other[None, 1:2], nodes)
     summed = run_first(
         near, x, side, send_ids.reshape(1, ngroup * cap), returned.reshape(ngroup * cap, width)
@@ -348,47 +373,39 @@
         jnp.where(core == 0, one, three),
         [(i, (i - 2 if i % 2 == 0 else i + 2) % nblk) for i in ring],
     )
-    one_b = moved(one, swap)
-    three_b = moved(three, swap)
-    half = width // 2
-    self_part = jnp.where(core == 0, self_part[:half], self_part[half:]) + moved(
-        jnp.where(core == 0, self_part[half:], self_part[:half]), swap
-    )
-    self_part = over_group(self_part.reshape(ngroup, half // ngroup, width)).sum(0)
+    one_b = swapped(one)
+    three_b = swapped(three)
     summed = run_middle(summed, mine, theirs, (one, three, one_b, three_b))
-    two = fence((two, summed, self_part))[0]
-
-    two_b = moved(two, swap)
+    two = fence((two, summed))[0]
+
+    two_b = swapped(two)
     summed, send, keep = run_last(summed, mid_own, mid_other, (two, two_b), features)
 
-    part = keep + moved(send, swap)
-    part = over_group(part.reshape(ngroup, half // ngroup, width)).sum(0)
-    rest = nblk // 2
-    size = half // ngroup // rest
-    planes = [[2 * i + c for i in range(rest)] for c in range(2)]
-
-    def over_plane(v):
-        return lax.all_to_all(
-            v, "blk", split_axis=0, concat_axis=0, tiled=True, axis_index_groups=planes
-        )
-
-    part = jnp.stack([self_part, part]).reshape(2, rest, size, width).transpose(1, 0, 2, 3)
-    part = over_plane(part).sum(0)
-    part = over_plane(jnp.broadcast_to(part[None], (rest, 2, size, width)))
-    part = part.transpose(1, 0, 2, 3).reshape(2, rest * size, width)
-    held = [part] + [
-        lax.ppermute(part, "group", [(i, (i + s) % ngroup) for i in range(ngroup)])
-        for s in range(1, ngroup)
-    ]
-    held = held + [moved(v, swap) for v in held]
+    part = keep + swapped(send)
+    size = half // ngroup // ny
+    part = jnp.stack([self_part, part]).reshape(2, ngroup * ny, size, width).transpose(1, 0, 2, 3)
+    part = lax.all_to_all(part, ("group", "y"), split_axis=0, concat_axis=0, tiled=True).sum(0)
+
+    def zflip(v, k):
+        return lax.ppermute(v, "z", [(i, i ^ k) for i in range(nz)])
+
+    part = (part + zflip(part, 1)) + (zflip(part, 2) + zflip(part, 3))
+    part = part + zflip(part, 4)
+    part = jnp.stack([part] + [turned(part, "y", t) for t in range(1, ny)])
+    held = [part] + [turned(part, "group", s) for s in range(1, ngroup)]
+    held = held + [swapped(v) for v in held]
     total = run_finish(summed, cotangent, w_self, w_neigh)
-    factor = 1.0 / math.sqrt(nodes * lax.axis_size("group") * nblk)
+    factor = 1.0 / math.sqrt(nodes * ngroup * nblk)
     grad_self, grad_neigh = run_place(held, factor, width)
     return (total, grad_self, grad_neigh)
 
 
 def solution(mesh):
-    both = ("group", "blk")
+    blk = mesh.shape["blk"]
+    fine = Mesh(
+        mesh.devices.reshape(mesh.shape["group"], blk // 8, 4, 2), ("group",) + BLK
+    )
+    both = ("group",) + BLK
     placed = (
         P(both, None),
         P(both, None),
@@ -403,7 +420,7 @@
     )
     return jax.shard_map(
         on_device,
-        mesh=mesh,
+        mesh=fine,
         in_specs=placed,
         out_specs=(P(both, None), P(), P()),
         check_vma=False,

time: 171 us -> 157 us (0.918)
  blocking collectives: 40.3 us -> 21 us
  local copies, waits for them, and re-layouts: 12.3 us -> 3.42 us
  waiting for transfers between devices: 26.8 us -> 35.4 us
  Pallas kernels: 31.4 us -> 36.1 us
    ppermute x22 -> x29, waiting for transfers between devices: 11.6 us -> 35.4 us  [the longest x9 12.9 us: turned(): lax.ppermute(value, axis, [(i, (i + by) % length) for i in range(length)])]
    all_to_all x3 -> x1, blocking collectives: 40.3 us -> 21 us  [on_device(): lax.all_to_all(part, ('group', 'y'), split_axis=0, concat_axis=0, tiled=T...]
    unnamed x45 -> x33, local copies, waits for them, and re-layouts: 11.9 us -> 2.17 us
    all_to_all x1 -> x0, waiting for transfers between devices: 9.11 us -> none  [over_group(): lax.all_to_all(value, 'group', split_axis=0, concat_axis=0, tiled=True)]
    all_to_all x1, waiting for transfers between devices: 6.15 us -> 0.01 us  [on_device(): lax.all_to_all(rows, 'group', split_axis=0, concat_axis=0, tiled=True)]
    pallas_call x5, Pallas kernels: 10.2 us -> 14.7 us  [run_build(): pl.pallas_call(build, grid=(slots,), in_specs=[pl.BlockSpec((1, 1, ept),...]
    all_to_all x1 -> x0, starting transfers between devices: 3.47 us -> none  [over_group(): lax.all_to_all(value, 'group', split_axis=0, concat_axis=0, tiled=True)]
    all_to_all x1, starting transfers between devices: 4 us -> 5.94 us  [on_device(): lax.all_to_all(rows, 'group', split_axis=0, concat_axis=0, tiled=True)]
  transfers between devices with their start and end apart: 24 -> 30, of which waited for: 9 -> 14; matrix products, arithmetic and copies ran while one was open for 5% -> 6% of each run, Pallas kernels for 13% -> 19%
where the time goes in v3:
time: 157 us; the launch traced here: 155 us
  starting transfers between devices  48.4 us (31%)
  Pallas kernels  36.1 us (23%)
  waiting for transfers between devices  35.4 us (23%)
  blocking collectives  21 us (13%)
  other arithmetic  8.27 us (5%)
  local copies, waits for them, and re-layouts  3.42 us (2%)
  matrix products  1.97 us (1%)
    all_to_all x1, blocking collectives, on_device(): lax.all_to_all(part, ('group', 'y'), split_axis=0, concat_axis=0, tiled=T...  21 us
    ppermute x11, starting transfers between devices, swapped(): return lax.ppermute(v, 'core', swap)  18 us
    pallas_call x5, Pallas kernels, run_build(): pl.pallas_call(build, grid=(slots,), in_specs=[pl.BlockSpec((1, 1, ept),...  14.7 us
    ppermute x9, waiting for transfers between devices, turned(): lax.ppermute(value, axis, [(i, (i + by) % length) for i in range(length)])  12.9 us
    ppermute x5, starting transfers between devices, moved(): return lax.ppermute(value, BLK, perm)  11.1 us
    ppermute x4, waiting for transfers between devices, zflip(): return lax.ppermute(v, 'z', [(i, i ^ k) for i in range(nz)])  8.53 us
    ppermute x9, starting transfers between devices, turned(): lax.ppermute(value, axis, [(i, (i + by) % length) for i in range(length)])  8.16 us
    ppermute x5, waiting for transfers between devices, moved(): return lax.ppermute(value, BLK, perm)  7.92 us
  transfers between devices with their start and end apart: 30, of which 14 were waited for; matrix products, arithmetic and copies ran while one was open for 6% of the time, Pallas kernels for 19%

profile of v3, /device:TPU:1, one launch (start us, length us, event | category | flops | bytes accessed | tf_op | source)
XLA Modules:
  0.0 155.4 jit_solution(6296878104100304572)
XLA Ops:
  2.3 3.2 %collective-permute-start = (s32[1,2048]{1,0:T(1,128)}, s32[1,2048]{1,0:T(1,128)S(1)}, u32[]{:S(2)}, u32[]{:S(2)}) collective-permute-start(s32[1,2048]{1,0:T(1,128)} %get-tuple-element.29), channel_id=1, source_target_pairs={{0,57},{1,0},{2,59},{3,2},{4,61},{5,4},{6,63},{7,6},{8,1},{9,8},{1... | collective-permute-start | bytes 24584 | tf_op jit(solution)/shard_map/ppermute | solution.py:292
  5.5 6.3 %collective-permute-start.1 = (s32[2,2048]{1,0:T(2,128)}, s32[2,2048]{1,0:T(2,128)S(1)}, u32[]{:S(2)}, u32[]{:S(2)}) collective-permute-start(s32[2,2048]{1,0:T(2,128)} %get-tuple-element.30), channel_id=1, source_target_pairs={{0,62},{1,63},{2,0},{3,1},{4,2},{5,3},{6,4},{7,5},{8,6},{9,7},{10,... | collective-permute-start | bytes 49160 | tf_op jit(solution)/shard_map/ppermute | solution.py:292
  18.4 4.5 %prepare.1 = (bf16[768,512]{1,0:T(8,128)(2,1)}, bf16[4,256,512]{2,1,0:T(8,128)(2,1)}) custom-call(s32[1,8]{1,0:T(1,128)} %tcount.3, s32[1,4]{1,0:T(1,128)} %rcount.1, s32[1,8,2048]{2,1,0:T(8,128)} %tdst.3, s32[1,4,256]{2,1,0:T(4,128)} %rdst.1, bf16[768,512]{1,0:T(8,128)(2,1)} %cot.3), custom_call_target="tpu_custom_call" | custom-call | flops 805306368 | bytes 821272 | tf_op jit(solution)/shard_map/prepare/pallas_call | solution.py:178
  25.5 3.2 %build.5.tile0.tile1 = bf16[2,768,768]{2,1,0:T(8,128)(2,1)} custom-call(s32[2,1,2048]{2,1,0:T(1,128)} %pad_add_fusion.1.edges), custom_call_target="tpu_custom_call" | custom-call | flops 301989888 | bytes 2359296 | tf_op jit(solution)/shard_map/build/pallas_call | solution.py:192
  28.7 5.9 %all-to-all-start = ((bf16[4,256,512]{2,1,0:T(8,128)(2,1)}), bf16[4,256,512]{2,1,0:T(8,128)(2,1)S(1)}, u32[]{:S(2)}, u32[]{:S(2)}) async-start(bf16[4,256,512]{2,1,0:T(8,128)(2,1)} %get-tuple-element.42), calls=%async_computation | async-start | bytes 2097152 | tf_op jit(solution)/shard_map/all_to_all | solution.py:357
  34.6 2.9 %build.7.t0 = bf16[1,768,768]{2,1,0:T(8,128)(2,1)} custom-call(s32[1,1,2048]{2,1,0:T(1,128)} %get-tuple-element.63.edges), custom_call_target="tpu_custom_call" | custom-call | flops 150994944 | bytes 1179648 | tf_op jit(solution)/shard_map/build/pallas_call | solution.py:192
  38.1 3.1 %build.6.t0.t1 = bf16[2,768,768]{2,1,0:T(8,128)(2,1)} custom-call(s32[2,1,2048]{2,1,0:T(1,128)} %pad_add_fusion.2.edges), custom_call_target="tpu_custom_call" | custom-call | flops 301989888 | bytes 2359296 | tf_op jit(solution)/shard_map/build/pallas_call | solution.py:192
  47.6 3.0 %build.9.t1 = bf16[1,768,768]{2,1,0:T(8,128)(2,1)} custom-call(s32[1,1,2048]{2,1,0:T(1,128)} %get-tuple-element.54.edges), custom_call_target="tpu_custom_call" | custom-call | flops 150994944 | bytes 1179648 | tf_op jit(solution)/shard_map/build/pallas_call | solution.py:192
  51.2 2.4 %build.8.t2.t3 = bf16[2,768,768]{2,1,0:T(8,128)(2,1)} custom-call(s32[2,1,2048]{2,1,0:T(1,128)} %pad_add_fusion.3.edges), custom_call_target="tpu_custom_call" | custom-call | flops 301989888 | bytes 2359296 | tf_op jit(solution)/shard_map/build/pallas_call | solution.py:192
  54.8 3.8 %first_sum.1.before = f32[768,512]{1,0:T(8,128)S(1)} custom-call(bf16[2,768,768]{2,1,0:T(8,128)(2,1)S(1)} %copy-done.1, bf16[2,768,768]{2,1,0:T(8,128)(2,1)S(1)} %copy-done.1, bf16[768,512]{1,0:T(8,128)(2,1)S(1)} %copy-done.5, bf16[768,512]{1,0:T(8,128)(2,1)} %collective-permute-done.7.x1, s32[1,1024]{1,0:T(1,128)S(1)} %bitcast.32, ...), custom_call_target="tpu_custom_call" | custom-call | flops 1811939328 | bytes 4718592 | tf_op jit(solution)/shard_map/first_sum/pallas_call | solution.py:207
  58.6 5.9 %collective-permute-done.8.x0 = bf16[768,512]{1,0:T(8,128)(2,1)} collective-permute-done((bf16[768,512]{1,0:T(8,128)(2,1)}, bf16[768,512]{1,0:T(8,128)(2,1)}, u32[]{:S(2)}, u32[]{:S(2)}) %collective-permute-start.8) | collective-permute-done | bytes 786464 | tf_op jit(solution)/shard_map/ppermute | solution.py:297
  64.5 2.5 %collective-permute-done.9.x1 = bf16[768,512]{1,0:T(8,128)(2,1)} collective-permute-done((bf16[768,512]{1,0:T(8,128)(2,1)}, bf16[768,512]{1,0:T(8,128)(2,1)}, u32[]{:S(2)}, u32[]{:S(2)}) %collective-permute-start.9) | collective-permute-done | bytes 786464 | tf_op jit(solution)/shard_map/ppermute | solution.py:297
  71.3 4.3 %middle_sum.1.before = f32[768,512]{1,0:T(8,128)S(1)} custom-call(f32[768,512]{1,0:T(8,128)S(1)} %first_sum.1.before, bf16[2,768,768]{2,1,0:T(8,128)(2,1)S(1)} %copy-done, bf16[2,768,768]{2,1,0:T(8,128)(2,1)S(1)} %copy-done, bf16[2,768,768]{2,1,0:T(8,128)(2,1)S(1)} %copy-done.2, bf16[2,768,768]{2,1,0:T(8,128)(2,1)S(1)} %copy-done.2, ...), custom_call_target="tpu_custom_call" | custom-call | flops 2415919104 | bytes 6291456 | tf_op jit(solution)/shard_map/middle_sum/pallas_call | solution.py:228
  75.7 7.9 %collective-permute-done.12.x0 = bf16[768,512]{1,0:T(8,128)(2,1)S(1)} collective-permute-done((bf16[768,512]{1,0:T(8,128)(2,1)S(1)}, bf16[768,512]{1,0:T(8,128)(2,1)S(1)}, u32[]{:S(2)}, u32[]{:S(2)}) %collective-permute-start.12) | collective-permute-done | bytes 786464 | tf_op jit(solution)/shard_map/ppermute | solution.py:292
  83.6 2.3 %collective-permute-done.13.x1 = bf16[768,512]{1,0:T(8,128)(2,1)S(1)} collective-permute-done((bf16[768,512]{1,0:T(8,128)(2,1)S(1)}, bf16[768,512]{1,0:T(8,128)(2,1)S(1)}, u32[]{:S(2)}, u32[]{:S(2)}) %collective-permute-start.13) | collective-permute-done | bytes 786464 | tf_op jit(solution)/shard_map/ppermute | solution.py:326
  85.9 2.7 %last_sum.1 = (f32[768,512]{1,0:T(8,128)S(1)}, f32[256,512]{1,0:T(8,128)S(1)}, f32[256,512]{1,0:T(8,128)S(1)}) custom-call(f32[768,512]{1,0:T(8,128)S(1)} %middle_sum.1.before, bf16[1,768,768]{2,1,0:T(8,128)(2,1)S(1)} %copy-done.6, bf16[1,768,768]{2,1,0:T(8,128)(2,1)S(1)} %copy-done.7, bf16[768,512]{1,0:T(8,128)(2,1)S(1)} %collective-permute-done.12.x0, ...), custom_call_target="tpu_custom_call" | custom-call | flops 1811939328 | bytes 6291456 | tf_op jit(solution)/shard_map/last_sum/pallas_call | solution.py:245
  90.8 21.0 %all_to_all.10 = f32[16,2,16,512]{3,2,1,0:T(8,128)} all-to-all(f32[16,2,16,512]{3,2,1,0:T(8,128)S(1)} %maximum_bitcast_fusion), channel_id=1, replica_groups=mesh['group'=4,'z'=8,'y'=4,'core'=2] {'group','y'}, dimensions={0} | all-to-all | bytes 2097152 | tf_op jit(solution)/shard_map/all_to_all | solution.py:387
  116.0 2.8 %collective-permute-done.16 = f32[2,16,512]{2,1,0:T(8,128)S(1)} collective-permute-done((f32[2,16,512]{2,1,0:T(8,128)S(1)}, f32[2,16,512]{2,1,0:T(8,128)S(1)}, u32[]{:S(2)}, u32[]{:S(2)}) %collective-permute-start.16) | collective-permute-done | bytes 65568 | tf_op jit(solution)/shard_map/ppermute | solution.py:390
  119.9 2.5 %collective-permute-start.18 = (f32[2,16,512]{2,1,0:T(8,128)S(1)}, f32[2,16,512]{2,1,0:T(8,128)S(1)}, u32[]{:S(2)}, u32[]{:S(2)}) collective-permute-start(f32[2,16,512]{2,1,0:T(8,128)S(1)} %add_add_fusion), channel_id=1, source_target_pairs={{0,32},{8,40},{16,48},{24,56},{32,0},{40,8},{48,16},{56,24},{1,33}... | collective-permute-start | bytes 196616 | tf_op jit(solution)/shard_map/ppermute | solution.py:390
  122.4 4.6 %collective-permute-done.18 = f32[2,16,512]{2,1,0:T(8,128)S(1)} collective-permute-done((f32[2,16,512]{2,1,0:T(8,128)S(1)}, f32[2,16,512]{2,1,0:T(8,128)S(1)}, u32[]{:S(2)}, u32[]{:S(2)}) %collective-permute-start.18) | collective-permute-done | bytes 65568 | tf_op jit(solution)/shard_map/ppermute | solution.py:390
  133.8 2.3 %collective-permute-start.23 = (f32[4,2,16,512]{3,2,1,0:T(8,128)S(1)}, f32[4,2,16,512]{3,2,1,0:T(8,128)S(1)}, u32[]{:S(2)}, u32[]{:S(2)}) collective-permute-start(f32[4,2,16,512]{3,2,1,0:T(8,128)S(1)} %pad_maximum_fusion.refs_0_), channel_id=1, source_target_pairs={{0,128},{64,192},{128,0},{192,64},{1,129},{65,193},{129,1},{193,65... | collective-permute-start | bytes 786440 | tf_op jit(solution)/shard_map/ppermute | solution.py:297
  136.8 6.5 %collective-permute-start.25 = (f32[4,2,16,512]{3,2,1,0:T(8,128)S(1)}, f32[4,2,16,512]{3,2,1,0:T(8,128)S(1)}, u32[]{:S(2)}, u32[]{:S(2)}) collective-permute-start(f32[4,2,16,512]{3,2,1,0:T(8,128)S(1)} %pad_maximum_fusion.refs_0_), channel_id=1, source_target_pairs={{0,1},{1,0},{2,3},{3,2},{4,5},{5,4},{6,7},{7,6},{8,9},{9,8},{10,11... | collective-permute-start | bytes 786440 | tf_op jit(solution)/shard_map/ppermute | solution.py:326
  143.3 6.7 %collective-permute-start.26 = (f32[4,2,16,512]{3,2,1,0:T(8,128)S(1)}, f32[4,2,16,512]{3,2,1,0:T(8,128)S(1)}, u32[]{:S(2)}, u32[]{:S(2)}) collective-permute-start(f32[4,2,16,512]{3,2,1,0:T(8,128)S(1)} %collective-permute-done.22.refs_1_), channel_id=1, source_target_pairs={{0,1},{1,0},{2,3},{3,2},{4,5},{5,4},{6,7},{7,6},{8,9},{9,8},{10,11... | collective-permute-start | bytes 786440 | tf_op jit(solution)/shard_map/ppermute | solution.py:326
  151.0 2.8 %finish.1 = f32[768,512]{1,0:T(8,128)} custom-call(f32[768,512]{1,0:T(8,128)S(1)} %get-tuple-element.46.summed, bf16[768,512]{1,0:T(8,128)(2,1)S(1)} %copy-done.3, bf16[512,512]{1,0:T(8,128)(2,1)S(1)} %copy-done.9, bf16[512,512]{1,0:T(8,128)(2,1)S(1)} %copy-done.10), custom_call_target="tpu_custom_call" | custom-call | flops 1207959552 | bytes 3932160 | tf_op jit(solution)/shard_map/finish/pallas_call | solution.py:276
  (100 shorter events, 41.2 us)
Async XLA Ops:
  2.3 20.7 %collective-permute-start = (s32[1,2048]{1,0:T(1,128)}, s32[1,2048]{1,0:T(1,128)S(1)}, u32[]{:S(2)}, u32[]{:S(2)}) collective-permute-start(s32[1,2048]{1,0:T(1,128)} %get-tuple-element.29), channel_id=1, source_target_pairs={{0,57},{1,0},{2,59},{3,2},{4,61},{5,4},{6,63},{7,6},{8,1},{9,8},{1... | collective-permute-start | bytes 24584 | tf_op jit(solution)/shard_map/ppermute | solution.py:292
  5.5 17.4 %collective-permute-start.1 = (s32[2,2048]{1,0:T(2,128)}, s32[2,2048]{1,0:T(2,128)S(1)}, u32[]{:S(2)}, u32[]{:S(2)}) collective-permute-start(s32[2,2048]{1,0:T(2,128)} %get-tuple-element.30), channel_id=1, source_target_pairs={{0,62},{1,63},{2,0},{3,1},{4,2},{5,3},{6,4},{7,5},{8,6},{9,7},{10,... | collective-permute-start | bytes 49160 | tf_op jit(solution)/shard_map/ppermute | solution.py:292
  11.8 11.2 %collective-permute-start.2 = (s32[2,2048]{1,0:T(2,128)}, s32[2,2048]{1,0:T(2,128)S(1)}, u32[]{:S(2)}, u32[]{:S(2)}) collective-permute-start(s32[2,2048]{1,0:T(2,128)} %get-tuple-element.31), channel_id=1, source_target_pairs={{0,60},{1,61},{2,62},{3,63},{4,0},{5,1},{6,2},{7,3},{8,4},{9,5},{1... | collective-permute-start | bytes 49160 | tf_op jit(solution)/shard_map/ppermute | solution.py:292
  12.2 10.8 %collective-permute-start.3 = (s32[2,2048]{1,0:T(2,128)}, s32[2,2048]{1,0:T(2,128)S(1)}, u32[]{:S(2)}, u32[]{:S(2)}) collective-permute-start(s32[2,2048]{1,0:T(2,128)} %get-tuple-element.32), channel_id=1, source_target_pairs={{0,58},{1,59},{2,60},{3,61},{4,62},{5,63},{6,0},{7,1},{8,2},{9,3},... | collective-permute-start | bytes 49160 | tf_op jit(solution)/shard_map/ppermute | solution.py:292
  17.1 24.1 %collective-permute-start.5 = (f32[256,512]{1,0:T(8,128)}, f32[256,512]{1,0:T(8,128)S(1)}, u32[]{:S(2)}, u32[]{:S(2)}) collective-permute-start(f32[256,512]{1,0:T(8,128)} %slice_select_fusion), channel_id=1, source_target_pairs={{0,1},{1,0},{2,3},{3,2},{4,5},{5,4},{6,7},{7,6},{8,9},{9,8},{10,11... | collective-permute-start | bytes 1572872 | tf_op jit(solution)/shard_map/ppermute | solution.py:326
  23.0 19.5 %collective-permute-start.4 = (bf16[768,512]{1,0:T(8,128)(2,1)}, bf16[768,512]{1,0:T(8,128)(2,1)S(1)}, u32[]{:S(2)}, u32[]{:S(2)}) collective-permute-start(bf16[768,512]{1,0:T(8,128)(2,1)} %get-tuple-element.39.x0), channel_id=1, source_target_pairs={{0,56},{8,0},{16,8},{24,16},{32,24},{40,32},{48,40},{56,48},{1,57}... | collective-permute-start | bytes 2359304 | tf_op jit(solution)/shard_map/ppermute | solution.py:297
  24.5 17.7 %collective-permute-start.6 = (s32[3,2048]{1,0:T(4,128)S(1)}, s32[3,2048]{1,0:T(4,128)S(1)}, u32[]{:S(2)}, u32[]{:S(2)}) collective-permute-start(s32[3,2048]{1,0:T(4,128)S(1)} %pad_add_fusion), channel_id=1, source_target_pairs={{0,1},{1,0},{2,3},{3,2},{4,5},{5,4},{6,7},{7,6},{8,9},{9,8},{10,11... | collective-permute-start | bytes 73736 | tf_op jit(solution)/shard_map/ppermute | solution.py:326
  28.7 25.0 %all-to-all-start = ((bf16[4,256,512]{2,1,0:T(8,128)(2,1)}), bf16[4,256,512]{2,1,0:T(8,128)(2,1)S(1)}, u32[]{:S(2)}, u32[]{:S(2)}) async-start(bf16[4,256,512]{2,1,0:T(8,128)(2,1)} %get-tuple-element.42), calls=%async_computation | async-start | bytes 2097152 | tf_op jit(solution)/shard_map/all_to_all | solution.py:357
  44.2 9.4 %collective-permute-start.7 = (bf16[768,512]{1,0:T(8,128)(2,1)}, bf16[768,512]{1,0:T(8,128)(2,1)}, u32[]{:S(2)}, u32[]{:S(2)}) collective-permute-start(bf16[768,512]{1,0:T(8,128)(2,1)} %get-tuple-element.53), channel_id=1, source_target_pairs={{0,1},{1,0},{2,3},{3,2},{4,5},{5,4},{6,7},{7,6},{8,9},{9,8},{10,11... | collective-permute-start | bytes 2359304 | tf_op jit(solution)/shard_map/ppermute | solution.py:326
  45.0 19.5 %collective-permute-start.8 = (bf16[768,512]{1,0:T(8,128)(2,1)}, bf16[768,512]{1,0:T(8,128)(2,1)}, u32[]{:S(2)}, u32[]{:S(2)}) collective-permute-start(bf16[768,512]{1,0:T(8,128)(2,1)} %get-tuple-element.52), channel_id=1, source_target_pairs={{0,6},{2,0},{4,2},{6,4},{1,7},{3,1},{5,3},{7,5},{8,14},{10,8},{12,... | collective-permute-start | bytes 2359304 | tf_op jit(solution)/shard_map/ppermute | solution.py:297
  46.6 20.3 %collective-permute-start.9 = (bf16[768,512]{1,0:T(8,128)(2,1)}, bf16[768,512]{1,0:T(8,128)(2,1)}, u32[]{:S(2)}, u32[]{:S(2)}) collective-permute-start(bf16[768,512]{1,0:T(8,128)(2,1)} %get-tuple-element.51), channel_id=1, source_target_pairs={{0,2},{2,4},{4,6},{6,0},{1,3},{3,5},{5,7},{7,1},{8,10},{10,12},{12... | collective-permute-start | bytes 2359304 | tf_op jit(solution)/shard_map/ppermute | solution.py:297
  69.3 14.2 %collective-permute-start.12 = (bf16[768,512]{1,0:T(8,128)(2,1)S(1)}, bf16[768,512]{1,0:T(8,128)(2,1)S(1)}, u32[]{:S(2)}, u32[]{:S(2)}) collective-permute-start(bf16[768,512]{1,0:T(8,128)(2,1)S(1)} %broadcast_select_fusion), channel_id=1, source_target_pairs={{0,62},{1,3},{2,0},{3,5},{4,2},{5,7},{6,4},{7,9},{8,6},{9,11},{10,... | collective-permute-start | bytes 2359304 | tf_op jit(solution)/shard_map/ppermute | solution.py:292
  113.3 5.6 %collective-permute-start.16 = (f32[2,16,512]{2,1,0:T(8,128)S(1)}, f32[2,16,512]{2,1,0:T(8,128)S(1)}, u32[]{:S(2)}, u32[]{:S(2)}) collective-permute-start(f32[2,16,512]{2,1,0:T(8,128)S(1)} %reduce_sum.9), channel_id=1, source_target_pairs={{0,16},{8,24},{16,0},{24,8},{32,48},{40,56},{48,32},{56,40},{1,17}... | collective-permute-start | bytes 196616 | tf_op jit(solution)/shard_map/ppermute | solution.py:390
  113.8 5.1 %collective-permute-start.17 = (f32[2,16,512]{2,1,0:T(8,128)S(1)}, f32[2,16,512]{2,1,0:T(8,128)S(1)}, u32[]{:S(2)}, u32[]{:S(2)}) collective-permute-start(f32[2,16,512]{2,1,0:T(8,128)S(1)} %reduce_sum.9), channel_id=1, source_target_pairs={{0,24},{8,16},{16,8},{24,0},{32,56},{40,48},{48,40},{56,32},{1,25}... | collective-permute-start | bytes 196616 | tf_op jit(solution)/shard_map/ppermute | solution.py:390
  115.9 4.0 %collective-permute-start.15 = (f32[2,16,512]{2,1,0:T(8,128)S(1)}, f32[2,16,512]{2,1,0:T(8,128)S(1)}, u32[]{:S(2)}, u32[]{:S(2)}) collective-permute-start(f32[2,16,512]{2,1,0:T(8,128)S(1)} %reduce_sum.9), channel_id=1, source_target_pairs={{0,8},{8,0},{16,24},{24,16},{32,40},{40,32},{48,56},{56,48},{1,9},... | collective-permute-start | bytes 196616 | tf_op jit(solution)/shard_map/ppermute | solution.py:390
  119.9 7.1 %collective-permute-start.18 = (f32[2,16,512]{2,1,0:T(8,128)S(1)}, f32[2,16,512]{2,1,0:T(8,128)S(1)}, u32[]{:S(2)}, u32[]{:S(2)}) collective-permute-start(f32[2,16,512]{2,1,0:T(8,128)S(1)} %add_add_fusion), channel_id=1, source_target_pairs={{0,32},{8,40},{16,48},{24,56},{32,0},{40,8},{48,16},{56,24},{1,33}... | collective-permute-start | bytes 196616 | tf_op jit(solution)/shard_map/ppermute | solution.py:390
  128.2 4.6 %collective-permute-start.20 = (f32[2,16,512]{2,1,0:T(8,128)S(1)}, f32[2,16,512]{2,1,0:T(8,128)S(1)}, u32[]{:S(2)}, u32[]{:S(2)}) collective-permute-start(f32[2,16,512]{2,1,0:T(8,128)S(1)} %add.23), channel_id=1, source_target_pairs={{0,4},{2,6},{4,0},{6,2},{1,5},{3,7},{5,1},{7,3},{8,12},{10,14},{12... | collective-permute-start | bytes 196616 | tf_op jit(solution)/shard_map/ppermute | solution.py:297
  129.3 4.3 %collective-permute-start.19 = (f32[2,16,512]{2,1,0:T(8,128)S(1)}, f32[2,16,512]{2,1,0:T(8,128)S(1)}, u32[]{:S(2)}, u32[]{:S(2)}) collective-permute-start(f32[2,16,512]{2,1,0:T(8,128)S(1)} %add.23), channel_id=1, source_target_pairs={{0,2},{2,4},{4,6},{6,0},{1,3},{3,5},{5,7},{7,1},{8,10},{10,12},{12... | collective-permute-start | bytes 196616 | tf_op jit(solution)/shard_map/ppermute | solution.py:297
  133.7 9.7 %collective-permute-start.22 = (f32[4,2,16,512]{3,2,1,0:T(8,128)S(1)}, f32[4,2,16,512]{3,2,1,0:T(8,128)S(1)}, u32[]{:S(2)}, u32[]{:S(2)}) collective-permute-start(f32[4,2,16,512]{3,2,1,0:T(8,128)S(1)} %pad_maximum_fusion.refs_0_), channel_id=1, source_target_pairs={{0,64},{64,128},{128,192},{192,0},{1,65},{65,129},{129,193},{193,1... | collective-permute-start | bytes 786440 | tf_op jit(solution)/shard_map/ppermute | solution.py:297
  133.8 16.3 %collective-permute-start.23 = (f32[4,2,16,512]{3,2,1,0:T(8,128)S(1)}, f32[4,2,16,512]{3,2,1,0:T(8,128)S(1)}, u32[]{:S(2)}, u32[]{:S(2)}) collective-permute-start(f32[4,2,16,512]{3,2,1,0:T(8,128)S(1)} %pad_maximum_fusion.refs_0_), channel_id=1, source_target_pairs={{0,128},{64,192},{128,0},{192,64},{1,129},{65,193},{129,1},{193,65... | collective-permute-start | bytes 786440 | tf_op jit(solution)/shard_map/ppermute | solution.py:297
  136.0 14.0 %collective-permute-start.24 = (f32[4,2,16,512]{3,2,1,0:T(8,128)S(1)}, f32[4,2,16,512]{3,2,1,0:T(8,128)S(1)}, u32[]{:S(2)}, u32[]{:S(2)}) collective-permute-start(f32[4,2,16,512]{3,2,1,0:T(8,128)S(1)} %pad_maximum_fusion.refs_0_), channel_id=1, source_target_pairs={{0,192},{64,0},{128,64},{192,128},{1,193},{65,1},{129,65},{193,129... | collective-permute-start | bytes 786440 | tf_op jit(solution)/shard_map/ppermute | solution.py:297
  136.8 17.0 %collective-permute-start.25 = (f32[4,2,16,512]{3,2,1,0:T(8,128)S(1)}, f32[4,2,16,512]{3,2,1,0:T(8,128)S(1)}, u32[]{:S(2)}, u32[]{:S(2)}) collective-permute-start(f32[4,2,16,512]{3,2,1,0:T(8,128)S(1)} %pad_maximum_fusion.refs_0_), channel_id=1, source_target_pairs={{0,1},{1,0},{2,3},{3,2},{4,5},{5,4},{6,7},{7,6},{8,9},{9,8},{10,11... | collective-permute-start | bytes 786440 | tf_op jit(solution)/shard_map/ppermute | solution.py:326
  143.3 10.5 %collective-permute-start.26 = (f32[4,2,16,512]{3,2,1,0:T(8,128)S(1)}, f32[4,2,16,512]{3,2,1,0:T(8,128)S(1)}, u32[]{:S(2)}, u32[]{:S(2)}) collective-permute-start(f32[4,2,16,512]{3,2,1,0:T(8,128)S(1)} %collective-permute-done.22.refs_1_), channel_id=1, source_target_pairs={{0,1},{1,0},{2,3},{3,2},{4,5},{5,4},{6,7},{7,6},{8,9},{9,8},{10,11... | collective-permute-start | bytes 786440 | tf_op jit(solution)/shard_map/ppermute | solution.py:326
  150.1 3.7 %collective-permute-start.27 = (f32[4,2,16,512]{3,2,1,0:T(8,128)S(1)}, f32[4,2,16,512]{3,2,1,0:T(8,128)S(1)}, u32[]{:S(2)}, u32[]{:S(2)}) collective-permute-start(f32[4,2,16,512]{3,2,1,0:T(8,128)S(1)} %collective-permute-done.23.refs_2_), channel_id=1, source_target_pairs={{0,1},{1,0},{2,3},{3,2},{4,5},{5,4},{6,7},{7,6},{8,9},{9,8},{10,11... | collective-permute-start | bytes 786440 | tf_op jit(solution)/shard_map/ppermute | solution.py:326
  (22 other events, 243.1 us)

commit v4 on v3

v4 whole, which is shorter than its diff:
```python
import functools
import math

import jax
import jax.numpy as jnp
from jax import lax
from jax.experimental import pallas as pl
from jax.experimental.pallas import tpu as pltpu
from jax.sharding import Mesh
from jax.sharding import PartitionSpec as P

F32 = jnp.float32
BF16 = jnp.bfloat16
I32 = jnp.int32
CHUNK = 1024
ALONG = (((1,), (1,)), ((), ()))
DOWN = (((0,), (0,)), ((), ()))


def dot(a, b, dims=(((1,), (0,)), ((), ()))):
    return lax.dot_general(a, b, dims, preferred_element_type=F32)


def hot(rows, ids):
    spots = lax.broadcasted_iota(I32, (rows, ids.shape[1]), 0)
    return jnp.where(spots == ids, 1.0, 0.0).astype(BF16)


def small_hot(rows, ids):
    spots = lax.broadcasted_iota(jnp.int16, (rows, ids.shape[1]), 0)
    ones = jnp.where(spots == ids.astype(jnp.int16), jnp.ones((), BF16), jnp.zeros((), BF16))
    return ones.astype(jnp.float8_e4m3fn)


def prepare(
    tcount, rcount, tsrc, tdst, rdst, cot, x_out, rows_out, own, first, pair1, pair2, pair3
):
    nodes = cot.shape[0]
    odd = lax.axis_index("core") == 1
    offs, ept = tdst.shape[1], tdst.shape[2]
    ngroup, cap = rdst.shape[1], rdst.shape[2]
    slot = lax.broadcasted_iota(I32, (1, ept), 1)
    counts = jnp.zeros((32, 32), F32)
    lists = []
    for s in range(offs):
        live = slot < tcount[0:1, s : s + 1]
        ids = jnp.where(live, tdst[0, s : s + 1, :], 1023)
        counts = counts + dot(hot(32, ids >> 5), hot(32, ids & 31), ALONG)
        lists.append(jnp.where(live, tsrc[0, s : s + 1, :] * 1024 + ids, -1))
    own[...] = lists[0]
    first[...] = jnp.where(odd, lists[1], lists[7])
    for j, pair in ((1, pair1), (2, pair2), (3, pair3)):
        pair[0:1, :] = lists[2 * j]
        pair[1:2, :] = jnp.where(odd, lists[2 * j + 1], lists[2 * j - 1])
    slot = lax.broadcasted_iota(I32, (1, cap), 1)
    marked = []
    for g in range(ngroup):
        ids = jnp.where(slot < rcount[0:1, g : g + 1], rdst[0, g : g + 1, :], 1023)
        counts = counts + dot(hot(32, ids >> 5), hot(32, ids & 31), ALONG)
        marked.append(hot(nodes, ids))
    upper = jnp.floor(counts * (1.0 / 128.0))
    lower = counts - upper * 128.0
    node = lax.broadcasted_iota(I32, (nodes, 32), 0)
    lane = lax.broadcasted_iota(I32, (nodes, 32), 1)
    pick = jnp.where((node >> 5) == lane, 1.0, 0.0).astype(BF16)
    spread = dot(pick, upper.astype(BF16)) * 128.0 + dot(pick, lower.astype(BF16))
    degree = jnp.sum(jnp.where((node & 31) == lane, spread, 0.0), axis=1, keepdims=True)
    inverse = 1.0 / jnp.maximum(degree, 1.0)
    x = (inverse * cot[...].astype(F32)).astype(BF16)
    x_out[...] = x
    for g in range(ngroup):
        rows_out[g] = dot(marked[g], x, DOWN).astype(BF16)


def build(rows, *refs):
    lists, (tile_out, acc, edges) = refs[:-3], refs[-3:]
    s = pl.program_id(0)
    nodes = acc.shape[0]

    @pl.when(s == 0)
    def _():
        for k, row in enumerate(rows):
            edges[k] = lists[k][row : row + 1, :]

    acc[...] = jnp.zeros_like(acc)
    live = jnp.sum((edges[s] >= 0).astype(I32))

    def step(i, carry):
        packed = edges[s, :, pl.ds(pl.multiple_of(i * CHUNK, CHUNK), CHUNK)]
        acc[...] += dot(small_hot(nodes, packed >> 10), small_hot(nodes, packed & 1023), ALONG)
        return carry

    lax.fori_loop(0, (live + CHUNK - 1) // CHUNK, step, 0)
    tile_out[0] = acc[...].astype(BF16)


def most_sum(t0, t1, t2, t3, t4, t5, x0, x1, x2, x3, x4, x5, ids, rows, out):
    i = pl.program_id(0)
    block = out.shape[0]
    spots = lax.broadcasted_iota(I32, (block, ids.shape[1]), 0) + i * block
    total = dot(jnp.where(spots == ids[...], 1.0, 0.0).astype(BF16), rows[...])
    for tile, x in ((t0, x0), (t1, x1), (t2, x2), (t3, x3), (t4, x4), (t5, x5)):
        total = total + dot(tile[0], x[...])
    out[...] = total


def last_sum(before, tiles, x0, x1, feats, cot, out, send, keep, grad_self, grad_neigh):
    nodes = before.shape[0]
    grad_self[...] = dot(feats[...], cot[...], DOWN)
    for i in range(nodes // BLOCK):
        rows = slice(i * BLOCK, (i + 1) * BLOCK)
        total = before[rows, :] + dot(tiles[0, rows, :], x0[...])
        total = total + dot(tiles[1, rows, :], x1[...])
        out[rows, :] = total
        top = total.astype(BF16)
        rest = (total - top.astype(F32)).astype(BF16)
        part = dot(feats[rows, :], top, DOWN) + dot(feats[rows, :], rest, DOWN)
        if i == 0:
            grad_neigh[...] = part
        else:
            grad_neigh[...] += part
    pieces, _, size, _ = send.shape
    core = lax.axis_index("core")
    for n in range(pieces):
        here = pl.ds(pl.multiple_of((core * pieces + n) * size, size), size)
        there = pl.ds(pl.multiple_of(((1 - core) * pieces + n) * size, size), size)
        for m, grad in enumerate((grad_self, grad_neigh)):
            keep[n, m] = grad[here, :]
            send[n, m] = grad[there, :]


def place(factor, *refs):
    out_self, out_neigh = refs[-2], refs[-1]
    ngroup = (len(refs) - 2) // 2
    ny, _, size, _ = refs[0].shape
    group, core, ypos = (lax.axis_index(a) for a in ("group", "core", "y"))
    for n in range(2 * ngroup):
        k = core if n < ngroup else 1 - core
        g = lax.rem(group - n % ngroup + ngroup, ngroup)
        for t in range(ny):
            y = lax.rem(ypos - t + ny, ny)
            at = pl.multiple_of(((k * ngroup + g) * ny + y) * size, size)
            out_self[pl.ds(at, size), :] = refs[n][t, 0] * factor
            out_neigh[pl.ds(at, size), :] = refs[n][t, 1] * factor


def finish(summed, cot, w_self, w_neigh, out):
    total = summed[...]
    top = total.astype(BF16)
    rest = (total - top.astype(F32)).astype(BF16)
    out[...] = (
        dot(cot[...], w_self[...], ALONG)
        + dot(top, w_neigh[...], ALONG)
        + dot(rest, w_neigh[...], ALONG)
    )


BLOCK = 256
MIB = 1024 * 1024


def params(mib):
    return pltpu.CompilerParams(vmem_limit_bytes=mib * MIB)


def whole(shape):
    return pl.BlockSpec(shape, lambda i: (0,) * len(shape))


def tile_spec(slot, nodes):
    return pl.BlockSpec((1, BLOCK, nodes), lambda i: (slot, i, 0))


def row_spec(width):
    return pl.BlockSpec((BLOCK, width), lambda i: (i, 0))


def estimate(macs, moved):
    return pl.CostEstimate(flops=2 * macs, bytes_accessed=moved, transcendentals=0)


def run_whole(kernel, given, made, macs, name):
    return pl.pallas_call(
        kernel,
        grid=(1,),
        out_shape=[jax.ShapeDtypeStruct(*m) for m in made],
        in_specs=[whole(v.shape) for v in given],
        out_specs=[whole(m[0]) for m in made],
        compiler_params=params(63),
        cost_estimate=estimate(macs, sum(2 * v.size for v in given)),
        name=name,
    )(*given)


def run_build(chosen, nodes):
    slots, ept = len(chosen), chosen[0][0].shape[1]
    rows = tuple(row for _, row in chosen)
    lists = [v for v, _ in chosen]
    return pl.pallas_call(
        functools.partial(build, rows),
        grid=(slots,),
        in_specs=[whole(v.shape) for v in lists],
        out_specs=pl.BlockSpec((1, nodes, nodes), lambda s: (s, 0, 0)),
        scratch_shapes=[pltpu.VMEM((nodes, nodes), F32), pltpu.VMEM((slots, 1, ept), I32)],
        out_shape=jax.ShapeDtypeStruct((slots, nodes, nodes), BF16),
        compiler_params=params(60),
        cost_estimate=estimate(nodes * ept, nodes * ept),
        name="build",
    )(*lists)


def run_most(near, quad, xs, ids, rows):
    nodes, width = xs[0].shape
    return pl.pallas_call(
        most_sum,
        grid=(nodes // BLOCK,),
        in_specs=[tile_spec(s, nodes) for s in (0, 1, 0, 1, 2, 3)]
        + [whole(v.shape) for v in (*xs, ids, rows)],
        out_specs=row_spec(width),
        out_shape=jax.ShapeDtypeStruct((nodes, width), F32),
        compiler_params=params(36),
        cost_estimate=estimate(7 * nodes * nodes * width, 16 * nodes * width),
        name="most_sum",
    )(near, near, quad, quad, quad, quad, *xs, ids, rows)


def run_last(before, tiles, xs, features, cotangent, pieces):
    nodes, width = before.shape
    vm = pl.BlockSpec(memory_space=pltpu.VMEM)
    half = jax.ShapeDtypeStruct((pieces, 2, width // (2 * pieces), width), F32)
    return pl.pallas_call(
        last_sum,
        in_specs=[vm] * 6,
        out_specs=[vm] * 3,
        out_shape=(jax.ShapeDtypeStruct((nodes, width), F32), half, half),
        scratch_shapes=[pltpu.VMEM((width, width), F32)] * 2,
        compiler_params=params(24),
        cost_estimate=estimate(3 * nodes * nodes * width, 16 * nodes * width),
        name="last_sum",
    )(before, tiles, *xs, features, cotangent)


def run_place(pieces, factor, width):
    return pl.pallas_call(
        lambda *refs: place(factor, *refs),
        grid=(1,),
        in_specs=[whole(v.shape) for v in pieces],
        out_specs=[whole((width, width))] * 2,
        out_shape=[jax.ShapeDtypeStruct((width, width), F32)] * 2,
        compiler_params=params(24),
        cost_estimate=estimate(width * width, 16 * width * width),
        name="place",
    )(*pieces)


def run_finish(summed, cotangent, w_self, w_neigh):
    nodes, width = summed.shape
    return pl.pallas_call(
        finish,
        grid=(nodes // BLOCK,),
        in_specs=[row_spec(width), row_spec(width), whole(w_self.shape), whole(w_neigh.shape)],
        out_specs=row_spec(width),
        out_shape=jax.ShapeDtypeStruct((nodes, width), F32),
        compiler_params=params(24),
        cost_estimate=estimate(3 * nodes * width * width, 10 * nodes * width),
        name="finish",
    )(summed, cotangent, w_self, w_neigh)


BLK = ("z", "y", "core")


def moved(value, perm):
    return lax.ppermute(value, BLK, perm)


def turned(value, axis, by):
    length = lax.axis_size(axis)
    return lax.ppermute(value, axis, [(i, (i + by) % length) for i in range(length)])


def fence(values):
    return lax.optimization_barrier(values)


def on_device(
    features,
    cotangent,
    w_self,
    w_neigh,
    tile_src,
    tile_dst,
    tile_count,
    send_ids,
    recv_dst,
    recv_count,
):
    nodes, width = features.shape
    ngroup, cap = send_ids.shape[1], send_ids.shape[2]
    ept = tile_src.shape[2]
    nz, ny = lax.axis_size("z"), lax.axis_size("y")
    nblk = nz * ny * 2
    core, ypos = lax.axis_index("core"), lax.axis_index("y")
    ring = range(nblk)
    swap = [(0, 1), (1, 0)]

    def swapped(v):
        return lax.ppermute(v, "core", swap)

    x, rows, own, first, pair1, pair2, pair3 = run_whole(
        prepare,
        (tile_count, recv_count, tile_src, tile_dst, recv_dst, cotangent),
        [((nodes, width), BF16), ((ngroup, cap, width), BF16)]
        + [((1, ept), I32)] * 2
        + [((2, ept), I32)] * 3,
        ngroup * cap * nodes * width,
        "prepare",
    )
    far = turned(x, "z", -1)
    first = moved(first, [(i, (i - 1 if i % 2 else i - 7) % nblk) for i in ring])
    pairs = [
        moved(p, [(i, (i - 2 * j) % nblk) for i in ring])
        for j, p in ((1, pair1), (2, pair2), (3, pair3))
    ]
    rows = fence((rows, first))[0]
    returned = lax.all_to_all(rows, "group", split_axis=0, concat_axis=0, tiled=True)
    x, far = fence((x, far, first, pairs))[:2]

    one = turned(jnp.where(ypos == 0, far, x), "y", -1)
    three = turned(jnp.where(ypos == ny - 1, x, far), "y", 1)
    side = swapped(jnp.where(core == 1, x, far))
    other = swapped(jnp.concatenate([p[1:2] for p in pairs], axis=0))
    near = run_build(((own, 0), (first, 0)), nodes)
    quad = run_build(((pairs[0], 0), (pairs[2], 0), (other, 0), (other, 2)), nodes)
    mid = run_build(((pairs[1], 0), (other, 1)), nodes)
    one, three = fence((one, three, near, quad, mid, side))[:2]
    relay = jnp.where(core == 0, one, three)

    two = moved(
        relay,
        [(i, (i - 2 if i % 2 == 0 else i + 2) % nblk) for i in ring],
    )
    one_b = swapped(one)
    three_b = swapped(three)
    summed = run_most(
        near,
        quad,
        (x, side, one, three, one_b, three_b),
        send_ids.reshape(1, ngroup * cap),
        returned.reshape(ngroup * cap, width),
    )
    two = fence((two, summed))[0]

    two_b = swapped(two)
    summed, send, keep = run_last(
        summed, mid, (two, two_b), features, cotangent, ngroup * ny
    )

    part = keep + swapped(send)
    part = lax.all_to_all(part, ("group", "y"), split_axis=0, concat_axis=0, tiled=True).sum(0)

    def zflip(v, k):
        return lax.ppermute(v, "z", [(i, i ^ k) for i in range(nz)])

    part = (part + zflip(part, 1)) + (zflip(part, 2) + zflip(part, 3))
    part, total = fence((part, run_finish(summed, cotangent, w_self, w_neigh)))
    part = part + zflip(part, 4)
    part = jnp.stack([part] + [turned(part, "y", t) for t in range(1, ny)])
    held = [part] + [turned(part, "group", s) for s in range(1, ngroup)]
    held = held + [swapped(v) for v in held]
    factor = 1.0 / math.sqrt(nodes * ngroup * nblk)
    grad_self, grad_neigh = run_place(held, factor, width)
    return (total, grad_self, grad_neigh)


def solution(mesh):
    blk = mesh.shape["blk"]
    fine = Mesh(
        mesh.devices.reshape(mesh.shape["group"], blk // 8, 4, 2), ("group",) + BLK
    )
    both = ("group",) + BLK
    placed = (
        P(both, None),
        P(both, None),
        P(),
        P(),
        P(both, None, None),
        P(both, None, None),
        P(both, None),
        P(both, None, None),
        P(both, None, None),
        P(both, None),
    )
    return jax.shard_map(
        on_device,
        mesh=fine,
        in_specs=placed,
        out_specs=(P(both, None), P(), P()),
        check_vma=False,
    )
```

time: 157 us -> 152 us (0.968)
  waiting for transfers between devices: 35.4 us -> 27.9 us
  starting transfers between devices: 48.4 us -> 53.3 us
  blocking collectives: 21 us -> 23.5 us
  matrix products: 1.97 us -> 0 us
  other arithmetic: 8.27 us -> 6.41 us
    ppermute x9, waiting for transfers between devices: 12.9 us -> 4.64 us  [turned(): lax.ppermute(value, axis, [(i, (i + by) % length) for i in range(length)])]
    ppermute x5, waiting for transfers between devices: 7.92 us -> 15.6 us  [moved(): return lax.ppermute(value, BLK, perm)]
    ppermute x4, waiting for transfers between devices: 8.53 us -> 2.04 us  [zflip(): return lax.ppermute(v, 'z', [(i, i ^ k) for i in range(nz)])]
    ppermute x9, starting transfers between devices: 8.16 us -> 13.5 us  [turned(): lax.ppermute(value, axis, [(i, (i + by) % length) for i in range(length)])]
    ppermute x4, starting transfers between devices: 5.21 us -> 8.34 us  [zflip(): return lax.ppermute(v, 'z', [(i, i ^ k) for i in range(nz)])]
    ppermute x5, starting transfers between devices: 11.1 us -> 8.25 us  [moved(): return lax.ppermute(value, BLK, perm)]
    all_to_all x1, blocking collectives: 21 us -> 23.5 us  [on_device(): lax.all_to_all(part, ('group', 'y'), split_axis=0, concat_axis=0, tiled=T...]
    dot_general x1 -> x0, matrix products: 1.97 us -> none  [dot(): return lax.dot_general(a, b, dims, preferred_element_type=F32)]
  transfers between devices with their start and end apart: 30 -> 29, of which waited for: 14 -> 17; matrix products, arithmetic and copies ran while one was open for 6% -> 1% of each run, Pallas kernels for 19% -> 17%
where the time goes in v4:
time: 152 us
  starting transfers between devices  53.3 us (35%)
  Pallas kernels  35.8 us (24%)
  waiting for transfers between devices  27.9 us (18%)
  blocking collectives  23.5 us (15%)
  other arithmetic  6.41 us (4%)
  local copies, waits for them, and re-layouts  4.16 us (3%)
    all_to_all x1, blocking collectives, on_device(): lax.all_to_all(part, ('group', 'y'), split_axis=0, concat_axis=0, tiled=T...  23.5 us
    ppermute x10, starting transfers between devices, swapped(): return lax.ppermute(v, 'core', swap)  19.2 us
    ppermute x5, waiting for transfers between devices, moved(): return lax.ppermute(value, BLK, perm)  15.6 us
    pallas_call x3, Pallas kernels, run_build(): pl.pallas_call(functools.partial(build, rows), grid=(slots,), in_specs=[w...  15.1 us
    ppermute x9, starting transfers between devices, turned(): lax.ppermute(value, axis, [(i, (i + by) % length) for i in range(length)])  13.5 us
    ppermute x4, starting transfers between devices, zflip(): return lax.ppermute(v, 'z', [(i, i ^ k) for i in range(nz)])  8.34 us
    ppermute x5, starting transfers between devices, moved(): return lax.ppermute(value, BLK, perm)  8.25 us
    pallas_call x1, Pallas kernels, run_most(): pl.pallas_call(most_sum, grid=(nodes // BLOCK,), in_specs=[tile_spec(s, n...  7.24 us
  transfers between devices with their start and end apart: 29, of which 17 were waited for; matrix products, arithmetic and copies ran while one was open for 1% of the time, Pallas kernels for 17%

profile of v4, /device:TPU:1, one launch (start us, length us, event | category | flops | bytes accessed | tf_op | source)
XLA Modules:
  0.0 151.9 jit_solution(12031486160758380348)
XLA Ops:
  0.6 4.7 %prepare.1 = (bf16[768,512]{1,0:T(8,128)(2,1)}, bf16[4,256,512]{2,1,0:T(8,128)(2,1)}, s32[1,2048]{1,0:T(1,128)}, s32[1,2048]{1,0:T(1,128)}, s32[2,2048]{1,0:T(2,...) custom-call(s32[1,8]{1,0:T(1,128)} %tcount.1, s32[1,4]{1,0:T(1,128)} %rcount.1, s32[1,8,2048]{2,1,0:T(8,128)} %tsrc.1, ...), custom_call_target="tpu_custom_call" | custom-call | flops 805306368 | bytes 854040 | tf_op jit(solution)/shard_map/prepare/pallas_call | solution.py:183
  5.3 6.4 %collective-permute-start.5 = (bf16[768,512]{1,0:T(8,128)(2,1)}, bf16[768,512]{1,0:T(8,128)(2,1)S(1)}, u32[]{:S(2)}, u32[]{:S(2)}) collective-permute-start(bf16[768,512]{1,0:T(8,128)(2,1)} %get-tuple-element.29.x0), channel_id=1, source_target_pairs={{0,56},{8,0},{16,8},{24,16},{32,24},{40,32},{48,40},{56,48},{1,57}... | collective-permute-start | bytes 2359304 | tf_op jit(solution)/shard_map/ppermute | solution.py:279
  11.7 3.2 %collective-permute-start.1 = (s32[2,2048]{1,0:T(2,128)}, s32[2,2048]{1,0:T(2,128)S(1)}, u32[]{:S(2)}, u32[]{:S(2)}) collective-permute-start(s32[2,2048]{1,0:T(2,128)} %get-tuple-element.25), channel_id=1, source_target_pairs={{0,62},{1,63},{2,0},{3,1},{4,2},{5,3},{6,4},{7,5},{8,6},{9,7},{10,... | collective-permute-start | bytes 49160 | tf_op jit(solution)/shard_map/ppermute | solution.py:274
  18.8 8.2 %collective-permute-done.refs_1_ = s32[1,2048]{1,0:T(1,128)S(1)} collective-permute-done((s32[1,2048]{1,0:T(1,128)}, s32[1,2048]{1,0:T(1,128)S(1)}, u32[]{:S(2)}, u32[]{:S(2)}) %collective-permute-start) | collective-permute-done | bytes 8224 | tf_op jit(solution)/shard_map/ppermute | solution.py:274
  29.2 2.7 %broadcast_select_fusion.1 = (bf16[768,512]{1,0:T(8,128)(2,1)}, bf16[768,512]{1,0:T(8,128)(2,1)}, bf16[768,512]{1,0:T(8,128)(2,1)}) fusion(bf16[768,512]{1,0:T(8,128)(2,1)} %get-tuple-element.29.x0, bf16[768,512]{1,0:T(8,128)(2,1)S(1)} %collective-permute-done.5, pred[]{:T(512)S(6)} %eq.14, pred[]{:T(512)S(6)} %eq.13, pred[]{:T(512)S(6)} %eq.12), kind=kLoop, calls=%fused_computation.1 | loop fusion | flops 1179648 | bytes 3932163 | tf_op jit(solution)/shard_map/jit(_where)/select_n | solution.py:330
  35.8 4.0 %all-to-all-start = ((bf16[4,256,512]{2,1,0:T(8,128)(2,1)}), bf16[4,256,512]{2,1,0:T(8,128)(2,1)S(1)}, u32[]{:S(2)}, u32[]{:S(2)}) async-start(bf16[4,256,512]{2,1,0:T(8,128)(2,1)} %get-tuple-element.34), calls=%async_computation | async-start | bytes 2097152 | tf_op jit(solution)/shard_map/all_to_all | solution.py:326
  39.8 2.5 %build.3.t0.t1 = bf16[2,768,768]{2,1,0:T(8,128)(2,1)} custom-call(s32[1,2048]{1,0:T(1,128)} %get-tuple-element.23.refs_0_, s32[1,2048]{1,0:T(1,128)} %copy-done.13), custom_call_target="tpu_custom_call" | custom-call | flops 3145728 | bytes 1572864 | tf_op jit(solution)/shard_map/build/pallas_call | solution.py:199
  42.9 7.7 %build.4.t2.t3.t4.t5 = bf16[4,768,768]{2,1,0:T(8,128)(2,1)} custom-call(s32[2,2048]{1,0:T(2,128)} %copy-done.10, s32[2,2048]{1,0:T(2,128)} %copy-done.11, s32[3,2048]{1,0:T(4,128)} %copy-done.9, s32[3,2048]{1,0:T(4,128)} %copy-done.9), custom_call_target="tpu_custom_call" | custom-call | flops 3145728 | bytes 1572864 | tf_op jit(solution)/shard_map/build/pallas_call | solution.py:199
  50.6 4.9 %build.5.tiles = bf16[2,768,768]{2,1,0:T(8,128)(2,1)} custom-call(s32[2,2048]{1,0:T(2,128)} %copy-done.12, s32[3,2048]{1,0:T(4,128)} %copy-done.9), custom_call_target="tpu_custom_call" | custom-call | flops 3145728 | bytes 1572864 | tf_op jit(solution)/shard_map/build/pallas_call | solution.py:199
  56.8 2.1 %broadcast_select_fusion = bf16[768,512]{1,0:T(8,128)(2,1)} fusion(bf16[768,512]{1,0:T(8,128)(2,1)} %collective-permute-done.7.x2, bf16[768,512]{1,0:T(8,128)(2,1)} %collective-permute-done.8.x3, pred[]{:T(512)S(6)} %eq.15), kind=kLoop, calls=%fused_computation | loop fusion | flops 393216 | bytes 2359297 | tf_op jit(solution)/shard_map/jit(_where)/select_n | solution.py:337
  60.1 2.3 %copy-done = bf16[4,768,768]{2,1,0:T(8,128)(2,1)S(1)} copy-done((bf16[4,768,768]{2,1,0:T(8,128)(2,1)S(1)}, bf16[4,768,768]{2,1,0:T(8,128)(2,1)}, u32[]{:S(2)}) %copy-start) | copy-done | bytes 4718616
  63.6 7.2 %most_sum.1.before = f32[768,512]{1,0:T(8,128)S(1)} custom-call(bf16[2,768,768]{2,1,0:T(8,128)(2,1)S(1)} %copy-done.1, bf16[2,768,768]{2,1,0:T(8,128)(2,1)S(1)} %copy-done.1, bf16[4,768,768]{2,1,0:T(8,128)(2,1)S(1)} %copy-done, bf16[4,768,768]{2,1,0:T(8,128)(2,1)S(1)} %copy-done, bf16[4,768,768]{2,1,0:T(8,128)(2,1)S(1)} %copy-done, ...), custom_call_target="tpu_custom_call" | custom-call | flops 4227858432 | bytes 6291456 | tf_op jit(solution)/shard_map/most_sum/pallas_call | solution.py:214
  70.9 5.2 %collective-permute-done.11.x0 = bf16[768,512]{1,0:T(8,128)(2,1)} collective-permute-done((bf16[768,512]{1,0:T(8,128)(2,1)}, bf16[768,512]{1,0:T(8,128)(2,1)}, u32[]{:S(2)}, u32[]{:S(2)}) %collective-permute-start.11) | collective-permute-done | bytes 786464 | tf_op jit(solution)/shard_map/ppermute | solution.py:274
  77.8 2.1 %collective-permute-done.12.x1 = bf16[768,512]{1,0:T(8,128)(2,1)S(1)} collective-permute-done((bf16[768,512]{1,0:T(8,128)(2,1)}, bf16[768,512]{1,0:T(8,128)(2,1)S(1)}, u32[]{:S(2)}, u32[]{:S(2)}) %collective-permute-start.12) | collective-permute-done | bytes 786464 | tf_op jit(solution)/shard_map/ppermute | solution.py:308
  79.9 4.4 %last_sum.1 = (f32[768,512]{1,0:T(8,128)S(1)}, f32[16,2,16,512]{3,2,1,0:T(8,128)S(1)}, f32[16,2,16,512]{3,2,1,0:T(8,128)S(1)}) custom-call(f32[768,512]{1,0:T(8,128)S(1)} %most_sum.1.before, bf16[2,768,768]{2,1,0:T(8,128)(2,1)S(1)} %copy-done.2, bf16[768,512]{1,0:T(8,128)(2,1)} %collective-permute-done.11.x0, ...), custom_call_target="tpu_custom_call" | custom-call | flops 1811939328 | bytes 6291456 | tf_op jit(solution)/shard_map/last_sum/pallas_call | solution.py:231
  84.8 2.3 %collective-permute-done.13 = f32[16,2,16,512]{3,2,1,0:T(8,128)S(1)} collective-permute-done((f32[16,2,16,512]{3,2,1,0:T(8,128)S(1)}, f32[16,2,16,512]{3,2,1,0:T(8,128)S(1)}, u32[]{:S(2)}, u32[]{:S(2)}) %collective-permute-start.13) | collective-permute-done | bytes 1048608 | tf_op jit(solution)/shard_map/ppermute | solution.py:308
  87.4 23.5 %all_to_all.10 = f32[16,2,16,512]{3,2,1,0:T(8,128)} all-to-all(f32[16,2,16,512]{3,2,1,0:T(8,128)S(1)} %add.15), channel_id=1, replica_groups=mesh['group'=4,'z'=8,'y'=4,'core'=2] {'group','y'}, dimensions={0} | all-to-all | bytes 2097152 | tf_op jit(solution)/shard_map/all_to_all | solution.py:360
  112.5 2.4 %collective-permute-start.14 = (f32[2,16,512]{2,1,0:T(8,128)S(1)}, f32[2,16,512]{2,1,0:T(8,128)S(1)}, u32[]{:S(2)}, u32[]{:S(2)}) collective-permute-start(f32[2,16,512]{2,1,0:T(8,128)S(1)} %reduce_sum.9), channel_id=1, source_target_pairs={{0,8},{8,0},{16,24},{24,16},{32,40},{40,32},{48,56},{56,48},{1,9},... | collective-permute-start | bytes 196616 | tf_op jit(solution)/shard_map/ppermute | solution.py:363
  114.9 2.8 %finish.1 = f32[768,512]{1,0:T(8,128)} custom-call(f32[768,512]{1,0:T(8,128)S(1)} %get-tuple-element.38.summed, bf16[768,512]{1,0:T(8,128)(2,1)S(1)} %copy-done.4, bf16[512,512]{1,0:T(8,128)(2,1)S(1)} %copy-done.7, bf16[512,512]{1,0:T(8,128)(2,1)S(1)} %copy-done.8), custom_call_target="tpu_custom_call" | custom-call | flops 1207959552 | bytes 3932160 | tf_op jit(solution)/shard_map/finish/pallas_call | solution.py:258
  117.8 5.6 %collective-permute-start.17 = (f32[2,16,512]{2,1,0:T(8,128)S(1)}, f32[2,16,512]{2,1,0:T(8,128)S(1)}, u32[]{:S(2)}, u32[]{:S(2)}) collective-permute-start(f32[2,16,512]{2,1,0:T(8,128)S(1)} %add_add_fusion), channel_id=1, source_target_pairs={{0,32},{8,40},{16,48},{24,56},{32,0},{40,8},{48,16},{56,24},{1,33}... | collective-permute-start | bytes 196616 | tf_op jit(solution)/shard_map/ppermute | solution.py:363
  128.9 2.6 %collective-permute-done.19 = f32[2,16,512]{2,1,0:T(8,128)S(1)} collective-permute-done((f32[2,16,512]{2,1,0:T(8,128)S(1)}, f32[2,16,512]{2,1,0:T(8,128)S(1)}, u32[]{:S(2)}, u32[]{:S(2)}) %collective-permute-start.19) | collective-permute-done | bytes 65568 | tf_op jit(solution)/shard_map/ppermute | solution.py:279
  132.3 2.1 %collective-permute-start.22 = (f32[4,2,16,512]{3,2,1,0:T(8,128)S(1)}, f32[4,2,16,512]{3,2,1,0:T(8,128)S(1)}, u32[]{:S(2)}, u32[]{:S(2)}) collective-permute-start(f32[4,2,16,512]{3,2,1,0:T(8,128)S(1)} %pad_maximum_fusion.refs_0_), channel_id=1, source_target_pairs={{0,128},{64,192},{128,0},{192,64},{1,129},{65,193},{129,1},{193,65... | collective-permute-start | bytes 786440 | tf_op jit(solution)/shard_map/ppermute | solution.py:279
  135.3 6.2 %collective-permute-start.24 = (f32[4,2,16,512]{3,2,1,0:T(8,128)S(1)}, f32[4,2,16,512]{3,2,1,0:T(8,128)S(1)}, u32[]{:S(2)}, u32[]{:S(2)}) collective-permute-start(f32[4,2,16,512]{3,2,1,0:T(8,128)S(1)} %pad_maximum_fusion.refs_0_), channel_id=1, source_target_pairs={{0,1},{1,0},{2,3},{3,2},{4,5},{5,4},{6,7},{7,6},{8,9},{9,8},{10,11... | collective-permute-start | bytes 786440 | tf_op jit(solution)/shard_map/ppermute | solution.py:308
  141.6 6.8 %collective-permute-start.25 = (f32[4,2,16,512]{3,2,1,0:T(8,128)S(1)}, f32[4,2,16,512]{3,2,1,0:T(8,128)S(1)}, u32[]{:S(2)}, u32[]{:S(2)}) collective-permute-start(f32[4,2,16,512]{3,2,1,0:T(8,128)S(1)} %collective-permute-done.21.refs_1_), channel_id=1, source_target_pairs={{0,1},{1,0},{2,3},{3,2},{4,5},{5,4},{6,7},{7,6},{8,9},{9,8},{10,11... | collective-permute-start | bytes 786440 | tf_op jit(solution)/shard_map/ppermute | solution.py:308
  (85 shorter events, 29.2 us)
Async XLA Ops:
  5.3 23.9 %collective-permute-start.5 = (bf16[768,512]{1,0:T(8,128)(2,1)}, bf16[768,512]{1,0:T(8,128)(2,1)S(1)}, u32[]{:S(2)}, u32[]{:S(2)}) collective-permute-start(bf16[768,512]{1,0:T(8,128)(2,1)} %get-tuple-element.29.x0), channel_id=1, source_target_pairs={{0,56},{8,0},{16,8},{24,16},{32,24},{40,32},{48,40},{56,48},{1,57}... | collective-permute-start | bytes 2359304 | tf_op jit(solution)/shard_map/ppermute | solution.py:279
  11.7 16.8 %collective-permute-start.1 = (s32[2,2048]{1,0:T(2,128)}, s32[2,2048]{1,0:T(2,128)S(1)}, u32[]{:S(2)}, u32[]{:S(2)}) collective-permute-start(s32[2,2048]{1,0:T(2,128)} %get-tuple-element.25), channel_id=1, source_target_pairs={{0,62},{1,63},{2,0},{3,1},{4,2},{5,3},{6,4},{7,5},{8,6},{9,7},{10,... | collective-permute-start | bytes 49160 | tf_op jit(solution)/shard_map/ppermute | solution.py:274
  14.9 13.9 %collective-permute-start.2 = (s32[2,2048]{1,0:T(2,128)}, s32[2,2048]{1,0:T(2,128)S(1)}, u32[]{:S(2)}, u32[]{:S(2)}) collective-permute-start(s32[2,2048]{1,0:T(2,128)} %get-tuple-element.26), channel_id=1, source_target_pairs={{0,58},{1,59},{2,60},{3,61},{4,62},{5,63},{6,0},{7,1},{8,2},{9,3},... | collective-permute-start | bytes 49160 | tf_op jit(solution)/shard_map/ppermute | solution.py:274
  14.9 14.3 %collective-permute-start.3 = (s32[2,2048]{1,0:T(2,128)}, s32[2,2048]{1,0:T(2,128)S(1)}, u32[]{:S(2)}, u32[]{:S(2)}) collective-permute-start(s32[2,2048]{1,0:T(2,128)} %get-tuple-element.27), channel_id=1, source_target_pairs={{0,60},{1,61},{2,62},{3,63},{4,0},{5,1},{6,2},{7,3},{8,4},{9,5},{1... | collective-permute-start | bytes 49160 | tf_op jit(solution)/shard_map/ppermute | solution.py:274
  17.0 10.0 %collective-permute-start = (s32[1,2048]{1,0:T(1,128)}, s32[1,2048]{1,0:T(1,128)S(1)}, u32[]{:S(2)}, u32[]{:S(2)}) collective-permute-start(s32[1,2048]{1,0:T(1,128)} %get-tuple-element.24), channel_id=1, source_target_pairs={{0,57},{1,0},{2,59},{3,2},{4,61},{5,4},{6,63},{7,6},{8,1},{9,8},{1... | collective-permute-start | bytes 24584 | tf_op jit(solution)/shard_map/ppermute | solution.py:274
  31.9 23.6 %collective-permute-start.6 = (bf16[768,512]{1,0:T(8,128)(2,1)}, bf16[768,512]{1,0:T(8,128)(2,1)}, u32[]{:S(2)}, u32[]{:S(2)}) collective-permute-start(bf16[768,512]{1,0:T(8,128)(2,1)} %get-tuple-element.45), channel_id=1, source_target_pairs={{0,1},{1,0},{2,3},{3,2},{4,5},{5,4},{6,7},{7,6},{8,9},{9,8},{10,11... | collective-permute-start | bytes 2359304 | tf_op jit(solution)/shard_map/ppermute | solution.py:308
  33.6 22.0 %collective-permute-start.7 = (bf16[768,512]{1,0:T(8,128)(2,1)}, bf16[768,512]{1,0:T(8,128)(2,1)}, u32[]{:S(2)}, u32[]{:S(2)}) collective-permute-start(bf16[768,512]{1,0:T(8,128)(2,1)} %get-tuple-element.44), channel_id=1, source_target_pairs={{0,6},{2,0},{4,2},{6,4},{1,7},{3,1},{5,3},{7,5},{8,14},{10,8},{12,... | collective-permute-start | bytes 2359304 | tf_op jit(solution)/shard_map/ppermute | solution.py:279
  35.3 20.4 %collective-permute-start.8 = (bf16[768,512]{1,0:T(8,128)(2,1)}, bf16[768,512]{1,0:T(8,128)(2,1)}, u32[]{:S(2)}, u32[]{:S(2)}) collective-permute-start(bf16[768,512]{1,0:T(8,128)(2,1)} %get-tuple-element.43), channel_id=1, source_target_pairs={{0,2},{2,4},{4,6},{6,0},{1,3},{3,5},{5,7},{7,1},{8,10},{10,12},{12... | collective-permute-start | bytes 2359304 | tf_op jit(solution)/shard_map/ppermute | solution.py:279
  35.4 6.9 %collective-permute-start.4 = (s32[3,2048]{1,0:T(4,128)S(1)}, s32[3,2048]{1,0:T(4,128)S(1)}, u32[]{:S(2)}, u32[]{:S(2)}) collective-permute-start(s32[3,2048]{1,0:T(4,128)S(1)} %pad_add_fusion), channel_id=1, source_target_pairs={{0,1},{1,0},{2,3},{3,2},{4,5},{5,4},{6,7},{7,6},{8,9},{9,8},{10,11... | collective-permute-start | bytes 73736 | tf_op jit(solution)/shard_map/ppermute | solution.py:308
  35.8 24.3 %all-to-all-start = ((bf16[4,256,512]{2,1,0:T(8,128)(2,1)}), bf16[4,256,512]{2,1,0:T(8,128)(2,1)S(1)}, u32[]{:S(2)}, u32[]{:S(2)}) async-start(bf16[4,256,512]{2,1,0:T(8,128)(2,1)} %get-tuple-element.34), calls=%async_computation | async-start | bytes 2097152 | tf_op jit(solution)/shard_map/all_to_all | solution.py:326
  55.7 4.4 %collective-permute-start.9 = (bf16[768,512]{1,0:T(8,128)(2,1)}, bf16[768,512]{1,0:T(8,128)(2,1)}, u32[]{:S(2)}, u32[]{:S(2)}) collective-permute-start(bf16[768,512]{1,0:T(8,128)(2,1)} %collective-permute-done.7.x2), channel_id=1, source_target_pairs={{0,1},{1,0},{2,3},{3,2},{4,5},{5,4},{6,7},{7,6},{8,9},{9,8},{10,11... | collective-permute-start | bytes 2359304 | tf_op jit(solution)/shard_map/ppermute | solution.py:308
  58.9 17.2 %collective-permute-start.11 = (bf16[768,512]{1,0:T(8,128)(2,1)}, bf16[768,512]{1,0:T(8,128)(2,1)}, u32[]{:S(2)}, u32[]{:S(2)}) collective-permute-start(bf16[768,512]{1,0:T(8,128)(2,1)} %broadcast_select_fusion), channel_id=1, source_target_pairs={{0,62},{1,3},{2,0},{3,5},{4,2},{5,7},{6,4},{7,9},{8,6},{9,11},{10,... | collective-permute-start | bytes 2359304 | tf_op jit(solution)/shard_map/ppermute | solution.py:274
  76.0 3.9 %collective-permute-start.12 = (bf16[768,512]{1,0:T(8,128)(2,1)}, bf16[768,512]{1,0:T(8,128)(2,1)S(1)}, u32[]{:S(2)}, u32[]{:S(2)}) collective-permute-start(bf16[768,512]{1,0:T(8,128)(2,1)} %collective-permute-done.11.x0), channel_id=1, source_target_pairs={{0,1},{1,0},{2,3},{3,2},{4,5},{5,4},{6,7},{7,6},{8,9},{9,8},{10,11... | collective-permute-start | bytes 2359304 | tf_op jit(solution)/shard_map/ppermute | solution.py:308
  112.2 5.6 %collective-permute-start.15 = (f32[2,16,512]{2,1,0:T(8,128)S(1)}, f32[2,16,512]{2,1,0:T(8,128)S(1)}, u32[]{:S(2)}, u32[]{:S(2)}) collective-permute-start(f32[2,16,512]{2,1,0:T(8,128)S(1)} %reduce_sum.9), channel_id=1, source_target_pairs={{0,16},{8,24},{16,0},{24,8},{32,48},{40,56},{48,32},{56,40},{1,17}... | collective-permute-start | bytes 196616 | tf_op jit(solution)/shard_map/ppermute | solution.py:363
  112.3 5.5 %collective-permute-start.16 = (f32[2,16,512]{2,1,0:T(8,128)S(1)}, f32[2,16,512]{2,1,0:T(8,128)S(1)}, u32[]{:S(2)}, u32[]{:S(2)}) collective-permute-start(f32[2,16,512]{2,1,0:T(8,128)S(1)} %reduce_sum.9), channel_id=1, source_target_pairs={{0,24},{8,16},{16,8},{24,0},{32,56},{40,48},{48,40},{56,32},{1,25}... | collective-permute-start | bytes 196616 | tf_op jit(solution)/shard_map/ppermute | solution.py:363
  112.5 5.2 %collective-permute-start.14 = (f32[2,16,512]{2,1,0:T(8,128)S(1)}, f32[2,16,512]{2,1,0:T(8,128)S(1)}, u32[]{:S(2)}, u32[]{:S(2)}) collective-permute-start(f32[2,16,512]{2,1,0:T(8,128)S(1)} %reduce_sum.9), channel_id=1, source_target_pairs={{0,8},{8,0},{16,24},{24,16},{32,40},{40,32},{48,56},{56,48},{1,9},... | collective-permute-start | bytes 196616 | tf_op jit(solution)/shard_map/ppermute | solution.py:363
  117.8 7.6 %collective-permute-start.17 = (f32[2,16,512]{2,1,0:T(8,128)S(1)}, f32[2,16,512]{2,1,0:T(8,128)S(1)}, u32[]{:S(2)}, u32[]{:S(2)}) collective-permute-start(f32[2,16,512]{2,1,0:T(8,128)S(1)} %add_add_fusion), channel_id=1, source_target_pairs={{0,32},{8,40},{16,48},{24,56},{32,0},{40,8},{48,16},{56,24},{1,33}... | collective-permute-start | bytes 196616 | tf_op jit(solution)/shard_map/ppermute | solution.py:363
  126.9 4.6 %collective-permute-start.19 = (f32[2,16,512]{2,1,0:T(8,128)S(1)}, f32[2,16,512]{2,1,0:T(8,128)S(1)}, u32[]{:S(2)}, u32[]{:S(2)}) collective-permute-start(f32[2,16,512]{2,1,0:T(8,128)S(1)} %add.19), channel_id=1, source_target_pairs={{0,4},{2,6},{4,0},{6,2},{1,5},{3,7},{5,1},{7,3},{8,12},{10,14},{12... | collective-permute-start | bytes 196616 | tf_op jit(solution)/shard_map/ppermute | solution.py:279
  127.6 4.6 %collective-permute-start.18 = (f32[2,16,512]{2,1,0:T(8,128)S(1)}, f32[2,16,512]{2,1,0:T(8,128)S(1)}, u32[]{:S(2)}, u32[]{:S(2)}) collective-permute-start(f32[2,16,512]{2,1,0:T(8,128)S(1)} %add.19), channel_id=1, source_target_pairs={{0,2},{2,4},{4,6},{6,0},{1,3},{3,5},{5,7},{7,1},{8,10},{10,12},{12... | collective-permute-start | bytes 196616 | tf_op jit(solution)/shard_map/ppermute | solution.py:279
  132.2 9.3 %collective-permute-start.21 = (f32[4,2,16,512]{3,2,1,0:T(8,128)S(1)}, f32[4,2,16,512]{3,2,1,0:T(8,128)S(1)}, u32[]{:S(2)}, u32[]{:S(2)}) collective-permute-start(f32[4,2,16,512]{3,2,1,0:T(8,128)S(1)} %pad_maximum_fusion.refs_0_), channel_id=1, source_target_pairs={{0,64},{64,128},{128,192},{192,0},{1,65},{65,129},{129,193},{193,1... | collective-permute-start | bytes 786440 | tf_op jit(solution)/shard_map/ppermute | solution.py:279
  132.3 16.0 %collective-permute-start.22 = (f32[4,2,16,512]{3,2,1,0:T(8,128)S(1)}, f32[4,2,16,512]{3,2,1,0:T(8,128)S(1)}, u32[]{:S(2)}, u32[]{:S(2)}) collective-permute-start(f32[4,2,16,512]{3,2,1,0:T(8,128)S(1)} %pad_maximum_fusion.refs_0_), channel_id=1, source_target_pairs={{0,128},{64,192},{128,0},{192,64},{1,129},{65,193},{129,1},{193,65... | collective-permute-start | bytes 786440 | tf_op jit(solution)/shard_map/ppermute | solution.py:279
  134.5 13.9 %collective-permute-start.23 = (f32[4,2,16,512]{3,2,1,0:T(8,128)S(1)}, f32[4,2,16,512]{3,2,1,0:T(8,128)S(1)}, u32[]{:S(2)}, u32[]{:S(2)}) collective-permute-start(f32[4,2,16,512]{3,2,1,0:T(8,128)S(1)} %pad_maximum_fusion.refs_0_), channel_id=1, source_target_pairs={{0,192},{64,0},{128,64},{192,128},{1,193},{65,1},{129,65},{193,129... | collective-permute-start | bytes 786440 | tf_op jit(solution)/shard_map/ppermute | solution.py:279
  135.3 13.9 %collective-permute-start.24 = (f32[4,2,16,512]{3,2,1,0:T(8,128)S(1)}, f32[4,2,16,512]{3,2,1,0:T(8,128)S(1)}, u32[]{:S(2)}, u32[]{:S(2)}) collective-permute-start(f32[4,2,16,512]{3,2,1,0:T(8,128)S(1)} %pad_maximum_fusion.refs_0_), channel_id=1, source_target_pairs={{0,1},{1,0},{2,3},{3,2},{4,5},{5,4},{6,7},{7,6},{8,9},{9,8},{10,11... | collective-permute-start | bytes 786440 | tf_op jit(solution)/shard_map/ppermute | solution.py:308
  141.6 7.9 %collective-permute-start.25 = (f32[4,2,16,512]{3,2,1,0:T(8,128)S(1)}, f32[4,2,16,512]{3,2,1,0:T(8,128)S(1)}, u32[]{:S(2)}, u32[]{:S(2)}) collective-permute-start(f32[4,2,16,512]{3,2,1,0:T(8,128)S(1)} %collective-permute-done.21.refs_1_), channel_id=1, source_target_pairs={{0,1},{1,0},{2,3},{3,2},{4,5},{5,4},{6,7},{7,6},{8,9},{9,8},{10,11... | collective-permute-start | bytes 786440 | tf_op jit(solution)/shard_map/ppermute | solution.py:308
  (20 other events, 197.7 us)

commit v5 on v4

--- a/solution.py
+++ b/solution.py
@@ -12,7 +12,7 @@
 F32 = jnp.float32
 BF16 = jnp.bfloat16
 I32 = jnp.int32
-CHUNK = 1024
+CHUNK = 512
 ALONG = (((1,), (1,)), ((), ()))
 DOWN = (((0,), (0,)), ((), ()))
 
@@ -73,25 +73,22 @@
 
 
 def build(rows, *refs):
-    lists, (tile_out, acc, edges) = refs[:-3], refs[-3:]
+    lists, (tile_out, edges) = refs[:-2], refs[-2:]
     s = pl.program_id(0)
-    nodes = acc.shape[0]
+    nodes, ept = tile_out.shape[1], edges.shape[2]
 
     @pl.when(s == 0)
     def _():
         for k, row in enumerate(rows):
             edges[k] = lists[k][row : row + 1, :]
 
-    acc[...] = jnp.zeros_like(acc)
     live = jnp.sum((edges[s] >= 0).astype(I32))
-
-    def step(i, carry):
-        packed = edges[s, :, pl.ds(pl.multiple_of(i * CHUNK, CHUNK), CHUNK)]
-        acc[...] += dot(small_hot(nodes, packed >> 10), small_hot(nodes, packed & 1023), ALONG)
-        return carry
-
-    lax.fori_loop(0, (live + CHUNK - 1) // CHUNK, step, 0)
-    tile_out[0] = acc[...].astype(BF16)
+    for low in range(0, ept, CHUNK):
+        @pl.when((live <= low + CHUNK) & ((live > low) | (low == 0)))
+        def _():
+            packed = edges[s, :, : low + CHUNK]
+            tile = dot(small_hot(nodes, packed >> 10), small_hot(nodes, packed & 1023), ALONG)
+            tile_out[0] = tile.astype(BF16)
 
 
 def most_sum(t0, t1, t2, t3, t4, t5, x0, x1, x2, x3, x4, x5, ids, rows, out):
@@ -201,7 +198,7 @@
         grid=(slots,),
         in_specs=[whole(v.shape) for v in lists],
         out_specs=pl.BlockSpec((1, nodes, nodes), lambda s: (s, 0, 0)),
-        scratch_shapes=[pltpu.VMEM((nodes, nodes), F32), pltpu.VMEM((slots, 1, ept), I32)],
+        scratch_shapes=[pltpu.VMEM((slots, 1, ept), I32)],
         out_shape=jax.ShapeDtypeStruct((slots, nodes, nodes), BF16),
         compiler_params=params(60),
         cost_estimate=estimate(nodes * ept, nodes * ept),
@@ -218,7 +215,7 @@
         + [whole(v.shape) for v in (*xs, ids, rows)],
         out_specs=row_spec(width),
         out_shape=jax.ShapeDtypeStruct((nodes, width), F32),
-        compiler_params=params(36),
+        compiler_params=params(56),
         cost_estimate=estimate(7 * nodes * nodes * width, 16 * nodes * width),
         name="most_sum",
     )(near, near, quad, quad, quad, quad, *xs, ids, rows)
@@ -362,9 +359,9 @@
     def zflip(v, k):
         return lax.ppermute(v, "z", [(i, i ^ k) for i in range(nz)])
 
+    part = part + zflip(part, 4)
+    part, total = fence((part, run_finish(summed, cotangent, w_self, w_neigh)))
     part = (part + zflip(part, 1)) + (zflip(part, 2) + zflip(part, 3))
-    part, total = fence((part, run_finish(summed, cotangent, w_self, w_neigh)))
-    part = part + zflip(part, 4)
     part = jnp.stack([part] + [turned(part, "y", t) for t in range(1, ny)])
     held = [part] + [turned(part, "group", s) for s in range(1, ngroup)]
     held = held + [swapped(v) for v in held]

time: 152 us -> 147 us (0.967)
  starting transfers between devices: 53.3 us -> 49.7 us
  waiting for transfers between devices: 27.9 us -> 30.1 us
  blocking collectives: 23.5 us -> 21.3 us
    ppermute x4, waiting for transfers between devices: 2.04 us -> 4.56 us  [zflip(): return lax.ppermute(v, 'z', [(i, i ^ k) for i in range(nz)])]
    pallas_call x1, Pallas kernels: 7.24 us -> 9.61 us  [run_most(): pl.pallas_call(most_sum, grid=(nodes // BLOCK,), in_specs=[tile_spec(s, n...]
    all_to_all x1, blocking collectives: 23.5 us -> 21.3 us  [on_device(): lax.all_to_all(part, ('group', 'y'), split_axis=0, concat_axis=0, tiled=T...]
    ppermute x5, waiting for transfers between devices: 15.6 us -> 13.6 us  [moved(): return lax.ppermute(value, BLK, perm)]
    ppermute x4, starting transfers between devices: 8.34 us -> 6.66 us  [zflip(): return lax.ppermute(v, 'z', [(i, i ^ k) for i in range(nz)])]
    pallas_call x3, Pallas kernels: 15.1 us -> 13.5 us  [run_build(): pl.pallas_call(functools.partial(build, rows), grid=(slots,), in_specs=[w...]
    unnamed x31 -> x29, local copies, waits for them, and re-layouts: 4.13 us -> 2.95 us
  transfers between devices with their start and end apart: 29 -> 29, of which waited for: 17 -> 19; matrix products, arithmetic and copies ran while one was open for 1% -> 2% of each run, Pallas kernels for 17% -> 18%
where the time goes in v5:
time: 147 us; the launch traced here: 146 us
  starting transfers between devices  49.7 us (34%)
  Pallas kernels  35.3 us (24%)
  waiting for transfers between devices  30.1 us (20%)
  blocking collectives  21.3 us (14%)
  other arithmetic  5.87 us (4%)
  local copies, waits for them, and re-layouts  2.99 us (2%)
    all_to_all x1, blocking collectives, on_device(): lax.all_to_all(part, ('group', 'y'), split_axis=0, concat_axis=0, tiled=T...  21.3 us
    ppermute x10, starting transfers between devices, swapped(): return lax.ppermute(v, 'core', swap)  18.5 us
    ppermute x5, waiting for transfers between devices, moved(): return lax.ppermute(value, BLK, perm)  13.6 us
    ppermute x9, starting transfers between devices, turned(): lax.ppermute(value, axis, [(i, (i + by) % length) for i in range(length)])  13.5 us
    pallas_call x3, Pallas kernels, run_build(): pl.pallas_call(functools.partial(build, rows), grid=(slots,), in_specs=[w...  13.5 us
    pallas_call x1, Pallas kernels, run_most(): pl.pallas_call(most_sum, grid=(nodes // BLOCK,), in_specs=[tile_spec(s, n...  9.61 us
    ppermute x5, starting transfers between devices, moved(): return lax.ppermute(value, BLK, perm)  7.06 us
    ppermute x4, starting transfers between devices, zflip(): return lax.ppermute(v, 'z', [(i, i ^ k) for i in range(nz)])  6.66 us
  transfers between devices with their start and end apart: 29, of which 19 were waited for; matrix products, arithmetic and copies ran while one was open for 2% of the time, Pallas kernels for 18%

profile of v5, /device:TPU:1, one launch (start us, length us, event | category | flops | bytes accessed | tf_op | source)
XLA Modules:
  0.0 146.0 jit_solution(6828805026263004997)
XLA Ops:
  0.6 4.7 %prepare.1 = (bf16[768,512]{1,0:T(8,128)(2,1)}, bf16[4,256,512]{2,1,0:T(8,128)(2,1)}, s32[1,2048]{1,0:T(1,128)}, s32[1,2048]{1,0:T(1,128)}, s32[2,2048]{1,0:T(2,...) custom-call(s32[1,8]{1,0:T(1,128)} %tcount.1, s32[1,4]{1,0:T(1,128)} %rcount.1, s32[1,8,2048]{2,1,0:T(8,128)} %tsrc.1, ...), custom_call_target="tpu_custom_call" | custom-call | flops 805306368 | bytes 854040 | tf_op jit(solution)/shard_map/prepare/pallas_call | solution.py:180
  5.3 6.4 %collective-permute-start.5 = (bf16[768,512]{1,0:T(8,128)(2,1)}, bf16[768,512]{1,0:T(8,128)(2,1)S(1)}, u32[]{:S(2)}, u32[]{:S(2)}) collective-permute-start(bf16[768,512]{1,0:T(8,128)(2,1)} %get-tuple-element.29.x0), channel_id=1, source_target_pairs={{0,56},{8,0},{16,8},{24,16},{32,24},{40,32},{48,40},{56,48},{1,57}... | collective-permute-start | bytes 2359304 | tf_op jit(solution)/shard_map/ppermute | solution.py:276
  11.7 3.2 %collective-permute-start.1 = (s32[2,2048]{1,0:T(2,128)}, s32[2,2048]{1,0:T(2,128)S(1)}, u32[]{:S(2)}, u32[]{:S(2)}) collective-permute-start(s32[2,2048]{1,0:T(2,128)} %get-tuple-element.25), channel_id=1, source_target_pairs={{0,62},{1,63},{2,0},{3,1},{4,2},{5,3},{6,4},{7,5},{8,6},{9,7},{10,... | collective-permute-start | bytes 49160 | tf_op jit(solution)/shard_map/ppermute | solution.py:271
  14.9 2.1 %collective-permute-start.3 = (s32[2,2048]{1,0:T(2,128)}, s32[2,2048]{1,0:T(2,128)S(1)}, u32[]{:S(2)}, u32[]{:S(2)}) collective-permute-start(s32[2,2048]{1,0:T(2,128)} %get-tuple-element.27), channel_id=1, source_target_pairs={{0,60},{1,61},{2,62},{3,63},{4,0},{5,1},{6,2},{7,3},{8,4},{9,5},{1... | collective-permute-start | bytes 49160 | tf_op jit(solution)/shard_map/ppermute | solution.py:271
  18.8 8.2 %collective-permute-done.refs_1_ = s32[1,2048]{1,0:T(1,128)S(1)} collective-permute-done((s32[1,2048]{1,0:T(1,128)}, s32[1,2048]{1,0:T(1,128)S(1)}, u32[]{:S(2)}, u32[]{:S(2)}) %collective-permute-start) | collective-permute-done | bytes 8224 | tf_op jit(solution)/shard_map/ppermute | solution.py:271
  29.2 2.2 %broadcast_select_fusion.1 = (bf16[768,512]{1,0:T(8,128)(2,1)S(1)}, bf16[768,512]{1,0:T(8,128)(2,1)S(1)}, bf16[768,512]{1,0:T(8,128)(2,1)}) fusion(bf16[768,512]{1,0:T(8,128)(2,1)} %get-tuple-element.29.x0, bf16[768,512]{1,0:T(8,128)(2,1)S(1)} %collective-permute-done.5, pred[]{:T(512)S(6)} %eq.14, pred[]{:T(512)S(6)} %eq.13, pred[]{:T(512)S(6)} %eq.12), kind=kLoop, calls=%fused_computation.1 | loop fusion | flops 1179648 | bytes 3932163 | tf_op jit(solution)/shard_map/jit(_where)/select_n | solution.py:327
  35.2 4.0 %all-to-all-start = ((bf16[4,256,512]{2,1,0:T(8,128)(2,1)}), bf16[4,256,512]{2,1,0:T(8,128)(2,1)S(1)}, u32[]{:S(2)}, u32[]{:S(2)}) async-start(bf16[4,256,512]{2,1,0:T(8,128)(2,1)} %get-tuple-element.34), calls=%async_computation | async-start | bytes 2097152 | tf_op jit(solution)/shard_map/all_to_all | solution.py:323
  39.3 3.6 %build.3.t0.t1 = bf16[2,768,768]{2,1,0:T(8,128)(2,1)} custom-call(s32[1,2048]{1,0:T(1,128)} %get-tuple-element.23.refs_0_, s32[1,2048]{1,0:T(1,128)} %copy-done.12), custom_call_target="tpu_custom_call" | custom-call | flops 3145728 | bytes 1572864 | tf_op jit(solution)/shard_map/build/pallas_call | solution.py:196
  43.4 6.5 %build.4.t2.t3.t4.t5 = bf16[4,768,768]{2,1,0:T(8,128)(2,1)} custom-call(s32[2,2048]{1,0:T(2,128)} %copy-done.9, s32[2,2048]{1,0:T(2,128)} %copy-done.10, s32[3,2048]{1,0:T(4,128)} %copy-done.8, s32[3,2048]{1,0:T(4,128)} %copy-done.8), custom_call_target="tpu_custom_call" | custom-call | flops 3145728 | bytes 1572864 | tf_op jit(solution)/shard_map/build/pallas_call | solution.py:196
  50.0 3.4 %build.5.tiles = bf16[2,768,768]{2,1,0:T(8,128)(2,1)} custom-call(s32[2,2048]{1,0:T(2,128)} %copy-done.11, s32[3,2048]{1,0:T(4,128)} %copy-done.8), custom_call_target="tpu_custom_call" | custom-call | flops 3145728 | bytes 1572864 | tf_op jit(solution)/shard_map/build/pallas_call | solution.py:196
  56.0 2.1 %broadcast_select_fusion = bf16[768,512]{1,0:T(8,128)(2,1)} fusion(bf16[768,512]{1,0:T(8,128)(2,1)S(1)} %collective-permute-done.7.x2, bf16[768,512]{1,0:T(8,128)(2,1)} %collective-permute-done.8.x3, pred[]{:T(512)S(6)} %eq.15), kind=kLoop, calls=%fused_computation | loop fusion | flops 393216 | bytes 2359297 | tf_op jit(solution)/shard_map/jit(_where)/select_n | solution.py:334
  59.7 9.6 %most_sum.1.before = f32[768,512]{1,0:T(8,128)} custom-call(bf16[2,768,768]{2,1,0:T(8,128)(2,1)} %build.3.t0.t1, bf16[2,768,768]{2,1,0:T(8,128)(2,1)} %build.3.t0.t1, bf16[4,768,768]{2,1,0:T(8,128)(2,1)} %build.4.t2.t3.t4.t5, bf16[4,768,768]{2,1,0:T(8,128)(2,1)} %build.4.t2.t3.t4.t5, bf16[4,768,768]{2,1,0:T(8,128)(2,1)} %build.4.t2.t3.t4.t5, ...), custom_call_target="tpu_custom_call" | custom-call | flops 4227858432 | bytes 6291456 | tf_op jit(solution)/shard_map/most_sum/pallas_call | solution.py:211
  69.3 3.2 %collective-permute-done.11.x0 = bf16[768,512]{1,0:T(8,128)(2,1)S(1)} collective-permute-done((bf16[768,512]{1,0:T(8,128)(2,1)}, bf16[768,512]{1,0:T(8,128)(2,1)S(1)}, u32[]{:S(2)}, u32[]{:S(2)}) %collective-permute-start.11) | collective-permute-done | bytes 786464 | tf_op jit(solution)/shard_map/ppermute | solution.py:271
  77.1 3.2 %last_sum.1 = (f32[768,512]{1,0:T(8,128)S(1)}, f32[16,2,16,512]{3,2,1,0:T(8,128)S(1)}, f32[16,2,16,512]{3,2,1,0:T(8,128)S(1)}) custom-call(f32[768,512]{1,0:T(8,128)S(1)} %copy-done.1, bf16[2,768,768]{2,1,0:T(8,128)(2,1)S(1)} %copy-done, bf16[768,512]{1,0:T(8,128)(2,1)S(1)} %collective-permute-done.11.x0, bf16[768,512]{1,0:T(8,128)(2,1)S(1)} %collective-permute-done.12.x1, ...), custom_call_target="tpu_custom_call" | custom-call | flops 1811939328 | bytes 6291456 | tf_op jit(solution)/shard_map/last_sum/pallas_call | solution.py:228
  80.8 2.3 %collective-permute-done.13 = f32[16,2,16,512]{3,2,1,0:T(8,128)S(1)} collective-permute-done((f32[16,2,16,512]{3,2,1,0:T(8,128)S(1)}, f32[16,2,16,512]{3,2,1,0:T(8,128)S(1)}, u32[]{:S(2)}, u32[]{:S(2)}) %collective-permute-start.13) | collective-permute-done | bytes 1048608 | tf_op jit(solution)/shard_map/ppermute | solution.py:305
  83.3 21.3 %all_to_all.10 = f32[16,2,16,512]{3,2,1,0:T(8,128)} all-to-all(f32[16,2,16,512]{3,2,1,0:T(8,128)S(1)} %add.15), channel_id=1, replica_groups=mesh['group'=4,'z'=8,'y'=4,'core'=2] {'group','y'}, dimensions={0} | all-to-all | bytes 2097152 | tf_op jit(solution)/shard_map/all_to_all | solution.py:357
  105.8 3.6 %collective-permute-start.14 = (f32[2,16,512]{2,1,0:T(8,128)S(1)}, f32[2,16,512]{2,1,0:T(8,128)S(1)}, u32[]{:S(2)}, u32[]{:S(2)}) collective-permute-start(f32[2,16,512]{2,1,0:T(8,128)S(1)} %reduce_sum.9), channel_id=1, source_target_pairs={{0,32},{8,40},{16,48},{24,56},{32,0},{40,8},{48,16},{56,24},{1,33}... | collective-permute-start | bytes 196616 | tf_op jit(solution)/shard_map/ppermute | solution.py:360
  109.4 2.8 %finish.1 = f32[768,512]{1,0:T(8,128)} custom-call(f32[768,512]{1,0:T(8,128)S(1)} %get-tuple-element.38.summed, bf16[768,512]{1,0:T(8,128)(2,1)S(1)} %copy-done.2, bf16[512,512]{1,0:T(8,128)(2,1)S(1)} %copy-done.4, bf16[512,512]{1,0:T(8,128)(2,1)S(1)} %copy-done.5), custom_call_target="tpu_custom_call" | custom-call | flops 1207959552 | bytes 3932160 | tf_op jit(solution)/shard_map/finish/pallas_call | solution.py:255
  113.8 2.1 %collective-permute-start.17 = (f32[2,16,512]{2,1,0:T(8,128)S(1)}, f32[2,16,512]{2,1,0:T(8,128)S(1)}, u32[]{:S(2)}, u32[]{:S(2)}) collective-permute-start(f32[2,16,512]{2,1,0:T(8,128)S(1)} %add.16), channel_id=1, source_target_pairs={{0,24},{8,16},{16,8},{24,0},{32,56},{40,48},{48,40},{56,32},{1,25}... | collective-permute-start | bytes 196616 | tf_op jit(solution)/shard_map/ppermute | solution.py:360
  116.0 3.2 %collective-permute-done.16 = f32[2,16,512]{2,1,0:T(8,128)S(1)} collective-permute-done((f32[2,16,512]{2,1,0:T(8,128)S(1)}, f32[2,16,512]{2,1,0:T(8,128)S(1)}, u32[]{:S(2)}, u32[]{:S(2)}) %collective-permute-start.16) | collective-permute-done | bytes 65568 | tf_op jit(solution)/shard_map/ppermute | solution.py:360
  123.2 2.5 %collective-permute-done.19 = f32[2,16,512]{2,1,0:T(8,128)S(1)} collective-permute-done((f32[2,16,512]{2,1,0:T(8,128)S(1)}, f32[2,16,512]{2,1,0:T(8,128)S(1)}, u32[]{:S(2)}, u32[]{:S(2)}) %collective-permute-start.19) | collective-permute-done | bytes 65568 | tf_op jit(solution)/shard_map/ppermute | solution.py:276
  126.5 2.4 %collective-permute-start.22 = (f32[4,2,16,512]{3,2,1,0:T(8,128)S(1)}, f32[4,2,16,512]{3,2,1,0:T(8,128)S(1)}, u32[]{:S(2)}, u32[]{:S(2)}) collective-permute-start(f32[4,2,16,512]{3,2,1,0:T(8,128)S(1)} %pad_maximum_fusion.refs_0_), channel_id=1, source_target_pairs={{0,128},{64,192},{128,0},{192,64},{1,129},{65,193},{129,1},{193,65... | collective-permute-start | bytes 786440 | tf_op jit(solution)/shard_map/ppermute | solution.py:276
  129.6 6.1 %collective-permute-start.24 = (f32[4,2,16,512]{3,2,1,0:T(8,128)S(1)}, f32[4,2,16,512]{3,2,1,0:T(8,128)S(1)}, u32[]{:S(2)}, u32[]{:S(2)}) collective-permute-start(f32[4,2,16,512]{3,2,1,0:T(8,128)S(1)} %pad_maximum_fusion.refs_0_), channel_id=1, source_target_pairs={{0,1},{1,0},{2,3},{3,2},{4,5},{5,4},{6,7},{7,6},{8,9},{9,8},{10,11... | collective-permute-start | bytes 786440 | tf_op jit(solution)/shard_map/ppermute | solution.py:305
  135.7 6.7 %collective-permute-start.25 = (f32[4,2,16,512]{3,2,1,0:T(8,128)S(1)}, f32[4,2,16,512]{3,2,1,0:T(8,128)S(1)}, u32[]{:S(2)}, u32[]{:S(2)}) collective-permute-start(f32[4,2,16,512]{3,2,1,0:T(8,128)S(1)} %collective-permute-done.21.refs_1_), channel_id=1, source_target_pairs={{0,1},{1,0},{2,3},{3,2},{4,5},{5,4},{6,7},{7,6},{8,9},{9,8},{10,11... | collective-permute-start | bytes 786440 | tf_op jit(solution)/shard_map/ppermute | solution.py:305
  (83 shorter events, 30.2 us)
Async XLA Ops:
  5.3 23.9 %collective-permute-start.5 = (bf16[768,512]{1,0:T(8,128)(2,1)}, bf16[768,512]{1,0:T(8,128)(2,1)S(1)}, u32[]{:S(2)}, u32[]{:S(2)}) collective-permute-start(bf16[768,512]{1,0:T(8,128)(2,1)} %get-tuple-element.29.x0), channel_id=1, source_target_pairs={{0,56},{8,0},{16,8},{24,16},{32,24},{40,32},{48,40},{56,48},{1,57}... | collective-permute-start | bytes 2359304 | tf_op jit(solution)/shard_map/ppermute | solution.py:276
  11.7 16.8 %collective-permute-start.1 = (s32[2,2048]{1,0:T(2,128)}, s32[2,2048]{1,0:T(2,128)S(1)}, u32[]{:S(2)}, u32[]{:S(2)}) collective-permute-start(s32[2,2048]{1,0:T(2,128)} %get-tuple-element.25), channel_id=1, source_target_pairs={{0,62},{1,63},{2,0},{3,1},{4,2},{5,3},{6,4},{7,5},{8,6},{9,7},{10,... | collective-permute-start | bytes 49160 | tf_op jit(solution)/shard_map/ppermute | solution.py:271
  14.9 13.9 %collective-permute-start.2 = (s32[2,2048]{1,0:T(2,128)}, s32[2,2048]{1,0:T(2,128)S(1)}, u32[]{:S(2)}, u32[]{:S(2)}) collective-permute-start(s32[2,2048]{1,0:T(2,128)} %get-tuple-element.26), channel_id=1, source_target_pairs={{0,58},{1,59},{2,60},{3,61},{4,62},{5,63},{6,0},{7,1},{8,2},{9,3},... | collective-permute-start | bytes 49160 | tf_op jit(solution)/shard_map/ppermute | solution.py:271
  14.9 14.3 %collective-permute-start.3 = (s32[2,2048]{1,0:T(2,128)}, s32[2,2048]{1,0:T(2,128)S(1)}, u32[]{:S(2)}, u32[]{:S(2)}) collective-permute-start(s32[2,2048]{1,0:T(2,128)} %get-tuple-element.27), channel_id=1, source_target_pairs={{0,60},{1,61},{2,62},{3,63},{4,0},{5,1},{6,2},{7,3},{8,4},{9,5},{1... | collective-permute-start | bytes 49160 | tf_op jit(solution)/shard_map/ppermute | solution.py:271
  17.0 10.0 %collective-permute-start = (s32[1,2048]{1,0:T(1,128)}, s32[1,2048]{1,0:T(1,128)S(1)}, u32[]{:S(2)}, u32[]{:S(2)}) collective-permute-start(s32[1,2048]{1,0:T(1,128)} %get-tuple-element.24), channel_id=1, source_target_pairs={{0,57},{1,0},{2,59},{3,2},{4,61},{5,4},{6,63},{7,6},{8,1},{9,8},{1... | collective-permute-start | bytes 24584 | tf_op jit(solution)/shard_map/ppermute | solution.py:271
  31.3 22.0 %collective-permute-start.6 = (bf16[768,512]{1,0:T(8,128)(2,1)}, bf16[768,512]{1,0:T(8,128)(2,1)}, u32[]{:S(2)}, u32[]{:S(2)}) collective-permute-start(bf16[768,512]{1,0:T(8,128)(2,1)} %get-tuple-element.45), channel_id=1, source_target_pairs={{0,1},{1,0},{2,3},{3,2},{4,5},{5,4},{6,7},{7,6},{8,9},{9,8},{10,11... | collective-permute-start | bytes 2359304 | tf_op jit(solution)/shard_map/ppermute | solution.py:305
  33.0 20.3 %collective-permute-start.7 = (bf16[768,512]{1,0:T(8,128)(2,1)S(1)}, bf16[768,512]{1,0:T(8,128)(2,1)S(1)}, u32[]{:S(2)}, u32[]{:S(2)}) collective-permute-start(bf16[768,512]{1,0:T(8,128)(2,1)S(1)} %get-tuple-element.44), channel_id=1, source_target_pairs={{0,6},{2,0},{4,2},{6,4},{1,7},{3,1},{5,3},{7,5},{8,14},{10,8},{12,... | collective-permute-start | bytes 2359304 | tf_op jit(solution)/shard_map/ppermute | solution.py:276
  34.7 20.2 %collective-permute-start.8 = (bf16[768,512]{1,0:T(8,128)(2,1)S(1)}, bf16[768,512]{1,0:T(8,128)(2,1)}, u32[]{:S(2)}, u32[]{:S(2)}) collective-permute-start(bf16[768,512]{1,0:T(8,128)(2,1)S(1)} %get-tuple-element.43), channel_id=1, source_target_pairs={{0,2},{2,4},{4,6},{6,0},{1,3},{3,5},{5,7},{7,1},{8,10},{10,12},{12... | collective-permute-start | bytes 2359304 | tf_op jit(solution)/shard_map/ppermute | solution.py:276
  34.8 8.0 %collective-permute-start.4 = (s32[3,2048]{1,0:T(4,128)S(1)}, s32[3,2048]{1,0:T(4,128)S(1)}, u32[]{:S(2)}, u32[]{:S(2)}) collective-permute-start(s32[3,2048]{1,0:T(4,128)S(1)} %pad_add_fusion), channel_id=1, source_target_pairs={{0,1},{1,0},{2,3},{3,2},{4,5},{5,4},{6,7},{7,6},{8,9},{9,8},{10,11... | collective-permute-start | bytes 73736 | tf_op jit(solution)/shard_map/ppermute | solution.py:305
  35.2 23.5 %all-to-all-start = ((bf16[4,256,512]{2,1,0:T(8,128)(2,1)}), bf16[4,256,512]{2,1,0:T(8,128)(2,1)S(1)}, u32[]{:S(2)}, u32[]{:S(2)}) async-start(bf16[4,256,512]{2,1,0:T(8,128)(2,1)} %get-tuple-element.34), calls=%async_computation | async-start | bytes 2097152 | tf_op jit(solution)/shard_map/all_to_all | solution.py:323
  54.9 4.2 %collective-permute-start.9 = (bf16[768,512]{1,0:T(8,128)(2,1)S(1)}, bf16[768,512]{1,0:T(8,128)(2,1)}, u32[]{:S(2)}, u32[]{:S(2)}) collective-permute-start(bf16[768,512]{1,0:T(8,128)(2,1)S(1)} %collective-permute-done.7.x2), channel_id=1, source_target_pairs={{0,1},{1,0},{2,3},{3,2},{4,5},{5,4},{6,7},{7,6},{8,9},{9,8},{10,11... | collective-permute-start | bytes 2359304 | tf_op jit(solution)/shard_map/ppermute | solution.py:305
  56.0 3.4 %collective-permute-start.10 = (bf16[768,512]{1,0:T(8,128)(2,1)}, bf16[768,512]{1,0:T(8,128)(2,1)}, u32[]{:S(2)}, u32[]{:S(2)}) collective-permute-start(bf16[768,512]{1,0:T(8,128)(2,1)} %collective-permute-done.8.x3), channel_id=1, source_target_pairs={{0,1},{1,0},{2,3},{3,2},{4,5},{5,4},{6,7},{7,6},{8,9},{9,8},{10,11... | collective-permute-start | bytes 2359304 | tf_op jit(solution)/shard_map/ppermute | solution.py:305
  58.1 14.4 %collective-permute-start.11 = (bf16[768,512]{1,0:T(8,128)(2,1)}, bf16[768,512]{1,0:T(8,128)(2,1)S(1)}, u32[]{:S(2)}, u32[]{:S(2)}) collective-permute-start(bf16[768,512]{1,0:T(8,128)(2,1)} %broadcast_select_fusion), channel_id=1, source_target_pairs={{0,62},{1,3},{2,0},{3,5},{4,2},{5,7},{6,4},{7,9},{8,6},{9,11},{10,... | collective-permute-start | bytes 2359304 | tf_op jit(solution)/shard_map/ppermute | solution.py:271
  105.8 7.1 %collective-permute-start.14 = (f32[2,16,512]{2,1,0:T(8,128)S(1)}, f32[2,16,512]{2,1,0:T(8,128)S(1)}, u32[]{:S(2)}, u32[]{:S(2)}) collective-permute-start(f32[2,16,512]{2,1,0:T(8,128)S(1)} %reduce_sum.9), channel_id=1, source_target_pairs={{0,32},{8,40},{16,48},{24,56},{32,0},{40,8},{48,16},{56,24},{1,33}... | collective-permute-start | bytes 196616 | tf_op jit(solution)/shard_map/ppermute | solution.py:360
  113.0 6.3 %collective-permute-start.16 = (f32[2,16,512]{2,1,0:T(8,128)S(1)}, f32[2,16,512]{2,1,0:T(8,128)S(1)}, u32[]{:S(2)}, u32[]{:S(2)}) collective-permute-start(f32[2,16,512]{2,1,0:T(8,128)S(1)} %add.16), channel_id=1, source_target_pairs={{0,16},{8,24},{16,0},{24,8},{32,48},{40,56},{48,32},{56,40},{1,17}... | collective-permute-start | bytes 196616 | tf_op jit(solution)/shard_map/ppermute | solution.py:360
  113.8 5.5 %collective-permute-start.17 = (f32[2,16,512]{2,1,0:T(8,128)S(1)}, f32[2,16,512]{2,1,0:T(8,128)S(1)}, u32[]{:S(2)}, u32[]{:S(2)}) collective-permute-start(f32[2,16,512]{2,1,0:T(8,128)S(1)} %add.16), channel_id=1, source_target_pairs={{0,24},{8,16},{16,8},{24,0},{32,56},{40,48},{48,40},{56,32},{1,25}... | collective-permute-start | bytes 196616 | tf_op jit(solution)/shard_map/ppermute | solution.py:360
  115.9 4.0 %collective-permute-start.15 = (f32[2,16,512]{2,1,0:T(8,128)S(1)}, f32[2,16,512]{2,1,0:T(8,128)S(1)}, u32[]{:S(2)}, u32[]{:S(2)}) collective-permute-start(f32[2,16,512]{2,1,0:T(8,128)S(1)} %add.16), channel_id=1, source_target_pairs={{0,8},{8,0},{16,24},{24,16},{32,40},{40,32},{48,56},{56,48},{1,9},... | collective-permute-start | bytes 196616 | tf_op jit(solution)/shard_map/ppermute | solution.py:360
  121.0 4.6 %collective-permute-start.19 = (f32[2,16,512]{2,1,0:T(8,128)S(1)}, f32[2,16,512]{2,1,0:T(8,128)S(1)}, u32[]{:S(2)}, u32[]{:S(2)}) collective-permute-start(f32[2,16,512]{2,1,0:T(8,128)S(1)} %add_add_fusion), channel_id=1, source_target_pairs={{0,4},{2,6},{4,0},{6,2},{1,5},{3,7},{5,1},{7,3},{8,12},{10,14},{12... | collective-permute-start | bytes 196616 | tf_op jit(solution)/shard_map/ppermute | solution.py:276
  122.0 4.3 %collective-permute-start.18 = (f32[2,16,512]{2,1,0:T(8,128)S(1)}, f32[2,16,512]{2,1,0:T(8,128)S(1)}, u32[]{:S(2)}, u32[]{:S(2)}) collective-permute-start(f32[2,16,512]{2,1,0:T(8,128)S(1)} %add_add_fusion), channel_id=1, source_target_pairs={{0,2},{2,4},{4,6},{6,0},{1,3},{3,5},{5,7},{7,1},{8,10},{10,12},{12... | collective-permute-start | bytes 196616 | tf_op jit(solution)/shard_map/ppermute | solution.py:276
  126.4 9.3 %collective-permute-start.21 = (f32[4,2,16,512]{3,2,1,0:T(8,128)S(1)}, f32[4,2,16,512]{3,2,1,0:T(8,128)S(1)}, u32[]{:S(2)}, u32[]{:S(2)}) collective-permute-start(f32[4,2,16,512]{3,2,1,0:T(8,128)S(1)} %pad_maximum_fusion.refs_0_), channel_id=1, source_target_pairs={{0,64},{64,128},{128,192},{192,0},{1,65},{65,129},{129,193},{193,1... | collective-permute-start | bytes 786440 | tf_op jit(solution)/shard_map/ppermute | solution.py:276
  126.5 15.9 %collective-permute-start.22 = (f32[4,2,16,512]{3,2,1,0:T(8,128)S(1)}, f32[4,2,16,512]{3,2,1,0:T(8,128)S(1)}, u32[]{:S(2)}, u32[]{:S(2)}) collective-permute-start(f32[4,2,16,512]{3,2,1,0:T(8,128)S(1)} %pad_maximum_fusion.refs_0_), channel_id=1, source_target_pairs={{0,128},{64,192},{128,0},{192,64},{1,129},{65,193},{129,1},{193,65... | collective-permute-start | bytes 786440 | tf_op jit(solution)/shard_map/ppermute | solution.py:276
  128.9 13.5 %collective-permute-start.23 = (f32[4,2,16,512]{3,2,1,0:T(8,128)S(1)}, f32[4,2,16,512]{3,2,1,0:T(8,128)S(1)}, u32[]{:S(2)}, u32[]{:S(2)}) collective-permute-start(f32[4,2,16,512]{3,2,1,0:T(8,128)S(1)} %pad_maximum_fusion.refs_0_), channel_id=1, source_target_pairs={{0,192},{64,0},{128,64},{192,128},{1,193},{65,1},{129,65},{193,129... | collective-permute-start | bytes 786440 | tf_op jit(solution)/shard_map/ppermute | solution.py:276
  129.6 13.6 %collective-permute-start.24 = (f32[4,2,16,512]{3,2,1,0:T(8,128)S(1)}, f32[4,2,16,512]{3,2,1,0:T(8,128)S(1)}, u32[]{:S(2)}, u32[]{:S(2)}) collective-permute-start(f32[4,2,16,512]{3,2,1,0:T(8,128)S(1)} %pad_maximum_fusion.refs_0_), channel_id=1, source_target_pairs={{0,1},{1,0},{2,3},{3,2},{4,5},{5,4},{6,7},{7,6},{8,9},{9,8},{10,11... | collective-permute-start | bytes 786440 | tf_op jit(solution)/shard_map/ppermute | solution.py:305
  135.7 7.8 %collective-permute-start.25 = (f32[4,2,16,512]{3,2,1,0:T(8,128)S(1)}, f32[4,2,16,512]{3,2,1,0:T(8,128)S(1)}, u32[]{:S(2)}, u32[]{:S(2)}) collective-permute-start(f32[4,2,16,512]{3,2,1,0:T(8,128)S(1)} %collective-permute-done.21.refs_1_), channel_id=1, source_target_pairs={{0,1},{1,0},{2,3},{3,2},{4,5},{5,4},{6,7},{7,6},{8,9},{9,8},{10,11... | collective-permute-start | bytes 786440 | tf_op jit(solution)/shard_map/ppermute | solution.py:305
  (19 other events, 157.8 us)

commit v6 on v5

--- a/solution.py
+++ b/solution.py
@@ -33,7 +33,7 @@
 
 
 def prepare(
-    tcount, rcount, tsrc, tdst, rdst, cot, x_out, rows_out, own, first, pair1, pair2, pair3
+    tcount, rcount, tsrc, tdst, rdst, cot, x_out, rows_out, own, beside, deep, pair1, pair2, pair3
 ):
     nodes = cot.shape[0]
     odd = lax.axis_index("core") == 1
@@ -48,7 +48,8 @@
         counts = counts + dot(hot(32, ids >> 5), hot(32, ids & 31), ALONG)
         lists.append(jnp.where(live, tsrc[0, s : s + 1, :] * 1024 + ids, -1))
     own[...] = lists[0]
-    first[...] = jnp.where(odd, lists[1], lists[7])
+    beside[...] = lists[1]
+    deep[0:1, :] = lists[7]
     for j, pair in ((1, pair1), (2, pair2), (3, pair3)):
         pair[0:1, :] = lists[2 * j]
         pair[1:2, :] = jnp.where(odd, lists[2 * j + 1], lists[2 * j - 1])
@@ -66,6 +67,9 @@
     spread = dot(pick, upper.astype(BF16)) * 128.0 + dot(pick, lower.astype(BF16))
     degree = jnp.sum(jnp.where((node & 31) == lane, spread, 0.0), axis=1, keepdims=True)
     inverse = 1.0 / jnp.maximum(degree, 1.0)
+    along = jnp.transpose(jnp.broadcast_to(degree, (nodes, 128)))[0:1, :]
+    deep[1:2, :] = jnp.zeros((1, ept), I32)
+    deep[1:2, :nodes] = along.astype(I32)
     x = (inverse * cot[...].astype(F32)).astype(BF16)
     x_out[...] = x
     for g in range(ngroup):
@@ -126,19 +130,14 @@
             send[n, m] = grad[there, :]
 
 
-def place(factor, *refs):
-    out_self, out_neigh = refs[-2], refs[-1]
-    ngroup = (len(refs) - 2) // 2
-    ny, _, size, _ = refs[0].shape
-    group, core, ypos = (lax.axis_index(a) for a in ("group", "core", "y"))
-    for n in range(2 * ngroup):
-        k = core if n < ngroup else 1 - core
-        g = lax.rem(group - n % ngroup + ngroup, ngroup)
-        for t in range(ny):
-            y = lax.rem(ypos - t + ny, ny)
-            at = pl.multiple_of(((k * ngroup + g) * ny + y) * size, size)
-            out_self[pl.ds(at, size), :] = refs[n][t, 0] * factor
-            out_neigh[pl.ds(at, size), :] = refs[n][t, 1] * factor
+def place(factor, mine, theirs, out_self, out_neigh):
+    pieces, _, size, _ = mine.shape
+    core = lax.axis_index("core")
+    for k, half in ((core, mine), (1 - core, theirs)):
+        for n in range(pieces):
+            at = pl.ds(pl.multiple_of((k * pieces + n) * size, size), size)
+            out_self[at, :] = half[n, 0] * factor
+            out_neigh[at, :] = half[n, 1] * factor
 
 
 def finish(summed, cot, w_self, w_neigh, out):
@@ -239,7 +238,7 @@
 
 def run_place(pieces, factor, width):
     return pl.pallas_call(
-        lambda *refs: place(factor, *refs),
+        functools.partial(place, factor),
         grid=(1,),
         in_specs=[whole(v.shape) for v in pieces],
         out_specs=[whole((width, width))] * 2,
@@ -304,30 +303,33 @@
     def swapped(v):
         return lax.ppermute(v, "core", swap)
 
-    x, rows, own, first, pair1, pair2, pair3 = run_whole(
+    far = turned(cotangent, "z", -1)
+    x, rows, own, beside, deep, pair1, pair2, pair3 = run_whole(
         prepare,
         (tile_count, recv_count, tile_src, tile_dst, recv_dst, cotangent),
         [((nodes, width), BF16), ((ngroup, cap, width), BF16)]
         + [((1, ept), I32)] * 2
-        + [((2, ept), I32)] * 3,
+        + [((2, ept), I32)] * 4,
         ngroup * cap * nodes * width,
         "prepare",
     )
-    far = turned(x, "z", -1)
-    first = moved(first, [(i, (i - 1 if i % 2 else i - 7) % nblk) for i in ring])
+    deep = turned(deep, "z", -1)
     pairs = [
         moved(p, [(i, (i - 2 * j) % nblk) for i in ring])
         for j, p in ((1, pair1), (2, pair2), (3, pair3))
     ]
-    rows = fence((rows, first))[0]
     returned = lax.all_to_all(rows, "group", split_axis=0, concat_axis=0, tiled=True)
-    x, far = fence((x, far, first, pairs))[:2]
+    x, far, deep, pairs = fence((x, far, deep, pairs))
+    degree = deep[1, :nodes].astype(F32)
+    inverse = 1.0 / jnp.maximum(degree, 1.0)
+    far = (inverse[:, None] * far.astype(F32)).astype(BF16)
 
     one = turned(jnp.where(ypos == 0, far, x), "y", -1)
     three = turned(jnp.where(ypos == ny - 1, x, far), "y", 1)
     side = swapped(jnp.where(core == 1, x, far))
-    other = swapped(jnp.concatenate([p[1:2] for p in pairs], axis=0))
-    near = run_build(((own, 0), (first, 0)), nodes)
+    beside = jnp.where(core == 1, beside, deep[0:1])
+    other = swapped(jnp.concatenate([p[1:2] for p in pairs] + [beside], axis=0))
+    near = run_build(((own, 0), (other, 3)), nodes)
     quad = run_build(((pairs[0], 0), (pairs[2], 0), (other, 0), (other, 2)), nodes)
     mid = run_build(((pairs[1], 0), (other, 1)), nodes)
     one, three = fence((one, three, near, quad, mid, side))[:2]
@@ -362,9 +364,9 @@
     part = part + zflip(part, 4)
     part, total = fence((part, run_finish(summed, cotangent, w_self, w_neigh)))
     part = (part + zflip(part, 1)) + (zflip(part, 2) + zflip(part, 3))
-    part = jnp.stack([part] + [turned(part, "y", t) for t in range(1, ny)])
-    held = [part] + [turned(part, "group", s) for s in range(1, ngroup)]
-    held = held + [swapped(v) for v in held]
+    part = jnp.broadcast_to(part[None], (ngroup * ny,) + part.shape)
+    part = lax.all_to_all(part, ("group", "y"), split_axis=0, concat_axis=0, tiled=True)
+    held = (part, swapped(part))
     factor = 1.0 / math.sqrt(nodes * ngroup * nblk)
     grad_self, grad_neigh = run_place(held, factor, width)
     return (total, grad_self, grad_neigh)

time: 147 us -> 143 us (0.973)
  blocking collectives: 21.3 us -> 38.1 us
  starting transfers between devices: 49.7 us -> 33.8 us
  waiting for transfers between devices: 30.1 us -> 25.1 us
    all_to_all x1 -> x2, blocking collectives: 21.3 us -> 38.1 us  [on_device(): lax.all_to_all(part, ('group', 'y'), split_axis=0, concat_axis=0, tiled=T...]
    ppermute x10 -> x7, starting transfers between devices: 18.5 us -> 9.15 us  [swapped(): return lax.ppermute(v, 'core', swap)]
    ppermute x5 -> x4, waiting for transfers between devices: 13.6 us -> 4.85 us  [moved(): return lax.ppermute(value, BLK, perm)]
    ppermute x9 -> x4, starting transfers between devices: 13.5 us -> 8.93 us  [turned(): lax.ppermute(value, axis, [(i, (i + by) % length) for i in range(length)])]
    ppermute x9 -> x4, waiting for transfers between devices: 5.91 us -> 8.94 us  [turned(): lax.ppermute(value, axis, [(i, (i + by) % length) for i in range(length)])]
    ppermute x5 -> x4, starting transfers between devices: 7.06 us -> 4.67 us  [moved(): return lax.ppermute(value, BLK, perm)]
    ppermute x10 -> x7, waiting for transfers between devices: 6.02 us -> 7.14 us  [swapped(): return lax.ppermute(v, 'core', swap)]
    unnamed x29 -> x31, local copies, waits for them, and re-layouts: 2.95 us -> 2.97 us
  transfers between devices with their start and end apart: 29 -> 20, of which waited for: 19 -> 14; matrix products, arithmetic and copies ran while one was open for 2% -> 2% of each run, Pallas kernels for 18% -> 21%
where the time goes in v6:
time: 143 us; the launch traced here: 142 us
  blocking collectives  38.1 us (27%)
  Pallas kernels  34.7 us (24%)
  starting transfers between devices  33.8 us (24%)
  waiting for transfers between devices  25.1 us (18%)
  other arithmetic  6.53 us (5%)
  local copies, waits for them, and re-layouts  3.12 us (2%)
    all_to_all x2, blocking collectives, on_device(): lax.all_to_all(part, ('group', 'y'), split_axis=0, concat_axis=0, tiled=T...  38.1 us
    pallas_call x3, Pallas kernels, run_build(): pl.pallas_call(functools.partial(build, rows), grid=(slots,), in_specs=[w...  13 us
    pallas_call x1, Pallas kernels, run_most(): pl.pallas_call(most_sum, grid=(nodes // BLOCK,), in_specs=[tile_spec(s, n...  9.61 us
    ppermute x7, starting transfers between devices, swapped(): return lax.ppermute(v, 'core', swap)  9.15 us
    ppermute x4, waiting for transfers between devices, turned(): lax.ppermute(value, axis, [(i, (i + by) % length) for i in range(length)])  8.94 us
    ppermute x4, starting transfers between devices, turned(): lax.ppermute(value, axis, [(i, (i + by) % length) for i in range(length)])  8.93 us
    ppermute x7, waiting for transfers between devices, swapped(): return lax.ppermute(v, 'core', swap)  7.14 us
    ppermute x4, starting transfers between devices, zflip(): return lax.ppermute(v, 'z', [(i, i ^ k) for i in range(nz)])  6.99 us
  transfers between devices with their start and end apart: 20, of which 14 were waited for; matrix products, arithmetic and copies ran while one was open for 2% of the time, Pallas kernels for 21%

profile of v6, /device:TPU:1, one launch (start us, length us, event | category | flops | bytes accessed | tf_op | source)
XLA Modules:
  0.0 142.1 jit_solution(15793416107537988762)
XLA Ops:
  0.6 6.5 %collective-permute-start = (bf16[768,512]{1,0:T(8,128)(2,1)}, bf16[768,512]{1,0:T(8,128)(2,1)S(1)}, u32[]{:S(2)}, u32[]{:S(2)}) collective-permute-start(bf16[768,512]{1,0:T(8,128)(2,1)} %cot.5), channel_id=1, source_target_pairs={{0,56},{8,0},{16,8},{24,16},{32,24},{40,32},{48,40},{56,48},{1,57}... | collective-permute-start | bytes 2359304 | tf_op jit(solution)/shard_map/ppermute | solution.py:275
  7.1 4.6 %prepare.1 = (bf16[768,512]{1,0:T(8,128)(2,1)}, bf16[4,256,512]{2,1,0:T(8,128)(2,1)}, s32[1,2048]{1,0:T(1,128)}, s32[1,2048]{1,0:T(1,128)}, s32[2,2048]{1,0:T(2,...) custom-call(s32[1,8]{1,0:T(1,128)} %tcount.1, s32[1,4]{1,0:T(1,128)} %rcount.1, ...), custom_call_target="tpu_custom_call" | custom-call | flops 805306368 | bytes 854040 | tf_op jit(solution)/shard_map/prepare/pallas_call | solution.py:179
  12.5 3.2 %collective-permute-start.2 = (s32[2,2048]{1,0:T(2,128)}, s32[2,2048]{1,0:T(2,128)S(1)}, u32[]{:S(2)}, u32[]{:S(2)}) collective-permute-start(s32[2,2048]{1,0:T(2,128)} %get-tuple-element.30), channel_id=1, source_target_pairs={{0,62},{1,63},{2,0},{3,1},{4,2},{5,3},{6,4},{7,5},{8,6},{9,7},{10,... | collective-permute-start | bytes 49160 | tf_op jit(solution)/shard_map/ppermute | solution.py:270
  17.1 6.8 %collective-permute-done.1 = s32[2,2048]{1,0:T(2,128)S(1)} collective-permute-done((s32[2,2048]{1,0:T(2,128)}, s32[2,2048]{1,0:T(2,128)S(1)}, u32[]{:S(2)}, u32[]{:S(2)}) %collective-permute-start.1) | collective-permute-done | bytes 16416 | tf_op jit(solution)/shard_map/ppermute | solution.py:275
  25.0 2.8 %broadcast_select_fusion.1 = (bf16[768,512]{1,0:T(8,128)(2,1)}, bf16[768,512]{1,0:T(8,128)(2,1)}, bf16[768,512]{1,0:T(8,128)(2,1)}) fusion(bf16[768,512]{1,0:T(8,128)(2,1)} %get-tuple-element.38.x0, pred[]{:T(512)S(6)} %eq.15, bf16[768,512]{1,0:T(8,128)(2,1)S(1)} %collective-permute-done, f32[768]{0:T(1024)S(1)} %divide_reduce_fusion, pred[]{:T(512)S(6)} %eq.14, ...), kind=kLoop, calls=%fused_computation.2 | loop fusion | flops 2359296 | bytes 3935235 | tf_op jit(solution)/shard_map/jit(_where)/select_n | solution.py:328
  31.6 4.0 %all-to-all-start = ((bf16[4,256,512]{2,1,0:T(8,128)(2,1)}), bf16[4,256,512]{2,1,0:T(8,128)(2,1)S(1)}, u32[]{:S(2)}, u32[]{:S(2)}) async-start(bf16[4,256,512]{2,1,0:T(8,128)(2,1)} %get-tuple-element.42), calls=%async_computation | async-start | bytes 2097152 | tf_op jit(solution)/shard_map/all_to_all | solution.py:321
  36.2 5.9 %build.4.t2.t3.t4.t5 = bf16[4,768,768]{2,1,0:T(8,128)(2,1)} custom-call(s32[2,2048]{1,0:T(2,128)} %copy-done.10, s32[2,2048]{1,0:T(2,128)} %copy-done.12, s32[4,2048]{1,0:T(4,128)} %copy-done.9, s32[4,2048]{1,0:T(4,128)} %copy-done.9), custom_call_target="tpu_custom_call" | custom-call | flops 3145728 | bytes 1572864 | tf_op jit(solution)/shard_map/build/pallas_call | solution.py:195
  42.2 3.3 %build.5.tiles = bf16[2,768,768]{2,1,0:T(8,128)(2,1)} custom-call(s32[2,2048]{1,0:T(2,128)} %copy-done.11, s32[4,2048]{1,0:T(4,128)} %copy-done.9), custom_call_target="tpu_custom_call" | custom-call | flops 3145728 | bytes 1572864 | tf_op jit(solution)/shard_map/build/pallas_call | solution.py:195
  45.5 3.7 %build.3.t0.t1 = bf16[2,768,768]{2,1,0:T(8,128)(2,1)} custom-call(s32[1,2048]{1,0:T(1,128)} %get-tuple-element.27.refs_0_, s32[4,2048]{1,0:T(4,128)} %copy-done.9), custom_call_target="tpu_custom_call" | custom-call | flops 3145728 | bytes 1572864 | tf_op jit(solution)/shard_map/build/pallas_call | solution.py:195
  49.3 2.2 %collective-permute-done.8.x3 = bf16[768,512]{1,0:T(8,128)(2,1)} collective-permute-done((bf16[768,512]{1,0:T(8,128)(2,1)}, bf16[768,512]{1,0:T(8,128)(2,1)}, u32[]{:S(2)}, u32[]{:S(2)}) %collective-permute-start.8) | collective-permute-done | bytes 786464 | tf_op jit(solution)/shard_map/ppermute | solution.py:275
  52.6 2.1 %broadcast_select_fusion = bf16[768,512]{1,0:T(8,128)(2,1)} fusion(bf16[768,512]{1,0:T(8,128)(2,1)S(1)} %collective-permute-done.7.x2, bf16[768,512]{1,0:T(8,128)(2,1)} %collective-permute-done.8.x3, pred[]{:T(512)S(6)} %eq.16), kind=kLoop, calls=%fused_computation.1 | loop fusion | flops 393216 | bytes 2359297 | tf_op jit(solution)/shard_map/jit(_where)/select_n | solution.py:336
  56.3 9.6 %most_sum.1.before = f32[768,512]{1,0:T(8,128)} custom-call(bf16[2,768,768]{2,1,0:T(8,128)(2,1)} %build.3.t0.t1, bf16[2,768,768]{2,1,0:T(8,128)(2,1)} %build.3.t0.t1, bf16[4,768,768]{2,1,0:T(8,128)(2,1)} %build.4.t2.t3.t4.t5, bf16[4,768,768]{2,1,0:T(8,128)(2,1)} %build.4.t2.t3.t4.t5, bf16[4,768,768]{2,1,0:T(8,128)(2,1)} %build.4.t2.t3.t4.t5, ...), custom_call_target="tpu_custom_call" | custom-call | flops 4227858432 | bytes 6291456 | tf_op jit(solution)/shard_map/most_sum/pallas_call | solution.py:210
  65.9 3.8 %collective-permute-done.11.x0 = bf16[768,512]{1,0:T(8,128)(2,1)S(1)} collective-permute-done((bf16[768,512]{1,0:T(8,128)(2,1)}, bf16[768,512]{1,0:T(8,128)(2,1)S(1)}, u32[]{:S(2)}, u32[]{:S(2)}) %collective-permute-start.11) | collective-permute-done | bytes 786464 | tf_op jit(solution)/shard_map/ppermute | solution.py:270
  70.4 1.9 %collective-permute-done.12.x1 = bf16[768,512]{1,0:T(8,128)(2,1)S(1)} collective-permute-done((bf16[768,512]{1,0:T(8,128)(2,1)S(1)}, bf16[768,512]{1,0:T(8,128)(2,1)S(1)}, u32[]{:S(2)}, u32[]{:S(2)}) %collective-permute-start.12) | collective-permute-done | bytes 786464 | tf_op jit(solution)/shard_map/ppermute | solution.py:304
  73.7 3.2 %last_sum.1 = (f32[768,512]{1,0:T(8,128)S(1)}, f32[16,2,16,512]{3,2,1,0:T(8,128)S(1)}, f32[16,2,16,512]{3,2,1,0:T(8,128)S(1)}) custom-call(f32[768,512]{1,0:T(8,128)S(1)} %copy-done.1, bf16[2,768,768]{2,1,0:T(8,128)(2,1)S(1)} %copy-done, bf16[768,512]{1,0:T(8,128)(2,1)S(1)} %collective-permute-done.11.x0, bf16[768,512]{1,0:T(8,128)(2,1)S(1)} %collective-permute-done.12.x1, ...), custom_call_target="tpu_custom_call" | custom-call | flops 1811939328 | bytes 6291456 | tf_op jit(solution)/shard_map/last_sum/pallas_call | solution.py:227
  77.3 2.3 %collective-permute-done.13 = f32[16,2,16,512]{3,2,1,0:T(8,128)S(1)} collective-permute-done((f32[16,2,16,512]{3,2,1,0:T(8,128)S(1)}, f32[16,2,16,512]{3,2,1,0:T(8,128)S(1)}, u32[]{:S(2)}, u32[]{:S(2)}) %collective-permute-start.13) | collective-permute-done | bytes 1048608 | tf_op jit(solution)/shard_map/ppermute | solution.py:304
  79.9 20.7 %all_to_all.15 = f32[16,2,16,512]{3,2,1,0:T(8,128)} all-to-all(f32[16,2,16,512]{3,2,1,0:T(8,128)S(1)} %add.15), channel_id=1, replica_groups=mesh['group'=4,'z'=8,'y'=4,'core'=2] {'group','y'}, dimensions={0} | all-to-all | bytes 2097152 | tf_op jit(solution)/shard_map/all_to_all | solution.py:359
  101.9 3.3 %collective-permute-start.14 = (f32[2,16,512]{2,1,0:T(8,128)S(1)}, f32[2,16,512]{2,1,0:T(8,128)S(1)}, u32[]{:S(2)}, u32[]{:S(2)}) collective-permute-start(f32[2,16,512]{2,1,0:T(8,128)S(1)} %reduce_sum.9), channel_id=1, source_target_pairs={{0,32},{8,40},{16,48},{24,56},{32,0},{40,8},{48,16},{56,24},{1,33}... | collective-permute-start | bytes 196616 | tf_op jit(solution)/shard_map/ppermute | solution.py:362
  105.2 2.8 %finish.1 = f32[768,512]{1,0:T(8,128)} custom-call(f32[768,512]{1,0:T(8,128)S(1)} %get-tuple-element.46.summed, bf16[768,512]{1,0:T(8,128)(2,1)S(1)} %copy-done.2, bf16[512,512]{1,0:T(8,128)(2,1)S(1)} %copy-done.4, bf16[512,512]{1,0:T(8,128)(2,1)S(1)} %copy-done.5), custom_call_target="tpu_custom_call" | custom-call | flops 1207959552 | bytes 3932160 | tf_op jit(solution)/shard_map/finish/pallas_call | solution.py:254
  110.2 2.3 %collective-permute-start.17 = (f32[2,16,512]{2,1,0:T(8,128)S(1)}, f32[2,16,512]{2,1,0:T(8,128)S(1)}, u32[]{:S(2)}, u32[]{:S(2)}) collective-permute-start(f32[2,16,512]{2,1,0:T(8,128)S(1)} %add.16), channel_id=1, source_target_pairs={{0,24},{8,16},{16,8},{24,0},{32,56},{40,48},{48,40},{56,32},{1,25}... | collective-permute-start | bytes 196616 | tf_op jit(solution)/shard_map/ppermute | solution.py:362
  112.7 2.6 %collective-permute-done.16 = f32[2,16,512]{2,1,0:T(8,128)S(1)} collective-permute-done((f32[2,16,512]{2,1,0:T(8,128)S(1)}, f32[2,16,512]{2,1,0:T(8,128)S(1)}, u32[]{:S(2)}, u32[]{:S(2)}) %collective-permute-start.16) | collective-permute-done | bytes 65568 | tf_op jit(solution)/shard_map/ppermute | solution.py:362
  116.1 17.3 %all_to_all.16.mine = f32[16,2,16,512]{3,2,1,0:T(8,128)S(1)} all-to-all(f32[16,2,16,512]{3,2,1,0:T(8,128)S(1)} %broadcast_in_dim.2), channel_id=1, replica_groups=mesh['group'=4,'z'=8,'y'=4,'core'=2] {'group','y'}, dimensions={0} | all-to-all | bytes 2097152 | tf_op jit(solution)/shard_map/all_to_all | solution.py:368
  133.4 4.9 %collective-permute-start.18 = (f32[16,2,16,512]{3,2,1,0:T(8,128)S(1)}, f32[16,2,16,512]{3,2,1,0:T(8,128)S(1)}, u32[]{:S(2)}, u32[]{:S(2)}) collective-permute-start(f32[16,2,16,512]{3,2,1,0:T(8,128)S(1)} %all_to_all.16.mine), channel_id=1, source_target_pairs={{0,1},{1,0},{2,3},{3,2},{4,5},{5,4},{6,7},{7,6},{8,9},{9,8},{10,11... | collective-permute-start | bytes 3145736 | tf_op jit(solution)/shard_map/ppermute | solution.py:304
  138.3 2.3 %collective-permute-done.18.theirs = f32[16,2,16,512]{3,2,1,0:T(8,128)S(1)} collective-permute-done((f32[16,2,16,512]{3,2,1,0:T(8,128)S(1)}, f32[16,2,16,512]{3,2,1,0:T(8,128)S(1)}, u32[]{:S(2)}, u32[]{:S(2)}) %collective-permute-start.18) | collective-permute-done | bytes 1048608 | tf_op jit(solution)/shard_map/ppermute | solution.py:304
  (70 shorter events, 19.1 us)
Async XLA Ops:
  0.6 24.3 %collective-permute-start = (bf16[768,512]{1,0:T(8,128)(2,1)}, bf16[768,512]{1,0:T(8,128)(2,1)S(1)}, u32[]{:S(2)}, u32[]{:S(2)}) collective-permute-start(bf16[768,512]{1,0:T(8,128)(2,1)} %cot.5), channel_id=1, source_target_pairs={{0,56},{8,0},{16,8},{24,16},{32,24},{40,32},{48,40},{56,48},{1,57}... | collective-permute-start | bytes 2359304 | tf_op jit(solution)/shard_map/ppermute | solution.py:275
  11.7 12.1 %collective-permute-start.1 = (s32[2,2048]{1,0:T(2,128)}, s32[2,2048]{1,0:T(2,128)S(1)}, u32[]{:S(2)}, u32[]{:S(2)}) collective-permute-start(s32[2,2048]{1,0:T(2,128)} %get-tuple-element.29), channel_id=1, source_target_pairs={{0,56},{8,0},{16,8},{24,16},{32,24},{40,32},{48,40},{56,48},{1,57}... | collective-permute-start | bytes 49160 | tf_op jit(solution)/shard_map/ppermute | solution.py:275
  12.5 11.8 %collective-permute-start.2 = (s32[2,2048]{1,0:T(2,128)}, s32[2,2048]{1,0:T(2,128)S(1)}, u32[]{:S(2)}, u32[]{:S(2)}) collective-permute-start(s32[2,2048]{1,0:T(2,128)} %get-tuple-element.30), channel_id=1, source_target_pairs={{0,62},{1,63},{2,0},{3,1},{4,2},{5,3},{6,4},{7,5},{8,6},{9,7},{10,... | collective-permute-start | bytes 49160 | tf_op jit(solution)/shard_map/ppermute | solution.py:270
  15.6 8.9 %collective-permute-start.3 = (s32[2,2048]{1,0:T(2,128)}, s32[2,2048]{1,0:T(2,128)S(1)}, u32[]{:S(2)}, u32[]{:S(2)}) collective-permute-start(s32[2,2048]{1,0:T(2,128)} %get-tuple-element.31), channel_id=1, source_target_pairs={{0,60},{1,61},{2,62},{3,63},{4,0},{5,1},{6,2},{7,3},{8,4},{9,5},{1... | collective-permute-start | bytes 49160 | tf_op jit(solution)/shard_map/ppermute | solution.py:270
  16.0 8.9 %collective-permute-start.4 = (s32[2,2048]{1,0:T(2,128)}, s32[2,2048]{1,0:T(2,128)S(1)}, u32[]{:S(2)}, u32[]{:S(2)}) collective-permute-start(s32[2,2048]{1,0:T(2,128)} %get-tuple-element.32), channel_id=1, source_target_pairs={{0,58},{1,59},{2,60},{3,61},{4,62},{5,63},{6,0},{7,1},{8,2},{9,3},... | collective-permute-start | bytes 49160 | tf_op jit(solution)/shard_map/ppermute | solution.py:270
  27.8 21.4 %collective-permute-start.6 = (bf16[768,512]{1,0:T(8,128)(2,1)}, bf16[768,512]{1,0:T(8,128)(2,1)S(1)}, u32[]{:S(2)}, u32[]{:S(2)}) collective-permute-start(bf16[768,512]{1,0:T(8,128)(2,1)} %get-tuple-element.53), channel_id=1, source_target_pairs={{0,1},{1,0},{2,3},{3,2},{4,5},{5,4},{6,7},{7,6},{8,9},{9,8},{10,11... | collective-permute-start | bytes 2359304 | tf_op jit(solution)/shard_map/ppermute | solution.py:304
  29.3 19.9 %collective-permute-start.7 = (bf16[768,512]{1,0:T(8,128)(2,1)}, bf16[768,512]{1,0:T(8,128)(2,1)S(1)}, u32[]{:S(2)}, u32[]{:S(2)}) collective-permute-start(bf16[768,512]{1,0:T(8,128)(2,1)} %get-tuple-element.52), channel_id=1, source_target_pairs={{0,6},{2,0},{4,2},{6,4},{1,7},{3,1},{5,3},{7,5},{8,14},{10,8},{12,... | collective-permute-start | bytes 2359304 | tf_op jit(solution)/shard_map/ppermute | solution.py:275
  31.1 20.4 %collective-permute-start.8 = (bf16[768,512]{1,0:T(8,128)(2,1)}, bf16[768,512]{1,0:T(8,128)(2,1)}, u32[]{:S(2)}, u32[]{:S(2)}) collective-permute-start(bf16[768,512]{1,0:T(8,128)(2,1)} %get-tuple-element.51), channel_id=1, source_target_pairs={{0,2},{2,4},{4,6},{6,0},{1,3},{3,5},{5,7},{7,1},{8,10},{10,12},{12... | collective-permute-start | bytes 2359304 | tf_op jit(solution)/shard_map/ppermute | solution.py:275
  31.2 4.4 %collective-permute-start.5 = (s32[4,2048]{1,0:T(4,128)S(1)}, s32[4,2048]{1,0:T(4,128)S(1)}, u32[]{:S(2)}, u32[]{:S(2)}) collective-permute-start(s32[4,2048]{1,0:T(4,128)S(1)} %pad_add_fusion), channel_id=1, source_target_pairs={{0,1},{1,0},{2,3},{3,2},{4,5},{5,4},{6,7},{7,6},{8,9},{9,8},{10,11... | collective-permute-start | bytes 98312 | tf_op jit(solution)/shard_map/ppermute | solution.py:304
  31.6 23.7 %all-to-all-start = ((bf16[4,256,512]{2,1,0:T(8,128)(2,1)}), bf16[4,256,512]{2,1,0:T(8,128)(2,1)S(1)}, u32[]{:S(2)}, u32[]{:S(2)}) async-start(bf16[4,256,512]{2,1,0:T(8,128)(2,1)} %get-tuple-element.42), calls=%async_computation | async-start | bytes 2097152 | tf_op jit(solution)/shard_map/all_to_all | solution.py:321
  51.4 4.2 %collective-permute-start.9 = (bf16[768,512]{1,0:T(8,128)(2,1)S(1)}, bf16[768,512]{1,0:T(8,128)(2,1)}, u32[]{:S(2)}, u32[]{:S(2)}) collective-permute-start(bf16[768,512]{1,0:T(8,128)(2,1)S(1)} %collective-permute-done.7.x2), channel_id=1, source_target_pairs={{0,1},{1,0},{2,3},{3,2},{4,5},{5,4},{6,7},{7,6},{8,9},{9,8},{10,11... | collective-permute-start | bytes 2359304 | tf_op jit(solution)/shard_map/ppermute | solution.py:304
  52.6 3.4 %collective-permute-start.10 = (bf16[768,512]{1,0:T(8,128)(2,1)}, bf16[768,512]{1,0:T(8,128)(2,1)}, u32[]{:S(2)}, u32[]{:S(2)}) collective-permute-start(bf16[768,512]{1,0:T(8,128)(2,1)} %collective-permute-done.8.x3), channel_id=1, source_target_pairs={{0,1},{1,0},{2,3},{3,2},{4,5},{5,4},{6,7},{7,6},{8,9},{9,8},{10,11... | collective-permute-start | bytes 2359304 | tf_op jit(solution)/shard_map/ppermute | solution.py:304
  54.7 15.0 %collective-permute-start.11 = (bf16[768,512]{1,0:T(8,128)(2,1)}, bf16[768,512]{1,0:T(8,128)(2,1)S(1)}, u32[]{:S(2)}, u32[]{:S(2)}) collective-permute-start(bf16[768,512]{1,0:T(8,128)(2,1)} %broadcast_select_fusion), channel_id=1, source_target_pairs={{0,62},{1,3},{2,0},{3,5},{4,2},{5,7},{6,4},{7,9},{8,6},{9,11},{10,... | collective-permute-start | bytes 2359304 | tf_op jit(solution)/shard_map/ppermute | solution.py:270
  56.2 16.0 %copy-start.2 = (bf16[768,512]{1,0:T(8,128)(2,1)S(1)}, bf16[768,512]{1,0:T(8,128)(2,1)}, u32[]{:S(2)}) copy-start(bf16[768,512]{1,0:T(8,128)(2,1)} %cot.5) | copy-start | bytes 2359300
  56.3 16.0 %copy-start.3 = (bf16[768,512]{1,0:T(8,128)(2,1)S(1)}, bf16[768,512]{1,0:T(8,128)(2,1)}, u32[]{:S(2)}) copy-start(bf16[768,512]{1,0:T(8,128)(2,1)} %feats.1) | copy-start | bytes 2359300
  69.7 2.6 %collective-permute-start.12 = (bf16[768,512]{1,0:T(8,128)(2,1)S(1)}, bf16[768,512]{1,0:T(8,128)(2,1)S(1)}, u32[]{:S(2)}, u32[]{:S(2)}) collective-permute-start(bf16[768,512]{1,0:T(8,128)(2,1)S(1)} %collective-permute-done.11.x0), channel_id=1, source_target_pairs={{0,1},{1,0},{2,3},{3,2},{4,5},{5,4},{6,7},{7,6},{8,9},{9,8},{10,11... | collective-permute-start | bytes 2359304 | tf_op jit(solution)/shard_map/ppermute | solution.py:304
  76.9 2.8 %collective-permute-start.13 = (f32[16,2,16,512]{3,2,1,0:T(8,128)S(1)}, f32[16,2,16,512]{3,2,1,0:T(8,128)S(1)}, u32[]{:S(2)}, u32[]{:S(2)}) collective-permute-start(f32[16,2,16,512]{3,2,1,0:T(8,128)S(1)} %get-tuple-element.45), channel_id=1, source_target_pairs={{0,1},{1,0},{2,3},{3,2},{4,5},{5,4},{6,7},{7,6},{8,9},{9,8},{10,11... | collective-permute-start | bytes 3145736 | tf_op jit(solution)/shard_map/ppermute | solution.py:304
  79.8 25.4 %copy-start.4 = (bf16[512,512]{1,0:T(8,128)(2,1)S(1)}, bf16[512,512]{1,0:T(8,128)(2,1)}, u32[]{:S(2)}) copy-start(bf16[512,512]{1,0:T(8,128)(2,1)} %w_self.1) | copy-start | bytes 1572868
  79.9 25.4 %copy-start.5 = (bf16[512,512]{1,0:T(8,128)(2,1)S(1)}, bf16[512,512]{1,0:T(8,128)(2,1)}, u32[]{:S(2)}) copy-start(bf16[512,512]{1,0:T(8,128)(2,1)} %w_neigh.1) | copy-start | bytes 1572868
  101.9 7.1 %collective-permute-start.14 = (f32[2,16,512]{2,1,0:T(8,128)S(1)}, f32[2,16,512]{2,1,0:T(8,128)S(1)}, u32[]{:S(2)}, u32[]{:S(2)}) collective-permute-start(f32[2,16,512]{2,1,0:T(8,128)S(1)} %reduce_sum.9), channel_id=1, source_target_pairs={{0,32},{8,40},{16,48},{24,56},{32,0},{40,8},{48,16},{56,24},{1,33}... | collective-permute-start | bytes 196616 | tf_op jit(solution)/shard_map/ppermute | solution.py:362
  109.0 6.2 %collective-permute-start.16 = (f32[2,16,512]{2,1,0:T(8,128)S(1)}, f32[2,16,512]{2,1,0:T(8,128)S(1)}, u32[]{:S(2)}, u32[]{:S(2)}) collective-permute-start(f32[2,16,512]{2,1,0:T(8,128)S(1)} %add.16), channel_id=1, source_target_pairs={{0,16},{8,24},{16,0},{24,8},{32,48},{40,56},{48,32},{56,40},{1,17}... | collective-permute-start | bytes 196616 | tf_op jit(solution)/shard_map/ppermute | solution.py:362
  110.2 5.0 %collective-permute-start.17 = (f32[2,16,512]{2,1,0:T(8,128)S(1)}, f32[2,16,512]{2,1,0:T(8,128)S(1)}, u32[]{:S(2)}, u32[]{:S(2)}) collective-permute-start(f32[2,16,512]{2,1,0:T(8,128)S(1)} %add.16), channel_id=1, source_target_pairs={{0,24},{8,16},{16,8},{24,0},{32,56},{40,48},{48,40},{56,32},{1,25}... | collective-permute-start | bytes 196616 | tf_op jit(solution)/shard_map/ppermute | solution.py:362
  112.5 3.4 %collective-permute-start.15 = (f32[2,16,512]{2,1,0:T(8,128)S(1)}, f32[2,16,512]{2,1,0:T(8,128)S(1)}, u32[]{:S(2)}, u32[]{:S(2)}) collective-permute-start(f32[2,16,512]{2,1,0:T(8,128)S(1)} %add.16), channel_id=1, source_target_pairs={{0,8},{8,0},{16,24},{24,16},{32,40},{40,32},{48,56},{56,48},{1,9},... | collective-permute-start | bytes 196616 | tf_op jit(solution)/shard_map/ppermute | solution.py:362
  133.4 7.2 %collective-permute-start.18 = (f32[16,2,16,512]{3,2,1,0:T(8,128)S(1)}, f32[16,2,16,512]{3,2,1,0:T(8,128)S(1)}, u32[]{:S(2)}, u32[]{:S(2)}) collective-permute-start(f32[16,2,16,512]{3,2,1,0:T(8,128)S(1)} %all_to_all.16.mine), channel_id=1, source_target_pairs={{0,1},{1,0},{2,3},{3,2},{4,5},{5,4},{6,7},{7,6},{8,9},{9,8},{10,11... | collective-permute-start | bytes 3145736 | tf_op jit(solution)/shard_map/ppermute | solution.py:304
  (11 other events, 60.1 us)

commit v7 on v6

--- a/solution.py
+++ b/solution.py
@@ -105,6 +105,23 @@
     out[...] = total
 
 
+def choose(deep, x, far, one, three, side):
+    i = pl.program_id(0)
+    block = x.shape[0]
+    degree = deep[1:2, pl.ds(pl.multiple_of(i * block, block), block)].astype(F32)
+    column = jnp.transpose(jnp.broadcast_to(degree, (128, block)))[:, 0:1]
+    scaled = ((1.0 / jnp.maximum(column, 1.0)) * far[...].astype(F32)).astype(BF16)
+    near = x[...]
+    y, core = lax.axis_index("y"), lax.axis_index("core")
+    one[...] = jnp.where(y == 0, scaled, near)
+    three[...] = jnp.where(y == lax.axis_size("y") - 1, near, scaled)
+    side[...] = jnp.where(core == 1, near, scaled)
+
+
+def relay(one, three, out):
+    out[...] = jnp.where(lax.axis_index("core") == 0, one[...], three[...])
+
+
 def last_sum(before, tiles, x0, x1, feats, cot, out, send, keep, grad_self, grad_neigh):
     nodes = before.shape[0]
     grad_self[...] = dot(feats[...], cot[...], DOWN)
@@ -136,8 +153,8 @@
     for k, half in ((core, mine), (1 - core, theirs)):
         for n in range(pieces):
             at = pl.ds(pl.multiple_of((k * pieces + n) * size, size), size)
-            out_self[at, :] = half[n, 0] * factor
-            out_neigh[at, :] = half[n, 1] * factor
+            out_self[at, :] = half[n, 0].astype(F32) * factor
+            out_neigh[at, :] = (half[n, 1].astype(F32) + half[n, 2].astype(F32)) * factor
 
 
 def finish(summed, cot, w_self, w_neigh, out):
@@ -218,6 +235,21 @@
         cost_estimate=estimate(7 * nodes * nodes * width, 16 * nodes * width),
         name="most_sum",
     )(near, near, quad, quad, quad, quad, *xs, ids, rows)
+
+
+def run_rows(kernel, given, made, name):
+    nodes, width = given[-1].shape
+    lead = [whole(v.shape) for v in given if v.shape[0] != nodes]
+    return pl.pallas_call(
+        kernel,
+        grid=(nodes // BLOCK,),
+        in_specs=lead + [row_spec(width)] * (len(given) - len(lead)),
+        out_specs=[row_spec(width)] * made,
+        out_shape=[jax.ShapeDtypeStruct((nodes, width), BF16)] * made,
+        compiler_params=params(64),
+        cost_estimate=estimate(nodes * width, 2 * (made + 2) * nodes * width),
+        name=name,
+    )(*given)
 
 
 def run_last(before, tiles, xs, features, cotangent, pieces):
@@ -296,7 +328,7 @@
     ept = tile_src.shape[2]
     nz, ny = lax.axis_size("z"), lax.axis_size("y")
     nblk = nz * ny * 2
-    core, ypos = lax.axis_index("core"), lax.axis_index("y")
+    core = lax.axis_index("core")
     ring = range(nblk)
     swap = [(0, 1), (1, 0)]
 
@@ -320,25 +352,21 @@
     ]
     returned = lax.all_to_all(rows, "group", split_axis=0, concat_axis=0, tiled=True)
     x, far, deep, pairs = fence((x, far, deep, pairs))
-    degree = deep[1, :nodes].astype(F32)
-    inverse = 1.0 / jnp.maximum(degree, 1.0)
-    far = (inverse[:, None] * far.astype(F32)).astype(BF16)
-
-    one = turned(jnp.where(ypos == 0, far, x), "y", -1)
-    three = turned(jnp.where(ypos == ny - 1, x, far), "y", 1)
-    side = swapped(jnp.where(core == 1, x, far))
+
+    one, three, side = run_rows(choose, (deep, x, far), 3, "choose")
+    one = turned(one, "y", -1)
+    three = turned(three, "y", 1)
+    side = swapped(side)
     beside = jnp.where(core == 1, beside, deep[0:1])
     other = swapped(jnp.concatenate([p[1:2] for p in pairs] + [beside], axis=0))
     near = run_build(((own, 0), (other, 3)), nodes)
     quad = run_build(((pairs[0], 0), (pairs[2], 0), (other, 0), (other, 2)), nodes)
     mid = run_build(((pairs[1], 0), (other, 1)), nodes)
     one, three = fence((one, three, near, quad, mid, side))[:2]
-    relay = jnp.where(core == 0, one, three)
-
-    two = moved(
-        relay,
-        [(i, (i - 2 if i % 2 == 0 else i + 2) % nblk) for i in ring],
-    )
+
+    (two,) = run_rows(relay, (one, three), 1, "relay")
+    one, three, two = fence((one, three, two))
+    two = moved(two, [(i, (i - 2 if i % 2 == 0 else i + 2) % nblk) for i in ring])
     one_b = swapped(one)
     three_b = swapped(three)
     summed = run_most(
@@ -364,6 +392,8 @@
     part = part + zflip(part, 4)
     part, total = fence((part, run_finish(summed, cotangent, w_self, w_neigh)))
     part = (part + zflip(part, 1)) + (zflip(part, 2) + zflip(part, 3))
+    top = part[1].astype(BF16)
+    part = jnp.stack([part[0].astype(BF16), top, (part[1] - top.astype(F32)).astype(BF16)])
     part = jnp.broadcast_to(part[None], (ngroup * ny,) + part.shape)
     part = lax.all_to_all(part, ("group", "y"), split_axis=0, concat_axis=0, tiled=True)
     held = (part, swapped(part))

time: 143 us -> 147 us (1.028)
  Pallas kernels: 34.7 us -> 41 us
  other arithmetic: 6.53 us -> 2.34 us
  starting transfers between devices: 33.8 us -> 37.9 us
  local copies, waits for them, and re-layouts: 3.12 us -> 6.47 us
  blocking collectives: 38.1 us -> 34.8 us
  waiting for transfers between devices: 25.1 us -> 22.6 us
    pallas_call x0 -> x2, Pallas kernels: none -> 6.88 us  [run_rows(): pl.pallas_call(kernel, grid=(nodes // BLOCK,), in_specs=lead + [row_spec(...]
    select_n x2 -> x0, other arithmetic: 4.93 us -> none  [the longest x1 2.82 us: on_device(): three = turned(jnp.where(ypos == ny - 1, x, far), 'y', 1)]
    ppermute x7, starting transfers between devices: 9.15 us -> 12.5 us  [swapped(): return lax.ppermute(v, 'core', swap)]
    all_to_all x2, blocking collectives: 38.1 us -> 34.8 us  [on_device(): lax.all_to_all(part, ('group', 'y'), split_axis=0, concat_axis=0, tiled=T...]
    ppermute x4, waiting for transfers between devices: 8.94 us -> 6.76 us  [turned(): lax.ppermute(value, axis, [(i, (i + by) % length) for i in range(length)])]
    slice x3, local copies, waits for them, and re-layouts: 0.03 us -> 2.19 us  [on_device(): other = swapped(jnp.concatenate([p[1:2] for p in pairs] + [beside], axis=0))]
    unnamed x31 -> x19, local copies, waits for them, and re-layouts: 2.97 us -> 4.19 us
  transfers between devices with their start and end apart: 20 -> 20, of which waited for: 14 -> 12; matrix products, arithmetic and copies ran while one was open for 2% -> 3% of each run, Pallas kernels for 21% -> 22%
where the time goes in v7:
time: 147 us; the launch traced here: 146 us
  Pallas kernels  41 us (28%)
  starting transfers between devices  37.9 us (26%)
  blocking collectives  34.8 us (24%)
  waiting for transfers between devices  22.6 us (15%)
  local copies, waits for them, and re-layouts  6.47 us (4%)
  other arithmetic  2.34 us (2%)
    all_to_all x2, blocking collectives, on_device(): lax.all_to_all(part, ('group', 'y'), split_axis=0, concat_axis=0, tiled=T...  34.8 us
    ppermute x7, starting transfers between devices, swapped(): return lax.ppermute(v, 'core', swap)  12.5 us
    pallas_call x3, Pallas kernels, run_build(): pl.pallas_call(functools.partial(build, rows), grid=(slots,), in_specs=[w...  12.4 us
    pallas_call x1, Pallas kernels, run_most(): pl.pallas_call(most_sum, grid=(nodes // BLOCK,), in_specs=[tile_spec(s, n...  9.61 us
    ppermute x4, starting transfers between devices, turned(): lax.ppermute(value, axis, [(i, (i + by) % length) for i in range(length)])  8.93 us
    pallas_call x2, Pallas kernels, run_rows(): pl.pallas_call(kernel, grid=(nodes // BLOCK,), in_specs=lead + [row_spec(...  6.88 us
    ppermute x7, waiting for transfers between devices, swapped(): return lax.ppermute(v, 'core', swap)  6.81 us
    ppermute x4, waiting for transfers between devices, turned(): lax.ppermute(value, axis, [(i, (i + by) % length) for i in range(length)])  6.76 us
  transfers between devices with their start and end apart: 20, of which 12 were waited for; matrix products, arithmetic and copies ran while one was open for 3% of the time, Pallas kernels for 22%

profile of v7, /device:TPU:1, one launch (start us, length us, event | category | flops | bytes accessed | tf_op | source)
XLA Modules:
  0.0 145.9 jit_solution(14528178336328056441)
XLA Ops:
  0.6 6.5 %collective-permute-start = (bf16[768,512]{1,0:T(8,128)(2,1)}, bf16[768,512]{1,0:T(8,128)(2,1)}, u32[]{:S(2)}, u32[]{:S(2)}) collective-permute-start(bf16[768,512]{1,0:T(8,128)(2,1)} %cot.5), channel_id=1, source_target_pairs={{0,56},{8,0},{16,8},{24,16},{32,24},{40,32},{48,40},{56,48},{1,57}... | collective-permute-start | bytes 2359304 | tf_op jit(solution)/shard_map/ppermute | solution.py:307
  7.1 4.6 %prepare.1 = (bf16[768,512]{1,0:T(8,128)(2,1)}, bf16[4,256,512]{2,1,0:T(8,128)(2,1)}, s32[1,2048]{1,0:T(1,128)}, s32[1,2048]{1,0:T(1,128)}, s32[2,2048]{1,0:T(2,...) custom-call(s32[1,8]{1,0:T(1,128)} %tcount.1, s32[1,4]{1,0:T(1,128)} %rcount.1, ...), custom_call_target="tpu_custom_call" | custom-call | flops 805306368 | bytes 854040 | tf_op jit(solution)/shard_map/prepare/pallas_call | solution.py:196
  12.5 3.2 %collective-permute-start.2 = (s32[2,2048]{1,0:T(2,128)}, s32[2,2048]{1,0:T(2,128)}, u32[]{:S(2)}, u32[]{:S(2)}) collective-permute-start(s32[2,2048]{1,0:T(2,128)} %get-tuple-element.36), channel_id=1, source_target_pairs={{0,62},{1,63},{2,0},{3,1},{4,2},{5,3},{6,4},{7,5},{8,6},{9,7},{10,... | collective-permute-start | bytes 49160 | tf_op jit(solution)/shard_map/ppermute | solution.py:302
  17.1 6.8 %collective-permute-done.1.deep = s32[2,2048]{1,0:T(2,128)} collective-permute-done((s32[2,2048]{1,0:T(2,128)}, s32[2,2048]{1,0:T(2,128)}, u32[]{:S(2)}, u32[]{:S(2)}) %collective-permute-start.1) | collective-permute-done | bytes 16416 | tf_op jit(solution)/shard_map/ppermute | solution.py:307
  24.9 3.8 %choose.1 = (bf16[768,512]{1,0:T(8,128)(2,1)}, bf16[768,512]{1,0:T(8,128)(2,1)}, bf16[768,512]{1,0:T(8,128)(2,1)}) custom-call(s32[2,2048]{1,0:T(2,128)} %collective-permute-done.1.deep, bf16[768,512]{1,0:T(8,128)(2,1)} %get-tuple-element.44.x.x0, bf16[768,512]{1,0:T(8,128)(2,1)} %collective-permute-done.far), custom_call_target="tpu_custom_call" | custom-call | flops 786432 | bytes 3932160 | tf_op jit(solution)/shard_map/choose/pallas_call | solution.py:243
  35.5 4.4 %all-to-all-start = ((bf16[4,256,512]{2,1,0:T(8,128)(2,1)}), bf16[4,256,512]{2,1,0:T(8,128)(2,1)}, u32[]{:S(2)}, u32[]{:S(2)}) async-start(bf16[4,256,512]{2,1,0:T(8,128)(2,1)} %get-tuple-element.53), calls=%async_computation | async-start | bytes 2097152 | tf_op jit(solution)/shard_map/all_to_all | solution.py:353
  40.5 3.1 %build.5.tiles = bf16[2,768,768]{2,1,0:T(8,128)(2,1)} custom-call(s32[2,2048]{1,0:T(2,128)} %collective-permute-done.3.refs_0_, s32[4,2048]{1,0:T(4,128)} %copy-done.8), custom_call_target="tpu_custom_call" | custom-call | flops 3145728 | bytes 1572864 | tf_op jit(solution)/shard_map/build/pallas_call | solution.py:212
  43.6 5.9 %build.4.t2.t3.t4.t5 = bf16[4,768,768]{2,1,0:T(8,128)(2,1)} custom-call(s32[2,2048]{1,0:T(2,128)} %collective-permute-done.2.refs_0_, s32[2,2048]{1,0:T(2,128)} %collective-permute-done.4.refs_1_, s32[4,2048]{1,0:T(4,128)} %copy-done.8, s32[4,2048]{1,0:T(4,128)} %copy-done.8), custom_call_target="tpu_custom_call" | custom-call | flops 3145728 | bytes 1572864 | tf_op jit(solution)/shard_map/build/pallas_call | solution.py:212
  49.5 3.4 %build.3.t0.t1 = bf16[2,768,768]{2,1,0:T(8,128)(2,1)} custom-call(s32[1,2048]{1,0:T(1,128)} %get-tuple-element.33.refs_0_, s32[4,2048]{1,0:T(4,128)} %copy-done.8), custom_call_target="tpu_custom_call" | custom-call | flops 3145728 | bytes 1572864 | tf_op jit(solution)/shard_map/build/pallas_call | solution.py:212
  52.9 3.0 %relay.1 = bf16[768,512]{1,0:T(8,128)(2,1)} custom-call(bf16[768,512]{1,0:T(8,128)(2,1)} %collective-permute-done.7.one.x2, bf16[768,512]{1,0:T(8,128)(2,1)} %collective-permute-done.8.three.x3), custom_call_target="tpu_custom_call" | custom-call | flops 786432 | bytes 2359296 | tf_op jit(solution)/shard_map/relay/pallas_call | solution.py:243
  56.0 2.0 %collective-permute-start.9 = (bf16[768,512]{1,0:T(8,128)(2,1)}, bf16[768,512]{1,0:T(8,128)(2,1)S(1)}, u32[]{:S(2)}, u32[]{:S(2)}) collective-permute-start(bf16[768,512]{1,0:T(8,128)(2,1)} %collective-permute-done.7.one.x2), channel_id=1, source_target_pairs={{0,1},{1,0},{2,3},{3,2},{4,5},{5,4},{6,7},{7,6},{8,9},{9,8},{10,11... | collective-permute-start | bytes 2359304 | tf_op jit(solution)/shard_map/ppermute | solution.py:336
  62.1 9.6 %most_sum.1.before = f32[768,512]{1,0:T(8,128)} custom-call(bf16[2,768,768]{2,1,0:T(8,128)(2,1)} %build.3.t0.t1, bf16[2,768,768]{2,1,0:T(8,128)(2,1)} %build.3.t0.t1, bf16[4,768,768]{2,1,0:T(8,128)(2,1)} %build.4.t2.t3.t4.t5, bf16[4,768,768]{2,1,0:T(8,128)(2,1)} %build.4.t2.t3.t4.t5, bf16[4,768,768]{2,1,0:T(8,128)(2,1)} %build.4.t2.t3.t4.t5, ...), custom_call_target="tpu_custom_call" | custom-call | flops 4227858432 | bytes 6291456 | tf_op jit(solution)/shard_map/most_sum/pallas_call | solution.py:227
  71.7 2.6 %collective-permute-done.11.x0 = bf16[768,512]{1,0:T(8,128)(2,1)S(1)} collective-permute-done((bf16[768,512]{1,0:T(8,128)(2,1)}, bf16[768,512]{1,0:T(8,128)(2,1)S(1)}, u32[]{:S(2)}, u32[]{:S(2)}) %collective-permute-start.11) | collective-permute-done | bytes 786464 | tf_op jit(solution)/shard_map/ppermute | solution.py:302
  74.3 2.8 %collective-permute-start.12 = (bf16[768,512]{1,0:T(8,128)(2,1)S(1)}, bf16[768,512]{1,0:T(8,128)(2,1)S(1)}, u32[]{:S(2)}, u32[]{:S(2)}) collective-permute-start(bf16[768,512]{1,0:T(8,128)(2,1)S(1)} %collective-permute-done.11.x0), channel_id=1, source_target_pairs={{0,1},{1,0},{2,3},{3,2},{4,5},{5,4},{6,7},{7,6},{8,9},{9,8},{10,11... | collective-permute-start | bytes 2359304 | tf_op jit(solution)/shard_map/ppermute | solution.py:336
  77.2 1.9 %collective-permute-done.12.x1 = bf16[768,512]{1,0:T(8,128)(2,1)S(1)} collective-permute-done((bf16[768,512]{1,0:T(8,128)(2,1)S(1)}, bf16[768,512]{1,0:T(8,128)(2,1)S(1)}, u32[]{:S(2)}, u32[]{:S(2)}) %collective-permute-start.12) | collective-permute-done | bytes 786464 | tf_op jit(solution)/shard_map/ppermute | solution.py:336
  80.5 3.2 %last_sum.1 = (f32[768,512]{1,0:T(8,128)S(1)}, f32[16,2,16,512]{3,2,1,0:T(8,128)S(1)}, f32[16,2,16,512]{3,2,1,0:T(8,128)S(1)}) custom-call(f32[768,512]{1,0:T(8,128)S(1)} %copy-done.1, bf16[2,768,768]{2,1,0:T(8,128)(2,1)S(1)} %copy-done, bf16[768,512]{1,0:T(8,128)(2,1)S(1)} %collective-permute-done.11.x0, bf16[768,512]{1,0:T(8,128)(2,1)S(1)} %collective-permute-done.12.x1, ...), custom_call_target="tpu_custom_call" | custom-call | flops 1811939328 | bytes 6291456 | tf_op jit(solution)/shard_map/last_sum/pallas_call | solution.py:259
  84.2 2.3 %collective-permute-done.13 = f32[16,2,16,512]{3,2,1,0:T(8,128)S(1)} collective-permute-done((f32[16,2,16,512]{3,2,1,0:T(8,128)S(1)}, f32[16,2,16,512]{3,2,1,0:T(8,128)S(1)}, u32[]{:S(2)}, u32[]{:S(2)}) %collective-permute-start.13) | collective-permute-done | bytes 1048608 | tf_op jit(solution)/shard_map/ppermute | solution.py:336
  86.7 21.1 %all_to_all.15 = f32[16,2,16,512]{3,2,1,0:T(8,128)} all-to-all(f32[16,2,16,512]{3,2,1,0:T(8,128)S(1)} %add.15), channel_id=1, replica_groups=mesh['group'=4,'z'=8,'y'=4,'core'=2] {'group','y'}, dimensions={0} | all-to-all | bytes 2097152 | tf_op jit(solution)/shard_map/all_to_all | solution.py:387
  109.1 2.4 %collective-permute-start.14 = (f32[2,16,512]{2,1,0:T(8,128)S(1)}, f32[2,16,512]{2,1,0:T(8,128)S(1)}, u32[]{:S(2)}, u32[]{:S(2)}) collective-permute-start(f32[2,16,512]{2,1,0:T(8,128)S(1)} %reduce_sum.9), channel_id=1, source_target_pairs={{0,32},{8,40},{16,48},{24,56},{32,0},{40,8},{48,16},{56,24},{1,33}... | collective-permute-start | bytes 196616 | tf_op jit(solution)/shard_map/ppermute | solution.py:390
  111.5 2.8 %finish.1 = f32[768,512]{1,0:T(8,128)} custom-call(f32[768,512]{1,0:T(8,128)S(1)} %get-tuple-element.58.summed, bf16[768,512]{1,0:T(8,128)(2,1)S(1)} %copy-done.2, bf16[512,512]{1,0:T(8,128)(2,1)S(1)} %copy-done.4, bf16[512,512]{1,0:T(8,128)(2,1)S(1)} %copy-done.5), custom_call_target="tpu_custom_call" | custom-call | flops 1207959552 | bytes 3932160 | tf_op jit(solution)/shard_map/finish/pallas_call | solution.py:286
  114.3 2.6 %collective-permute-done.14 = f32[2,16,512]{2,1,0:T(8,128)S(1)} collective-permute-done((f32[2,16,512]{2,1,0:T(8,128)S(1)}, f32[2,16,512]{2,1,0:T(8,128)S(1)}, u32[]{:S(2)}, u32[]{:S(2)}) %collective-permute-start.14) | collective-permute-done | bytes 65568 | tf_op jit(solution)/shard_map/ppermute | solution.py:390
  118.2 2.4 %collective-permute-start.15 = (f32[2,16,512]{2,1,0:T(8,128)S(1)}, f32[2,16,512]{2,1,0:T(8,128)S(1)}, u32[]{:S(2)}, u32[]{:S(2)}) collective-permute-start(f32[2,16,512]{2,1,0:T(8,128)S(1)} %add.16), channel_id=1, source_target_pairs={{0,8},{8,0},{16,24},{24,16},{32,40},{40,32},{48,56},{56,48},{1,9},... | collective-permute-start | bytes 196616 | tf_op jit(solution)/shard_map/ppermute | solution.py:390
  123.5 13.7 %all_to_all.16.mine = bf16[16,3,16,512]{3,2,1,0:T(8,128)(2,1)S(1)} all-to-all(bf16[16,3,16,512]{3,2,1,0:T(8,128)(2,1)S(1)} %broadcast_in_dim.2), channel_id=1, replica_groups=mesh['group'=4,'z'=8,'y'=4,'core'=2] {'group','y'}, dimensions={0} | all-to-all | bytes 1572864 | tf_op jit(solution)/shard_map/all_to_all | solution.py:398
  137.2 5.2 %collective-permute-start.18 = (bf16[16,3,16,512]{3,2,1,0:T(8,128)(2,1)S(1)}, bf16[16,3,16,512]{3,2,1,0:T(8,128)(2,1)S(1)}, u32[]{:S(2)}, u32[]{:S(2)}) collective-permute-start(bf16[16,3,16,512]{3,2,1,0:T(8,128)(2,1)S(1)} %all_to_all.16.mine), channel_id=1, source_target_pairs={{0,1},{1,0},{2,3},{3,2},{4,5},{5,4},{6,7},{7,6},{8,9},{9,8},{10,11... | collective-permute-start | bytes 2359304 | tf_op jit(solution)/shard_map/ppermute | solution.py:336
  (60 shorter events, 25.7 us)
Async XLA Ops:
  0.6 24.3 %collective-permute-start = (bf16[768,512]{1,0:T(8,128)(2,1)}, bf16[768,512]{1,0:T(8,128)(2,1)}, u32[]{:S(2)}, u32[]{:S(2)}) collective-permute-start(bf16[768,512]{1,0:T(8,128)(2,1)} %cot.5), channel_id=1, source_target_pairs={{0,56},{8,0},{16,8},{24,16},{32,24},{40,32},{48,40},{56,48},{1,57}... | collective-permute-start | bytes 2359304 | tf_op jit(solution)/shard_map/ppermute | solution.py:307
  11.7 12.1 %collective-permute-start.1 = (s32[2,2048]{1,0:T(2,128)}, s32[2,2048]{1,0:T(2,128)}, u32[]{:S(2)}, u32[]{:S(2)}) collective-permute-start(s32[2,2048]{1,0:T(2,128)} %get-tuple-element.35), channel_id=1, source_target_pairs={{0,56},{8,0},{16,8},{24,16},{32,24},{40,32},{48,40},{56,48},{1,57}... | collective-permute-start | bytes 49160 | tf_op jit(solution)/shard_map/ppermute | solution.py:307
  12.5 11.8 %collective-permute-start.2 = (s32[2,2048]{1,0:T(2,128)}, s32[2,2048]{1,0:T(2,128)}, u32[]{:S(2)}, u32[]{:S(2)}) collective-permute-start(s32[2,2048]{1,0:T(2,128)} %get-tuple-element.36), channel_id=1, source_target_pairs={{0,62},{1,63},{2,0},{3,1},{4,2},{5,3},{6,4},{7,5},{8,6},{9,7},{10,... | collective-permute-start | bytes 49160 | tf_op jit(solution)/shard_map/ppermute | solution.py:302
  15.6 8.9 %collective-permute-start.3 = (s32[2,2048]{1,0:T(2,128)}, s32[2,2048]{1,0:T(2,128)}, u32[]{:S(2)}, u32[]{:S(2)}) collective-permute-start(s32[2,2048]{1,0:T(2,128)} %get-tuple-element.37), channel_id=1, source_target_pairs={{0,60},{1,61},{2,62},{3,63},{4,0},{5,1},{6,2},{7,3},{8,4},{9,5},{1... | collective-permute-start | bytes 49160 | tf_op jit(solution)/shard_map/ppermute | solution.py:302
  16.0 8.9 %collective-permute-start.4 = (s32[2,2048]{1,0:T(2,128)}, s32[2,2048]{1,0:T(2,128)}, u32[]{:S(2)}, u32[]{:S(2)}) collective-permute-start(s32[2,2048]{1,0:T(2,128)} %get-tuple-element.38), channel_id=1, source_target_pairs={{0,58},{1,59},{2,60},{3,61},{4,62},{5,63},{6,0},{7,1},{8,2},{9,3},... | collective-permute-start | bytes 49160 | tf_op jit(solution)/shard_map/ppermute | solution.py:302
  28.8 24.1 %collective-permute-start.6 = (bf16[768,512]{1,0:T(8,128)(2,1)}, bf16[768,512]{1,0:T(8,128)(2,1)}, u32[]{:S(2)}, u32[]{:S(2)}) collective-permute-start(bf16[768,512]{1,0:T(8,128)(2,1)} %get-tuple-element.46), channel_id=1, source_target_pairs={{0,1},{1,0},{2,3},{3,2},{4,5},{5,4},{6,7},{7,6},{8,9},{9,8},{10,11... | collective-permute-start | bytes 2359304 | tf_op jit(solution)/shard_map/ppermute | solution.py:336
  30.3 22.6 %collective-permute-start.7 = (bf16[768,512]{1,0:T(8,128)(2,1)}, bf16[768,512]{1,0:T(8,128)(2,1)}, u32[]{:S(2)}, u32[]{:S(2)}) collective-permute-start(bf16[768,512]{1,0:T(8,128)(2,1)} %get-tuple-element.47), channel_id=1, source_target_pairs={{0,6},{2,0},{4,2},{6,4},{1,7},{3,1},{5,3},{7,5},{8,14},{10,8},{12,... | collective-permute-start | bytes 2359304 | tf_op jit(solution)/shard_map/ppermute | solution.py:307
  32.0 20.9 %collective-permute-start.8 = (bf16[768,512]{1,0:T(8,128)(2,1)}, bf16[768,512]{1,0:T(8,128)(2,1)}, u32[]{:S(2)}, u32[]{:S(2)}) collective-permute-start(bf16[768,512]{1,0:T(8,128)(2,1)} %get-tuple-element.48), channel_id=1, source_target_pairs={{0,2},{2,4},{4,6},{6,0},{1,3},{3,5},{5,7},{7,1},{8,10},{10,12},{12... | collective-permute-start | bytes 2359304 | tf_op jit(solution)/shard_map/ppermute | solution.py:307
  35.0 4.9 %collective-permute-start.5 = (s32[4,2048]{1,0:T(4,128)S(1)}, s32[4,2048]{1,0:T(4,128)S(1)}, u32[]{:S(2)}, u32[]{:S(2)}) collective-permute-start(s32[4,2048]{1,0:T(4,128)S(1)} %pad_add_fusion), channel_id=1, source_target_pairs={{0,1},{1,0},{2,3},{3,2},{4,5},{5,4},{6,7},{7,6},{8,9},{9,8},{10,11... | collective-permute-start | bytes 98312 | tf_op jit(solution)/shard_map/ppermute | solution.py:336
  35.5 25.1 %all-to-all-start = ((bf16[4,256,512]{2,1,0:T(8,128)(2,1)}), bf16[4,256,512]{2,1,0:T(8,128)(2,1)}, u32[]{:S(2)}, u32[]{:S(2)}) async-start(bf16[4,256,512]{2,1,0:T(8,128)(2,1)} %get-tuple-element.53), calls=%async_computation | async-start | bytes 2097152 | tf_op jit(solution)/shard_map/all_to_all | solution.py:353
  56.0 4.6 %collective-permute-start.9 = (bf16[768,512]{1,0:T(8,128)(2,1)}, bf16[768,512]{1,0:T(8,128)(2,1)S(1)}, u32[]{:S(2)}, u32[]{:S(2)}) collective-permute-start(bf16[768,512]{1,0:T(8,128)(2,1)} %collective-permute-done.7.one.x2), channel_id=1, source_target_pairs={{0,1},{1,0},{2,3},{3,2},{4,5},{5,4},{6,7},{7,6},{8,9},{9,8},{10,11... | collective-permute-start | bytes 2359304 | tf_op jit(solution)/shard_map/ppermute | solution.py:336
  58.0 3.2 %collective-permute-start.10 = (bf16[768,512]{1,0:T(8,128)(2,1)}, bf16[768,512]{1,0:T(8,128)(2,1)S(1)}, u32[]{:S(2)}, u32[]{:S(2)}) collective-permute-start(bf16[768,512]{1,0:T(8,128)(2,1)} %collective-permute-done.8.three.x3), channel_id=1, source_target_pairs={{0,1},{1,0},{2,3},{3,2},{4,5},{5,4},{6,7},{7,6},{8,9},{9,8},{10,11... | collective-permute-start | bytes 2359304 | tf_op jit(solution)/shard_map/ppermute | solution.py:336
  58.0 16.4 %collective-permute-start.11 = (bf16[768,512]{1,0:T(8,128)(2,1)}, bf16[768,512]{1,0:T(8,128)(2,1)S(1)}, u32[]{:S(2)}, u32[]{:S(2)}) collective-permute-start(bf16[768,512]{1,0:T(8,128)(2,1)} %relay.1), channel_id=1, source_target_pairs={{0,62},{1,3},{2,0},{3,5},{4,2},{5,7},{6,4},{7,9},{8,6},{9,11},{10,... | collective-permute-start | bytes 2359304 | tf_op jit(solution)/shard_map/ppermute | solution.py:302
  62.1 17.0 %copy-start.2 = (bf16[768,512]{1,0:T(8,128)(2,1)S(1)}, bf16[768,512]{1,0:T(8,128)(2,1)}, u32[]{:S(2)}) copy-start(bf16[768,512]{1,0:T(8,128)(2,1)} %cot.5) | copy-start | bytes 2359300
  62.1 17.0 %copy-start.3 = (bf16[768,512]{1,0:T(8,128)(2,1)S(1)}, bf16[768,512]{1,0:T(8,128)(2,1)}, u32[]{:S(2)}) copy-start(bf16[768,512]{1,0:T(8,128)(2,1)} %feats.1) | copy-start | bytes 2359300
  74.3 4.7 %collective-permute-start.12 = (bf16[768,512]{1,0:T(8,128)(2,1)S(1)}, bf16[768,512]{1,0:T(8,128)(2,1)S(1)}, u32[]{:S(2)}, u32[]{:S(2)}) collective-permute-start(bf16[768,512]{1,0:T(8,128)(2,1)S(1)} %collective-permute-done.11.x0), channel_id=1, source_target_pairs={{0,1},{1,0},{2,3},{3,2},{4,5},{5,4},{6,7},{7,6},{8,9},{9,8},{10,11... | collective-permute-start | bytes 2359304 | tf_op jit(solution)/shard_map/ppermute | solution.py:336
  83.7 2.8 %collective-permute-start.13 = (f32[16,2,16,512]{3,2,1,0:T(8,128)S(1)}, f32[16,2,16,512]{3,2,1,0:T(8,128)S(1)}, u32[]{:S(2)}, u32[]{:S(2)}) collective-permute-start(f32[16,2,16,512]{3,2,1,0:T(8,128)S(1)} %get-tuple-element.57), channel_id=1, source_target_pairs={{0,1},{1,0},{2,3},{3,2},{4,5},{5,4},{6,7},{7,6},{8,9},{9,8},{10,11... | collective-permute-start | bytes 3145736 | tf_op jit(solution)/shard_map/ppermute | solution.py:336
  86.7 24.8 %copy-start.4 = (bf16[512,512]{1,0:T(8,128)(2,1)S(1)}, bf16[512,512]{1,0:T(8,128)(2,1)}, u32[]{:S(2)}) copy-start(bf16[512,512]{1,0:T(8,128)(2,1)} %w_self.1) | copy-start | bytes 1572868
  86.7 24.8 %copy-start.5 = (bf16[512,512]{1,0:T(8,128)(2,1)S(1)}, bf16[512,512]{1,0:T(8,128)(2,1)}, u32[]{:S(2)}) copy-start(bf16[512,512]{1,0:T(8,128)(2,1)} %w_neigh.1) | copy-start | bytes 1572868
  109.1 7.8 %collective-permute-start.14 = (f32[2,16,512]{2,1,0:T(8,128)S(1)}, f32[2,16,512]{2,1,0:T(8,128)S(1)}, u32[]{:S(2)}, u32[]{:S(2)}) collective-permute-start(f32[2,16,512]{2,1,0:T(8,128)S(1)} %reduce_sum.9), channel_id=1, source_target_pairs={{0,32},{8,40},{16,48},{24,56},{32,0},{40,8},{48,16},{56,24},{1,33}... | collective-permute-start | bytes 196616 | tf_op jit(solution)/shard_map/ppermute | solution.py:390
  116.9 5.1 %collective-permute-start.17 = (f32[2,16,512]{2,1,0:T(8,128)S(1)}, f32[2,16,512]{2,1,0:T(8,128)S(1)}, u32[]{:S(2)}, u32[]{:S(2)}) collective-permute-start(f32[2,16,512]{2,1,0:T(8,128)S(1)} %add.16), channel_id=1, source_target_pairs={{0,24},{8,16},{16,8},{24,0},{32,56},{40,48},{48,40},{56,32},{1,25}... | collective-permute-start | bytes 196616 | tf_op jit(solution)/shard_map/ppermute | solution.py:390
  118.2 5.2 %collective-permute-start.16 = (f32[2,16,512]{2,1,0:T(8,128)S(1)}, f32[2,16,512]{2,1,0:T(8,128)S(1)}, u32[]{:S(2)}, u32[]{:S(2)}) collective-permute-start(f32[2,16,512]{2,1,0:T(8,128)S(1)} %add.16), channel_id=1, source_target_pairs={{0,16},{8,24},{16,0},{24,8},{32,48},{40,56},{48,32},{56,40},{1,17}... | collective-permute-start | bytes 196616 | tf_op jit(solution)/shard_map/ppermute | solution.py:390
  118.2 5.2 %collective-permute-start.15 = (f32[2,16,512]{2,1,0:T(8,128)S(1)}, f32[2,16,512]{2,1,0:T(8,128)S(1)}, u32[]{:S(2)}, u32[]{:S(2)}) collective-permute-start(f32[2,16,512]{2,1,0:T(8,128)S(1)} %add.16), channel_id=1, source_target_pairs={{0,8},{8,0},{16,24},{24,16},{32,40},{40,32},{48,56},{56,48},{1,9},... | collective-permute-start | bytes 196616 | tf_op jit(solution)/shard_map/ppermute | solution.py:390
  137.2 7.2 %collective-permute-start.18 = (bf16[16,3,16,512]{3,2,1,0:T(8,128)(2,1)S(1)}, bf16[16,3,16,512]{3,2,1,0:T(8,128)(2,1)S(1)}, u32[]{:S(2)}, u32[]{:S(2)}) collective-permute-start(bf16[16,3,16,512]{3,2,1,0:T(8,128)(2,1)S(1)} %all_to_all.16.mine), channel_id=1, source_target_pairs={{0,1},{1,0},{2,3},{3,2},{4,5},{5,4},{6,7},{7,6},{8,9},{9,8},{10,11... | collective-permute-start | bytes 2359304 | tf_op jit(solution)/shard_map/ppermute | solution.py:336
  (5 other events, 20.8 us)

commit v8 on v6

--- a/solution.py
+++ b/solution.py
@@ -136,8 +136,8 @@
     for k, half in ((core, mine), (1 - core, theirs)):
         for n in range(pieces):
             at = pl.ds(pl.multiple_of((k * pieces + n) * size, size), size)
-            out_self[at, :] = half[n, 0] * factor
-            out_neigh[at, :] = half[n, 1] * factor
+            out_self[at, :] = half[n, 0].astype(F32) * factor
+            out_neigh[at, :] = (half[n, 1].astype(F32) + half[n, 2].astype(F32)) * factor
 
 
 def finish(summed, cot, w_self, w_neigh, out):
@@ -334,6 +334,7 @@
     mid = run_build(((pairs[1], 0), (other, 1)), nodes)
     one, three = fence((one, three, near, quad, mid, side))[:2]
     relay = jnp.where(core == 0, one, three)
+    one, three, relay = fence((one, three, relay))
 
     two = moved(
         relay,
@@ -364,6 +365,8 @@
     part = part + zflip(part, 4)
     part, total = fence((part, run_finish(summed, cotangent, w_self, w_neigh)))
     part = (part + zflip(part, 1)) + (zflip(part, 2) + zflip(part, 3))
+    top = lax.reduce_precision(part[1], 8, 7)
+    part = jnp.stack([part[0], top, part[1] - top]).astype(BF16)
     part = jnp.broadcast_to(part[None], (ngroup * ny,) + part.shape)
     part = lax.all_to_all(part, ("group", "y"), split_axis=0, concat_axis=0, tiled=True)
     held = (part, swapped(part))

time: 143 us -> 141 us (0.986)
  blocking collectives: 38.1 us -> 33.6 us
  starting transfers between devices: 33.8 us -> 36.9 us
    all_to_all x2, blocking collectives: 38.1 us -> 33.6 us  [on_device(): lax.all_to_all(part, ('group', 'y'), split_axis=0, concat_axis=0, tiled=T...]
    ppermute x7, starting transfers between devices: 9.15 us -> 11.9 us  [swapped(): return lax.ppermute(v, 'core', swap)]
    ppermute x4, waiting for transfers between devices: 8.94 us -> 6.76 us  [turned(): lax.ppermute(value, axis, [(i, (i + by) % length) for i in range(length)])]
    ppermute x7, waiting for transfers between devices: 7.14 us -> 8.81 us  [swapped(): return lax.ppermute(v, 'core', swap)]
  transfers between devices with their start and end apart: 20 -> 20, of which waited for: 14 -> 12; matrix products, arithmetic and copies ran while one was open for 2% -> 1% of each run, Pallas kernels for 21% -> 22%
where the time goes in v8:
time: 141 us; the launch traced here: 140 us
  starting transfers between devices  36.9 us (26%)
  Pallas kernels  35.3 us (25%)
  blocking collectives  33.6 us (24%)
  waiting for transfers between devices  24.9 us (18%)
  other arithmetic  5.42 us (4%)
  local copies, waits for them, and re-layouts  2.77 us (2%)
    all_to_all x2, blocking collectives, on_device(): lax.all_to_all(part, ('group', 'y'), split_axis=0, concat_axis=0, tiled=T...  33.6 us
    pallas_call x3, Pallas kernels, run_build(): pl.pallas_call(functools.partial(build, rows), grid=(slots,), in_specs=[w...  13.6 us
    ppermute x7, starting transfers between devices, swapped(): return lax.ppermute(v, 'core', swap)  11.9 us
    ppermute x4, starting transfers between devices, turned(): lax.ppermute(value, axis, [(i, (i + by) % length) for i in range(length)])  9.89 us
    pallas_call x1, Pallas kernels, run_most(): pl.pallas_call(most_sum, grid=(nodes // BLOCK,), in_specs=[tile_spec(s, n...  9.62 us
    ppermute x7, waiting for transfers between devices, swapped(): return lax.ppermute(v, 'core', swap)  8.81 us
    ppermute x4, waiting for transfers between devices, turned(): lax.ppermute(value, axis, [(i, (i + by) % length) for i in range(length)])  6.76 us
    ppermute x4, starting transfers between devices, zflip(): return lax.ppermute(v, 'z', [(i, i ^ k) for i in range(nz)])  6.37 us
  transfers between devices with their start and end apart: 20, of which 12 were waited for; matrix products, arithmetic and copies ran while one was open for 1% of the time, Pallas kernels for 22%

profile of v8, /device:TPU:1, one launch (start us, length us, event | category | flops | bytes accessed | tf_op | source)
XLA Modules:
  0.0 139.7 jit_solution(17426553116401336880)
XLA Ops:
  0.6 6.5 %collective-permute-start = (bf16[768,512]{1,0:T(8,128)(2,1)}, bf16[768,512]{1,0:T(8,128)(2,1)S(1)}, u32[]{:S(2)}, u32[]{:S(2)}) collective-permute-start(bf16[768,512]{1,0:T(8,128)(2,1)} %cot.5), channel_id=1, source_target_pairs={{0,56},{8,0},{16,8},{24,16},{32,24},{40,32},{48,40},{56,48},{1,57}... | collective-permute-start | bytes 2359304 | tf_op jit(solution)/shard_map/ppermute | solution.py:275
  7.1 4.6 %prepare.1 = (bf16[768,512]{1,0:T(8,128)(2,1)}, bf16[4,256,512]{2,1,0:T(8,128)(2,1)}, s32[1,2048]{1,0:T(1,128)}, s32[1,2048]{1,0:T(1,128)}, s32[2,2048]{1,0:T(2,...) custom-call(s32[1,8]{1,0:T(1,128)} %tcount.1, s32[1,4]{1,0:T(1,128)} %rcount.1, ...), custom_call_target="tpu_custom_call" | custom-call | flops 805306368 | bytes 854040 | tf_op jit(solution)/shard_map/prepare/pallas_call | solution.py:179
  12.5 3.2 %collective-permute-start.2 = (s32[2,2048]{1,0:T(2,128)}, s32[2,2048]{1,0:T(2,128)S(1)}, u32[]{:S(2)}, u32[]{:S(2)}) collective-permute-start(s32[2,2048]{1,0:T(2,128)} %get-tuple-element.33), channel_id=1, source_target_pairs={{0,62},{1,63},{2,0},{3,1},{4,2},{5,3},{6,4},{7,5},{8,6},{9,7},{10,... | collective-permute-start | bytes 49160 | tf_op jit(solution)/shard_map/ppermute | solution.py:270
  17.1 6.8 %collective-permute-done.1 = s32[2,2048]{1,0:T(2,128)S(1)} collective-permute-done((s32[2,2048]{1,0:T(2,128)}, s32[2,2048]{1,0:T(2,128)S(1)}, u32[]{:S(2)}, u32[]{:S(2)}) %collective-permute-start.1) | collective-permute-done | bytes 16416 | tf_op jit(solution)/shard_map/ppermute | solution.py:275
  25.0 2.8 %broadcast_select_fusion.1 = (bf16[768,512]{1,0:T(8,128)(2,1)}, bf16[768,512]{1,0:T(8,128)(2,1)}, bf16[768,512]{1,0:T(8,128)(2,1)}) fusion(bf16[768,512]{1,0:T(8,128)(2,1)} %get-tuple-element.41.x0, pred[]{:T(512)S(6)} %eq.15, bf16[768,512]{1,0:T(8,128)(2,1)S(1)} %collective-permute-done, f32[768]{0:T(1024)S(1)} %divide_reduce_fusion, pred[]{:T(512)S(6)} %eq.14, ...), kind=kLoop, calls=%fused_computation.2 | loop fusion | flops 2359296 | bytes 3935235 | tf_op jit(solution)/shard_map/jit(_where)/select_n | solution.py:328
  30.5 2.1 %collective-permute-start.6 = (bf16[768,512]{1,0:T(8,128)(2,1)}, bf16[768,512]{1,0:T(8,128)(2,1)S(1)}, u32[]{:S(2)}, u32[]{:S(2)}) collective-permute-start(bf16[768,512]{1,0:T(8,128)(2,1)} %get-tuple-element.59), channel_id=1, source_target_pairs={{0,1},{1,0},{2,3},{3,2},{4,5},{5,4},{6,7},{7,6},{8,9},{9,8},{10,11... | collective-permute-start | bytes 2359304 | tf_op jit(solution)/shard_map/ppermute | solution.py:304
  32.8 4.0 %all-to-all-start = ((bf16[4,256,512]{2,1,0:T(8,128)(2,1)}), bf16[4,256,512]{2,1,0:T(8,128)(2,1)S(1)}, u32[]{:S(2)}, u32[]{:S(2)}) async-start(bf16[4,256,512]{2,1,0:T(8,128)(2,1)} %get-tuple-element.47), calls=%async_computation | async-start | bytes 2097152 | tf_op jit(solution)/shard_map/all_to_all | solution.py:321
  37.5 4.3 %build.5.tiles = bf16[2,768,768]{2,1,0:T(8,128)(2,1)} custom-call(s32[2,2048]{1,0:T(2,128)} %copy-done.11, s32[4,2048]{1,0:T(4,128)} %copy-done.9), custom_call_target="tpu_custom_call" | custom-call | flops 3145728 | bytes 1572864 | tf_op jit(solution)/shard_map/build/pallas_call | solution.py:195
  41.7 5.6 %build.4.t2.t3.t4.t5 = bf16[4,768,768]{2,1,0:T(8,128)(2,1)} custom-call(s32[2,2048]{1,0:T(2,128)} %copy-done.10, s32[2,2048]{1,0:T(2,128)} %copy-done.12, s32[4,2048]{1,0:T(4,128)} %copy-done.9, s32[4,2048]{1,0:T(4,128)} %copy-done.9), custom_call_target="tpu_custom_call" | custom-call | flops 3145728 | bytes 1572864 | tf_op jit(solution)/shard_map/build/pallas_call | solution.py:195
  47.3 3.7 %build.3.t0.t1 = bf16[2,768,768]{2,1,0:T(8,128)(2,1)} custom-call(s32[1,2048]{1,0:T(1,128)} %get-tuple-element.30.refs_0_, s32[4,2048]{1,0:T(4,128)} %copy-done.9), custom_call_target="tpu_custom_call" | custom-call | flops 3145728 | bytes 1572864 | tf_op jit(solution)/shard_map/build/pallas_call | solution.py:195
  54.5 2.7 %collective-permute-done.9.x4 = bf16[768,512]{1,0:T(8,128)(2,1)} collective-permute-done((bf16[768,512]{1,0:T(8,128)(2,1)}, bf16[768,512]{1,0:T(8,128)(2,1)}, u32[]{:S(2)}, u32[]{:S(2)}) %collective-permute-start.9) | collective-permute-done | bytes 786464 | tf_op jit(solution)/shard_map/ppermute | solution.py:304
  57.3 9.6 %most_sum.1.before = f32[768,512]{1,0:T(8,128)} custom-call(bf16[2,768,768]{2,1,0:T(8,128)(2,1)} %build.3.t0.t1, bf16[2,768,768]{2,1,0:T(8,128)(2,1)} %build.3.t0.t1, bf16[4,768,768]{2,1,0:T(8,128)(2,1)} %build.4.t2.t3.t4.t5, bf16[4,768,768]{2,1,0:T(8,128)(2,1)} %build.4.t2.t3.t4.t5, bf16[4,768,768]{2,1,0:T(8,128)(2,1)} %build.4.t2.t3.t4.t5, ...), custom_call_target="tpu_custom_call" | custom-call | flops 4227858432 | bytes 6291456 | tf_op jit(solution)/shard_map/most_sum/pallas_call | solution.py:210
  66.9 2.9 %collective-permute-done.11.x0 = bf16[768,512]{1,0:T(8,128)(2,1)S(1)} collective-permute-done((bf16[768,512]{1,0:T(8,128)(2,1)}, bf16[768,512]{1,0:T(8,128)(2,1)S(1)}, u32[]{:S(2)}, u32[]{:S(2)}) %collective-permute-start.11) | collective-permute-done | bytes 786464 | tf_op jit(solution)/shard_map/ppermute | solution.py:270
  69.8 2.5 %collective-permute-start.12 = (bf16[768,512]{1,0:T(8,128)(2,1)S(1)}, bf16[768,512]{1,0:T(8,128)(2,1)S(1)}, u32[]{:S(2)}, u32[]{:S(2)}) collective-permute-start(bf16[768,512]{1,0:T(8,128)(2,1)S(1)} %collective-permute-done.11.x0), channel_id=1, source_target_pairs={{0,1},{1,0},{2,3},{3,2},{4,5},{5,4},{6,7},{7,6},{8,9},{9,8},{10,11... | collective-permute-start | bytes 2359304 | tf_op jit(solution)/shard_map/ppermute | solution.py:304
  72.2 1.9 %collective-permute-done.12.x1 = bf16[768,512]{1,0:T(8,128)(2,1)S(1)} collective-permute-done((bf16[768,512]{1,0:T(8,128)(2,1)S(1)}, bf16[768,512]{1,0:T(8,128)(2,1)S(1)}, u32[]{:S(2)}, u32[]{:S(2)}) %collective-permute-start.12) | collective-permute-done | bytes 786464 | tf_op jit(solution)/shard_map/ppermute | solution.py:304
  75.6 3.2 %last_sum.1 = (f32[768,512]{1,0:T(8,128)S(1)}, f32[16,2,16,512]{3,2,1,0:T(8,128)S(1)}, f32[16,2,16,512]{3,2,1,0:T(8,128)S(1)}) custom-call(f32[768,512]{1,0:T(8,128)S(1)} %copy-done.1, bf16[2,768,768]{2,1,0:T(8,128)(2,1)S(1)} %copy-done, bf16[768,512]{1,0:T(8,128)(2,1)S(1)} %collective-permute-done.11.x0, bf16[768,512]{1,0:T(8,128)(2,1)S(1)} %collective-permute-done.12.x1, ...), custom_call_target="tpu_custom_call" | custom-call | flops 1811939328 | bytes 6291456 | tf_op jit(solution)/shard_map/last_sum/pallas_call | solution.py:227
  79.2 2.3 %collective-permute-done.13 = f32[16,2,16,512]{3,2,1,0:T(8,128)S(1)} collective-permute-done((f32[16,2,16,512]{3,2,1,0:T(8,128)S(1)}, f32[16,2,16,512]{3,2,1,0:T(8,128)S(1)}, u32[]{:S(2)}, u32[]{:S(2)}) %collective-permute-start.13) | collective-permute-done | bytes 1048608 | tf_op jit(solution)/shard_map/ppermute | solution.py:304
  81.7 19.3 %all_to_all.15 = f32[16,2,16,512]{3,2,1,0:T(8,128)} all-to-all(f32[16,2,16,512]{3,2,1,0:T(8,128)S(1)} %add.15), channel_id=1, replica_groups=mesh['group'=4,'z'=8,'y'=4,'core'=2] {'group','y'}, dimensions={0} | all-to-all | bytes 2097152 | tf_op jit(solution)/shard_map/all_to_all | solution.py:360
  102.3 2.6 %collective-permute-start.14 = (f32[2,16,512]{2,1,0:T(8,128)S(1)}, f32[2,16,512]{2,1,0:T(8,128)S(1)}, u32[]{:S(2)}, u32[]{:S(2)}) collective-permute-start(f32[2,16,512]{2,1,0:T(8,128)S(1)} %reduce_sum.9), channel_id=1, source_target_pairs={{0,32},{8,40},{16,48},{24,56},{32,0},{40,8},{48,16},{56,24},{1,33}... | collective-permute-start | bytes 196616 | tf_op jit(solution)/shard_map/ppermute | solution.py:363
  104.9 2.8 %finish.1 = f32[768,512]{1,0:T(8,128)} custom-call(f32[768,512]{1,0:T(8,128)S(1)} %get-tuple-element.52.summed, bf16[768,512]{1,0:T(8,128)(2,1)S(1)} %copy-done.2, bf16[512,512]{1,0:T(8,128)(2,1)S(1)} %copy-done.4, bf16[512,512]{1,0:T(8,128)(2,1)S(1)} %copy-done.5), custom_call_target="tpu_custom_call" | custom-call | flops 1207959552 | bytes 3932160 | tf_op jit(solution)/shard_map/finish/pallas_call | solution.py:254
  109.5 3.4 %collective-permute-start.17 = (f32[2,16,512]{2,1,0:T(8,128)S(1)}, f32[2,16,512]{2,1,0:T(8,128)S(1)}, u32[]{:S(2)}, u32[]{:S(2)}) collective-permute-start(f32[2,16,512]{2,1,0:T(8,128)S(1)} %add.16), channel_id=1, source_target_pairs={{0,24},{8,16},{16,8},{24,0},{32,56},{40,48},{48,40},{56,32},{1,25}... | collective-permute-start | bytes 196616 | tf_op jit(solution)/shard_map/ppermute | solution.py:363
  114.6 2.3 %collective-permute-done.16 = f32[2,16,512]{2,1,0:T(8,128)S(1)} collective-permute-done((f32[2,16,512]{2,1,0:T(8,128)S(1)}, f32[2,16,512]{2,1,0:T(8,128)S(1)}, u32[]{:S(2)}, u32[]{:S(2)}) %collective-permute-start.16) | collective-permute-done | bytes 65568 | tf_op jit(solution)/shard_map/ppermute | solution.py:363
  117.1 14.3 %all_to_all.16.mine = bf16[16,3,16,512]{3,2,1,0:T(8,128)(2,1)S(1)} all-to-all(bf16[16,3,16,512]{3,2,1,0:T(8,128)(2,1)S(1)} %broadcast_in_dim.2), channel_id=1, replica_groups=mesh['group'=4,'z'=8,'y'=4,'core'=2] {'group','y'}, dimensions={0} | all-to-all | bytes 1572864 | tf_op jit(solution)/shard_map/all_to_all | solution.py:371
  131.3 5.0 %collective-permute-start.18 = (bf16[16,3,16,512]{3,2,1,0:T(8,128)(2,1)S(1)}, bf16[16,3,16,512]{3,2,1,0:T(8,128)(2,1)S(1)}, u32[]{:S(2)}, u32[]{:S(2)}) collective-permute-start(bf16[16,3,16,512]{3,2,1,0:T(8,128)(2,1)S(1)} %all_to_all.16.mine), channel_id=1, source_target_pairs={{0,1},{1,0},{2,3},{3,2},{4,5},{5,4},{6,7},{7,6},{8,9},{9,8},{10,11... | collective-permute-start | bytes 2359304 | tf_op jit(solution)/shard_map/ppermute | solution.py:304
  (73 shorter events, 20.6 us)
Async XLA Ops:
  0.6 24.3 %collective-permute-start = (bf16[768,512]{1,0:T(8,128)(2,1)}, bf16[768,512]{1,0:T(8,128)(2,1)S(1)}, u32[]{:S(2)}, u32[]{:S(2)}) collective-permute-start(bf16[768,512]{1,0:T(8,128)(2,1)} %cot.5), channel_id=1, source_target_pairs={{0,56},{8,0},{16,8},{24,16},{32,24},{40,32},{48,40},{56,48},{1,57}... | collective-permute-start | bytes 2359304 | tf_op jit(solution)/shard_map/ppermute | solution.py:275
  11.7 12.1 %collective-permute-start.1 = (s32[2,2048]{1,0:T(2,128)}, s32[2,2048]{1,0:T(2,128)S(1)}, u32[]{:S(2)}, u32[]{:S(2)}) collective-permute-start(s32[2,2048]{1,0:T(2,128)} %get-tuple-element.32), channel_id=1, source_target_pairs={{0,56},{8,0},{16,8},{24,16},{32,24},{40,32},{48,40},{56,48},{1,57}... | collective-permute-start | bytes 49160 | tf_op jit(solution)/shard_map/ppermute | solution.py:275
  12.5 11.8 %collective-permute-start.2 = (s32[2,2048]{1,0:T(2,128)}, s32[2,2048]{1,0:T(2,128)S(1)}, u32[]{:S(2)}, u32[]{:S(2)}) collective-permute-start(s32[2,2048]{1,0:T(2,128)} %get-tuple-element.33), channel_id=1, source_target_pairs={{0,62},{1,63},{2,0},{3,1},{4,2},{5,3},{6,4},{7,5},{8,6},{9,7},{10,... | collective-permute-start | bytes 49160 | tf_op jit(solution)/shard_map/ppermute | solution.py:270
  15.6 8.9 %collective-permute-start.3 = (s32[2,2048]{1,0:T(2,128)}, s32[2,2048]{1,0:T(2,128)S(1)}, u32[]{:S(2)}, u32[]{:S(2)}) collective-permute-start(s32[2,2048]{1,0:T(2,128)} %get-tuple-element.34), channel_id=1, source_target_pairs={{0,60},{1,61},{2,62},{3,63},{4,0},{5,1},{6,2},{7,3},{8,4},{9,5},{1... | collective-permute-start | bytes 49160 | tf_op jit(solution)/shard_map/ppermute | solution.py:270
  16.0 8.9 %collective-permute-start.4 = (s32[2,2048]{1,0:T(2,128)}, s32[2,2048]{1,0:T(2,128)S(1)}, u32[]{:S(2)}, u32[]{:S(2)}) collective-permute-start(s32[2,2048]{1,0:T(2,128)} %get-tuple-element.35), channel_id=1, source_target_pairs={{0,58},{1,59},{2,60},{3,61},{4,62},{5,63},{6,0},{7,1},{8,2},{9,3},... | collective-permute-start | bytes 49160 | tf_op jit(solution)/shard_map/ppermute | solution.py:270
  27.8 23.3 %collective-permute-start.8 = (bf16[768,512]{1,0:T(8,128)(2,1)}, bf16[768,512]{1,0:T(8,128)(2,1)S(1)}, u32[]{:S(2)}, u32[]{:S(2)}) collective-permute-start(bf16[768,512]{1,0:T(8,128)(2,1)} %get-tuple-element.57), channel_id=1, source_target_pairs={{0,2},{2,4},{4,6},{6,0},{1,3},{3,5},{5,7},{7,1},{8,10},{10,12},{12... | collective-permute-start | bytes 2359304 | tf_op jit(solution)/shard_map/ppermute | solution.py:275
  28.7 22.3 %collective-permute-start.7 = (bf16[768,512]{1,0:T(8,128)(2,1)}, bf16[768,512]{1,0:T(8,128)(2,1)}, u32[]{:S(2)}, u32[]{:S(2)}) collective-permute-start(bf16[768,512]{1,0:T(8,128)(2,1)} %get-tuple-element.58), channel_id=1, source_target_pairs={{0,6},{2,0},{4,2},{6,4},{1,7},{3,1},{5,3},{7,5},{8,14},{10,8},{12,... | collective-permute-start | bytes 2359304 | tf_op jit(solution)/shard_map/ppermute | solution.py:275
  30.5 20.6 %collective-permute-start.6 = (bf16[768,512]{1,0:T(8,128)(2,1)}, bf16[768,512]{1,0:T(8,128)(2,1)S(1)}, u32[]{:S(2)}, u32[]{:S(2)}) collective-permute-start(bf16[768,512]{1,0:T(8,128)(2,1)} %get-tuple-element.59), channel_id=1, source_target_pairs={{0,1},{1,0},{2,3},{3,2},{4,5},{5,4},{6,7},{7,6},{8,9},{9,8},{10,11... | collective-permute-start | bytes 2359304 | tf_op jit(solution)/shard_map/ppermute | solution.py:304
  32.7 4.1 %collective-permute-start.5 = (s32[4,2048]{1,0:T(4,128)S(1)}, s32[4,2048]{1,0:T(4,128)S(1)}, u32[]{:S(2)}, u32[]{:S(2)}) collective-permute-start(s32[4,2048]{1,0:T(4,128)S(1)} %pad_add_fusion), channel_id=1, source_target_pairs={{0,1},{1,0},{2,3},{3,2},{4,5},{5,4},{6,7},{7,6},{8,9},{9,8},{10,11... | collective-permute-start | bytes 98312 | tf_op jit(solution)/shard_map/ppermute | solution.py:304
  32.8 21.7 %all-to-all-start = ((bf16[4,256,512]{2,1,0:T(8,128)(2,1)}), bf16[4,256,512]{2,1,0:T(8,128)(2,1)S(1)}, u32[]{:S(2)}, u32[]{:S(2)}) async-start(bf16[4,256,512]{2,1,0:T(8,128)(2,1)} %get-tuple-element.47), calls=%async_computation | async-start | bytes 2097152 | tf_op jit(solution)/shard_map/all_to_all | solution.py:321
  52.1 5.1 %collective-permute-start.9 = (bf16[768,512]{1,0:T(8,128)(2,1)}, bf16[768,512]{1,0:T(8,128)(2,1)}, u32[]{:S(2)}, u32[]{:S(2)}) collective-permute-start(bf16[768,512]{1,0:T(8,128)(2,1)} %collective-permute-done.7.x2), channel_id=1, source_target_pairs={{0,1},{1,0},{2,3},{3,2},{4,5},{5,4},{6,7},{7,6},{8,9},{9,8},{10,11... | collective-permute-start | bytes 2359304 | tf_op jit(solution)/shard_map/ppermute | solution.py:304
  53.9 3.3 %collective-permute-start.10 = (bf16[768,512]{1,0:T(8,128)(2,1)S(1)}, bf16[768,512]{1,0:T(8,128)(2,1)}, u32[]{:S(2)}, u32[]{:S(2)}) collective-permute-start(bf16[768,512]{1,0:T(8,128)(2,1)S(1)} %collective-permute-done.8.x3), channel_id=1, source_target_pairs={{0,1},{1,0},{2,3},{3,2},{4,5},{5,4},{6,7},{7,6},{8,9},{9,8},{10,11... | collective-permute-start | bytes 2359304 | tf_op jit(solution)/shard_map/ppermute | solution.py:304
  53.9 15.8 %collective-permute-start.11 = (bf16[768,512]{1,0:T(8,128)(2,1)}, bf16[768,512]{1,0:T(8,128)(2,1)S(1)}, u32[]{:S(2)}, u32[]{:S(2)}) collective-permute-start(bf16[768,512]{1,0:T(8,128)(2,1)} %broadcast_select_fusion), channel_id=1, source_target_pairs={{0,62},{1,3},{2,0},{3,5},{4,2},{5,7},{6,4},{7,9},{8,6},{9,11},{10,... | collective-permute-start | bytes 2359304 | tf_op jit(solution)/shard_map/ppermute | solution.py:270
  57.2 16.9 %copy-start = (bf16[2,768,768]{2,1,0:T(8,128)(2,1)S(1)}, bf16[2,768,768]{2,1,0:T(8,128)(2,1)}, u32[]{:S(2)}) copy-start(bf16[2,768,768]{2,1,0:T(8,128)(2,1)} %build.5.tiles) | copy-start | bytes 7077892
  57.2 16.9 %copy-start.2 = (bf16[768,512]{1,0:T(8,128)(2,1)S(1)}, bf16[768,512]{1,0:T(8,128)(2,1)}, u32[]{:S(2)}) copy-start(bf16[768,512]{1,0:T(8,128)(2,1)} %cot.5) | copy-start | bytes 2359300
  69.8 4.4 %collective-permute-start.12 = (bf16[768,512]{1,0:T(8,128)(2,1)S(1)}, bf16[768,512]{1,0:T(8,128)(2,1)S(1)}, u32[]{:S(2)}, u32[]{:S(2)}) collective-permute-start(bf16[768,512]{1,0:T(8,128)(2,1)S(1)} %collective-permute-done.11.x0), channel_id=1, source_target_pairs={{0,1},{1,0},{2,3},{3,2},{4,5},{5,4},{6,7},{7,6},{8,9},{9,8},{10,11... | collective-permute-start | bytes 2359304 | tf_op jit(solution)/shard_map/ppermute | solution.py:304
  78.8 2.8 %collective-permute-start.13 = (f32[16,2,16,512]{3,2,1,0:T(8,128)S(1)}, f32[16,2,16,512]{3,2,1,0:T(8,128)S(1)}, u32[]{:S(2)}, u32[]{:S(2)}) collective-permute-start(f32[16,2,16,512]{3,2,1,0:T(8,128)S(1)} %get-tuple-element.51), channel_id=1, source_target_pairs={{0,1},{1,0},{2,3},{3,2},{4,5},{5,4},{6,7},{7,6},{8,9},{9,8},{10,11... | collective-permute-start | bytes 3145736 | tf_op jit(solution)/shard_map/ppermute | solution.py:304
  81.7 23.2 %copy-start.4 = (bf16[512,512]{1,0:T(8,128)(2,1)S(1)}, bf16[512,512]{1,0:T(8,128)(2,1)}, u32[]{:S(2)}) copy-start(bf16[512,512]{1,0:T(8,128)(2,1)} %w_self.1) | copy-start | bytes 1572868
  81.7 23.2 %copy-start.5 = (bf16[512,512]{1,0:T(8,128)(2,1)S(1)}, bf16[512,512]{1,0:T(8,128)(2,1)}, u32[]{:S(2)}) copy-start(bf16[512,512]{1,0:T(8,128)(2,1)} %w_neigh.1) | copy-start | bytes 1572868
  102.3 7.1 %collective-permute-start.14 = (f32[2,16,512]{2,1,0:T(8,128)S(1)}, f32[2,16,512]{2,1,0:T(8,128)S(1)}, u32[]{:S(2)}, u32[]{:S(2)}) collective-permute-start(f32[2,16,512]{2,1,0:T(8,128)S(1)} %reduce_sum.9), channel_id=1, source_target_pairs={{0,32},{8,40},{16,48},{24,56},{32,0},{40,8},{48,16},{56,24},{1,33}... | collective-permute-start | bytes 196616 | tf_op jit(solution)/shard_map/ppermute | solution.py:363
  109.5 5.1 %collective-permute-start.17 = (f32[2,16,512]{2,1,0:T(8,128)S(1)}, f32[2,16,512]{2,1,0:T(8,128)S(1)}, u32[]{:S(2)}, u32[]{:S(2)}) collective-permute-start(f32[2,16,512]{2,1,0:T(8,128)S(1)} %add.16), channel_id=1, source_target_pairs={{0,24},{8,16},{16,8},{24,0},{32,56},{40,48},{48,40},{56,32},{1,25}... | collective-permute-start | bytes 196616 | tf_op jit(solution)/shard_map/ppermute | solution.py:363
  112.9 4.0 %collective-permute-start.16 = (f32[2,16,512]{2,1,0:T(8,128)S(1)}, f32[2,16,512]{2,1,0:T(8,128)S(1)}, u32[]{:S(2)}, u32[]{:S(2)}) collective-permute-start(f32[2,16,512]{2,1,0:T(8,128)S(1)} %add.16), channel_id=1, source_target_pairs={{0,16},{8,24},{16,0},{24,8},{32,48},{40,56},{48,32},{56,40},{1,17}... | collective-permute-start | bytes 196616 | tf_op jit(solution)/shard_map/ppermute | solution.py:363
  112.9 4.0 %collective-permute-start.15 = (f32[2,16,512]{2,1,0:T(8,128)S(1)}, f32[2,16,512]{2,1,0:T(8,128)S(1)}, u32[]{:S(2)}, u32[]{:S(2)}) collective-permute-start(f32[2,16,512]{2,1,0:T(8,128)S(1)} %add.16), channel_id=1, source_target_pairs={{0,8},{8,0},{16,24},{24,16},{32,40},{40,32},{48,56},{56,48},{1,9},... | collective-permute-start | bytes 196616 | tf_op jit(solution)/shard_map/ppermute | solution.py:363
  131.3 6.9 %collective-permute-start.18 = (bf16[16,3,16,512]{3,2,1,0:T(8,128)(2,1)S(1)}, bf16[16,3,16,512]{3,2,1,0:T(8,128)(2,1)S(1)}, u32[]{:S(2)}, u32[]{:S(2)}) collective-permute-start(bf16[16,3,16,512]{3,2,1,0:T(8,128)(2,1)S(1)} %all_to_all.16.mine), channel_id=1, source_target_pairs={{0,1},{1,0},{2,3},{3,2},{4,5},{5,4},{6,7},{7,6},{8,9},{9,8},{10,11... | collective-permute-start | bytes 2359304 | tf_op jit(solution)/shard_map/ppermute | solution.py:304
  (11 other events, 65.2 us)

commit v9 on v8

--- a/solution.py
+++ b/solution.py
@@ -87,8 +87,13 @@
             edges[k] = lists[k][row : row + 1, :]
 
     live = jnp.sum((edges[s] >= 0).astype(I32))
+
+    @pl.when(live == 0)
+    def _():
+        tile_out[0] = jnp.zeros((nodes, nodes), BF16)
+
     for low in range(0, ept, CHUNK):
-        @pl.when((live <= low + CHUNK) & ((live > low) | (low == 0)))
+        @pl.when((live <= low + CHUNK) & (live > low))
         def _():
             packed = edges[s, :, : low + CHUNK]
             tile = dot(small_hot(nodes, packed >> 10), small_hot(nodes, packed & 1023), ALONG)
@@ -205,19 +210,19 @@
     )(*lists)
 
 
-def run_most(near, quad, xs, ids, rows):
+def run_most(near, five, xs, ids, rows):
     nodes, width = xs[0].shape
     return pl.pallas_call(
         most_sum,
         grid=(nodes // BLOCK,),
-        in_specs=[tile_spec(s, nodes) for s in (0, 1, 0, 1, 2, 3)]
+        in_specs=[tile_spec(s, nodes) for s in (0, 0, 1, 2, 3, 4)]
         + [whole(v.shape) for v in (*xs, ids, rows)],
         out_specs=row_spec(width),
         out_shape=jax.ShapeDtypeStruct((nodes, width), F32),
         compiler_params=params(56),
         cost_estimate=estimate(7 * nodes * nodes * width, 16 * nodes * width),
         name="most_sum",
-    )(near, near, quad, quad, quad, quad, *xs, ids, rows)
+    )(near, *([five] * 5), *xs, ids, rows)
 
 
 def run_last(before, tiles, xs, features, cotangent, pieces):
@@ -319,7 +324,8 @@
         for j, p in ((1, pair1), (2, pair2), (3, pair3))
     ]
     returned = lax.all_to_all(rows, "group", split_axis=0, concat_axis=0, tiled=True)
-    x, far, deep, pairs = fence((x, far, deep, pairs))
+    near = run_build(((own, 0),), nodes)
+    x, far, deep, pairs = fence((x, far, deep, pairs, near))[:4]
     degree = deep[1, :nodes].astype(F32)
     inverse = 1.0 / jnp.maximum(degree, 1.0)
     far = (inverse[:, None] * far.astype(F32)).astype(BF16)
@@ -329,10 +335,11 @@
     side = swapped(jnp.where(core == 1, x, far))
     beside = jnp.where(core == 1, beside, deep[0:1])
     other = swapped(jnp.concatenate([p[1:2] for p in pairs] + [beside], axis=0))
-    near = run_build(((own, 0), (other, 3)), nodes)
-    quad = run_build(((pairs[0], 0), (pairs[2], 0), (other, 0), (other, 2)), nodes)
+    five = run_build(
+        ((other, 3), (pairs[0], 0), (pairs[2], 0), (other, 0), (other, 2)), nodes
+    )
     mid = run_build(((pairs[1], 0), (other, 1)), nodes)
-    one, three = fence((one, three, near, quad, mid, side))[:2]
+    one, three = fence((one, three, five, mid, side))[:2]
     relay = jnp.where(core == 0, one, three)
     one, three, relay = fence((one, three, relay))
 
@@ -344,7 +351,7 @@
     three_b = swapped(three)
     summed = run_most(
         near,
-        quad,
+        five,
         (x, side, one, three, one_b, three_b),
         send_ids.reshape(1, ngroup * cap),
         returned.reshape(ngroup * cap, width),

time: 141 us -> 137 us (0.972)
  waiting for transfers between devices: 24.9 us -> 20.2 us
  starting transfers between devices: 36.9 us -> 40.6 us
  Pallas kernels: 35.3 us -> 33.6 us
    ppermute x7, starting transfers between devices: 11.9 us -> 15.2 us  [swapped(): return lax.ppermute(v, 'core', swap)]
    ppermute x4, waiting for transfers between devices: 6.76 us -> 3.97 us  [turned(): lax.ppermute(value, axis, [(i, (i + by) % length) for i in range(length)])]
    pallas_call x3, Pallas kernels: 13.6 us -> 11.8 us  [run_build(): pl.pallas_call(functools.partial(build, rows), grid=(slots,), in_specs=[w...]
  transfers between devices with their start and end apart: 20 -> 20, of which waited for: 12 -> 12; matrix products, arithmetic and copies ran while one was open for 1% -> 1% of each run, Pallas kernels for 22% -> 21%
where the time goes in v9:
time: 137 us
  starting transfers between devices  40.6 us (30%)
  blocking collectives  34.7 us (25%)
  Pallas kernels  33.6 us (25%)
  waiting for transfers between devices  20.2 us (15%)
  other arithmetic  4.27 us (3%)
  local copies, waits for them, and re-layouts  2.79 us (2%)
    all_to_all x2, blocking collectives, on_device(): lax.all_to_all(part, ('group', 'y'), split_axis=0, concat_axis=0, tiled=T...  34.7 us
    ppermute x7, starting transfers between devices, swapped(): return lax.ppermute(v, 'core', swap)  15.2 us
    pallas_call x3, Pallas kernels, run_build(): pl.pallas_call(functools.partial(build, rows), grid=(slots,), in_specs=[w...  11.8 us
    ppermute x4, starting transfers between devices, turned(): lax.ppermute(value, axis, [(i, (i + by) % length) for i in range(length)])  9.96 us
    pallas_call x1, Pallas kernels, run_most(): pl.pallas_call(most_sum, grid=(nodes // BLOCK,), in_specs=[tile_spec(s, n...  9.62 us
    ppermute x7, waiting for transfers between devices, swapped(): return lax.ppermute(v, 'core', swap)  8.33 us
    ppermute x4, starting transfers between devices, zflip(): return lax.ppermute(v, 'z', [(i, i ^ k) for i in range(nz)])  6.32 us
    ppermute x4, starting transfers between devices, moved(): return lax.ppermute(value, BLK, perm)  5.15 us
  transfers between devices with their start and end apart: 20, of which 12 were waited for; matrix products, arithmetic and copies ran while one was open for 1% of the time, Pallas kernels for 21%

profile of v9, /device:TPU:1, one launch (start us, length us, event | category | flops | bytes accessed | tf_op | source)
XLA Modules:
  0.0 137.0 jit_solution(1247530262369500867)
XLA Ops:
  0.6 6.5 %collective-permute-start = (bf16[768,512]{1,0:T(8,128)(2,1)}, bf16[768,512]{1,0:T(8,128)(2,1)S(1)}, u32[]{:S(2)}, u32[]{:S(2)}) collective-permute-start(bf16[768,512]{1,0:T(8,128)(2,1)} %cot.5), channel_id=1, source_target_pairs={{0,56},{8,0},{16,8},{24,16},{32,24},{40,32},{48,40},{56,48},{1,57}... | collective-permute-start | bytes 2359304 | tf_op jit(solution)/shard_map/ppermute | solution.py:280
  7.1 4.6 %prepare.1 = (bf16[768,512]{1,0:T(8,128)(2,1)}, bf16[4,256,512]{2,1,0:T(8,128)(2,1)}, s32[1,2048]{1,0:T(1,128)}, s32[1,2048]{1,0:T(1,128)}, s32[2,2048]{1,0:T(2,...) custom-call(s32[1,8]{1,0:T(1,128)} %tcount.1, s32[1,4]{1,0:T(1,128)} %rcount.1, ...), custom_call_target="tpu_custom_call" | custom-call | flops 805306368 | bytes 854040 | tf_op jit(solution)/shard_map/prepare/pallas_call | solution.py:184
  12.5 3.2 %collective-permute-start.2 = (s32[2,2048]{1,0:T(2,128)}, s32[2,2048]{1,0:T(2,128)S(1)}, u32[]{:S(2)}, u32[]{:S(2)}) collective-permute-start(s32[2,2048]{1,0:T(2,128)} %get-tuple-element.33), channel_id=1, source_target_pairs={{0,62},{1,63},{2,0},{3,1},{4,2},{5,3},{6,4},{7,5},{8,6},{9,7},{10,... | collective-permute-start | bytes 49160 | tf_op jit(solution)/shard_map/ppermute | solution.py:275
  17.2 2.7 %build.3.t0 = bf16[1,768,768]{2,1,0:T(8,128)(2,1)} custom-call(s32[1,2048]{1,0:T(1,128)} %get-tuple-element.30.refs_0_), custom_call_target="tpu_custom_call" | custom-call | flops 3145728 | bytes 1572864 | tf_op jit(solution)/shard_map/build/pallas_call | solution.py:200
  19.9 4.0 %collective-permute-done.1 = s32[2,2048]{1,0:T(2,128)S(1)} collective-permute-done((s32[2,2048]{1,0:T(2,128)}, s32[2,2048]{1,0:T(2,128)S(1)}, u32[]{:S(2)}, u32[]{:S(2)}) %collective-permute-start.1) | collective-permute-done | bytes 16416 | tf_op jit(solution)/shard_map/ppermute | solution.py:280
  29.3 2.1 %collective-permute-start.6 = (bf16[768,512]{1,0:T(8,128)(2,1)}, bf16[768,512]{1,0:T(8,128)(2,1)S(1)}, u32[]{:S(2)}, u32[]{:S(2)}) collective-permute-start(bf16[768,512]{1,0:T(8,128)(2,1)} %get-tuple-element.59), channel_id=1, source_target_pairs={{0,1},{1,0},{2,3},{3,2},{4,5},{5,4},{6,7},{7,6},{8,9},{9,8},{10,11... | collective-permute-start | bytes 2359304 | tf_op jit(solution)/shard_map/ppermute | solution.py:309
  31.9 4.0 %all-to-all-start = ((bf16[4,256,512]{2,1,0:T(8,128)(2,1)}), bf16[4,256,512]{2,1,0:T(8,128)(2,1)S(1)}, u32[]{:S(2)}, u32[]{:S(2)}) async-start(bf16[4,256,512]{2,1,0:T(8,128)(2,1)} %get-tuple-element.47), calls=%async_computation | async-start | bytes 2097152 | tf_op jit(solution)/shard_map/all_to_all | solution.py:326
  36.5 2.9 %build.5.tiles = bf16[2,768,768]{2,1,0:T(8,128)(2,1)} custom-call(s32[2,2048]{1,0:T(2,128)} %copy-done.12, s32[4,2048]{1,0:T(4,128)} %copy-done.10), custom_call_target="tpu_custom_call" | custom-call | flops 3145728 | bytes 1572864 | tf_op jit(solution)/shard_map/build/pallas_call | solution.py:200
  39.4 6.2 %build.4.t1.t2.t3.t4.t5 = bf16[5,768,768]{2,1,0:T(8,128)(2,1)} custom-call(s32[4,2048]{1,0:T(4,128)} %copy-done.10, s32[2,2048]{1,0:T(2,128)} %copy-done.11, s32[2,2048]{1,0:T(2,128)} %copy-done.13, s32[4,2048]{1,0:T(4,128)} %copy-done.10, s32[4,2048]{1,0:T(4,128)} %copy-done.10), custom_call_target="tpu_custom_call" | custom-call | flops 3145728 | bytes 1572864 | tf_op jit(solution)/shard_map/build/pallas_call | solution.py:200
  46.7 4.1 %collective-permute-start.9 = (bf16[768,512]{1,0:T(8,128)(2,1)}, bf16[768,512]{1,0:T(8,128)(2,1)}, u32[]{:S(2)}, u32[]{:S(2)}) collective-permute-start(bf16[768,512]{1,0:T(8,128)(2,1)} %collective-permute-done.7.x2), channel_id=1, source_target_pairs={{0,1},{1,0},{2,3},{3,2},{4,5},{5,4},{6,7},{7,6},{8,9},{9,8},{10,11... | collective-permute-start | bytes 2359304 | tf_op jit(solution)/shard_map/ppermute | solution.py:309
  51.8 2.2 %collective-permute-done.9.x4 = bf16[768,512]{1,0:T(8,128)(2,1)} collective-permute-done((bf16[768,512]{1,0:T(8,128)(2,1)}, bf16[768,512]{1,0:T(8,128)(2,1)}, u32[]{:S(2)}, u32[]{:S(2)}) %collective-permute-start.9) | collective-permute-done | bytes 786464 | tf_op jit(solution)/shard_map/ppermute | solution.py:309
  54.1 9.6 %most_sum.1.before = f32[768,512]{1,0:T(8,128)} custom-call(bf16[1,768,768]{2,1,0:T(8,128)(2,1)} %build.3.t0, bf16[5,768,768]{2,1,0:T(8,128)(2,1)} %build.4.t1.t2.t3.t4.t5, bf16[5,768,768]{2,1,0:T(8,128)(2,1)} %build.4.t1.t2.t3.t4.t5, bf16[5,768,768]{2,1,0:T(8,128)(2,1)} %build.4.t1.t2.t3.t4.t5, bf16[5,768,768]{2,1,0:T(8,128)(2,1)} %build.4.t1.t2.t3.t4.t5, ...), custom_call_target="tpu_custom_call" | custom-call | flops 4227858432 | bytes 6291456 | tf_op jit(solution)/shard_map/most_sum/pallas_call | solution.py:215
  63.7 2.0 %collective-permute-done.11.x0 = bf16[768,512]{1,0:T(8,128)(2,1)S(1)} collective-permute-done((bf16[768,512]{1,0:T(8,128)(2,1)}, bf16[768,512]{1,0:T(8,128)(2,1)S(1)}, u32[]{:S(2)}, u32[]{:S(2)}) %collective-permute-start.11) | collective-permute-done | bytes 786464 | tf_op jit(solution)/shard_map/ppermute | solution.py:275
  65.7 2.7 %collective-permute-start.12 = (bf16[768,512]{1,0:T(8,128)(2,1)S(1)}, bf16[768,512]{1,0:T(8,128)(2,1)S(1)}, u32[]{:S(2)}, u32[]{:S(2)}) collective-permute-start(bf16[768,512]{1,0:T(8,128)(2,1)S(1)} %collective-permute-done.11.x0), channel_id=1, source_target_pairs={{0,1},{1,0},{2,3},{3,2},{4,5},{5,4},{6,7},{7,6},{8,9},{9,8},{10,11... | collective-permute-start | bytes 2359304 | tf_op jit(solution)/shard_map/ppermute | solution.py:309
  68.4 1.9 %collective-permute-done.12.x1 = bf16[768,512]{1,0:T(8,128)(2,1)S(1)} collective-permute-done((bf16[768,512]{1,0:T(8,128)(2,1)S(1)}, bf16[768,512]{1,0:T(8,128)(2,1)S(1)}, u32[]{:S(2)}, u32[]{:S(2)}) %collective-permute-start.12) | collective-permute-done | bytes 786464 | tf_op jit(solution)/shard_map/ppermute | solution.py:309
  71.7 3.2 %last_sum.1 = (f32[768,512]{1,0:T(8,128)S(1)}, f32[16,2,16,512]{3,2,1,0:T(8,128)S(1)}, f32[16,2,16,512]{3,2,1,0:T(8,128)S(1)}) custom-call(f32[768,512]{1,0:T(8,128)S(1)} %copy-done.1, bf16[2,768,768]{2,1,0:T(8,128)(2,1)S(1)} %copy-done, bf16[768,512]{1,0:T(8,128)(2,1)S(1)} %collective-permute-done.11.x0, bf16[768,512]{1,0:T(8,128)(2,1)S(1)} %collective-permute-done.12.x1, ...), custom_call_target="tpu_custom_call" | custom-call | flops 1811939328 | bytes 6291456 | tf_op jit(solution)/shard_map/last_sum/pallas_call | solution.py:232
  75.4 2.3 %collective-permute-done.13 = f32[16,2,16,512]{3,2,1,0:T(8,128)S(1)} collective-permute-done((f32[16,2,16,512]{3,2,1,0:T(8,128)S(1)}, f32[16,2,16,512]{3,2,1,0:T(8,128)S(1)}, u32[]{:S(2)}, u32[]{:S(2)}) %collective-permute-start.13) | collective-permute-done | bytes 1048608 | tf_op jit(solution)/shard_map/ppermute | solution.py:309
  77.9 20.9 %all_to_all.15 = f32[16,2,16,512]{3,2,1,0:T(8,128)} all-to-all(f32[16,2,16,512]{3,2,1,0:T(8,128)S(1)} %add.15), channel_id=1, replica_groups=mesh['group'=4,'z'=8,'y'=4,'core'=2] {'group','y'}, dimensions={0} | all-to-all | bytes 2097152 | tf_op jit(solution)/shard_map/all_to_all | solution.py:367
  100.1 2.7 %collective-permute-start.14 = (f32[2,16,512]{2,1,0:T(8,128)S(1)}, f32[2,16,512]{2,1,0:T(8,128)S(1)}, u32[]{:S(2)}, u32[]{:S(2)}) collective-permute-start(f32[2,16,512]{2,1,0:T(8,128)S(1)} %reduce_sum.9), channel_id=1, source_target_pairs={{0,32},{8,40},{16,48},{24,56},{32,0},{40,8},{48,16},{56,24},{1,33}... | collective-permute-start | bytes 196616 | tf_op jit(solution)/shard_map/ppermute | solution.py:370
  102.8 2.8 %finish.1 = f32[768,512]{1,0:T(8,128)} custom-call(f32[768,512]{1,0:T(8,128)S(1)} %get-tuple-element.52.summed, bf16[768,512]{1,0:T(8,128)(2,1)S(1)} %copy-done.2, bf16[512,512]{1,0:T(8,128)(2,1)S(1)} %copy-done.4, bf16[512,512]{1,0:T(8,128)(2,1)S(1)} %copy-done.5), custom_call_target="tpu_custom_call" | custom-call | flops 1207959552 | bytes 3932160 | tf_op jit(solution)/shard_map/finish/pallas_call | solution.py:259
  107.3 2.9 %collective-permute-start.17 = (f32[2,16,512]{2,1,0:T(8,128)S(1)}, f32[2,16,512]{2,1,0:T(8,128)S(1)}, u32[]{:S(2)}, u32[]{:S(2)}) collective-permute-start(f32[2,16,512]{2,1,0:T(8,128)S(1)} %add.16), channel_id=1, source_target_pairs={{0,24},{8,16},{16,8},{24,0},{32,56},{40,48},{48,40},{56,32},{1,25}... | collective-permute-start | bytes 196616 | tf_op jit(solution)/shard_map/ppermute | solution.py:370
  114.3 13.7 %all_to_all.16.mine = bf16[16,3,16,512]{3,2,1,0:T(8,128)(2,1)S(1)} all-to-all(bf16[16,3,16,512]{3,2,1,0:T(8,128)(2,1)S(1)} %broadcast_in_dim.2), channel_id=1, replica_groups=mesh['group'=4,'z'=8,'y'=4,'core'=2] {'group','y'}, dimensions={0} | all-to-all | bytes 1572864 | tf_op jit(solution)/shard_map/all_to_all | solution.py:378
  128.0 5.5 %collective-permute-start.18 = (bf16[16,3,16,512]{3,2,1,0:T(8,128)(2,1)S(1)}, bf16[16,3,16,512]{3,2,1,0:T(8,128)(2,1)S(1)}, u32[]{:S(2)}, u32[]{:S(2)}) collective-permute-start(bf16[16,3,16,512]{3,2,1,0:T(8,128)(2,1)S(1)} %all_to_all.16.mine), channel_id=1, source_target_pairs={{0,1},{1,0},{2,3},{3,2},{4,5},{5,4},{6,7},{7,6},{8,9},{9,8},{10,11... | collective-permute-start | bytes 2359304 | tf_op jit(solution)/shard_map/ppermute | solution.py:309
  133.5 1.9 %collective-permute-done.18.theirs = bf16[16,3,16,512]{3,2,1,0:T(8,128)(2,1)S(1)} collective-permute-done((bf16[16,3,16,512]{3,2,1,0:T(8,128)(2,1)S(1)}, bf16[16,3,16,512]{3,2,1,0:T(8,128)(2,1)S(1)}, u32[]{:S(2)}, u32[]{:S(2)}) %collective-permute-start.18) | collective-permute-done | bytes 786464 | tf_op jit(solution)/shard_map/ppermute | solution.py:309
  (75 shorter events, 21.5 us)
Async XLA Ops:
  0.6 24.3 %collective-permute-start = (bf16[768,512]{1,0:T(8,128)(2,1)}, bf16[768,512]{1,0:T(8,128)(2,1)S(1)}, u32[]{:S(2)}, u32[]{:S(2)}) collective-permute-start(bf16[768,512]{1,0:T(8,128)(2,1)} %cot.5), channel_id=1, source_target_pairs={{0,56},{8,0},{16,8},{24,16},{32,24},{40,32},{48,40},{56,48},{1,57}... | collective-permute-start | bytes 2359304 | tf_op jit(solution)/shard_map/ppermute | solution.py:280
  11.7 12.1 %collective-permute-start.1 = (s32[2,2048]{1,0:T(2,128)}, s32[2,2048]{1,0:T(2,128)S(1)}, u32[]{:S(2)}, u32[]{:S(2)}) collective-permute-start(s32[2,2048]{1,0:T(2,128)} %get-tuple-element.32), channel_id=1, source_target_pairs={{0,56},{8,0},{16,8},{24,16},{32,24},{40,32},{48,40},{56,48},{1,57}... | collective-permute-start | bytes 49160 | tf_op jit(solution)/shard_map/ppermute | solution.py:280
  12.5 11.7 %collective-permute-start.2 = (s32[2,2048]{1,0:T(2,128)}, s32[2,2048]{1,0:T(2,128)S(1)}, u32[]{:S(2)}, u32[]{:S(2)}) collective-permute-start(s32[2,2048]{1,0:T(2,128)} %get-tuple-element.33), channel_id=1, source_target_pairs={{0,62},{1,63},{2,0},{3,1},{4,2},{5,3},{6,4},{7,5},{8,6},{9,7},{10,... | collective-permute-start | bytes 49160 | tf_op jit(solution)/shard_map/ppermute | solution.py:275
  15.7 8.9 %collective-permute-start.3 = (s32[2,2048]{1,0:T(2,128)}, s32[2,2048]{1,0:T(2,128)S(1)}, u32[]{:S(2)}, u32[]{:S(2)}) collective-permute-start(s32[2,2048]{1,0:T(2,128)} %get-tuple-element.34), channel_id=1, source_target_pairs={{0,60},{1,61},{2,62},{3,63},{4,0},{5,1},{6,2},{7,3},{8,4},{9,5},{1... | collective-permute-start | bytes 49160 | tf_op jit(solution)/shard_map/ppermute | solution.py:275
  16.1 8.9 %collective-permute-start.4 = (s32[2,2048]{1,0:T(2,128)}, s32[2,2048]{1,0:T(2,128)S(1)}, u32[]{:S(2)}, u32[]{:S(2)}) collective-permute-start(s32[2,2048]{1,0:T(2,128)} %get-tuple-element.35), channel_id=1, source_target_pairs={{0,58},{1,59},{2,60},{3,61},{4,62},{5,63},{6,0},{7,1},{8,2},{9,3},... | collective-permute-start | bytes 49160 | tf_op jit(solution)/shard_map/ppermute | solution.py:275
  26.7 19.0 %collective-permute-start.8 = (bf16[768,512]{1,0:T(8,128)(2,1)}, bf16[768,512]{1,0:T(8,128)(2,1)S(1)}, u32[]{:S(2)}, u32[]{:S(2)}) collective-permute-start(bf16[768,512]{1,0:T(8,128)(2,1)} %get-tuple-element.57), channel_id=1, source_target_pairs={{0,2},{2,4},{4,6},{6,0},{1,3},{3,5},{5,7},{7,1},{8,10},{10,12},{12... | collective-permute-start | bytes 2359304 | tf_op jit(solution)/shard_map/ppermute | solution.py:280
  27.6 18.0 %collective-permute-start.7 = (bf16[768,512]{1,0:T(8,128)(2,1)}, bf16[768,512]{1,0:T(8,128)(2,1)}, u32[]{:S(2)}, u32[]{:S(2)}) collective-permute-start(bf16[768,512]{1,0:T(8,128)(2,1)} %get-tuple-element.58), channel_id=1, source_target_pairs={{0,6},{2,0},{4,2},{6,4},{1,7},{3,1},{5,3},{7,5},{8,14},{10,8},{12,... | collective-permute-start | bytes 2359304 | tf_op jit(solution)/shard_map/ppermute | solution.py:280
  29.3 16.3 %collective-permute-start.6 = (bf16[768,512]{1,0:T(8,128)(2,1)}, bf16[768,512]{1,0:T(8,128)(2,1)S(1)}, u32[]{:S(2)}, u32[]{:S(2)}) collective-permute-start(bf16[768,512]{1,0:T(8,128)(2,1)} %get-tuple-element.59), channel_id=1, source_target_pairs={{0,1},{1,0},{2,3},{3,2},{4,5},{5,4},{6,7},{7,6},{8,9},{9,8},{10,11... | collective-permute-start | bytes 2359304 | tf_op jit(solution)/shard_map/ppermute | solution.py:309
  31.6 4.3 %collective-permute-start.5 = (s32[4,2048]{1,0:T(4,128)S(1)}, s32[4,2048]{1,0:T(4,128)S(1)}, u32[]{:S(2)}, u32[]{:S(2)}) collective-permute-start(s32[4,2048]{1,0:T(4,128)S(1)} %pad_add_fusion), channel_id=1, source_target_pairs={{0,1},{1,0},{2,3},{3,2},{4,5},{5,4},{6,7},{7,6},{8,9},{9,8},{10,11... | collective-permute-start | bytes 98312 | tf_op jit(solution)/shard_map/ppermute | solution.py:309
  31.9 20.0 %all-to-all-start = ((bf16[4,256,512]{2,1,0:T(8,128)(2,1)}), bf16[4,256,512]{2,1,0:T(8,128)(2,1)S(1)}, u32[]{:S(2)}, u32[]{:S(2)}) async-start(bf16[4,256,512]{2,1,0:T(8,128)(2,1)} %get-tuple-element.47), calls=%async_computation | async-start | bytes 2097152 | tf_op jit(solution)/shard_map/all_to_all | solution.py:326
  46.7 7.4 %collective-permute-start.9 = (bf16[768,512]{1,0:T(8,128)(2,1)}, bf16[768,512]{1,0:T(8,128)(2,1)}, u32[]{:S(2)}, u32[]{:S(2)}) collective-permute-start(bf16[768,512]{1,0:T(8,128)(2,1)} %collective-permute-done.7.x2), channel_id=1, source_target_pairs={{0,1},{1,0},{2,3},{3,2},{4,5},{5,4},{6,7},{7,6},{8,9},{9,8},{10,11... | collective-permute-start | bytes 2359304 | tf_op jit(solution)/shard_map/ppermute | solution.py:309
  50.7 3.3 %collective-permute-start.10 = (bf16[768,512]{1,0:T(8,128)(2,1)S(1)}, bf16[768,512]{1,0:T(8,128)(2,1)}, u32[]{:S(2)}, u32[]{:S(2)}) collective-permute-start(bf16[768,512]{1,0:T(8,128)(2,1)S(1)} %collective-permute-done.8.x3), channel_id=1, source_target_pairs={{0,1},{1,0},{2,3},{3,2},{4,5},{5,4},{6,7},{7,6},{8,9},{9,8},{10,11... | collective-permute-start | bytes 2359304 | tf_op jit(solution)/shard_map/ppermute | solution.py:309
  50.7 14.9 %collective-permute-start.11 = (bf16[768,512]{1,0:T(8,128)(2,1)}, bf16[768,512]{1,0:T(8,128)(2,1)S(1)}, u32[]{:S(2)}, u32[]{:S(2)}) collective-permute-start(bf16[768,512]{1,0:T(8,128)(2,1)} %broadcast_select_fusion), channel_id=1, source_target_pairs={{0,62},{1,3},{2,0},{3,5},{4,2},{5,7},{6,4},{7,9},{8,6},{9,11},{10,... | collective-permute-start | bytes 2359304 | tf_op jit(solution)/shard_map/ppermute | solution.py:275
  54.1 16.2 %copy-start = (bf16[2,768,768]{2,1,0:T(8,128)(2,1)S(1)}, bf16[2,768,768]{2,1,0:T(8,128)(2,1)}, u32[]{:S(2)}) copy-start(bf16[2,768,768]{2,1,0:T(8,128)(2,1)} %build.5.tiles) | copy-start | bytes 7077892
  54.1 16.2 %copy-start.2 = (bf16[768,512]{1,0:T(8,128)(2,1)S(1)}, bf16[768,512]{1,0:T(8,128)(2,1)}, u32[]{:S(2)}) copy-start(bf16[768,512]{1,0:T(8,128)(2,1)} %cot.5) | copy-start | bytes 2359300
  65.7 4.6 %collective-permute-start.12 = (bf16[768,512]{1,0:T(8,128)(2,1)S(1)}, bf16[768,512]{1,0:T(8,128)(2,1)S(1)}, u32[]{:S(2)}, u32[]{:S(2)}) collective-permute-start(bf16[768,512]{1,0:T(8,128)(2,1)S(1)} %collective-permute-done.11.x0), channel_id=1, source_target_pairs={{0,1},{1,0},{2,3},{3,2},{4,5},{5,4},{6,7},{7,6},{8,9},{9,8},{10,11... | collective-permute-start | bytes 2359304 | tf_op jit(solution)/shard_map/ppermute | solution.py:309
  74.9 2.8 %collective-permute-start.13 = (f32[16,2,16,512]{3,2,1,0:T(8,128)S(1)}, f32[16,2,16,512]{3,2,1,0:T(8,128)S(1)}, u32[]{:S(2)}, u32[]{:S(2)}) collective-permute-start(f32[16,2,16,512]{3,2,1,0:T(8,128)S(1)} %get-tuple-element.51), channel_id=1, source_target_pairs={{0,1},{1,0},{2,3},{3,2},{4,5},{5,4},{6,7},{7,6},{8,9},{9,8},{10,11... | collective-permute-start | bytes 3145736 | tf_op jit(solution)/shard_map/ppermute | solution.py:309
  77.9 24.9 %copy-start.4 = (bf16[512,512]{1,0:T(8,128)(2,1)S(1)}, bf16[512,512]{1,0:T(8,128)(2,1)}, u32[]{:S(2)}) copy-start(bf16[512,512]{1,0:T(8,128)(2,1)} %w_self.1) | copy-start | bytes 1572868
  77.9 24.9 %copy-start.5 = (bf16[512,512]{1,0:T(8,128)(2,1)S(1)}, bf16[512,512]{1,0:T(8,128)(2,1)}, u32[]{:S(2)}) copy-start(bf16[512,512]{1,0:T(8,128)(2,1)} %w_neigh.1) | copy-start | bytes 1572868
  100.1 7.1 %collective-permute-start.14 = (f32[2,16,512]{2,1,0:T(8,128)S(1)}, f32[2,16,512]{2,1,0:T(8,128)S(1)}, u32[]{:S(2)}, u32[]{:S(2)}) collective-permute-start(f32[2,16,512]{2,1,0:T(8,128)S(1)} %reduce_sum.9), channel_id=1, source_target_pairs={{0,32},{8,40},{16,48},{24,56},{32,0},{40,8},{48,16},{56,24},{1,33}... | collective-permute-start | bytes 196616 | tf_op jit(solution)/shard_map/ppermute | solution.py:370
  107.3 5.1 %collective-permute-start.17 = (f32[2,16,512]{2,1,0:T(8,128)S(1)}, f32[2,16,512]{2,1,0:T(8,128)S(1)}, u32[]{:S(2)}, u32[]{:S(2)}) collective-permute-start(f32[2,16,512]{2,1,0:T(8,128)S(1)} %add.16), channel_id=1, source_target_pairs={{0,24},{8,16},{16,8},{24,0},{32,56},{40,48},{48,40},{56,32},{1,25}... | collective-permute-start | bytes 196616 | tf_op jit(solution)/shard_map/ppermute | solution.py:370
  110.1 4.0 %collective-permute-start.16 = (f32[2,16,512]{2,1,0:T(8,128)S(1)}, f32[2,16,512]{2,1,0:T(8,128)S(1)}, u32[]{:S(2)}, u32[]{:S(2)}) collective-permute-start(f32[2,16,512]{2,1,0:T(8,128)S(1)} %add.16), channel_id=1, source_target_pairs={{0,16},{8,24},{16,0},{24,8},{32,48},{40,56},{48,32},{56,40},{1,17}... | collective-permute-start | bytes 196616 | tf_op jit(solution)/shard_map/ppermute | solution.py:370
  110.1 4.0 %collective-permute-start.15 = (f32[2,16,512]{2,1,0:T(8,128)S(1)}, f32[2,16,512]{2,1,0:T(8,128)S(1)}, u32[]{:S(2)}, u32[]{:S(2)}) collective-permute-start(f32[2,16,512]{2,1,0:T(8,128)S(1)} %add.16), channel_id=1, source_target_pairs={{0,8},{8,0},{16,24},{24,16},{32,40},{40,32},{48,56},{56,48},{1,9},... | collective-permute-start | bytes 196616 | tf_op jit(solution)/shard_map/ppermute | solution.py:370
  128.0 7.4 %collective-permute-start.18 = (bf16[16,3,16,512]{3,2,1,0:T(8,128)(2,1)S(1)}, bf16[16,3,16,512]{3,2,1,0:T(8,128)(2,1)S(1)}, u32[]{:S(2)}, u32[]{:S(2)}) collective-permute-start(bf16[16,3,16,512]{3,2,1,0:T(8,128)(2,1)S(1)} %all_to_all.16.mine), channel_id=1, source_target_pairs={{0,1},{1,0},{2,3},{3,2},{4,5},{5,4},{6,7},{7,6},{8,9},{9,8},{10,11... | collective-permute-start | bytes 2359304 | tf_op jit(solution)/shard_map/ppermute | solution.py:309
  (12 other events, 80.0 us)

commit v10 on v9

--- a/solution.py
+++ b/solution.py
@@ -219,7 +219,7 @@
         + [whole(v.shape) for v in (*xs, ids, rows)],
         out_specs=row_spec(width),
         out_shape=jax.ShapeDtypeStruct((nodes, width), F32),
-        compiler_params=params(56),
+        compiler_params=params(60),
         cost_estimate=estimate(7 * nodes * nodes * width, 16 * nodes * width),
         name="most_sum",
     )(near, *([five] * 5), *xs, ids, rows)
@@ -325,7 +325,8 @@
     ]
     returned = lax.all_to_all(rows, "group", split_axis=0, concat_axis=0, tiled=True)
     near = run_build(((own, 0),), nodes)
-    x, far, deep, pairs = fence((x, far, deep, pairs, near))[:4]
+    ids = send_ids.reshape(1, ngroup * cap)
+    x, far, deep, pairs, ids = fence((x, far, deep, pairs, ids, near))[:5]
     degree = deep[1, :nodes].astype(F32)
     inverse = 1.0 / jnp.maximum(degree, 1.0)
     far = (inverse[:, None] * far.astype(F32)).astype(BF16)
@@ -353,7 +354,7 @@
         near,
         five,
         (x, side, one, three, one_b, three_b),
-        send_ids.reshape(1, ngroup * cap),
+        ids,
         returned.reshape(ngroup * cap, width),
     )
     two = fence((two, summed))[0]

time: 137 us -> 139 us (1.015)
  starting transfers between devices: 40.6 us -> 37.6 us
  Pallas kernels: 33.6 us -> 35.1 us
  local copies, waits for them, and re-layouts: 2.79 us -> 4.21 us
    ppermute x7, starting transfers between devices: 15.2 us -> 10.7 us  [swapped(): return lax.ppermute(v, 'core', swap)]
    ppermute x4, starting transfers between devices: 6.32 us -> 7.96 us  [zflip(): return lax.ppermute(v, 'z', [(i, i ^ k) for i in range(nz)])]
    unnamed x33 -> x39, local copies, waits for them, and re-layouts: 2.67 us -> 4.09 us
  transfers between devices with their start and end apart: 20 -> 20, of which waited for: 12 -> 13; matrix products, arithmetic and copies ran while one was open for 1% -> 1% of each run, Pallas kernels for 21% -> 21%
where the time goes in v10:
time: 139 us; the launch traced here: 138 us
  starting transfers between devices  37.6 us (27%)
  blocking collectives  36 us (26%)
  Pallas kernels  35.1 us (25%)
  waiting for transfers between devices  19.9 us (14%)
  other arithmetic  4.47 us (3%)
  local copies, waits for them, and re-layouts  4.21 us (3%)
    all_to_all x2, blocking collectives, on_device(): lax.all_to_all(part, ('group', 'y'), split_axis=0, concat_axis=0, tiled=T...  36 us
    pallas_call x3, Pallas kernels, run_build(): pl.pallas_call(functools.partial(build, rows), grid=(slots,), in_specs=[w...  12.1 us
    ppermute x7, starting transfers between devices, swapped(): return lax.ppermute(v, 'core', swap)  10.7 us
    ppermute x4, starting transfers between devices, turned(): lax.ppermute(value, axis, [(i, (i + by) % length) for i in range(length)])  9.97 us
    pallas_call x1, Pallas kernels, run_most(): pl.pallas_call(most_sum, grid=(nodes // BLOCK,), in_specs=[tile_spec(s, n...  9.63 us
    ppermute x7, waiting for transfers between devices, swapped(): return lax.ppermute(v, 'core', swap)  8.67 us
    ppermute x4, starting transfers between devices, zflip(): return lax.ppermute(v, 'z', [(i, i ^ k) for i in range(nz)])  7.96 us
    ppermute x4, starting transfers between devices, moved(): return lax.ppermute(value, BLK, perm)  4.98 us
  transfers between devices with their start and end apart: 20, of which 13 were waited for; matrix products, arithmetic and copies ran while one was open for 1% of the time, Pallas kernels for 21%

profile of v10, /device:TPU:1, one launch (start us, length us, event | category | flops | bytes accessed | tf_op | source)
XLA Modules:
  0.0 138.3 jit_solution(5037288116369790679)
XLA Ops:
  0.6 6.5 %collective-permute-start = (bf16[768,512]{1,0:T(8,128)(2,1)}, bf16[768,512]{1,0:T(8,128)(2,1)S(1)}, u32[]{:S(2)}, u32[]{:S(2)}) collective-permute-start(bf16[768,512]{1,0:T(8,128)(2,1)} %cot.5), channel_id=1, source_target_pairs={{0,56},{8,0},{16,8},{24,16},{32,24},{40,32},{48,40},{56,48},{1,57}... | collective-permute-start | bytes 2359304 | tf_op jit(solution)/shard_map/ppermute | solution.py:280
  7.1 4.6 %prepare.1 = (bf16[768,512]{1,0:T(8,128)(2,1)}, bf16[4,256,512]{2,1,0:T(8,128)(2,1)}, s32[1,2048]{1,0:T(1,128)}, s32[1,2048]{1,0:T(1,128)}, s32[2,2048]{1,0:T(2,...) custom-call(s32[1,8]{1,0:T(1,128)} %tcount.1, s32[1,4]{1,0:T(1,128)} %rcount.1, ...), custom_call_target="tpu_custom_call" | custom-call | flops 805306368 | bytes 854040 | tf_op jit(solution)/shard_map/prepare/pallas_call | solution.py:184
  12.6 3.2 %collective-permute-start.2 = (s32[2,2048]{1,0:T(2,128)}, s32[2,2048]{1,0:T(2,128)S(1)}, u32[]{:S(2)}, u32[]{:S(2)}) collective-permute-start(s32[2,2048]{1,0:T(2,128)} %get-tuple-element.34), channel_id=1, source_target_pairs={{0,62},{1,63},{2,0},{3,1},{4,2},{5,3},{6,4},{7,5},{8,6},{9,7},{10,... | collective-permute-start | bytes 49160 | tf_op jit(solution)/shard_map/ppermute | solution.py:275
  17.8 2.0 %build.3.t0 = bf16[1,768,768]{2,1,0:T(8,128)(2,1)} custom-call(s32[1,2048]{1,0:T(1,128)} %get-tuple-element.31.refs_0_), custom_call_target="tpu_custom_call" | custom-call | flops 3145728 | bytes 1572864 | tf_op jit(solution)/shard_map/build/pallas_call | solution.py:200
  19.8 4.1 %collective-permute-done.1 = s32[2,2048]{1,0:T(2,128)S(1)} collective-permute-done((s32[2,2048]{1,0:T(2,128)}, s32[2,2048]{1,0:T(2,128)S(1)}, u32[]{:S(2)}, u32[]{:S(2)}) %collective-permute-start.1) | collective-permute-done | bytes 16416 | tf_op jit(solution)/shard_map/ppermute | solution.py:280
  27.7 1.7 %collective-permute-start.7 = (bf16[768,512]{1,0:T(8,128)(2,1)}, bf16[768,512]{1,0:T(8,128)(2,1)S(1)}, u32[]{:S(2)}, u32[]{:S(2)}) collective-permute-start(bf16[768,512]{1,0:T(8,128)(2,1)} %get-tuple-element.60), channel_id=1, source_target_pairs={{0,6},{2,0},{4,2},{6,4},{1,7},{3,1},{5,3},{7,5},{8,14},{10,8},{12,... | collective-permute-start | bytes 2359304 | tf_op jit(solution)/shard_map/ppermute | solution.py:280
  29.4 2.1 %collective-permute-start.6 = (bf16[768,512]{1,0:T(8,128)(2,1)}, bf16[768,512]{1,0:T(8,128)(2,1)S(1)}, u32[]{:S(2)}, u32[]{:S(2)}) collective-permute-start(bf16[768,512]{1,0:T(8,128)(2,1)} %get-tuple-element.61), channel_id=1, source_target_pairs={{0,1},{1,0},{2,3},{3,2},{4,5},{5,4},{6,7},{7,6},{8,9},{9,8},{10,11... | collective-permute-start | bytes 2359304 | tf_op jit(solution)/shard_map/ppermute | solution.py:309
  31.9 4.0 %all-to-all-start = ((bf16[4,256,512]{2,1,0:T(8,128)(2,1)}), bf16[4,256,512]{2,1,0:T(8,128)(2,1)S(1)}, u32[]{:S(2)}, u32[]{:S(2)}) async-start(bf16[4,256,512]{2,1,0:T(8,128)(2,1)} %get-tuple-element.49), calls=%async_computation | async-start | bytes 2097152 | tf_op jit(solution)/shard_map/all_to_all | solution.py:326
  36.6 3.7 %build.5.tiles = bf16[2,768,768]{2,1,0:T(8,128)(2,1)} custom-call(s32[2,2048]{1,0:T(2,128)} %copy-done.15, s32[4,2048]{1,0:T(4,128)} %copy-done.13), custom_call_target="tpu_custom_call" | custom-call | flops 3145728 | bytes 1572864 | tf_op jit(solution)/shard_map/build/pallas_call | solution.py:200
  40.3 6.4 %build.4.t1.t2.t3.t4.t5 = bf16[5,768,768]{2,1,0:T(8,128)(2,1)} custom-call(s32[4,2048]{1,0:T(4,128)} %copy-done.13, s32[2,2048]{1,0:T(2,128)} %copy-done.14, s32[2,2048]{1,0:T(2,128)} %copy-done.16, s32[4,2048]{1,0:T(4,128)} %copy-done.13, s32[4,2048]{1,0:T(4,128)} %copy-done.13), custom_call_target="tpu_custom_call" | custom-call | flops 3145728 | bytes 1572864 | tf_op jit(solution)/shard_map/build/pallas_call | solution.py:200
  52.7 9.6 %most_sum.1.before = f32[768,512]{1,0:T(8,128)} custom-call(bf16[1,768,768]{2,1,0:T(8,128)(2,1)} %build.3.t0, bf16[5,768,768]{2,1,0:T(8,128)(2,1)} %build.4.t1.t2.t3.t4.t5, bf16[5,768,768]{2,1,0:T(8,128)(2,1)} %build.4.t1.t2.t3.t4.t5, bf16[5,768,768]{2,1,0:T(8,128)(2,1)} %build.4.t1.t2.t3.t4.t5, bf16[5,768,768]{2,1,0:T(8,128)(2,1)} %build.4.t1.t2.t3.t4.t5, ...), custom_call_target="tpu_custom_call" | custom-call | flops 4227858432 | bytes 6291456 | tf_op jit(solution)/shard_map/most_sum/pallas_call | solution.py:215
  62.4 2.0 %collective-permute-done.11.x0 = bf16[768,512]{1,0:T(8,128)(2,1)} collective-permute-done((bf16[768,512]{1,0:T(8,128)(2,1)}, bf16[768,512]{1,0:T(8,128)(2,1)}, u32[]{:S(2)}, u32[]{:S(2)}) %collective-permute-start.11) | collective-permute-done | bytes 786464 | tf_op jit(solution)/shard_map/ppermute | solution.py:275
  64.4 2.0 %collective-permute-start.12 = (bf16[768,512]{1,0:T(8,128)(2,1)}, bf16[768,512]{1,0:T(8,128)(2,1)S(1)}, u32[]{:S(2)}, u32[]{:S(2)}) collective-permute-start(bf16[768,512]{1,0:T(8,128)(2,1)} %collective-permute-done.11.x0), channel_id=1, source_target_pairs={{0,1},{1,0},{2,3},{3,2},{4,5},{5,4},{6,7},{7,6},{8,9},{9,8},{10,11... | collective-permute-start | bytes 2359304 | tf_op jit(solution)/shard_map/ppermute | solution.py:309
  66.4 2.1 %collective-permute-done.12.x1 = bf16[768,512]{1,0:T(8,128)(2,1)S(1)} collective-permute-done((bf16[768,512]{1,0:T(8,128)(2,1)}, bf16[768,512]{1,0:T(8,128)(2,1)S(1)}, u32[]{:S(2)}, u32[]{:S(2)}) %collective-permute-start.12) | collective-permute-done | bytes 786464 | tf_op jit(solution)/shard_map/ppermute | solution.py:309
  69.9 4.4 %last_sum.1 = (f32[768,512]{1,0:T(8,128)S(1)}, f32[16,2,16,512]{3,2,1,0:T(8,128)S(1)}, f32[16,2,16,512]{3,2,1,0:T(8,128)S(1)}) custom-call(f32[768,512]{1,0:T(8,128)S(1)} %copy-done.1, bf16[2,768,768]{2,1,0:T(8,128)(2,1)S(1)} %copy-done, bf16[768,512]{1,0:T(8,128)(2,1)} %collective-permute-done.11.x0, bf16[768,512]{1,0:T(8,128)(2,1)S(1)} %collective-permute-done.12.x1, ...), custom_call_target="tpu_custom_call" | custom-call | flops 1811939328 | bytes 6291456 | tf_op jit(solution)/shard_map/last_sum/pallas_call | solution.py:232
  74.9 2.3 %collective-permute-done.13 = f32[16,2,16,512]{3,2,1,0:T(8,128)S(1)} collective-permute-done((f32[16,2,16,512]{3,2,1,0:T(8,128)S(1)}, f32[16,2,16,512]{3,2,1,0:T(8,128)S(1)}, u32[]{:S(2)}, u32[]{:S(2)}) %collective-permute-start.13) | collective-permute-done | bytes 1048608 | tf_op jit(solution)/shard_map/ppermute | solution.py:309
  77.5 20.2 %all_to_all.15 = f32[16,2,16,512]{3,2,1,0:T(8,128)} all-to-all(f32[16,2,16,512]{3,2,1,0:T(8,128)S(1)} %add.15), channel_id=1, replica_groups=mesh['group'=4,'z'=8,'y'=4,'core'=2] {'group','y'}, dimensions={0} | all-to-all | bytes 2097152 | tf_op jit(solution)/shard_map/all_to_all | solution.py:368
  99.0 4.3 %collective-permute-start.14 = (f32[2,16,512]{2,1,0:T(8,128)S(1)}, f32[2,16,512]{2,1,0:T(8,128)S(1)}, u32[]{:S(2)}, u32[]{:S(2)}) collective-permute-start(f32[2,16,512]{2,1,0:T(8,128)S(1)} %reduce_sum.9), channel_id=1, source_target_pairs={{0,32},{8,40},{16,48},{24,56},{32,0},{40,8},{48,16},{56,24},{1,33}... | collective-permute-start | bytes 196616 | tf_op jit(solution)/shard_map/ppermute | solution.py:371
  104.7 2.8 %finish.1 = f32[768,512]{1,0:T(8,128)} custom-call(f32[768,512]{1,0:T(8,128)S(1)} %copy-done.4, bf16[768,512]{1,0:T(8,128)(2,1)S(1)} %copy-done.2, bf16[512,512]{1,0:T(8,128)(2,1)S(1)} %copy-done.6, bf16[512,512]{1,0:T(8,128)(2,1)S(1)} %copy-done.7), custom_call_target="tpu_custom_call" | custom-call | flops 1207959552 | bytes 3932160 | tf_op jit(solution)/shard_map/finish/pallas_call | solution.py:259
  107.5 3.2 %collective-permute-start.17 = (f32[2,16,512]{2,1,0:T(8,128)S(1)}, f32[2,16,512]{2,1,0:T(8,128)S(1)}, u32[]{:S(2)}, u32[]{:S(2)}) collective-permute-start(f32[2,16,512]{2,1,0:T(8,128)S(1)} %add.16), channel_id=1, source_target_pairs={{0,24},{8,16},{16,8},{24,0},{32,56},{40,48},{48,40},{56,32},{1,25}... | collective-permute-start | bytes 196616 | tf_op jit(solution)/shard_map/ppermute | solution.py:371
  112.5 2.2 %collective-permute-done.16 = f32[2,16,512]{2,1,0:T(8,128)S(1)} collective-permute-done((f32[2,16,512]{2,1,0:T(8,128)S(1)}, f32[2,16,512]{2,1,0:T(8,128)S(1)}, u32[]{:S(2)}, u32[]{:S(2)}) %collective-permute-start.16) | collective-permute-done | bytes 65568 | tf_op jit(solution)/shard_map/ppermute | solution.py:371
  114.9 15.8 %all_to_all.16.mine = bf16[16,3,16,512]{3,2,1,0:T(8,128)(2,1)S(1)} all-to-all(bf16[16,3,16,512]{3,2,1,0:T(8,128)(2,1)S(1)} %broadcast_in_dim.2), channel_id=1, replica_groups=mesh['group'=4,'z'=8,'y'=4,'core'=2] {'group','y'}, dimensions={0} | all-to-all | bytes 1572864 | tf_op jit(solution)/shard_map/all_to_all | solution.py:379
  130.7 4.2 %collective-permute-start.18 = (bf16[16,3,16,512]{3,2,1,0:T(8,128)(2,1)S(1)}, bf16[16,3,16,512]{3,2,1,0:T(8,128)(2,1)S(1)}, u32[]{:S(2)}, u32[]{:S(2)}) collective-permute-start(bf16[16,3,16,512]{3,2,1,0:T(8,128)(2,1)S(1)} %all_to_all.16.mine), channel_id=1, source_target_pairs={{0,1},{1,0},{2,3},{3,2},{4,5},{5,4},{6,7},{7,6},{8,9},{9,8},{10,11... | collective-permute-start | bytes 2359304 | tf_op jit(solution)/shard_map/ppermute | solution.py:309
  134.9 1.9 %collective-permute-done.18.theirs = bf16[16,3,16,512]{3,2,1,0:T(8,128)(2,1)S(1)} collective-permute-done((bf16[16,3,16,512]{3,2,1,0:T(8,128)(2,1)S(1)}, bf16[16,3,16,512]{3,2,1,0:T(8,128)(2,1)S(1)}, u32[]{:S(2)}, u32[]{:S(2)}) %collective-permute-start.18) | collective-permute-done | bytes 786464 | tf_op jit(solution)/shard_map/ppermute | solution.py:309
  (81 shorter events, 21.9 us)
Async XLA Ops:
  0.6 16.6 %copy-start.18 = (s32[1,4,256]{2,1,0:T(4,128)S(1)}, s32[1,4,256]{2,1,0:T(4,128)}, u32[]{:S(2)}) copy-start(s32[1,4,256]{2,1,0:T(4,128)} %param.17) | copy-start | bytes 12292
  0.6 24.3 %collective-permute-start = (bf16[768,512]{1,0:T(8,128)(2,1)}, bf16[768,512]{1,0:T(8,128)(2,1)S(1)}, u32[]{:S(2)}, u32[]{:S(2)}) collective-permute-start(bf16[768,512]{1,0:T(8,128)(2,1)} %cot.5), channel_id=1, source_target_pairs={{0,56},{8,0},{16,8},{24,16},{32,24},{40,32},{48,40},{56,48},{1,57}... | collective-permute-start | bytes 2359304 | tf_op jit(solution)/shard_map/ppermute | solution.py:280
  11.8 12.1 %collective-permute-start.1 = (s32[2,2048]{1,0:T(2,128)}, s32[2,2048]{1,0:T(2,128)S(1)}, u32[]{:S(2)}, u32[]{:S(2)}) collective-permute-start(s32[2,2048]{1,0:T(2,128)} %get-tuple-element.33), channel_id=1, source_target_pairs={{0,56},{8,0},{16,8},{24,16},{32,24},{40,32},{48,40},{56,48},{1,57}... | collective-permute-start | bytes 49160 | tf_op jit(solution)/shard_map/ppermute | solution.py:280
  12.6 11.7 %collective-permute-start.2 = (s32[2,2048]{1,0:T(2,128)}, s32[2,2048]{1,0:T(2,128)S(1)}, u32[]{:S(2)}, u32[]{:S(2)}) collective-permute-start(s32[2,2048]{1,0:T(2,128)} %get-tuple-element.34), channel_id=1, source_target_pairs={{0,62},{1,63},{2,0},{3,1},{4,2},{5,3},{6,4},{7,5},{8,6},{9,7},{10,... | collective-permute-start | bytes 49160 | tf_op jit(solution)/shard_map/ppermute | solution.py:275
  15.7 8.9 %collective-permute-start.3 = (s32[2,2048]{1,0:T(2,128)}, s32[2,2048]{1,0:T(2,128)S(1)}, u32[]{:S(2)}, u32[]{:S(2)}) collective-permute-start(s32[2,2048]{1,0:T(2,128)} %get-tuple-element.35), channel_id=1, source_target_pairs={{0,60},{1,61},{2,62},{3,63},{4,0},{5,1},{6,2},{7,3},{8,4},{9,5},{1... | collective-permute-start | bytes 49160 | tf_op jit(solution)/shard_map/ppermute | solution.py:275
  16.1 8.9 %collective-permute-start.4 = (s32[2,2048]{1,0:T(2,128)}, s32[2,2048]{1,0:T(2,128)S(1)}, u32[]{:S(2)}, u32[]{:S(2)}) collective-permute-start(s32[2,2048]{1,0:T(2,128)} %get-tuple-element.36), channel_id=1, source_target_pairs={{0,58},{1,59},{2,60},{3,61},{4,62},{5,63},{6,0},{7,1},{8,2},{9,3},... | collective-permute-start | bytes 49160 | tf_op jit(solution)/shard_map/ppermute | solution.py:275
  26.7 20.0 %collective-permute-start.8 = (bf16[768,512]{1,0:T(8,128)(2,1)}, bf16[768,512]{1,0:T(8,128)(2,1)S(1)}, u32[]{:S(2)}, u32[]{:S(2)}) collective-permute-start(bf16[768,512]{1,0:T(8,128)(2,1)} %get-tuple-element.59), channel_id=1, source_target_pairs={{0,2},{2,4},{4,6},{6,0},{1,3},{3,5},{5,7},{7,1},{8,10},{10,12},{12... | collective-permute-start | bytes 2359304 | tf_op jit(solution)/shard_map/ppermute | solution.py:280
  27.7 19.1 %collective-permute-start.7 = (bf16[768,512]{1,0:T(8,128)(2,1)}, bf16[768,512]{1,0:T(8,128)(2,1)S(1)}, u32[]{:S(2)}, u32[]{:S(2)}) collective-permute-start(bf16[768,512]{1,0:T(8,128)(2,1)} %get-tuple-element.60), channel_id=1, source_target_pairs={{0,6},{2,0},{4,2},{6,4},{1,7},{3,1},{5,3},{7,5},{8,14},{10,8},{12,... | collective-permute-start | bytes 2359304 | tf_op jit(solution)/shard_map/ppermute | solution.py:280
  29.4 17.3 %collective-permute-start.6 = (bf16[768,512]{1,0:T(8,128)(2,1)}, bf16[768,512]{1,0:T(8,128)(2,1)S(1)}, u32[]{:S(2)}, u32[]{:S(2)}) collective-permute-start(bf16[768,512]{1,0:T(8,128)(2,1)} %get-tuple-element.61), channel_id=1, source_target_pairs={{0,1},{1,0},{2,3},{3,2},{4,5},{5,4},{6,7},{7,6},{8,9},{9,8},{10,11... | collective-permute-start | bytes 2359304 | tf_op jit(solution)/shard_map/ppermute | solution.py:309
  31.6 4.3 %collective-permute-start.5 = (s32[4,2048]{1,0:T(4,128)S(1)}, s32[4,2048]{1,0:T(4,128)S(1)}, u32[]{:S(2)}, u32[]{:S(2)}) collective-permute-start(s32[4,2048]{1,0:T(4,128)S(1)} %pad_add_fusion), channel_id=1, source_target_pairs={{0,1},{1,0},{2,3},{3,2},{4,5},{5,4},{6,7},{7,6},{8,9},{9,8},{10,11... | collective-permute-start | bytes 98312 | tf_op jit(solution)/shard_map/ppermute | solution.py:309
  31.9 18.4 %all-to-all-start = ((bf16[4,256,512]{2,1,0:T(8,128)(2,1)}), bf16[4,256,512]{2,1,0:T(8,128)(2,1)S(1)}, u32[]{:S(2)}, u32[]{:S(2)}) async-start(bf16[4,256,512]{2,1,0:T(8,128)(2,1)} %get-tuple-element.49), calls=%async_computation | async-start | bytes 2097152 | tf_op jit(solution)/shard_map/all_to_all | solution.py:326
  47.8 3.7 %collective-permute-start.9 = (bf16[768,512]{1,0:T(8,128)(2,1)S(1)}, bf16[768,512]{1,0:T(8,128)(2,1)}, u32[]{:S(2)}, u32[]{:S(2)}) collective-permute-start(bf16[768,512]{1,0:T(8,128)(2,1)S(1)} %collective-permute-done.7.x2), channel_id=1, source_target_pairs={{0,1},{1,0},{2,3},{3,2},{4,5},{5,4},{6,7},{7,6},{8,9},{9,8},{10,11... | collective-permute-start | bytes 2359304 | tf_op jit(solution)/shard_map/ppermute | solution.py:309
  49.5 3.2 %collective-permute-start.10 = (bf16[768,512]{1,0:T(8,128)(2,1)S(1)}, bf16[768,512]{1,0:T(8,128)(2,1)}, u32[]{:S(2)}, u32[]{:S(2)}) collective-permute-start(bf16[768,512]{1,0:T(8,128)(2,1)S(1)} %collective-permute-done.8.x3), channel_id=1, source_target_pairs={{0,1},{1,0},{2,3},{3,2},{4,5},{5,4},{6,7},{7,6},{8,9},{9,8},{10,11... | collective-permute-start | bytes 2359304 | tf_op jit(solution)/shard_map/ppermute | solution.py:309
  49.5 14.9 %collective-permute-start.11 = (bf16[768,512]{1,0:T(8,128)(2,1)}, bf16[768,512]{1,0:T(8,128)(2,1)}, u32[]{:S(2)}, u32[]{:S(2)}) collective-permute-start(bf16[768,512]{1,0:T(8,128)(2,1)} %broadcast_select_fusion), channel_id=1, source_target_pairs={{0,62},{1,3},{2,0},{3,5},{4,2},{5,7},{6,4},{7,9},{8,6},{9,11},{10,... | collective-permute-start | bytes 2359304 | tf_op jit(solution)/shard_map/ppermute | solution.py:275
  52.7 15.8 %copy-start = (bf16[2,768,768]{2,1,0:T(8,128)(2,1)S(1)}, bf16[2,768,768]{2,1,0:T(8,128)(2,1)}, u32[]{:S(2)}) copy-start(bf16[2,768,768]{2,1,0:T(8,128)(2,1)} %build.5.tiles) | copy-start | bytes 7077892
  64.4 4.1 %collective-permute-start.12 = (bf16[768,512]{1,0:T(8,128)(2,1)}, bf16[768,512]{1,0:T(8,128)(2,1)S(1)}, u32[]{:S(2)}, u32[]{:S(2)}) collective-permute-start(bf16[768,512]{1,0:T(8,128)(2,1)} %collective-permute-done.11.x0), channel_id=1, source_target_pairs={{0,1},{1,0},{2,3},{3,2},{4,5},{5,4},{6,7},{7,6},{8,9},{9,8},{10,11... | collective-permute-start | bytes 2359304 | tf_op jit(solution)/shard_map/ppermute | solution.py:309
  74.4 2.8 %collective-permute-start.13 = (f32[16,2,16,512]{3,2,1,0:T(8,128)S(1)}, f32[16,2,16,512]{3,2,1,0:T(8,128)S(1)}, u32[]{:S(2)}, u32[]{:S(2)}) collective-permute-start(f32[16,2,16,512]{3,2,1,0:T(8,128)S(1)} %get-tuple-element.53), channel_id=1, source_target_pairs={{0,1},{1,0},{2,3},{3,2},{4,5},{5,4},{6,7},{7,6},{8,9},{9,8},{10,11... | collective-permute-start | bytes 3145736 | tf_op jit(solution)/shard_map/ppermute | solution.py:309
  77.4 25.9 %copy-start.6 = (bf16[512,512]{1,0:T(8,128)(2,1)S(1)}, bf16[512,512]{1,0:T(8,128)(2,1)}, u32[]{:S(2)}) copy-start(bf16[512,512]{1,0:T(8,128)(2,1)} %w_self.1) | copy-start | bytes 1572868
  77.4 25.9 %copy-start.7 = (bf16[512,512]{1,0:T(8,128)(2,1)S(1)}, bf16[512,512]{1,0:T(8,128)(2,1)}, u32[]{:S(2)}) copy-start(bf16[512,512]{1,0:T(8,128)(2,1)} %w_neigh.1) | copy-start | bytes 1572868
  99.0 8.5 %collective-permute-start.14 = (f32[2,16,512]{2,1,0:T(8,128)S(1)}, f32[2,16,512]{2,1,0:T(8,128)S(1)}, u32[]{:S(2)}, u32[]{:S(2)}) collective-permute-start(f32[2,16,512]{2,1,0:T(8,128)S(1)} %reduce_sum.9), channel_id=1, source_target_pairs={{0,32},{8,40},{16,48},{24,56},{32,0},{40,8},{48,16},{56,24},{1,33}... | collective-permute-start | bytes 196616 | tf_op jit(solution)/shard_map/ppermute | solution.py:371
  107.5 5.0 %collective-permute-start.17 = (f32[2,16,512]{2,1,0:T(8,128)S(1)}, f32[2,16,512]{2,1,0:T(8,128)S(1)}, u32[]{:S(2)}, u32[]{:S(2)}) collective-permute-start(f32[2,16,512]{2,1,0:T(8,128)S(1)} %add.16), channel_id=1, source_target_pairs={{0,24},{8,16},{16,8},{24,0},{32,56},{40,48},{48,40},{56,32},{1,25}... | collective-permute-start | bytes 196616 | tf_op jit(solution)/shard_map/ppermute | solution.py:371
  110.7 4.0 %collective-permute-start.16 = (f32[2,16,512]{2,1,0:T(8,128)S(1)}, f32[2,16,512]{2,1,0:T(8,128)S(1)}, u32[]{:S(2)}, u32[]{:S(2)}) collective-permute-start(f32[2,16,512]{2,1,0:T(8,128)S(1)} %add.16), channel_id=1, source_target_pairs={{0,16},{8,24},{16,0},{24,8},{32,48},{40,56},{48,32},{56,40},{1,17}... | collective-permute-start | bytes 196616 | tf_op jit(solution)/shard_map/ppermute | solution.py:371
  110.7 4.0 %collective-permute-start.15 = (f32[2,16,512]{2,1,0:T(8,128)S(1)}, f32[2,16,512]{2,1,0:T(8,128)S(1)}, u32[]{:S(2)}, u32[]{:S(2)}) collective-permute-start(f32[2,16,512]{2,1,0:T(8,128)S(1)} %add.16), channel_id=1, source_target_pairs={{0,8},{8,0},{16,24},{24,16},{32,40},{40,32},{48,56},{56,48},{1,9},... | collective-permute-start | bytes 196616 | tf_op jit(solution)/shard_map/ppermute | solution.py:371
  130.7 6.1 %collective-permute-start.18 = (bf16[16,3,16,512]{3,2,1,0:T(8,128)(2,1)S(1)}, bf16[16,3,16,512]{3,2,1,0:T(8,128)(2,1)S(1)}, u32[]{:S(2)}, u32[]{:S(2)}) collective-permute-start(bf16[16,3,16,512]{3,2,1,0:T(8,128)(2,1)S(1)} %all_to_all.16.mine), channel_id=1, source_target_pairs={{0,1},{1,0},{2,3},{3,2},{4,5},{5,4},{6,7},{7,6},{8,9},{9,8},{10,11... | collective-permute-start | bytes 2359304 | tf_op jit(solution)/shard_map/ppermute | solution.py:309
  (15 other events, 99.0 us)
